TPU v7x, 32 devices: a whole 2x2x4 slice. The times are simulated.
32 devices in a mesh: feat: 16 (over z, x, core), tok: 2 (over y).
Axes of the slice: x: 2, y: 2, z: 4, core: 2. Of those that a mesh axis runs over, the one named last changes fastest.
Arguments:
- features: bfloat16 [256, 131072], P('tok', 'feat'), may hold values from -6 to 6
- signs: int32 [131072], P('feat'), may hold values from -1 to 1, as said below
- columns: int32 [1024], replicated, may hold values from 0 to 131071, as said below
- labels: int32 [256, 1], P('tok'), may hold values from 0 to 31; in each aligned block of 128 rows (0 to 127, 128 to 255, ...) at most 8 rows name the same one
Outputs:
- gram: float32 [32, 1024, 1024], P('tok', 'feat')
Inputs may be any that keep to these rules, and one draw needn't show every extreme that they name: `signs`: every entry is -1 or 1. `columns`: the 1024 indices are distinct. `labels`: among the rows of one device no concept appears more than 8 times.
All inputs are finite; a program needn't handle non-finite values.
Results may differ from a plain program's by a relative error of at most 0.004.
Values may be sent and summed in bfloat16 or wider, within the bound.
No kernel may reach another device: no remote copies, remote signals or barrier semaphores. Data moves between devices by JAX's collectives and lax.ppermute only.
A program may use at most 64 MiB of HBM per device.

v0:
```python
import math

import jax
import jax.numpy as jnp
from jax import lax
from jax.sharding import PartitionSpec as P

C = 32


def from_partner(array, axis, distance):
    return lax.ppermute(array, axis, [(i, i ^ 1 << distance) for i in range(lax.axis_size(axis))])


def bit_parity(number, bit_count):
    total = jnp.zeros_like(number)
    for position in range(bit_count):
        total = total ^ number >> position & 1
    return total


def sylvester(order, dtype):
    index = lax.iota(jnp.int32, order)
    parity = bit_parity(index[:, None] & index[None, :], order.bit_length())
    return (1 - 2 * parity).astype(dtype)


def body(features, signs, columns, labels):
    rows, width = features.shape
    feat_count = lax.axis_size("feat")
    feat_index = lax.axis_index("feat")
    tok_count = lax.axis_size("tok")
    kept = columns.shape[0]
    shard_cols = kept // feat_count
    flat_labels = labels[:, 0]
    signed = features * signs.astype(jnp.bfloat16)[None, :]
    transformed = jnp.dot(
        signed, sylvester(width, jnp.bfloat16), preferred_element_type=jnp.float32
    )
    local_col = columns % width
    owner = columns // width
    sections = feat_count.bit_length() - 1
    for section in range(sections):
        partner = from_partner(transformed, "feat", section)
        upper = feat_index >> section & 1 == 1
        transformed = jnp.where(upper, partner - transformed, transformed + partner)
    picked = jnp.take(transformed, local_col, axis=1)
    owned = (owner == feat_index)[None, :]
    combined = lax.psum(jnp.where(owned, picked, 0.0), "feat")
    sketch = (combined * (1.0 / math.sqrt(width * feat_count))).astype(jnp.bfloat16)
    factor = C / (rows * tok_count)
    own_rows = lax.dynamic_slice_in_dim(sketch, feat_index * shard_cols, shard_cols, 1)
    wanted = lax.iota(jnp.int32, C // tok_count * lax.axis_size("tok"))
    onehot = (flat_labels[:, None] == wanted[None, :]).astype(jnp.bfloat16)
    weighted = (onehot[:, :, None] * own_rows[:, None, :]).reshape(
        rows, C // tok_count * lax.axis_size("tok") * shard_cols
    )
    partial_gram = jnp.einsum("rm,rk->mk", weighted, sketch, preferred_element_type=jnp.float32)
    return lax.psum_scatter(
        partial_gram.reshape(C // tok_count * lax.axis_size("tok"), shard_cols, kept) * factor,
        "tok",
        scatter_dimension=0,
        tiled=True,
    )


def solution(mesh):
    in_specs = (P("tok", "feat"), P("feat"), P(), P("tok", None))
    out_specs = P("tok", "feat", None)
    return jax.shard_map(body, mesh=mesh, in_specs=in_specs, out_specs=out_specs, check_vma=False)
```

profile of v0, /device:TPU:0, one launch (start us, length us, event | category | flops | bytes accessed | tf_op | source)
XLA Modules:
  0.0 1021.4 jit_solution(2561984469271374101)
XLA Ops:
  6.5 0.8 convert_element_type.17
  7.3 1.7 fusion.29
  9.0 396.6 %fusion = f32[128,8192]{1,0:T(8,128)} fusion(bf16[128,8192]{1,0:T(8,128)(2,1)S(1)} %fusion.29), kind=kOutput, calls=%fused_computation.2 | convolution fusion | flops 20199768064 | bytes 6291456 | tf_op jit(solution)/shard_map/dot_general | solution.py:37
  405.6 0.5 collective-permute-start
  406.0 7.1 collective-permute-done
  413.2 6.1 add_select_fusion.3
  419.2 2.8 collective-permute-start.1
  422.0 91.2 %collective-permute-done.1 = f32[128,8192]{1,0:T(8,128)} collective-permute-done((f32[128,8192]{1,0:T(8,128)}, f32[128,8192]{1,0:T(8,128)}, u32[]{:S(2)}, u32[]{:S(2)}) %collective-permute-start.1) | collective-permute-done | bytes 4194336 | tf_op jit(solution)/shard_map/ppermute | solution.py:12
  513.2 6.1 add_select_fusion.2
  519.3 1.9 collective-permute-start.2
  521.2 90.5 %collective-permute-done.2 = f32[128,8192]{1,0:T(8,128)} collective-permute-done((f32[128,8192]{1,0:T(8,128)}, f32[128,8192]{1,0:T(8,128)}, u32[]{:S(2)}, u32[]{:S(2)}) %collective-permute-start.2) | collective-permute-done | bytes 4194336 | tf_op jit(solution)/shard_map/ppermute | solution.py:12
  611.7 6.1 add_select_fusion.1
  617.8 2.5 collective-permute-start.3
  620.3 179.7 %collective-permute-done.3 = f32[128,8192]{1,0:T(8,128)} collective-permute-done((f32[128,8192]{1,0:T(8,128)}, f32[128,8192]{1,0:T(8,128)}, u32[]{:S(2)}, u32[]{:S(2)}) %collective-permute-start.3) | collective-permute-done | bytes 4194336 | tf_op jit(solution)/shard_map/ppermute | solution.py:12
  800.1 6.1 add_select_fusion
  806.1 5.6 copy.5
  811.7 5.0 gather_fusion
  816.7 0.2 copy.6
  816.9 0.9 select_bitcast_fusion
  817.9 90.9 %all-reduce.2.cloned.1.call-done = f32[128,1024]{1,0:T(8,128)} async-done(((f32[128,1024]{1,0:T(8,128)}), f32[128,1024]{1,0:T(8,128)}) %all-reduce.2.cloned.1.call-update) | async-done | bytes 524304 | tf_op jit(solution)/shard_map/psum | solution.py:49
  908.8 1.1 multiply_convert_fusion
  909.9 0.1 constant_dynamic-slice_fusion
  910.1 4.5 broadcast_multiply_fusion
  914.6 99.9 %reduce-scatter.2.cloned.1.call-done = f32[16,64,1024]{2,1,0:T(8,128)} async-done(((f32[32,64,1024]{2,1,0:T(8,128)}), f32[16,64,1024]{2,1,0:T(8,128)}) %reduce-scatter.2.cloned.1.call-update) | async-done | bytes 4194320 | tf_op jit(solution)/shard_map/reduce_scatter | solution.py:59
  (12 shorter events, 0.2 us)
Async XLA Ops:
  6.5 902.3 %all-reduce.2.cloned.1.call-start = ((), (), s32[]{:S(2)}) async-start(), calls=%async_computation.1 | async-start | bytes 1048576 | tf_op jit(solution)/shard_map/psum | solution.py:49
  405.6 7.6 collective-permute-start
  419.2 94.0 %collective-permute-start.1 = (f32[128,8192]{1,0:T(8,128)}, f32[128,8192]{1,0:T(8,128)}, u32[]{:S(2)}, u32[]{:S(2)}) collective-permute-start(f32[128,8192]{1,0:T(8,128)} %add_select_fusion.3), channel_id=1, source_target_pairs={{0,4},{2,6},{4,0},{6,2},{8,12},{10,14},{12,8},{14,10},{16,20},{18,... | collective-permute-start | bytes 12582920 | tf_op jit(solution)/shard_map/ppermute | solution.py:12
  519.3 101.0 %copy-start = (s32[1024]{0:T(1024)S(1)}, s32[1024]{0:T(1024)}, u32[]{:S(2)}) copy-start(s32[1024]{0:T(1024)} %param.6) | copy-start | bytes 12292
  519.3 92.4 %collective-permute-start.2 = (f32[128,8192]{1,0:T(8,128)}, f32[128,8192]{1,0:T(8,128)}, u32[]{:S(2)}, u32[]{:S(2)}) collective-permute-start(f32[128,8192]{1,0:T(8,128)} %add_select_fusion.2), channel_id=1, source_target_pairs={{0,8},{2,10},{4,12},{6,14},{8,0},{10,2},{12,4},{14,6},{16,24},{18,... | collective-permute-start | bytes 12582920 | tf_op jit(solution)/shard_map/ppermute | solution.py:12
  617.8 182.3 %collective-permute-start.3 = (f32[128,8192]{1,0:T(8,128)}, f32[128,8192]{1,0:T(8,128)}, u32[]{:S(2)}, u32[]{:S(2)}) collective-permute-start(f32[128,8192]{1,0:T(8,128)} %add_select_fusion.1), channel_id=1, source_target_pairs={{0,16},{2,18},{4,20},{6,22},{8,24},{10,26},{12,28},{14,30},{16,0},... | collective-permute-start | bytes 12582920 | tf_op jit(solution)/shard_map/ppermute | solution.py:12
  806.1 11.7 %copy-start.1 = (s32[128,1]{0,1:T(1,128)S(1)}, s32[128,1]{0,1:T(1,128)}, u32[]{:S(2)}) copy-start(s32[128,1]{0,1:T(1,128)} %param.7) | copy-start | bytes 1540
  817.8 196.7 %reduce-scatter.2.cloned.1.call-start = ((), (), s32[]{:S(2)}) async-start(), calls=%async_computation.2 | async-start | bytes 12582912 | tf_op jit(solution)/shard_map/reduce_scatter | solution.py:59
Sparse Core Ops, SparseCore 0:
  817.9 90.8 all-reduce.1
  914.7 99.7 reduce-scatter.1
where the time goes:
time: 1020 us
  waiting for transfers between devices  559 us (55%)
  matrix products  401 us (39%)
  other arithmetic  28.7 us (3%)
  between operations  13.5 us (1%)
  local copies, waits for them, and re-layouts  11 us (1%)
    dot_general x1, matrix products, body(): jnp.dot(signed, sylvester(width, jnp.bfloat16), preferred_element_type=jn...  397 us
    ppermute x4, waiting for transfers between devices, from_partner(): lax.ppermute(array, axis, [(i, i ^ 1 << distance) for i in range(lax.axis...  369 us
    reduce_scatter x1, waiting for transfers between devices, body(): lax.psum_scatter(partial_gram.reshape(C // tok_count * lax.axis_size('tok...  99.9 us
    psum x1, waiting for transfers between devices, body(): combined = lax.psum(jnp.where(owned, picked, 0.0), 'feat')  90.9 us
    select_n x4, other arithmetic, body(): transformed = jnp.where(upper, partner - transformed, transformed + partner)  24.3 us
  transfers between devices with their start and end apart: 6, of which 6 were waited for; matrix products, arithmetic and copies ran while one was open for 0% of the time, Pallas kernels for 0%

commit v1 on v0

v1 whole, which is shorter than its diff:
```python
import functools
import math

import jax
import jax.numpy as jnp
from jax import lax
from jax.experimental import pallas as pl
from jax.experimental.pallas import tpu as pltpu
from jax.sharding import PartitionSpec as P

C = 32
LOW = 256
LANES = 128
VMEM_LIMIT = 48 * 1024 * 1024


def parity_sign(number, bit_count):
    shift = 1
    while shift < bit_count:
        shift *= 2
    while shift > 1:
        shift //= 2
        number = number ^ (number >> shift)
    return (1 - 2 * (number & 1)).astype(jnp.float32)


def partial_kernel(high_count, total_bits, x_ref, s_ref, col_ref, send_ref, keep_ref, low, high, acc):
    step = pl.program_id(0)
    kept = col_ref.shape[1]
    blocks = x_ref.shape[1] // LOW
    me = lax.axis_index("feat")

    @pl.when(step == 0)
    def _():
        col = col_ref[...]
        low_index = lax.broadcasted_iota(jnp.int32, (LOW, kept), 0)
        low[...] = parity_sign(low_index & col, 8).astype(jnp.bfloat16)
        high_index = lax.broadcasted_iota(jnp.int32, high.shape, 0) + me * high_count
        high[...] = parity_sign(high_index & (col >> 8), total_bits - 8)
        acc[...] = jnp.zeros_like(acc)

    signs = s_ref[...].astype(jnp.bfloat16)
    signed = x_ref[...] * signs
    for part in range(kept // LOW):
        cols = slice(part * LOW, (part + 1) * LOW)
        table = low[:, cols]
        total = acc[:, cols]
        for block in range(blocks):
            inner = jnp.dot(
                signed[:, block * LOW:(block + 1) * LOW], table, preferred_element_type=jnp.float32
            )
            total = total + inner * high[pl.ds(step * blocks + block, 1), cols]
        acc[:, cols] = total

    @pl.when(step == pl.num_programs(0) - 1)
    def _():
        half = keep_ref.shape[0]
        mine = lax.rem(me, 2)
        keep_ref[...] = acc[pl.ds(pl.multiple_of(mine * half, half), half), :]
        send_ref[...] = acc[pl.ds(pl.multiple_of((1 - mine) * half, half), half), :]


def partial_halves(features, signs, columns, feat_count):
    rows, width = features.shape
    kept = columns.shape[0]
    step_width = min(width, 2048)
    high_count = width // LOW
    total_bits = (width * feat_count).bit_length() - 1
    half = jax.ShapeDtypeStruct((rows // 2, kept), jnp.float32)
    return pl.pallas_call(
        functools.partial(partial_kernel, high_count, total_bits),
        grid=(width // step_width,),
        in_specs=[
            pl.BlockSpec((rows, step_width), lambda i: (0, i)),
            pl.BlockSpec((1, step_width), lambda i: (0, i)),
            pl.BlockSpec((1, kept), lambda i: (0, 0)),
        ],
        out_specs=[pl.BlockSpec((rows // 2, kept), lambda i: (0, 0))] * 2,
        out_shape=[half, half],
        scratch_shapes=[
            pltpu.VMEM((LOW, kept), jnp.bfloat16),
            pltpu.VMEM((high_count, kept), jnp.float32),
            pltpu.VMEM((rows, kept), jnp.float32),
        ],
        compiler_params=pltpu.CompilerParams(vmem_limit_bytes=VMEM_LIMIT),
        cost_estimate=pl.CostEstimate(
            flops=2 * rows * width * kept, bytes_accessed=2 * rows * width + 4 * rows * kept, transcendentals=0
        ),
        name="partial_transform",
    )(features, signs.reshape(1, width), columns.reshape(1, kept))


def gram_kernel(shard, group, factor, a_ref, b_ref, out_ref, own):
    step = pl.program_id(0)
    kept = out_ref.shape[1]
    wide = group * shard
    steps = pl.num_programs(0)

    @pl.when(step == 0)
    def _():
        first = lax.axis_index("feat") * shard
        source = lax.broadcasted_iota(jnp.int32, (kept, wide), 0)
        lane = lax.broadcasted_iota(jnp.int32, (kept, wide), 1)
        pick = jnp.where(source == first + (lane & (shard - 1)), 1.0, 0.0).astype(jnp.bfloat16)
        for at, ref in enumerate((a_ref, b_ref)):
            own[at] = jnp.dot(ref[:, :kept], pick, preferred_element_type=jnp.float32).astype(jnp.bfloat16)

    lane = lax.broadcasted_iota(jnp.int32, (a_ref.shape[0], wide), 1)
    concept = (lax.axis_index("tok") * steps + step) * group + lane // shard
    total = None
    for at, ref in enumerate((a_ref, b_ref)):
        label = ref[:, kept:kept + 1].astype(jnp.float32).astype(jnp.int32)
        chosen = jnp.where(label == concept, own[at].astype(jnp.float32), 0.0).astype(jnp.bfloat16)
        gram = lax.dot_general(
            chosen, ref[:, :kept], (((0,), (0,)), ((), ())), preferred_element_type=jnp.float32
        )
        total = gram if total is None else total + gram
    out_ref[...] = total * factor


def gram_blocks(ours, theirs, concepts, shard, kept, factor):
    tokens, lanes = ours.shape
    group = max(1, min(concepts, LOW // shard))
    return pl.pallas_call(
        functools.partial(gram_kernel, shard, group, factor),
        grid=(concepts // group,),
        in_specs=[pl.BlockSpec((tokens, lanes), lambda i: (0, 0))] * 2,
        out_specs=pl.BlockSpec((group * shard, kept), lambda i: (i, 0)),
        out_shape=jax.ShapeDtypeStruct((concepts * shard, kept), jnp.float32),
        scratch_shapes=[pltpu.VMEM((2, tokens, group * shard), jnp.bfloat16)],
        compiler_params=pltpu.CompilerParams(vmem_limit_bytes=VMEM_LIMIT),
        cost_estimate=pl.CostEstimate(
            flops=4 * tokens * concepts * shard * kept, bytes_accessed=4 * concepts * shard * kept, transcendentals=0
        ),
        name="gram",
    )(ours, theirs)


def body(features, signs, columns, labels):
    rows, width = features.shape
    feat_count = lax.axis_size("feat")
    feat_index = lax.axis_index("feat")
    tok_count = lax.axis_size("tok")
    kept = columns.shape[0]
    shard = kept // feat_count
    peers = feat_count // 2
    chunk = rows // feat_count
    core_pairs = [(i, i ^ 1) for i in range(feat_count)]
    feat_groups = [list(range(core, feat_count, 2)) for core in range(2)]
    all_groups = [list(range(core, tok_count * feat_count, 2)) for core in range(2)]

    send, keep = partial_halves(features, signs, columns, feat_count)
    half = keep + lax.ppermute(send, "feat", core_pairs)
    parts = lax.all_to_all(
        half.reshape(peers, chunk, kept), "feat", 0, 0, axis_index_groups=feat_groups, tiled=True
    )
    summed = jnp.sum(parts, axis=0)
    sketch = (summed * (1.0 / math.sqrt(width * feat_count))).astype(jnp.bfloat16)

    first = (feat_index & 1) * (rows // 2) + (feat_index >> 1) * chunk
    own_labels = lax.dynamic_slice_in_dim(labels, first, chunk, 0).astype(jnp.bfloat16)
    row = jnp.concatenate([sketch, jnp.broadcast_to(own_labels, (chunk, LANES))], axis=1)
    spread = jnp.broadcast_to(row[None], (tok_count * peers,) + row.shape)
    ours = lax.all_to_all(
        spread, ("tok", "feat"), 0, 0, axis_index_groups=all_groups, tiled=True
    ).reshape(tok_count * peers * chunk, kept + LANES)
    theirs = lax.ppermute(ours, "feat", core_pairs)
    concepts = C // tok_count
    gram = gram_blocks(ours, theirs, concepts, shard, kept, C / (rows * tok_count))
    return gram.reshape(concepts, shard, kept)


def solution(mesh):
    in_specs = (P("tok", "feat"), P("feat"), P(), P("tok", None))
    out_specs = P("tok", "feat", None)
    return jax.shard_map(body, mesh=mesh, in_specs=in_specs, out_specs=out_specs, check_vma=False)
```

time: 1020 us -> 46.3 us (0.05)
  waiting for transfers between devices: 559 us -> 11.9 us
  matrix products: 401 us -> 0 us
  other arithmetic: 28.7 us -> 0.84 us
  blocking collectives: 0 us -> 14.8 us
  between operations: 13.5 us -> 0.03 us
    dot_general x2 -> x0, matrix products: 401 us -> none  [the longest x1 397 us: body(): jnp.dot(signed, sylvester(width, jnp.bfloat16), preferred_element_type=jn...]
    ppermute x4 -> x2, waiting for transfers between devices: 369 us -> 2.74 us  [the longest x1 1.58 us: body(): theirs = lax.ppermute(ours, 'feat', core_pairs)]
    reduce_scatter x1 -> x0, waiting for transfers between devices: 99.9 us -> none  [body(): lax.psum_scatter(partial_gram.reshape(C // tok_count * lax.axis_size('tok...]
    psum x1 -> x0, waiting for transfers between devices: 90.9 us -> none  [body(): combined = lax.psum(jnp.where(owned, picked, 0.0), 'feat')]
    select_n x5 -> x0, other arithmetic: 25.1 us -> none  [the longest x4 24.3 us: body(): transformed = jnp.where(upper, partner - transformed, transformed + partner)]
    all_to_all x0 -> x1, blocking collectives: none -> 14.8 us  [body(): lax.all_to_all(spread, ('tok', 'feat'), 0, 0, axis_index_groups=all_group...]
  transfers between devices with their start and end apart: 6 -> 3, of which waited for: 6 -> 3; matrix products, arithmetic and copies ran while one was open for 0% -> 0% of each run, Pallas kernels for 0% -> 0%
where the time goes in v1:
time: 46.3 us; the launch traced here: 45.9 us
  blocking collectives  14.8 us (32%)
  waiting for transfers between devices  11.9 us (26%)
  starting transfers between devices  7.69 us (17%)
  Pallas kernels  7.55 us (16%)
  local copies, waits for them, and re-layouts  3.14 us (7%)
  other arithmetic  0.84 us (2%)
    all_to_all x1, blocking collectives, body(): lax.all_to_all(spread, ('tok', 'feat'), 0, 0, axis_index_groups=all_group...  14.8 us
    all_to_all x1, waiting for transfers between devices, body(): lax.all_to_all(half.reshape(peers, chunk, kept), 'feat', 0, 0, axis_index...  9.14 us
    all_to_all x1, starting transfers between devices, body(): lax.all_to_all(half.reshape(peers, chunk, kept), 'feat', 0, 0, axis_index...  7.17 us
    pallas_call x1, Pallas kernels, gram_blocks(): pl.pallas_call(functools.partial(gram_kernel, shard, group, factor), grid...  3.88 us
    pallas_call x1, Pallas kernels, partial_halves(): pl.pallas_call(functools.partial(partial_kernel, high_count, total_bits),...  3.68 us
    unnamed x8, local copies, waits for them, and re-layouts  3.04 us
    ppermute x1, waiting for transfers between devices, body(): theirs = lax.ppermute(ours, 'feat', core_pairs)  1.58 us
    ppermute x1, waiting for transfers between devices, body(): half = keep + lax.ppermute(send, 'feat', core_pairs)  1.16 us
  transfers between devices with their start and end apart: 3, of which 3 were waited for; matrix products, arithmetic and copies ran while one was open for 0% of the time, Pallas kernels for 0%

profile of v1, /device:TPU:0, one launch (start us, length us, event | category | flops | bytes accessed | tf_op | source)
XLA Modules:
  0.0 45.9 jit_solution(15991315769347496362)
XLA Ops:
  0.0 0.0 copy-start
  0.0 1.6 %copy-done = bf16[128,8192]{1,0:T(8,128)(2,1)S(1)} copy-done((bf16[128,8192]{1,0:T(8,128)(2,1)S(1)}, bf16[128,8192]{1,0:T(8,128)(2,1)}, u32[]{:S(2)}) %copy-start) | copy-done | bytes 2097176
  1.6 0.0 copy-start.1
  1.6 0.8 %copy-done.1 = s32[8192]{0:T(1024)S(1)} copy-done((s32[8192]{0:T(1024)S(1)}, s32[8192]{0:T(1024)}, u32[]{:S(2)}) %copy-start.1) | copy-done | bytes 32792
  2.4 0.0 copy-start.2
  2.4 0.7 %copy-done.2 = s32[1024]{0:T(1024)S(1)} copy-done((s32[1024]{0:T(1024)S(1)}, s32[1024]{0:T(1024)}, u32[]{:S(2)}) %copy-start.2) | copy-done | bytes 4120
  3.0 0.0 copy-start.3
  3.0 3.7 %partial_transform.1 = (f32[64,1024]{1,0:T(8,128)S(1)}, f32[64,1024]{1,0:T(8,128)S(1)}) custom-call(bf16[128,8192]{1,0:T(8,128)(2,1)S(1)} %copy-done, s32[1,8192]{1,0:T(1,128)S(1)} %bitcast.10, s32[1,1024]{1,0:T(1,128)S(1)} %bitcast.11), custom_call_target="tpu_custom_call" | custom-call | flops 2147483648 | bytes 2621440 | tf_op jit(solution)/shard_map/partial_transform/pallas_call | solution.py:70
  6.7 0.5 %collective-permute-start = (f32[64,1024]{1,0:T(8,128)S(1)}, f32[64,1024]{1,0:T(8,128)S(1)}, u32[]{:S(2)}, u32[]{:S(2)}) collective-permute-start(f32[64,1024]{1,0:T(8,128)S(1)} %get-tuple-element.8), channel_id=1, source_target_pairs={{0,2},{2,0},{4,6},{6,4},{8,10},{10,8},{12,14},{14,12},{16,18},{18,... | collective-permute-start | bytes 786440 | tf_op jit(solution)/shard_map/ppermute | solution.py:153
  7.2 1.2 %collective-permute-done = f32[64,1024]{1,0:T(8,128)S(1)} collective-permute-done((f32[64,1024]{1,0:T(8,128)S(1)}, f32[64,1024]{1,0:T(8,128)S(1)}, u32[]{:S(2)}, u32[]{:S(2)}) %collective-permute-start) | collective-permute-done | bytes 262176 | tf_op jit(solution)/shard_map/ppermute | solution.py:153
  8.4 0.7 %add_bitcast_fusion = f32[8,8,1024]{2,1,0:T(8,128)} fusion(f32[64,1024]{1,0:T(8,128)S(1)} %get-tuple-element.7, f32[64,1024]{1,0:T(8,128)S(1)} %collective-permute-done), kind=kLoop, calls=%fused_computation | loop fusion | flops 65536 | bytes 786432 | tf_op jit(solution)/shard_map/reshape | solution.py:155
  9.1 7.2 %all-to-all-start = ((f32[8,8,1024]{2,1,0:T(8,128)}), f32[8,8,1024]{2,1,0:T(8,128)S(1)}, u32[]{:S(2)}, u32[]{:S(2)}) async-start(f32[8,8,1024]{2,1,0:T(8,128)} %add_bitcast_fusion), calls=%async_computation | async-start | bytes 524288 | tf_op jit(solution)/shard_map/all_to_all | solution.py:154
  16.3 0.0 copy-done.3
  16.3 0.1 convert_bitcast_fusion
  16.4 9.1 %all-to-all-done = f32[8,8,1024]{2,1,0:T(8,128)S(1)} async-done(((f32[8,8,1024]{2,1,0:T(8,128)}), f32[8,8,1024]{2,1,0:T(8,128)S(1)}, u32[]{:S(2)}, u32[]{:S(2)}) %all-to-all-start) | async-done | bytes 262176 | tf_op jit(solution)/shard_map/all_to_all | solution.py:154
  25.6 0.1 broadcast_in_dim.14
  25.7 14.8 %all_to_all.10 = bf16[16,8,1152]{2,1,0:T(8,128)(2,1)S(1)} all-to-all(bf16[16,8,1152]{2,1,0:T(8,128)(2,1)S(1)} %broadcast_in_dim.15), channel_id=1, replica_groups={{0,4,8,12,16,20,24,28,1,5,9,13,17,21,25,29},{2,6,10,14,18,22,26,30,3,7,..., dimensions={0} | all-to-all | bytes 589824 | tf_op jit(solution)/shard_map/all_to_all | solution.py:164
  40.5 0.0 collective-permute-start.1
  40.5 1.6 %collective-permute-done.1.b_ref = bf16[128,1152]{1,0:T(8,128)(2,1)S(1)} collective-permute-done((bf16[128,1152]{1,0:T(8,128)(2,1)S(1)}, bf16[128,1152]{1,0:T(8,128)(2,1)S(1)}, u32[]{:S(2)}, u32[]{:S(2)}) %collective-permute-start.1) | collective-permute-done | bytes 294944 | tf_op jit(solution)/shard_map/ppermute | solution.py:167
  42.0 3.9 %gram.1 = f32[1024,1024]{1,0:T(8,128)} custom-call(bf16[128,1152]{1,0:T(8,128)(2,1)S(1)} %bitcast.9, bf16[128,1152]{1,0:T(8,128)(2,1)S(1)} %collective-permute-done.1.b_ref), custom_call_target="tpu_custom_call" | custom-call | flops 536870912 | bytes 4194304 | tf_op jit(solution)/shard_map/gram/pallas_call | solution.py:124
  (4 shorter events, 0.1 us)
Async XLA Ops:
  0.0 1.6 %copy-start = (bf16[128,8192]{1,0:T(8,128)(2,1)S(1)}, bf16[128,8192]{1,0:T(8,128)(2,1)}, u32[]{:S(2)}) copy-start(bf16[128,8192]{1,0:T(8,128)(2,1)} %x_ref.1) | copy-start | bytes 6291460
  1.6 0.8 %copy-start.1 = (s32[8192]{0:T(1024)S(1)}, s32[8192]{0:T(1024)}, u32[]{:S(2)}) copy-start(s32[8192]{0:T(1024)} %param.5) | copy-start | bytes 98308
  2.4 0.7 %copy-start.2 = (s32[1024]{0:T(1024)S(1)}, s32[1024]{0:T(1024)}, u32[]{:S(2)}) copy-start(s32[1024]{0:T(1024)} %param.6) | copy-start | bytes 12292
  3.0 13.3 %copy-start.3 = (s32[128,1]{0,1:T(1,128)S(1)}, s32[128,1]{0,1:T(1,128)}, u32[]{:S(2)}) copy-start(s32[128,1]{0,1:T(1,128)} %param.7) | copy-start | bytes 1540
  6.7 1.7 %collective-permute-start = (f32[64,1024]{1,0:T(8,128)S(1)}, f32[64,1024]{1,0:T(8,128)S(1)}, u32[]{:S(2)}, u32[]{:S(2)}) collective-permute-start(f32[64,1024]{1,0:T(8,128)S(1)} %get-tuple-element.8), channel_id=1, source_target_pairs={{0,2},{2,0},{4,6},{6,4},{8,10},{10,8},{12,14},{14,12},{16,18},{18,... | collective-permute-start | bytes 786440 | tf_op jit(solution)/shard_map/ppermute | solution.py:153
  9.1 16.4 %all-to-all-start = ((f32[8,8,1024]{2,1,0:T(8,128)}), f32[8,8,1024]{2,1,0:T(8,128)S(1)}, u32[]{:S(2)}, u32[]{:S(2)}) async-start(f32[8,8,1024]{2,1,0:T(8,128)} %add_bitcast_fusion), calls=%async_computation | async-start | bytes 524288 | tf_op jit(solution)/shard_map/all_to_all | solution.py:154
  40.5 1.6 %collective-permute-start.1 = (bf16[128,1152]{1,0:T(8,128)(2,1)S(1)}, bf16[128,1152]{1,0:T(8,128)(2,1)S(1)}, u32[]{:S(2)}, u32[]{:S(2)}) collective-permute-start(bf16[128,1152]{1,0:T(8,128)(2,1)S(1)} %bitcast.8), channel_id=1, source_target_pairs={{0,2},{2,0},{4,6},{6,4},{8,10},{10,8},{12,14},{14,12},{16,18},{18,... | collective-permute-start | bytes 884744 | tf_op jit(solution)/shard_map/ppermute | solution.py:167

commit v2 on v1

v2 whole, which is shorter than its diff:
```python
import functools
import math

import jax
import jax.numpy as jnp
from jax import lax
from jax.experimental import pallas as pl
from jax.experimental.pallas import tpu as pltpu
from jax.sharding import PartitionSpec as P

C = 32
LOW = 256
LANES = 128
VMEM_LIMIT = 48 * 1024 * 1024


def parity_sign(number, bit_count):
    shift = 1
    while shift < bit_count:
        shift *= 2
    while shift > 1:
        shift //= 2
        number = number ^ (number >> shift)
    return (1 - 2 * (number & 1)).astype(jnp.float32)


def partial_kernel(high_count, total_bits, parts, x_hbm, s_hbm, col_hbm, send_ref, keep_ref, x_buf, s_buf, col_buf, low, high, acc, sems):
    kept = col_hbm.shape[1]
    wide = x_hbm.shape[1] // parts
    me = lax.axis_index("feat")
    col_copy = pltpu.make_async_copy(col_hbm, col_buf, sems.at[parts])
    sign_copy = pltpu.make_async_copy(s_hbm, s_buf, sems.at[parts + 1])
    col_copy.start()
    sign_copy.start()
    copies = []
    for part in range(parts):
        cols = pl.ds(part * wide, wide)
        copies.append(pltpu.make_async_copy(x_hbm.at[:, cols], x_buf.at[:, cols], sems.at[part]))
        copies[-1].start()
    col_copy.wait()
    col = col_buf[...]
    index = lax.broadcasted_iota(jnp.int32, (16, kept), 0)
    inner = parity_sign(index & col, 4)
    outer = parity_sign(index & (col >> 4), 4)
    for row in range(LOW // 16):
        low[row * 16:(row + 1) * 16] = (inner * outer[row:row + 1]).astype(jnp.bfloat16)
    high_index = lax.broadcasted_iota(jnp.int32, high.shape, 0) + me * high_count
    high[...] = parity_sign(high_index & (col >> 8), total_bits - 8)
    sign_copy.wait()
    blocks = wide // LOW
    rows = x_hbm.shape[0]
    for part in range(parts):
        copies[part].wait()
        stack = []
        for block in range(part * blocks, (part + 1) * blocks):
            cols = slice(block * LOW, (block + 1) * LOW)
            stack.append(x_buf[:, cols] * s_buf[:, cols].astype(jnp.bfloat16))
        stack = jnp.concatenate(stack, axis=0)
        for group in range(kept // LOW):
            cols = slice(group * LOW, (group + 1) * LOW)
            products = jnp.dot(stack, low[:, cols], preferred_element_type=jnp.float32)
            total = None
            for at in range(blocks):
                row = part * blocks + at
                term = products[at * rows:(at + 1) * rows] * high[row:row + 1, cols]
                total = term if total is None else total + term
            if part > 0:
                total = total + acc[:, cols]
            acc[:, cols] = total
    half = keep_ref.shape[0]
    mine = lax.rem(me, 2)
    keep_ref[...] = acc[pl.ds(pl.multiple_of(mine * half, half), half), :]
    send_ref[...] = acc[pl.ds(pl.multiple_of((1 - mine) * half, half), half), :]


def partial_halves(features, signs, columns, feat_count):
    rows, width = features.shape
    kept = columns.shape[0]
    parts = max(1, width // 2048)
    high_count = width // LOW
    total_bits = (width * feat_count).bit_length() - 1
    half = jax.ShapeDtypeStruct((rows // 2, kept), jnp.float32)
    return pl.pallas_call(
        functools.partial(partial_kernel, high_count, total_bits, parts),
        in_specs=[pl.BlockSpec(memory_space=pltpu.HBM)] * 3,
        out_specs=[pl.BlockSpec(memory_space=pltpu.VMEM)] * 2,
        out_shape=[half, half],
        scratch_shapes=[
            pltpu.VMEM((rows, width), jnp.bfloat16),
            pltpu.VMEM((1, width), jnp.int32),
            pltpu.VMEM((1, kept), jnp.int32),
            pltpu.VMEM((LOW, kept), jnp.bfloat16),
            pltpu.VMEM((high_count, kept), jnp.float32),
            pltpu.VMEM((rows, kept), jnp.float32),
            pltpu.SemaphoreType.DMA((parts + 2,)),
        ],
        compiler_params=pltpu.CompilerParams(vmem_limit_bytes=VMEM_LIMIT),
        cost_estimate=pl.CostEstimate(
            flops=2 * rows * width * kept, bytes_accessed=2 * rows * width + 4 * rows * kept, transcendentals=0
        ),
        name="partial_transform",
    )(*(
        pltpu.with_memory_space_constraint(operand, pltpu.HBM)
        for operand in (features, signs.reshape(1, width), columns.reshape(1, kept))
    ))


def gram_kernel(shard, group, factor, a_ref, b_ref, out_ref, rows, own, label):
    step = pl.program_id(0)
    kept = out_ref.shape[1]
    wide = group * shard
    steps = pl.num_programs(0)
    half = a_ref.shape[0]

    @pl.when(step == 0)
    def _():
        first = lax.axis_index("feat") * shard
        source = lax.broadcasted_iota(jnp.int32, (kept, wide), 0)
        lane = lax.broadcasted_iota(jnp.int32, (kept, wide), 1)
        pick = jnp.where(source == first + (lane & (shard - 1)), 1.0, 0.0).astype(jnp.bfloat16)
        lane = lax.broadcasted_iota(jnp.int32, (half, wide), 1)
        for at, ref in enumerate((a_ref, b_ref)):
            span = slice(at * half, (at + 1) * half)
            rows[span] = ref[:, :kept]
            named = ref[:, kept:kept + 1].astype(jnp.float32).astype(jnp.int32)
            label[span] = named - lane // shard
        own[...] = jnp.dot(rows[...], pick, preferred_element_type=jnp.float32)

    first = (lax.axis_index("tok") * steps + step) * group
    chosen = jnp.where(label[...] == first, own[...], 0.0).astype(jnp.bfloat16)
    gram = lax.dot_general(chosen, rows[...], (((0,), (0,)), ((), ())), preferred_element_type=jnp.float32)
    out_ref[...] = gram * factor


def gram_blocks(ours, theirs, concepts, shard, kept, factor):
    tokens, lanes = ours.shape
    group = max(1, min(concepts, LOW // shard))
    return pl.pallas_call(
        functools.partial(gram_kernel, shard, group, factor),
        grid=(concepts // group,),
        in_specs=[pl.BlockSpec((tokens, lanes), lambda i: (0, 0))] * 2,
        out_specs=pl.BlockSpec((group * shard, kept), lambda i: (i, 0)),
        out_shape=jax.ShapeDtypeStruct((concepts * shard, kept), jnp.float32),
        scratch_shapes=[
            pltpu.VMEM((2 * tokens, kept), jnp.bfloat16),
            pltpu.VMEM((2 * tokens, group * shard), jnp.float32),
            pltpu.VMEM((2 * tokens, group * shard), jnp.int32),
        ],
        compiler_params=pltpu.CompilerParams(vmem_limit_bytes=VMEM_LIMIT),
        cost_estimate=pl.CostEstimate(
            flops=4 * tokens * concepts * shard * kept, bytes_accessed=4 * concepts * shard * kept, transcendentals=0
        ),
        name="gram",
    )(ours, theirs)


def swap(array, axis, offset):
    return lax.ppermute(array, axis, [(i, i ^ offset) for i in range(lax.axis_size(axis))])


def radices(count):
    out = [2] if (count.bit_length() - 1) % 2 else []
    return out + [4] * ((count.bit_length() - 1) // 2)


def scatter_sum(array, index, stride, radix):
    digit = index // stride % radix
    size = array.shape[0] // radix

    def piece(at):
        return lax.dynamic_slice_in_dim(array, at * size, size, 0)

    total = piece(digit)
    for other in range(1, radix):
        total = total + swap(piece(digit ^ other), "feat", other * stride)
    return total


def gather_rows(array, axis, stride, radix):
    received = [swap(array, axis, other * stride) for other in range(1, radix)]
    return jnp.concatenate([array] + received, axis=0)


def body(features, signs, columns, labels):
    rows, width = features.shape
    feat_count = lax.axis_size("feat")
    feat_index = lax.axis_index("feat")
    tok_count = lax.axis_size("tok")
    kept = columns.shape[0]
    shard = kept // feat_count
    stages = []
    stride = 2
    for radix in radices(feat_count // 2):
        stages.append((stride, radix))
        stride *= radix

    send, keep = partial_halves(features, signs, columns, feat_count)
    summed = keep + swap(send, "feat", 1)
    first, size = (feat_index & 1) * (rows // 2), rows // 2
    for stride, radix in stages:
        summed = scatter_sum(summed, feat_index, stride, radix)
        size //= radix
        first = first + feat_index // stride % radix * size
    sketch = (summed * (1.0 / math.sqrt(width * feat_count))).astype(jnp.bfloat16)

    own_labels = lax.dynamic_slice_in_dim(labels, first, size, 0).astype(jnp.bfloat16)
    ours = jnp.concatenate([sketch, jnp.broadcast_to(own_labels, (size, LANES))], axis=1)
    for stride, radix in reversed(stages[1:]):
        ours = gather_rows(ours, "feat", stride, radix)
    stride = 1
    for radix in radices(tok_count):
        ours = gather_rows(ours, "tok", stride, radix)
        stride *= radix
    ours = gather_rows(ours, "feat", *stages[0])
    theirs = swap(ours, "feat", 1)
    concepts = C // tok_count
    gram = gram_blocks(ours, theirs, concepts, shard, kept, C / (rows * tok_count))
    return gram.reshape(concepts, shard, kept)


def solution(mesh):
    in_specs = (P("tok", "feat"), P("feat"), P(), P("tok", None))
    out_specs = P("tok", "feat", None)
    return jax.shard_map(body, mesh=mesh, in_specs=in_specs, out_specs=out_specs, check_vma=False)
```

time: 46.3 us -> 44.3 us (0.957)
  blocking collectives: 14.8 us -> 0 us
  waiting for transfers between devices: 11.9 us -> 20.9 us
  starting transfers between devices: 7.69 us -> 15.5 us
  local copies, waits for them, and re-layouts: 3.14 us -> 0.18 us
  other arithmetic: 0.84 us -> 0.15 us
    ppermute x2 -> x11, waiting for transfers between devices: 2.74 us -> 20.9 us  [swap(): lax.ppermute(array, axis, [(i, i ^ offset) for i in range(lax.axis_size(a...]
    ppermute x2 -> x11, starting transfers between devices: 0.52 us -> 15.5 us  [swap(): lax.ppermute(array, axis, [(i, i ^ offset) for i in range(lax.axis_size(a...]
    all_to_all x1 -> x0, blocking collectives: 14.8 us -> none  [body(): lax.all_to_all(spread, ('tok', 'feat'), 0, 0, axis_index_groups=all_group...]
    all_to_all x1 -> x0, waiting for transfers between devices: 9.14 us -> none  [body(): lax.all_to_all(half.reshape(peers, chunk, kept), 'feat', 0, 0, axis_index...]
    all_to_all x1 -> x0, starting transfers between devices: 7.17 us -> none  [body(): lax.all_to_all(half.reshape(peers, chunk, kept), 'feat', 0, 0, axis_index...]
    unnamed x8 -> x5, local copies, waits for them, and re-layouts: 3.04 us -> 0.03 us
    reshape x1 -> x0, other arithmetic: 0.73 us -> none  [body(): half.reshape(peers, chunk, kept)]
    pallas_call x1, Pallas kernels: 3.88 us -> 3.29 us  [gram_blocks(): pl.pallas_call(functools.partial(gram_kernel, shard, group, factor), grid...]
  transfers between devices with their start and end apart: 3 -> 11, of which waited for: 3 -> 9; matrix products, arithmetic and copies ran while one was open for 0% -> 0% of each run, Pallas kernels for 0% -> 0%
where the time goes in v2:
time: 44.3 us; the launch traced here: 44.2 us
  waiting for transfers between devices  20.9 us (47%)
  starting transfers between devices  15.5 us (35%)
  Pallas kernels  7.4 us (17%)
    ppermute x11, waiting for transfers between devices, swap(): lax.ppermute(array, axis, [(i, i ^ offset) for i in range(lax.axis_size(a...  20.9 us
    ppermute x11, starting transfers between devices, swap(): lax.ppermute(array, axis, [(i, i ^ offset) for i in range(lax.axis_size(a...  15.5 us
    pallas_call x1, Pallas kernels, partial_halves(): pl.pallas_call(functools.partial(partial_kernel, high_count, total_bits,...  4.11 us
    pallas_call x1, Pallas kernels, gram_blocks(): pl.pallas_call(functools.partial(gram_kernel, shard, group, factor), grid...  3.29 us
  transfers between devices with their start and end apart: 11, of which 9 were waited for; matrix products, arithmetic and copies ran while one was open for 0% of the time, Pallas kernels for 0%

profile of v2, /device:TPU:0, one launch (start us, length us, event | category | flops | bytes accessed | tf_op | source)
XLA Modules:
  0.0 44.2 jit_solution(15936553274847335884)
XLA Ops:
  0.0 4.1 %partial_transform.1 = (f32[64,1024]{1,0:T(8,128)S(1)}, f32[64,1024]{1,0:T(8,128)S(1)}) custom-call(bf16[128,8192]{1,0:T(8,128)(2,1)} %x_hbm.1, s32[1,8192]{1,0:T(1,128)} %bitcast.5, s32[1,1024]{1,0:T(1,128)} %bitcast.6), custom_call_target="tpu_custom_call" | custom-call | flops 2147483648 | bytes 2621440 | tf_op jit(solution)/shard_map/partial_transform/pallas_call | solution.py:83
  4.1 0.5 %collective-permute-start = (f32[64,1024]{1,0:T(8,128)S(1)}, f32[64,1024]{1,0:T(8,128)S(1)}, u32[]{:S(2)}, u32[]{:S(2)}) collective-permute-start(f32[64,1024]{1,0:T(8,128)S(1)} %get-tuple-element.8), channel_id=1, source_target_pairs={{0,2},{2,0},{4,6},{6,4},{8,10},{10,8},{12,14},{14,12},{16,18},{18,... | collective-permute-start | bytes 786440 | tf_op jit(solution)/shard_map/ppermute | solution.py:158
  4.6 1.2 %collective-permute-done = f32[64,1024]{1,0:T(8,128)S(1)} collective-permute-done((f32[64,1024]{1,0:T(8,128)S(1)}, f32[64,1024]{1,0:T(8,128)S(1)}, u32[]{:S(2)}, u32[]{:S(2)}) %collective-permute-start) | collective-permute-done | bytes 262176 | tf_op jit(solution)/shard_map/ppermute | solution.py:158
  5.9 2.9 %collective-permute-start.1 = (f32[32,1024]{1,0:T(8,128)S(1)}, f32[32,1024]{1,0:T(8,128)S(1)}, u32[]{:S(2)}, u32[]{:S(2)}) collective-permute-start(f32[32,1024]{1,0:T(8,128)S(1)} %constant_dynamic-slice_fusion.4), channel_id=1, source_target_pairs={{0,4},{2,6},{4,0},{6,2},{8,12},{10,14},{12,8},{14,10},{16,20},{18,... | collective-permute-start | bytes 393224 | tf_op jit(solution)/shard_map/ppermute | solution.py:158
  8.8 3.8 %collective-permute-done.1 = f32[32,1024]{1,0:T(8,128)S(1)} collective-permute-done((f32[32,1024]{1,0:T(8,128)S(1)}, f32[32,1024]{1,0:T(8,128)S(1)}, u32[]{:S(2)}, u32[]{:S(2)}) %collective-permute-start.1) | collective-permute-done | bytes 131104 | tf_op jit(solution)/shard_map/ppermute | solution.py:158
  12.6 1.9 %collective-permute-start.2 = (f32[8,1024]{1,0:T(8,128)S(1)}, f32[8,1024]{1,0:T(8,128)S(1)}, u32[]{:S(2)}, u32[]{:S(2)}) collective-permute-start(f32[8,1024]{1,0:T(8,128)S(1)} %get-tuple-element.9), channel_id=1, source_target_pairs={{0,8},{2,10},{4,12},{6,14},{8,0},{10,2},{12,4},{14,6},{16,24},{18,... | collective-permute-start | bytes 98312 | tf_op jit(solution)/shard_map/ppermute | solution.py:158
  14.5 2.5 %collective-permute-start.4 = (f32[8,1024]{1,0:T(8,128)S(1)}, f32[8,1024]{1,0:T(8,128)S(1)}, u32[]{:S(2)}, u32[]{:S(2)}) collective-permute-start(f32[8,1024]{1,0:T(8,128)S(1)} %get-tuple-element.10), channel_id=1, source_target_pairs={{0,24},{2,26},{4,28},{6,30},{8,16},{10,18},{12,20},{14,22},{16,8},... | collective-permute-start | bytes 98312 | tf_op jit(solution)/shard_map/ppermute | solution.py:158
  17.0 0.1 collective-permute-start.3
  17.1 0.1 fusion.1
  17.2 3.0 %collective-permute-done.4 = f32[8,1024]{1,0:T(8,128)S(1)} collective-permute-done((f32[8,1024]{1,0:T(8,128)S(1)}, f32[8,1024]{1,0:T(8,128)S(1)}, u32[]{:S(2)}, u32[]{:S(2)}) %collective-permute-start.4) | collective-permute-done | bytes 32800 | tf_op jit(solution)/shard_map/ppermute | solution.py:158
  20.2 1.9 %collective-permute-done.3 = f32[8,1024]{1,0:T(8,128)S(1)} collective-permute-done((f32[8,1024]{1,0:T(8,128)S(1)}, f32[8,1024]{1,0:T(8,128)S(1)}, u32[]{:S(2)}, u32[]{:S(2)}) %collective-permute-start.3) | collective-permute-done | bytes 32800 | tf_op jit(solution)/shard_map/ppermute | solution.py:158
  22.2 0.1 broadcast_in_dim.8
  22.3 0.0 collective-permute-start.6
  22.3 1.8 %collective-permute-start.5 = (bf16[8,1152]{1,0:T(8,128)(2,1)S(1)}, bf16[8,1152]{1,0:T(8,128)(2,1)S(1)}, u32[]{:S(2)}, u32[]{:S(2)}) collective-permute-start(bf16[8,1152]{1,0:T(8,128)(2,1)S(1)} %get-tuple-element.22), channel_id=1, source_target_pairs={{0,8},{2,10},{4,12},{6,14},{8,0},{10,2},{12,4},{14,6},{16,24},{18,... | collective-permute-start | bytes 55304 | tf_op jit(solution)/shard_map/ppermute | solution.py:158
  24.1 2.6 %collective-permute-start.7 = (bf16[8,1152]{1,0:T(8,128)(2,1)S(1)}, bf16[8,1152]{1,0:T(8,128)(2,1)S(1)}, u32[]{:S(2)}, u32[]{:S(2)}) collective-permute-start(bf16[8,1152]{1,0:T(8,128)(2,1)S(1)} %get-tuple-element.22), channel_id=1, source_target_pairs={{0,24},{2,26},{4,28},{6,30},{8,16},{10,18},{12,20},{14,22},{16,8},... | collective-permute-start | bytes 55304 | tf_op jit(solution)/shard_map/ppermute | solution.py:158
  26.7 0.3 collective-permute-done.6
  27.0 2.6 %collective-permute-done.7 = bf16[8,1152]{1,0:T(8,128)(2,1)S(1)} collective-permute-done((bf16[8,1152]{1,0:T(8,128)(2,1)S(1)}, bf16[8,1152]{1,0:T(8,128)(2,1)S(1)}, u32[]{:S(2)}, u32[]{:S(2)}) %collective-permute-start.7) | collective-permute-done | bytes 18464 | tf_op jit(solution)/shard_map/ppermute | solution.py:158
  29.7 1.5 %collective-permute-start.8 = (bf16[32,1152]{1,0:T(8,128)(2,1)S(1)}, bf16[32,1152]{1,0:T(8,128)(2,1)S(1)}, u32[]{:S(2)}, u32[]{:S(2)}) collective-permute-start(bf16[32,1152]{1,0:T(8,128)(2,1)S(1)} %pad_maximum_fusion), channel_id=1, source_target_pairs={{0,1},{1,0},{2,3},{3,2},{4,5},{5,4},{6,7},{7,6},{8,9},{9,8},{10,11... | collective-permute-start | bytes 221192 | tf_op jit(solution)/shard_map/ppermute | solution.py:158
  31.2 2.8 %collective-permute-done.8 = bf16[32,1152]{1,0:T(8,128)(2,1)S(1)} collective-permute-done((bf16[32,1152]{1,0:T(8,128)(2,1)S(1)}, bf16[32,1152]{1,0:T(8,128)(2,1)S(1)}, u32[]{:S(2)}, u32[]{:S(2)}) %collective-permute-start.8) | collective-permute-done | bytes 73760 | tf_op jit(solution)/shard_map/ppermute | solution.py:158
  34.0 1.5 %collective-permute-start.9 = (bf16[64,1152]{1,0:T(8,128)(2,1)S(1)}, bf16[64,1152]{1,0:T(8,128)(2,1)S(1)}, u32[]{:S(2)}, u32[]{:S(2)}) collective-permute-start(bf16[64,1152]{1,0:T(8,128)(2,1)S(1)} %get-tuple-element.12), channel_id=1, source_target_pairs={{0,4},{2,6},{4,0},{6,2},{8,12},{10,14},{12,8},{14,10},{16,20},{18,... | collective-permute-start | bytes 442376 | tf_op jit(solution)/shard_map/ppermute | solution.py:158
  35.6 3.7 %collective-permute-done.9 = bf16[64,1152]{1,0:T(8,128)(2,1)S(1)} collective-permute-done((bf16[64,1152]{1,0:T(8,128)(2,1)S(1)}, bf16[64,1152]{1,0:T(8,128)(2,1)S(1)}, u32[]{:S(2)}, u32[]{:S(2)}) %collective-permute-start.9) | collective-permute-done | bytes 147488 | tf_op jit(solution)/shard_map/ppermute | solution.py:158
  39.3 0.1 collective-permute-start.10
  39.3 1.6 %collective-permute-done.10.b_ref = bf16[128,1152]{1,0:T(8,128)(2,1)S(1)} collective-permute-done((bf16[128,1152]{1,0:T(8,128)(2,1)S(1)}, bf16[128,1152]{1,0:T(8,128)(2,1)S(1)}, u32[]{:S(2)}, u32[]{:S(2)}) %collective-permute-start.10) | collective-permute-done | bytes 294944 | tf_op jit(solution)/shard_map/ppermute | solution.py:158
  40.9 3.3 %gram.1 = f32[1024,1024]{1,0:T(8,128)} custom-call(bf16[128,1152]{1,0:T(8,128)(2,1)S(1)} %constant_dynamic-update-slice_fusion.5.a_ref, bf16[128,1152]{1,0:T(8,128)(2,1)S(1)} %collective-permute-done.10.b_ref), custom_call_target="tpu_custom_call" | custom-call | flops 536870912 | bytes 4194304 | tf_op jit(solution)/shard_map/gram/pallas_call | solution.py:138
  (16 shorter events, 0.2 us)
Async XLA Ops:
  0.0 17.1 %copy-start = (s32[128,1]{0,1:T(1,128)S(1)}, s32[128,1]{0,1:T(1,128)}, u32[]{:S(2)}) copy-start(s32[128,1]{0,1:T(1,128)} %param.7) | copy-start | bytes 1540
  4.1 1.7 %collective-permute-start = (f32[64,1024]{1,0:T(8,128)S(1)}, f32[64,1024]{1,0:T(8,128)S(1)}, u32[]{:S(2)}, u32[]{:S(2)}) collective-permute-start(f32[64,1024]{1,0:T(8,128)S(1)} %get-tuple-element.8), channel_id=1, source_target_pairs={{0,2},{2,0},{4,6},{6,4},{8,10},{10,8},{12,14},{14,12},{16,18},{18,... | collective-permute-start | bytes 786440 | tf_op jit(solution)/shard_map/ppermute | solution.py:158
  5.9 6.7 %collective-permute-start.1 = (f32[32,1024]{1,0:T(8,128)S(1)}, f32[32,1024]{1,0:T(8,128)S(1)}, u32[]{:S(2)}, u32[]{:S(2)}) collective-permute-start(f32[32,1024]{1,0:T(8,128)S(1)} %constant_dynamic-slice_fusion.4), channel_id=1, source_target_pairs={{0,4},{2,6},{4,0},{6,2},{8,12},{10,14},{12,8},{14,10},{16,20},{18,... | collective-permute-start | bytes 393224 | tf_op jit(solution)/shard_map/ppermute | solution.py:158
  12.6 4.6 %collective-permute-start.2 = (f32[8,1024]{1,0:T(8,128)S(1)}, f32[8,1024]{1,0:T(8,128)S(1)}, u32[]{:S(2)}, u32[]{:S(2)}) collective-permute-start(f32[8,1024]{1,0:T(8,128)S(1)} %get-tuple-element.9), channel_id=1, source_target_pairs={{0,8},{2,10},{4,12},{6,14},{8,0},{10,2},{12,4},{14,6},{16,24},{18,... | collective-permute-start | bytes 98312 | tf_op jit(solution)/shard_map/ppermute | solution.py:158
  14.5 5.7 %collective-permute-start.4 = (f32[8,1024]{1,0:T(8,128)S(1)}, f32[8,1024]{1,0:T(8,128)S(1)}, u32[]{:S(2)}, u32[]{:S(2)}) collective-permute-start(f32[8,1024]{1,0:T(8,128)S(1)} %get-tuple-element.10), channel_id=1, source_target_pairs={{0,24},{2,26},{4,28},{6,30},{8,16},{10,18},{12,20},{14,22},{16,8},... | collective-permute-start | bytes 98312 | tf_op jit(solution)/shard_map/ppermute | solution.py:158
  17.0 5.2 %collective-permute-start.3 = (f32[8,1024]{1,0:T(8,128)S(1)}, f32[8,1024]{1,0:T(8,128)S(1)}, u32[]{:S(2)}, u32[]{:S(2)}) collective-permute-start(f32[8,1024]{1,0:T(8,128)S(1)} %get-tuple-element.11), channel_id=1, source_target_pairs={{0,16},{2,18},{4,20},{6,22},{8,24},{10,26},{12,28},{14,30},{16,0},... | collective-permute-start | bytes 98312 | tf_op jit(solution)/shard_map/ppermute | solution.py:158
  22.3 4.7 %collective-permute-start.6 = (bf16[8,1152]{1,0:T(8,128)(2,1)S(1)}, bf16[8,1152]{1,0:T(8,128)(2,1)S(1)}, u32[]{:S(2)}, u32[]{:S(2)}) collective-permute-start(bf16[8,1152]{1,0:T(8,128)(2,1)S(1)} %get-tuple-element.22), channel_id=1, source_target_pairs={{0,16},{2,18},{4,20},{6,22},{8,24},{10,26},{12,28},{14,30},{16,0},... | collective-permute-start | bytes 55304 | tf_op jit(solution)/shard_map/ppermute | solution.py:158
  22.3 4.7 %collective-permute-start.5 = (bf16[8,1152]{1,0:T(8,128)(2,1)S(1)}, bf16[8,1152]{1,0:T(8,128)(2,1)S(1)}, u32[]{:S(2)}, u32[]{:S(2)}) collective-permute-start(bf16[8,1152]{1,0:T(8,128)(2,1)S(1)} %get-tuple-element.22), channel_id=1, source_target_pairs={{0,8},{2,10},{4,12},{6,14},{8,0},{10,2},{12,4},{14,6},{16,24},{18,... | collective-permute-start | bytes 55304 | tf_op jit(solution)/shard_map/ppermute | solution.py:158
  24.1 5.6 %collective-permute-start.7 = (bf16[8,1152]{1,0:T(8,128)(2,1)S(1)}, bf16[8,1152]{1,0:T(8,128)(2,1)S(1)}, u32[]{:S(2)}, u32[]{:S(2)}) collective-permute-start(bf16[8,1152]{1,0:T(8,128)(2,1)S(1)} %get-tuple-element.22), channel_id=1, source_target_pairs={{0,24},{2,26},{4,28},{6,30},{8,16},{10,18},{12,20},{14,22},{16,8},... | collective-permute-start | bytes 55304 | tf_op jit(solution)/shard_map/ppermute | solution.py:158
  29.7 4.4 %collective-permute-start.8 = (bf16[32,1152]{1,0:T(8,128)(2,1)S(1)}, bf16[32,1152]{1,0:T(8,128)(2,1)S(1)}, u32[]{:S(2)}, u32[]{:S(2)}) collective-permute-start(bf16[32,1152]{1,0:T(8,128)(2,1)S(1)} %pad_maximum_fusion), channel_id=1, source_target_pairs={{0,1},{1,0},{2,3},{3,2},{4,5},{5,4},{6,7},{7,6},{8,9},{9,8},{10,11... | collective-permute-start | bytes 221192 | tf_op jit(solution)/shard_map/ppermute | solution.py:158
  34.0 5.2 %collective-permute-start.9 = (bf16[64,1152]{1,0:T(8,128)(2,1)S(1)}, bf16[64,1152]{1,0:T(8,128)(2,1)S(1)}, u32[]{:S(2)}, u32[]{:S(2)}) collective-permute-start(bf16[64,1152]{1,0:T(8,128)(2,1)S(1)} %get-tuple-element.12), channel_id=1, source_target_pairs={{0,4},{2,6},{4,0},{6,2},{8,12},{10,14},{12,8},{14,10},{16,20},{18,... | collective-permute-start | bytes 442376 | tf_op jit(solution)/shard_map/ppermute | solution.py:158
  39.3 1.6 %collective-permute-start.10 = (bf16[128,1152]{1,0:T(8,128)(2,1)S(1)}, bf16[128,1152]{1,0:T(8,128)(2,1)S(1)}, u32[]{:S(2)}, u32[]{:S(2)}) collective-permute-start(bf16[128,1152]{1,0:T(8,128)(2,1)S(1)} %constant_dynamic-update-slice_fusion.5.a_ref), channel_id=1, source_target_pairs={{0,2},{2,0},{4,6},{6,4},{8,10},{10,8},{12,14},{14,12},{16,18},{18,... | collective-permute-start | bytes 884744 | tf_op jit(solution)/shard_map/ppermute | solution.py:158

commit v3 on v2

--- a/solution.py
+++ b/solution.py
@@ -154,31 +154,60 @@
     )(ours, theirs)
 
 
+def encode(values, word_ref):
+    kept = values.shape[1]
+    half = values.shape[0] // 2
+    top = jnp.max(jnp.abs(values), axis=1, keepdims=True)
+    power = jnp.ceil(jnp.log2(jnp.maximum(top, 2.0 ** -100)))
+    whole = jnp.round(values * jnp.exp2(15.0 - power))
+    whole = jnp.clip(whole, -32767.0, 32767.0).astype(jnp.int32)
+    power = jnp.broadcast_to(power, (values.shape[0], LANES)).astype(jnp.int32)
+    for cols, code in ((slice(0, kept), whole), (slice(kept, kept + LANES), power)):
+        word_ref[:, cols] = (code[:half] & 0xFFFF) | (code[half:] << 16)
+
+
+def decode(word_ref):
+    word = word_ref[...]
+    code = jnp.concatenate([(word << 16) >> 16, word >> 16], axis=0).astype(jnp.float32)
+    return code[:, :-LANES] * jnp.exp2(code[:, -LANES:-LANES + 1] - 15.0)
+
+
+def first_kernel(stride, keep_ref, got_ref, total_ref, word_ref):
+    size = total_ref.shape[0]
+    digit = lax.rem(lax.axis_index("feat") // stride, 2)
+
+    def piece(at):
+        span = pl.ds(pl.multiple_of(at * size, size), size)
+        return keep_ref[span, :] + got_ref[span, :]
+
+    total_ref[...] = piece(digit)
+    encode(piece(1 - digit), word_ref)
+
+
+def middle_kernel(total_ref, word_ref, sum_ref, out_ref):
+    total = total_ref[...] + decode(word_ref)
+    sum_ref[...] = total
+    encode(total, out_ref)
+
+
+def last_kernel(scale, total_ref, word_ref, label_ref, row_ref):
+    total = total_ref[...] + decode(word_ref)
+    kept = total.shape[1]
+    row_ref[:, :kept] = (total * scale).astype(jnp.bfloat16)
+    row_ref[:, kept:] = label_ref[...]
+
+
+def local_call(kernel, name, *operands, out_shape):
+    return pl.pallas_call(
+        kernel,
+        out_shape=out_shape,
+        compiler_params=pltpu.CompilerParams(vmem_limit_bytes=VMEM_LIMIT),
+        name=name,
+    )(*operands)
+
+
 def swap(array, axis, offset):
     return lax.ppermute(array, axis, [(i, i ^ offset) for i in range(lax.axis_size(axis))])
-
-
-def radices(count):
-    out = [2] if (count.bit_length() - 1) % 2 else []
-    return out + [4] * ((count.bit_length() - 1) // 2)
-
-
-def scatter_sum(array, index, stride, radix):
-    digit = index // stride % radix
-    size = array.shape[0] // radix
-
-    def piece(at):
-        return lax.dynamic_slice_in_dim(array, at * size, size, 0)
-
-    total = piece(digit)
-    for other in range(1, radix):
-        total = total + swap(piece(digit ^ other), "feat", other * stride)
-    return total
-
-
-def gather_rows(array, axis, stride, radix):
-    received = [swap(array, axis, other * stride) for other in range(1, radix)]
-    return jnp.concatenate([array] + received, axis=0)
 
 
 def body(features, signs, columns, labels):
@@ -188,30 +217,38 @@
     tok_count = lax.axis_size("tok")
     kept = columns.shape[0]
     shard = kept // feat_count
-    stages = []
-    stride = 2
-    for radix in radices(feat_count // 2):
-        stages.append((stride, radix))
-        stride *= radix
+    size = rows // 4
+    total_type = jax.ShapeDtypeStruct((size, kept), jnp.float32)
+    word_type = jax.ShapeDtypeStruct((size // 2, kept + LANES), jnp.int32)
+    row_type = jax.ShapeDtypeStruct((size, kept + LANES), jnp.bfloat16)
+
+    first = (feat_index & 1) * (rows // 2) + (feat_index >> 1 & 1) * size
+    own_labels = lax.dynamic_slice_in_dim(labels, first, size, 0).astype(jnp.bfloat16)
+    own_labels = jnp.broadcast_to(own_labels, (size, LANES))
 
     send, keep = partial_halves(features, signs, columns, feat_count)
-    summed = keep + swap(send, "feat", 1)
-    first, size = (feat_index & 1) * (rows // 2), rows // 2
-    for stride, radix in stages:
-        summed = scatter_sum(summed, feat_index, stride, radix)
-        size //= radix
-        first = first + feat_index // stride % radix * size
-    sketch = (summed * (1.0 / math.sqrt(width * feat_count))).astype(jnp.bfloat16)
-
-    own_labels = lax.dynamic_slice_in_dim(labels, first, size, 0).astype(jnp.bfloat16)
-    ours = jnp.concatenate([sketch, jnp.broadcast_to(own_labels, (size, LANES))], axis=1)
-    for stride, radix in reversed(stages[1:]):
-        ours = gather_rows(ours, "feat", stride, radix)
+    got = swap(send, "feat", 1)
+    total, word = local_call(
+        functools.partial(first_kernel, 2), "first_split", keep, got, out_shape=[total_type, word_type]
+    )
+    word = swap(word, "feat", 2)
+    stride = 4
+    while stride < feat_count:
+        total, word = local_call(
+            middle_kernel, "add_encode", total, word, out_shape=[total_type, word_type]
+        )
+        word = swap(word, "feat", stride)
+        stride *= 2
+    scale = 1.0 / math.sqrt(width * feat_count)
+    ours = local_call(
+        functools.partial(last_kernel, scale), "sketch_rows", total, word, own_labels, out_shape=row_type
+    )
+
     stride = 1
-    for radix in radices(tok_count):
-        ours = gather_rows(ours, "tok", stride, radix)
-        stride *= radix
-    ours = gather_rows(ours, "feat", *stages[0])
+    while stride < tok_count:
+        ours = jnp.concatenate([ours, swap(ours, "tok", stride)], axis=0)
+        stride *= 2
+    ours = jnp.concatenate([ours, swap(ours, "feat", 2)], axis=0)
     theirs = swap(ours, "feat", 1)
     concepts = C // tok_count
     gram = gram_blocks(ours, theirs, concepts, shard, kept, C / (rows * tok_count))

time: 44.3 us -> 36.5 us (0.82)
  waiting for transfers between devices: 20.9 us -> 16 us
  starting transfers between devices: 15.5 us -> 12.1 us
  Pallas kernels: 7.4 us -> 8.03 us
    ppermute x11 -> x7, waiting for transfers between devices: 20.9 us -> 16 us  [swap(): lax.ppermute(array, axis, [(i, i ^ offset) for i in range(lax.axis_size(a...]
    ppermute x11 -> x7, starting transfers between devices: 15.5 us -> 12.1 us  [swap(): lax.ppermute(array, axis, [(i, i ^ offset) for i in range(lax.axis_size(a...]
    pallas_call x0 -> x4, Pallas kernels: none -> 0.63 us  [local_call(): pl.pallas_call(kernel, out_shape=out_shape, compiler_params=pltpu.Compile...]
  transfers between devices with their start and end apart: 11 -> 7, of which waited for: 9 -> 7; matrix products, arithmetic and copies ran while one was open for 0% -> 0% of each run, Pallas kernels for 0% -> 0%
where the time goes in v3:
time: 36.5 us; the launch traced here: 36.4 us
  waiting for transfers between devices  16 us (44%)
  starting transfers between devices  12.1 us (33%)
  Pallas kernels  8.03 us (22%)
    ppermute x7, waiting for transfers between devices, swap(): lax.ppermute(array, axis, [(i, i ^ offset) for i in range(lax.axis_size(a...  16 us
    ppermute x7, starting transfers between devices, swap(): lax.ppermute(array, axis, [(i, i ^ offset) for i in range(lax.axis_size(a...  12.1 us
    pallas_call x1, Pallas kernels, partial_halves(): pl.pallas_call(functools.partial(partial_kernel, high_count, total_bits,...  4.11 us
    pallas_call x1, Pallas kernels, gram_blocks(): pl.pallas_call(functools.partial(gram_kernel, shard, group, factor), grid...  3.29 us
  transfers between devices with their start and end apart: 7, of which 7 were waited for; matrix products, arithmetic and copies ran while one was open for 0% of the time, Pallas kernels for 0%

profile of v3, /device:TPU:0, one launch (start us, length us, event | category | flops | bytes accessed | tf_op | source)
XLA Modules:
  0.0 36.4 jit_solution(4232493517488700553)
XLA Ops:
  0.0 0.0 copy-start
  0.0 4.1 %partial_transform.1 = (f32[64,1024]{1,0:T(8,128)S(1)}, f32[64,1024]{1,0:T(8,128)S(1)}) custom-call(bf16[128,8192]{1,0:T(8,128)(2,1)} %x_hbm.1, s32[1,8192]{1,0:T(1,128)} %bitcast.5, s32[1,1024]{1,0:T(1,128)} %bitcast.6), custom_call_target="tpu_custom_call" | custom-call | flops 2147483648 | bytes 2621440 | tf_op jit(solution)/shard_map/partial_transform/pallas_call | solution.py:83
  4.1 0.5 %collective-permute-start = (f32[64,1024]{1,0:T(8,128)S(1)}, f32[64,1024]{1,0:T(8,128)S(1)}, u32[]{:S(2)}, u32[]{:S(2)}) collective-permute-start(f32[64,1024]{1,0:T(8,128)S(1)} %get-tuple-element.14), channel_id=1, source_target_pairs={{0,2},{2,0},{4,6},{6,4},{8,10},{10,8},{12,14},{14,12},{16,18},{18,... | collective-permute-start | bytes 786440 | tf_op jit(solution)/shard_map/ppermute | solution.py:210
  4.6 1.2 %collective-permute-done.got_ref = f32[64,1024]{1,0:T(8,128)S(1)} collective-permute-done((f32[64,1024]{1,0:T(8,128)S(1)}, f32[64,1024]{1,0:T(8,128)S(1)}, u32[]{:S(2)}, u32[]{:S(2)}) %collective-permute-start) | collective-permute-done | bytes 262176 | tf_op jit(solution)/shard_map/ppermute | solution.py:210
  5.8 0.1 first_split.1
  5.9 2.9 %collective-permute-start.1 = (s32[16,1152]{1,0:T(8,128)S(1)}, s32[16,1152]{1,0:T(8,128)S(1)}, u32[]{:S(2)}, u32[]{:S(2)}) collective-permute-start(s32[16,1152]{1,0:T(8,128)S(1)} %get-tuple-element.16), channel_id=1, source_target_pairs={{0,4},{2,6},{4,0},{6,2},{8,12},{10,14},{12,8},{14,10},{16,20},{18,... | collective-permute-start | bytes 221192 | tf_op jit(solution)/shard_map/ppermute | solution.py:210
  8.9 2.6 %collective-permute-done.1.word_ref = s32[16,1152]{1,0:T(8,128)S(1)} collective-permute-done((s32[16,1152]{1,0:T(8,128)S(1)}, s32[16,1152]{1,0:T(8,128)S(1)}, u32[]{:S(2)}, u32[]{:S(2)}) %collective-permute-start.1) | collective-permute-done | bytes 73760 | tf_op jit(solution)/shard_map/ppermute | solution.py:210
  11.4 0.2 add_encode.2
  11.6 1.9 %collective-permute-start.2 = (s32[16,1152]{1,0:T(8,128)S(1)}, s32[16,1152]{1,0:T(8,128)S(1)}, u32[]{:S(2)}, u32[]{:S(2)}) collective-permute-start(s32[16,1152]{1,0:T(8,128)S(1)} %get-tuple-element.18), channel_id=1, source_target_pairs={{0,8},{2,10},{4,12},{6,14},{8,0},{10,2},{12,4},{14,6},{16,24},{18,... | collective-permute-start | bytes 221192 | tf_op jit(solution)/shard_map/ppermute | solution.py:210
  13.6 2.5 %collective-permute-done.2.word_ref = s32[16,1152]{1,0:T(8,128)S(1)} collective-permute-done((s32[16,1152]{1,0:T(8,128)S(1)}, s32[16,1152]{1,0:T(8,128)S(1)}, u32[]{:S(2)}, u32[]{:S(2)}) %collective-permute-start.2) | collective-permute-done | bytes 73760 | tf_op jit(solution)/shard_map/ppermute | solution.py:210
  16.1 0.2 add_encode.3
  16.3 3.0 %collective-permute-start.3 = (s32[16,1152]{1,0:T(8,128)S(1)}, s32[16,1152]{1,0:T(8,128)S(1)}, u32[]{:S(2)}, u32[]{:S(2)}) collective-permute-start(s32[16,1152]{1,0:T(8,128)S(1)} %get-tuple-element.20), channel_id=1, source_target_pairs={{0,16},{2,18},{4,20},{6,22},{8,24},{10,26},{12,28},{14,30},{16,0},... | collective-permute-start | bytes 221192 | tf_op jit(solution)/shard_map/ppermute | solution.py:210
  19.2 0.0 copy-done
  19.2 0.1 convert_bitcast_fusion
  19.3 2.3 %collective-permute-done.3.word_ref = s32[16,1152]{1,0:T(8,128)S(1)} collective-permute-done((s32[16,1152]{1,0:T(8,128)S(1)}, s32[16,1152]{1,0:T(8,128)S(1)}, u32[]{:S(2)}, u32[]{:S(2)}) %collective-permute-start.3) | collective-permute-done | bytes 73760 | tf_op jit(solution)/shard_map/ppermute | solution.py:210
  21.6 0.1 broadcast_in_dim.8.label_ref
  21.6 0.1 sketch_rows.1
  21.8 1.9 %collective-permute-start.4 = (bf16[32,1152]{1,0:T(8,128)(2,1)S(1)}, bf16[32,1152]{1,0:T(8,128)(2,1)S(1)}, u32[]{:S(2)}, u32[]{:S(2)}) collective-permute-start(bf16[32,1152]{1,0:T(8,128)(2,1)S(1)} %sketch_rows.1), channel_id=1, source_target_pairs={{0,1},{1,0},{2,3},{3,2},{4,5},{5,4},{6,7},{7,6},{8,9},{9,8},{10,11... | collective-permute-start | bytes 221192 | tf_op jit(solution)/shard_map/ppermute | solution.py:210
  23.6 2.5 %collective-permute-done.4 = bf16[32,1152]{1,0:T(8,128)(2,1)S(1)} collective-permute-done((bf16[32,1152]{1,0:T(8,128)(2,1)S(1)}, bf16[32,1152]{1,0:T(8,128)(2,1)S(1)}, u32[]{:S(2)}, u32[]{:S(2)}) %collective-permute-start.4) | collective-permute-done | bytes 73760 | tf_op jit(solution)/shard_map/ppermute | solution.py:210
  26.2 1.8 %collective-permute-start.5 = (bf16[64,1152]{1,0:T(8,128)(2,1)S(1)}, bf16[64,1152]{1,0:T(8,128)(2,1)S(1)}, u32[]{:S(2)}, u32[]{:S(2)}) collective-permute-start(bf16[64,1152]{1,0:T(8,128)(2,1)S(1)} %pad_maximum_fusion.1), channel_id=1, source_target_pairs={{0,4},{2,6},{4,0},{6,2},{8,12},{10,14},{12,8},{14,10},{16,20},{18,... | collective-permute-start | bytes 442376 | tf_op jit(solution)/shard_map/ppermute | solution.py:210
  28.0 3.4 %collective-permute-done.5 = bf16[64,1152]{1,0:T(8,128)(2,1)S(1)} collective-permute-done((bf16[64,1152]{1,0:T(8,128)(2,1)S(1)}, bf16[64,1152]{1,0:T(8,128)(2,1)S(1)}, u32[]{:S(2)}, u32[]{:S(2)}) %collective-permute-start.5) | collective-permute-done | bytes 147488 | tf_op jit(solution)/shard_map/ppermute | solution.py:210
  31.4 0.1 collective-permute-start.6
  31.5 1.6 %collective-permute-done.6.b_ref = bf16[128,1152]{1,0:T(8,128)(2,1)S(1)} collective-permute-done((bf16[128,1152]{1,0:T(8,128)(2,1)S(1)}, bf16[128,1152]{1,0:T(8,128)(2,1)S(1)}, u32[]{:S(2)}, u32[]{:S(2)}) %collective-permute-start.6) | collective-permute-done | bytes 294944 | tf_op jit(solution)/shard_map/ppermute | solution.py:210
  33.1 3.3 %gram.1 = f32[1024,1024]{1,0:T(8,128)} custom-call(bf16[128,1152]{1,0:T(8,128)(2,1)S(1)} %pad_maximum_fusion.a_ref, bf16[128,1152]{1,0:T(8,128)(2,1)S(1)} %collective-permute-done.6.b_ref), custom_call_target="tpu_custom_call" | custom-call | flops 536870912 | bytes 4194304 | tf_op jit(solution)/shard_map/gram/pallas_call | solution.py:138
  (2 shorter events, 0.0 us)
Async XLA Ops:
  0.0 19.2 %copy-start = (s32[128,1]{0,1:T(1,128)S(1)}, s32[128,1]{0,1:T(1,128)}, u32[]{:S(2)}) copy-start(s32[128,1]{0,1:T(1,128)} %param.7) | copy-start | bytes 1540
  4.1 1.7 %collective-permute-start = (f32[64,1024]{1,0:T(8,128)S(1)}, f32[64,1024]{1,0:T(8,128)S(1)}, u32[]{:S(2)}, u32[]{:S(2)}) collective-permute-start(f32[64,1024]{1,0:T(8,128)S(1)} %get-tuple-element.14), channel_id=1, source_target_pairs={{0,2},{2,0},{4,6},{6,4},{8,10},{10,8},{12,14},{14,12},{16,18},{18,... | collective-permute-start | bytes 786440 | tf_op jit(solution)/shard_map/ppermute | solution.py:210
  5.9 5.5 %collective-permute-start.1 = (s32[16,1152]{1,0:T(8,128)S(1)}, s32[16,1152]{1,0:T(8,128)S(1)}, u32[]{:S(2)}, u32[]{:S(2)}) collective-permute-start(s32[16,1152]{1,0:T(8,128)S(1)} %get-tuple-element.16), channel_id=1, source_target_pairs={{0,4},{2,6},{4,0},{6,2},{8,12},{10,14},{12,8},{14,10},{16,20},{18,... | collective-permute-start | bytes 221192 | tf_op jit(solution)/shard_map/ppermute | solution.py:210
  11.6 4.4 %collective-permute-start.2 = (s32[16,1152]{1,0:T(8,128)S(1)}, s32[16,1152]{1,0:T(8,128)S(1)}, u32[]{:S(2)}, u32[]{:S(2)}) collective-permute-start(s32[16,1152]{1,0:T(8,128)S(1)} %get-tuple-element.18), channel_id=1, source_target_pairs={{0,8},{2,10},{4,12},{6,14},{8,0},{10,2},{12,4},{14,6},{16,24},{18,... | collective-permute-start | bytes 221192 | tf_op jit(solution)/shard_map/ppermute | solution.py:210
  16.3 5.3 %collective-permute-start.3 = (s32[16,1152]{1,0:T(8,128)S(1)}, s32[16,1152]{1,0:T(8,128)S(1)}, u32[]{:S(2)}, u32[]{:S(2)}) collective-permute-start(s32[16,1152]{1,0:T(8,128)S(1)} %get-tuple-element.20), channel_id=1, source_target_pairs={{0,16},{2,18},{4,20},{6,22},{8,24},{10,26},{12,28},{14,30},{16,0},... | collective-permute-start | bytes 221192 | tf_op jit(solution)/shard_map/ppermute | solution.py:210
  21.8 4.4 %collective-permute-start.4 = (bf16[32,1152]{1,0:T(8,128)(2,1)S(1)}, bf16[32,1152]{1,0:T(8,128)(2,1)S(1)}, u32[]{:S(2)}, u32[]{:S(2)}) collective-permute-start(bf16[32,1152]{1,0:T(8,128)(2,1)S(1)} %sketch_rows.1), channel_id=1, source_target_pairs={{0,1},{1,0},{2,3},{3,2},{4,5},{5,4},{6,7},{7,6},{8,9},{9,8},{10,11... | collective-permute-start | bytes 221192 | tf_op jit(solution)/shard_map/ppermute | solution.py:210
  26.2 5.2 %collective-permute-start.5 = (bf16[64,1152]{1,0:T(8,128)(2,1)S(1)}, bf16[64,1152]{1,0:T(8,128)(2,1)S(1)}, u32[]{:S(2)}, u32[]{:S(2)}) collective-permute-start(bf16[64,1152]{1,0:T(8,128)(2,1)S(1)} %pad_maximum_fusion.1), channel_id=1, source_target_pairs={{0,4},{2,6},{4,0},{6,2},{8,12},{10,14},{12,8},{14,10},{16,20},{18,... | collective-permute-start | bytes 442376 | tf_op jit(solution)/shard_map/ppermute | solution.py:210
  31.4 1.6 %collective-permute-start.6 = (bf16[128,1152]{1,0:T(8,128)(2,1)S(1)}, bf16[128,1152]{1,0:T(8,128)(2,1)S(1)}, u32[]{:S(2)}, u32[]{:S(2)}) collective-permute-start(bf16[128,1152]{1,0:T(8,128)(2,1)S(1)} %pad_maximum_fusion.a_ref), channel_id=1, source_target_pairs={{0,2},{2,0},{4,6},{6,4},{8,10},{10,8},{12,14},{14,12},{16,18},{18,... | collective-permute-start | bytes 884744 | tf_op jit(solution)/shard_map/ppermute | solution.py:210

commit v4 on v3

--- a/solution.py
+++ b/solution.py
@@ -11,6 +11,7 @@
 C = 32
 LOW = 256
 LANES = 128
+CHAINS = 2
 VMEM_LIMIT = 48 * 1024 * 1024
 
 
@@ -24,7 +25,8 @@
     return (1 - 2 * (number & 1)).astype(jnp.float32)
 
 
-def partial_kernel(high_count, total_bits, parts, x_hbm, s_hbm, col_hbm, send_ref, keep_ref, x_buf, s_buf, col_buf, low, high, acc, sems):
+def partial_kernel(high_count, total_bits, parts, x_hbm, s_hbm, col_hbm, *refs):
+    out_refs, (x_buf, s_buf, col_buf, low, high, acc, sems) = refs[:2 * CHAINS], refs[2 * CHAINS:]
     kept = col_hbm.shape[1]
     wide = x_hbm.shape[1] // parts
     me = lax.axis_index("feat")
@@ -67,10 +69,12 @@
             if part > 0:
                 total = total + acc[:, cols]
             acc[:, cols] = total
-    half = keep_ref.shape[0]
+    size = out_refs[0].shape[0]
     mine = lax.rem(me, 2)
-    keep_ref[...] = acc[pl.ds(pl.multiple_of(mine * half, half), half), :]
-    send_ref[...] = acc[pl.ds(pl.multiple_of((1 - mine) * half, half), half), :]
+    for chain in range(CHAINS):
+        for at, half in enumerate((1 - mine, mine)):
+            first = pl.multiple_of((half * CHAINS + chain) * size, size)
+            out_refs[2 * chain + at][...] = acc[pl.ds(first, size), :]
 
 
 def partial_halves(features, signs, columns, feat_count):
@@ -79,12 +83,12 @@
     parts = max(1, width // 2048)
     high_count = width // LOW
     total_bits = (width * feat_count).bit_length() - 1
-    half = jax.ShapeDtypeStruct((rows // 2, kept), jnp.float32)
+    piece = jax.ShapeDtypeStruct((rows // (2 * CHAINS), kept), jnp.float32)
     return pl.pallas_call(
         functools.partial(partial_kernel, high_count, total_bits, parts),
         in_specs=[pl.BlockSpec(memory_space=pltpu.HBM)] * 3,
-        out_specs=[pl.BlockSpec(memory_space=pltpu.VMEM)] * 2,
-        out_shape=[half, half],
+        out_specs=[pl.BlockSpec(memory_space=pltpu.VMEM)] * (2 * CHAINS),
+        out_shape=[piece] * (2 * CHAINS),
         scratch_shapes=[
             pltpu.VMEM((rows, width), jnp.bfloat16),
             pltpu.VMEM((1, width), jnp.int32),
@@ -105,12 +109,13 @@
     ))
 
 
-def gram_kernel(shard, group, factor, a_ref, b_ref, out_ref, rows, own, label):
+def gram_kernel(shard, group, factor, *refs):
+    pieces, (out_ref, rows, own, label) = refs[:-4], refs[-4:]
     step = pl.program_id(0)
     kept = out_ref.shape[1]
     wide = group * shard
     steps = pl.num_programs(0)
-    half = a_ref.shape[0]
+    size = pieces[0].shape[0]
 
     @pl.when(step == 0)
     def _():
@@ -118,9 +123,9 @@
         source = lax.broadcasted_iota(jnp.int32, (kept, wide), 0)
         lane = lax.broadcasted_iota(jnp.int32, (kept, wide), 1)
         pick = jnp.where(source == first + (lane & (shard - 1)), 1.0, 0.0).astype(jnp.bfloat16)
-        lane = lax.broadcasted_iota(jnp.int32, (half, wide), 1)
-        for at, ref in enumerate((a_ref, b_ref)):
-            span = slice(at * half, (at + 1) * half)
+        lane = lax.broadcasted_iota(jnp.int32, (size, wide), 1)
+        for at, ref in enumerate(pieces):
+            span = slice(at * size, (at + 1) * size)
             rows[span] = ref[:, :kept]
             named = ref[:, kept:kept + 1].astype(jnp.float32).astype(jnp.int32)
             label[span] = named - lane // shard
@@ -132,26 +137,27 @@
     out_ref[...] = gram * factor
 
 
-def gram_blocks(ours, theirs, concepts, shard, kept, factor):
-    tokens, lanes = ours.shape
+def gram_blocks(pieces, concepts, shard, kept, factor):
+    size, lanes = pieces[0].shape
+    tokens = size * len(pieces)
     group = max(1, min(concepts, LOW // shard))
     return pl.pallas_call(
         functools.partial(gram_kernel, shard, group, factor),
         grid=(concepts // group,),
-        in_specs=[pl.BlockSpec((tokens, lanes), lambda i: (0, 0))] * 2,
+        in_specs=[pl.BlockSpec((size, lanes), lambda i: (0, 0))] * len(pieces),
         out_specs=pl.BlockSpec((group * shard, kept), lambda i: (i, 0)),
         out_shape=jax.ShapeDtypeStruct((concepts * shard, kept), jnp.float32),
         scratch_shapes=[
-            pltpu.VMEM((2 * tokens, kept), jnp.bfloat16),
-            pltpu.VMEM((2 * tokens, group * shard), jnp.float32),
-            pltpu.VMEM((2 * tokens, group * shard), jnp.int32),
+            pltpu.VMEM((tokens, kept), jnp.bfloat16),
+            pltpu.VMEM((tokens, group * shard), jnp.float32),
+            pltpu.VMEM((tokens, group * shard), jnp.int32),
         ],
         compiler_params=pltpu.CompilerParams(vmem_limit_bytes=VMEM_LIMIT),
         cost_estimate=pl.CostEstimate(
-            flops=4 * tokens * concepts * shard * kept, bytes_accessed=4 * concepts * shard * kept, transcendentals=0
+            flops=2 * tokens * concepts * shard * kept, bytes_accessed=4 * concepts * shard * kept, transcendentals=0
         ),
         name="gram",
-    )(ours, theirs)
+    )(*pieces)
 
 
 def encode(values, word_ref):
@@ -217,41 +223,44 @@
     tok_count = lax.axis_size("tok")
     kept = columns.shape[0]
     shard = kept // feat_count
-    size = rows // 4
+    size = rows // (4 * CHAINS)
     total_type = jax.ShapeDtypeStruct((size, kept), jnp.float32)
     word_type = jax.ShapeDtypeStruct((size // 2, kept + LANES), jnp.int32)
     row_type = jax.ShapeDtypeStruct((size, kept + LANES), jnp.bfloat16)
-
-    first = (feat_index & 1) * (rows // 2) + (feat_index >> 1 & 1) * size
-    own_labels = lax.dynamic_slice_in_dim(labels, first, size, 0).astype(jnp.bfloat16)
-    own_labels = jnp.broadcast_to(own_labels, (size, LANES))
-
-    send, keep = partial_halves(features, signs, columns, feat_count)
-    got = swap(send, "feat", 1)
-    total, word = local_call(
-        functools.partial(first_kernel, 2), "first_split", keep, got, out_shape=[total_type, word_type]
-    )
-    word = swap(word, "feat", 2)
+    scale = 1.0 / math.sqrt(width * feat_count)
+
+    pieces = partial_halves(features, signs, columns, feat_count)
+    chains = []
+    for chain in range(CHAINS):
+        first = ((feat_index & 1) * CHAINS + chain) * 2 * size + (feat_index >> 1 & 1) * size
+        own_labels = lax.dynamic_slice_in_dim(labels, first, size, 0).astype(jnp.bfloat16)
+        own_labels = jnp.broadcast_to(own_labels, (size, LANES))
+        chains.append([own_labels, pieces[2 * chain + 1], swap(pieces[2 * chain], "feat", 1)])
+    for chain in chains:
+        chain[1:] = local_call(
+            functools.partial(first_kernel, 2), "first_split", *chain[1:], out_shape=[total_type, word_type]
+        )
+        chain[2] = swap(chain[2], "feat", 2)
     stride = 4
     while stride < feat_count:
-        total, word = local_call(
-            middle_kernel, "add_encode", total, word, out_shape=[total_type, word_type]
+        for chain in chains:
+            chain[1:] = local_call(middle_kernel, "add_encode", *chain[1:], out_shape=[total_type, word_type])
+            chain[2] = swap(chain[2], "feat", stride)
+        stride *= 2
+    rows_of = [
+        local_call(
+            functools.partial(last_kernel, scale), "sketch_rows", total, word, own_labels, out_shape=row_type
         )
-        word = swap(word, "feat", stride)
-        stride *= 2
-    scale = 1.0 / math.sqrt(width * feat_count)
-    ours = local_call(
-        functools.partial(last_kernel, scale), "sketch_rows", total, word, own_labels, out_shape=row_type
-    )
-
+        for own_labels, total, word in chains
+    ]
     stride = 1
     while stride < tok_count:
-        ours = jnp.concatenate([ours, swap(ours, "tok", stride)], axis=0)
+        rows_of = [jnp.concatenate([ours, swap(ours, "tok", stride)], axis=0) for ours in rows_of]
         stride *= 2
-    ours = jnp.concatenate([ours, swap(ours, "feat", 2)], axis=0)
-    theirs = swap(ours, "feat", 1)
+    rows_of = [jnp.concatenate([ours, swap(ours, "feat", 2)], axis=0) for ours in rows_of]
+    rows_of = rows_of + [swap(ours, "feat", 1) for ours in rows_of]
     concepts = C // tok_count
-    gram = gram_blocks(ours, theirs, concepts, shard, kept, C / (rows * tok_count))
+    gram = gram_blocks(rows_of, concepts, shard, kept, C / (rows * tok_count))
     return gram.reshape(concepts, shard, kept)
 
 

time: 36.5 us -> 36.8 us (level)
  waiting for transfers between devices: 16 us -> 9.72 us
  starting transfers between devices: 12.1 us -> 18 us
  Pallas kernels: 8.03 us -> 8.52 us
    ppermute x7 -> x14, waiting for transfers between devices: 16 us -> 9.72 us  [swap(): lax.ppermute(array, axis, [(i, i ^ offset) for i in range(lax.axis_size(a...]
    ppermute x7 -> x14, starting transfers between devices: 12.1 us -> 18 us  [swap(): lax.ppermute(array, axis, [(i, i ^ offset) for i in range(lax.axis_size(a...]
    pallas_call x4 -> x8, Pallas kernels: 0.63 us -> 1.12 us  [local_call(): pl.pallas_call(kernel, out_shape=out_shape, compiler_params=pltpu.Compile...]
  transfers between devices with their start and end apart: 7 -> 14, of which waited for: 7 -> 9; matrix products, arithmetic and copies ran while one was open for 0% -> 1% of each run, Pallas kernels for 0% -> 3%
where the time goes in v4:
time: 36.8 us; the launch traced here: 36.7 us
  starting transfers between devices  18 us (49%)
  waiting for transfers between devices  9.72 us (26%)
  Pallas kernels  8.52 us (23%)
    ppermute x14, starting transfers between devices, swap(): lax.ppermute(array, axis, [(i, i ^ offset) for i in range(lax.axis_size(a...  18 us
    ppermute x14, waiting for transfers between devices, swap(): lax.ppermute(array, axis, [(i, i ^ offset) for i in range(lax.axis_size(a...  9.72 us
    pallas_call x1, Pallas kernels, partial_halves(): pl.pallas_call(functools.partial(partial_kernel, high_count, total_bits,...  4.1 us
    pallas_call x1, Pallas kernels, gram_blocks(): pl.pallas_call(functools.partial(gram_kernel, shard, group, factor), grid...  3.29 us
    pallas_call x8, Pallas kernels, local_call(): pl.pallas_call(kernel, out_shape=out_shape, compiler_params=pltpu.Compile...  1.12 us
  transfers between devices with their start and end apart: 14, of which 9 were waited for; matrix products, arithmetic and copies ran while one was open for 1% of the time, Pallas kernels for 3%

profile of v4, /device:TPU:0, one launch (start us, length us, event | category | flops | bytes accessed | tf_op | source)
XLA Modules:
  0.0 36.7 jit_solution(12266982523121587232)
XLA Ops:
  0.0 4.1 %partial_transform.1 = (f32[32,1024]{1,0:T(8,128)S(1)}, f32[32,1024]{1,0:T(8,128)S(1)}, f32[32,1024]{1,0:T(8,128)S(1)}, f32[32,1024]{1,0:T(8,128)S(1)}) custom-call(bf16[128,8192]{1,0:T(8,128)(2,1)} %x_hbm.1, s32[1,8192]{1,0:T(1,128)} %bitcast.7, s32[1,1024]{1,0:T(1,128)} %bitcast.8), custom_call_target="tpu_custom_call" | custom-call | flops 2147483648 | bytes 2621440 | tf_op jit(solution)/shard_map/partial_transform/pallas_call | solution.py:87
  4.1 0.5 %collective-permute-start.6 = (f32[32,1024]{1,0:T(8,128)S(1)}, f32[32,1024]{1,0:T(8,128)S(1)}, u32[]{:S(2)}, u32[]{:S(2)}) collective-permute-start(f32[32,1024]{1,0:T(8,128)S(1)} %get-tuple-element.30), channel_id=1, source_target_pairs={{0,2},{2,0},{4,6},{6,4},{8,10},{10,8},{12,14},{14,12},{16,18},{18,... | collective-permute-start | bytes 393224 | tf_op jit(solution)/shard_map/ppermute | solution.py:216
  4.7 0.9 %collective-permute-done.6.got_ref = f32[32,1024]{1,0:T(8,128)S(1)} collective-permute-done((f32[32,1024]{1,0:T(8,128)S(1)}, f32[32,1024]{1,0:T(8,128)S(1)}, u32[]{:S(2)}, u32[]{:S(2)}) %collective-permute-start.6) | collective-permute-done | bytes 131104 | tf_op jit(solution)/shard_map/ppermute | solution.py:216
  5.7 2.9 %collective-permute-start.7 = (s32[8,1152]{1,0:T(8,128)S(1)}, s32[8,1152]{1,0:T(8,128)S(1)}, u32[]{:S(2)}, u32[]{:S(2)}) collective-permute-start(s32[8,1152]{1,0:T(8,128)S(1)} %get-tuple-element.32), channel_id=1, source_target_pairs={{0,4},{2,6},{4,0},{6,2},{8,12},{10,14},{12,8},{14,10},{16,20},{18,... | collective-permute-start | bytes 110600 | tf_op jit(solution)/shard_map/ppermute | solution.py:216
  8.9 1.7 %collective-permute-done.7.word_ref = s32[8,1152]{1,0:T(8,128)S(1)} collective-permute-done((s32[8,1152]{1,0:T(8,128)S(1)}, s32[8,1152]{1,0:T(8,128)S(1)}, u32[]{:S(2)}, u32[]{:S(2)}) %collective-permute-start.7) | collective-permute-done | bytes 36896 | tf_op jit(solution)/shard_map/ppermute | solution.py:216
  10.8 2.2 %collective-permute-start.8 = (s32[8,1152]{1,0:T(8,128)S(1)}, s32[8,1152]{1,0:T(8,128)S(1)}, u32[]{:S(2)}, u32[]{:S(2)}) collective-permute-start(s32[8,1152]{1,0:T(8,128)S(1)} %get-tuple-element.34), channel_id=1, source_target_pairs={{0,8},{2,10},{4,12},{6,14},{8,0},{10,2},{12,4},{14,6},{16,24},{18,... | collective-permute-start | bytes 110600 | tf_op jit(solution)/shard_map/ppermute | solution.py:216
  12.9 0.2 add_encode.4
  13.1 1.5 %collective-permute-start.2 = (s32[8,1152]{1,0:T(8,128)S(1)}, s32[8,1152]{1,0:T(8,128)S(1)}, u32[]{:S(2)}, u32[]{:S(2)}) collective-permute-start(s32[8,1152]{1,0:T(8,128)S(1)} %get-tuple-element.26), channel_id=1, source_target_pairs={{0,8},{2,10},{4,12},{6,14},{8,0},{10,2},{12,4},{14,6},{16,24},{18,... | collective-permute-start | bytes 110600 | tf_op jit(solution)/shard_map/ppermute | solution.py:216
  14.6 0.6 %collective-permute-done.8.word_ref = s32[8,1152]{1,0:T(8,128)S(1)} collective-permute-done((s32[8,1152]{1,0:T(8,128)S(1)}, s32[8,1152]{1,0:T(8,128)S(1)}, u32[]{:S(2)}, u32[]{:S(2)}) %collective-permute-start.8) | collective-permute-done | bytes 36896 | tf_op jit(solution)/shard_map/ppermute | solution.py:216
  15.2 0.2 add_encode.7
  15.4 2.7 %collective-permute-start.9 = (s32[8,1152]{1,0:T(8,128)S(1)}, s32[8,1152]{1,0:T(8,128)S(1)}, u32[]{:S(2)}, u32[]{:S(2)}) collective-permute-start(s32[8,1152]{1,0:T(8,128)S(1)} %get-tuple-element.36), channel_id=1, source_target_pairs={{0,16},{2,18},{4,20},{6,22},{8,24},{10,26},{12,28},{14,30},{16,0},... | collective-permute-start | bytes 110600 | tf_op jit(solution)/shard_map/ppermute | solution.py:216
  18.2 0.2 add_encode.5
  18.4 1.6 %collective-permute-start.3 = (s32[8,1152]{1,0:T(8,128)S(1)}, s32[8,1152]{1,0:T(8,128)S(1)}, u32[]{:S(2)}, u32[]{:S(2)}) collective-permute-start(s32[8,1152]{1,0:T(8,128)S(1)} %get-tuple-element.28), channel_id=1, source_target_pairs={{0,16},{2,18},{4,20},{6,22},{8,24},{10,26},{12,28},{14,30},{16,0},... | collective-permute-start | bytes 110600 | tf_op jit(solution)/shard_map/ppermute | solution.py:216
  20.0 0.4 collective-permute-done.9.word_ref
  20.5 1.7 %collective-permute-start.10 = (bf16[16,1152]{1,0:T(8,128)(2,1)S(1)}, bf16[16,1152]{1,0:T(8,128)(2,1)S(1)}, u32[]{:S(2)}, u32[]{:S(2)}) collective-permute-start(bf16[16,1152]{1,0:T(8,128)(2,1)S(1)} %sketch_rows.3), channel_id=1, source_target_pairs={{0,1},{1,0},{2,3},{3,2},{4,5},{5,4},{6,7},{7,6},{8,9},{9,8},{10,11... | collective-permute-start | bytes 110600 | tf_op jit(solution)/shard_map/ppermute | solution.py:216
  22.2 1.2 %collective-permute-done.3.word_ref = s32[8,1152]{1,0:T(8,128)S(1)} collective-permute-done((s32[8,1152]{1,0:T(8,128)S(1)}, s32[8,1152]{1,0:T(8,128)S(1)}, u32[]{:S(2)}, u32[]{:S(2)}) %collective-permute-start.3) | collective-permute-done | bytes 36896 | tf_op jit(solution)/shard_map/ppermute | solution.py:216
  23.5 1.6 %collective-permute-start.4 = (bf16[16,1152]{1,0:T(8,128)(2,1)S(1)}, bf16[16,1152]{1,0:T(8,128)(2,1)S(1)}, u32[]{:S(2)}, u32[]{:S(2)}) collective-permute-start(bf16[16,1152]{1,0:T(8,128)(2,1)S(1)} %sketch_rows.2), channel_id=1, source_target_pairs={{0,1},{1,0},{2,3},{3,2},{4,5},{5,4},{6,7},{7,6},{8,9},{9,8},{10,11... | collective-permute-start | bytes 110600 | tf_op jit(solution)/shard_map/ppermute | solution.py:216
  25.1 1.6 %collective-permute-start.11 = (bf16[32,1152]{1,0:T(8,128)(2,1)S(1)}, bf16[32,1152]{1,0:T(8,128)(2,1)S(1)}, u32[]{:S(2)}, u32[]{:S(2)}) collective-permute-start(bf16[32,1152]{1,0:T(8,128)(2,1)S(1)} %pad_maximum_fusion.3), channel_id=1, source_target_pairs={{0,4},{2,6},{4,0},{6,2},{8,12},{10,14},{12,8},{14,10},{16,20},{18,... | collective-permute-start | bytes 221192 | tf_op jit(solution)/shard_map/ppermute | solution.py:216
  26.7 0.9 %collective-permute-done.4 = bf16[16,1152]{1,0:T(8,128)(2,1)S(1)} collective-permute-done((bf16[16,1152]{1,0:T(8,128)(2,1)S(1)}, bf16[16,1152]{1,0:T(8,128)(2,1)S(1)}, u32[]{:S(2)}, u32[]{:S(2)}) %collective-permute-start.4) | collective-permute-done | bytes 36896 | tf_op jit(solution)/shard_map/ppermute | solution.py:216
  27.6 1.5 %collective-permute-start.5 = (bf16[32,1152]{1,0:T(8,128)(2,1)S(1)}, bf16[32,1152]{1,0:T(8,128)(2,1)S(1)}, u32[]{:S(2)}, u32[]{:S(2)}) collective-permute-start(bf16[32,1152]{1,0:T(8,128)(2,1)S(1)} %pad_maximum_fusion.2), channel_id=1, source_target_pairs={{0,4},{2,6},{4,0},{6,2},{8,12},{10,14},{12,8},{14,10},{16,20},{18,... | collective-permute-start | bytes 221192 | tf_op jit(solution)/shard_map/ppermute | solution.py:216
  29.1 0.5 %collective-permute-done.11 = bf16[32,1152]{1,0:T(8,128)(2,1)S(1)} collective-permute-done((bf16[32,1152]{1,0:T(8,128)(2,1)S(1)}, bf16[32,1152]{1,0:T(8,128)(2,1)S(1)}, u32[]{:S(2)}, u32[]{:S(2)}) %collective-permute-start.11) | collective-permute-done | bytes 73760 | tf_op jit(solution)/shard_map/ppermute | solution.py:216
  29.6 2.3 %collective-permute-done.5 = bf16[32,1152]{1,0:T(8,128)(2,1)S(1)} collective-permute-done((bf16[32,1152]{1,0:T(8,128)(2,1)S(1)}, bf16[32,1152]{1,0:T(8,128)(2,1)S(1)}, u32[]{:S(2)}, u32[]{:S(2)}) %collective-permute-start.5) | collective-permute-done | bytes 73760 | tf_op jit(solution)/shard_map/ppermute | solution.py:216
  32.0 1.3 %collective-permute-done.12.refs_2_ = bf16[64,1152]{1,0:T(8,128)(2,1)S(1)} collective-permute-done((bf16[64,1152]{1,0:T(8,128)(2,1)S(1)}, bf16[64,1152]{1,0:T(8,128)(2,1)S(1)}, u32[]{:S(2)}, u32[]{:S(2)}) %collective-permute-start.12) | collective-permute-done | bytes 147488 | tf_op jit(solution)/shard_map/ppermute | solution.py:216
  33.4 3.3 %gram.1 = f32[1024,1024]{1,0:T(8,128)} custom-call(bf16[64,1152]{1,0:T(8,128)(2,1)S(1)} %pad_maximum_fusion.refs_0_, bf16[64,1152]{1,0:T(8,128)(2,1)S(1)} %pad_maximum_fusion.1.refs_1_, bf16[64,1152]{1,0:T(8,128)(2,1)S(1)} %collective-permute-done.12.refs_2_, bf16[64,1152]{1,0:T(8,128)(2,1)S(1)} %collective-permute-done.13.refs_3_), custom_call_target="tpu_custom_call" | custom-call | flops 536870912 | bytes 4194304 | tf_op jit(solution)/shard_map/gram/pallas_call | solution.py:144
  (23 shorter events, 1.2 us)
Async XLA Ops:
  0.0 18.2 %copy-start = (s32[128,1]{0,1:T(1,128)S(1)}, s32[128,1]{0,1:T(1,128)}, u32[]{:S(2)}) copy-start(s32[128,1]{0,1:T(1,128)} %param.7) | copy-start | bytes 1540
  4.1 1.5 %collective-permute-start.6 = (f32[32,1024]{1,0:T(8,128)S(1)}, f32[32,1024]{1,0:T(8,128)S(1)}, u32[]{:S(2)}, u32[]{:S(2)}) collective-permute-start(f32[32,1024]{1,0:T(8,128)S(1)} %get-tuple-element.30), channel_id=1, source_target_pairs={{0,2},{2,0},{4,6},{6,4},{8,10},{10,8},{12,14},{14,12},{16,18},{18,... | collective-permute-start | bytes 393224 | tf_op jit(solution)/shard_map/ppermute | solution.py:216
  4.6 4.0 %collective-permute-start = (f32[32,1024]{1,0:T(8,128)S(1)}, f32[32,1024]{1,0:T(8,128)S(1)}, u32[]{:S(2)}, u32[]{:S(2)}) collective-permute-start(f32[32,1024]{1,0:T(8,128)S(1)} %get-tuple-element.22), channel_id=1, source_target_pairs={{0,2},{2,0},{4,6},{6,4},{8,10},{10,8},{12,14},{14,12},{16,18},{18,... | collective-permute-start | bytes 393224 | tf_op jit(solution)/shard_map/ppermute | solution.py:216
  5.7 4.8 %collective-permute-start.7 = (s32[8,1152]{1,0:T(8,128)S(1)}, s32[8,1152]{1,0:T(8,128)S(1)}, u32[]{:S(2)}, u32[]{:S(2)}) collective-permute-start(s32[8,1152]{1,0:T(8,128)S(1)} %get-tuple-element.32), channel_id=1, source_target_pairs={{0,4},{2,6},{4,0},{6,2},{8,12},{10,14},{12,8},{14,10},{16,20},{18,... | collective-permute-start | bytes 110600 | tf_op jit(solution)/shard_map/ppermute | solution.py:216
  8.8 4.2 %collective-permute-start.1 = (s32[8,1152]{1,0:T(8,128)S(1)}, s32[8,1152]{1,0:T(8,128)S(1)}, u32[]{:S(2)}, u32[]{:S(2)}) collective-permute-start(s32[8,1152]{1,0:T(8,128)S(1)} %get-tuple-element.24), channel_id=1, source_target_pairs={{0,4},{2,6},{4,0},{6,2},{8,12},{10,14},{12,8},{14,10},{16,20},{18,... | collective-permute-start | bytes 110600 | tf_op jit(solution)/shard_map/ppermute | solution.py:216
  10.8 4.5 %collective-permute-start.8 = (s32[8,1152]{1,0:T(8,128)S(1)}, s32[8,1152]{1,0:T(8,128)S(1)}, u32[]{:S(2)}, u32[]{:S(2)}) collective-permute-start(s32[8,1152]{1,0:T(8,128)S(1)} %get-tuple-element.34), channel_id=1, source_target_pairs={{0,8},{2,10},{4,12},{6,14},{8,0},{10,2},{12,4},{14,6},{16,24},{18,... | collective-permute-start | bytes 110600 | tf_op jit(solution)/shard_map/ppermute | solution.py:216
  13.1 5.1 %collective-permute-start.2 = (s32[8,1152]{1,0:T(8,128)S(1)}, s32[8,1152]{1,0:T(8,128)S(1)}, u32[]{:S(2)}, u32[]{:S(2)}) collective-permute-start(s32[8,1152]{1,0:T(8,128)S(1)} %get-tuple-element.26), channel_id=1, source_target_pairs={{0,8},{2,10},{4,12},{6,14},{8,0},{10,2},{12,4},{14,6},{16,24},{18,... | collective-permute-start | bytes 110600 | tf_op jit(solution)/shard_map/ppermute | solution.py:216
  15.4 4.9 %collective-permute-start.9 = (s32[8,1152]{1,0:T(8,128)S(1)}, s32[8,1152]{1,0:T(8,128)S(1)}, u32[]{:S(2)}, u32[]{:S(2)}) collective-permute-start(s32[8,1152]{1,0:T(8,128)S(1)} %get-tuple-element.36), channel_id=1, source_target_pairs={{0,16},{2,18},{4,20},{6,22},{8,24},{10,26},{12,28},{14,30},{16,0},... | collective-permute-start | bytes 110600 | tf_op jit(solution)/shard_map/ppermute | solution.py:216
  18.4 4.9 %collective-permute-start.3 = (s32[8,1152]{1,0:T(8,128)S(1)}, s32[8,1152]{1,0:T(8,128)S(1)}, u32[]{:S(2)}, u32[]{:S(2)}) collective-permute-start(s32[8,1152]{1,0:T(8,128)S(1)} %get-tuple-element.28), channel_id=1, source_target_pairs={{0,16},{2,18},{4,20},{6,22},{8,24},{10,26},{12,28},{14,30},{16,0},... | collective-permute-start | bytes 110600 | tf_op jit(solution)/shard_map/ppermute | solution.py:216
  20.5 4.6 %collective-permute-start.10 = (bf16[16,1152]{1,0:T(8,128)(2,1)S(1)}, bf16[16,1152]{1,0:T(8,128)(2,1)S(1)}, u32[]{:S(2)}, u32[]{:S(2)}) collective-permute-start(bf16[16,1152]{1,0:T(8,128)(2,1)S(1)} %sketch_rows.3), channel_id=1, source_target_pairs={{0,1},{1,0},{2,3},{3,2},{4,5},{5,4},{6,7},{7,6},{8,9},{9,8},{10,11... | collective-permute-start | bytes 110600 | tf_op jit(solution)/shard_map/ppermute | solution.py:216
  23.5 4.0 %collective-permute-start.4 = (bf16[16,1152]{1,0:T(8,128)(2,1)S(1)}, bf16[16,1152]{1,0:T(8,128)(2,1)S(1)}, u32[]{:S(2)}, u32[]{:S(2)}) collective-permute-start(bf16[16,1152]{1,0:T(8,128)(2,1)S(1)} %sketch_rows.2), channel_id=1, source_target_pairs={{0,1},{1,0},{2,3},{3,2},{4,5},{5,4},{6,7},{7,6},{8,9},{9,8},{10,11... | collective-permute-start | bytes 110600 | tf_op jit(solution)/shard_map/ppermute | solution.py:216
  25.1 4.4 %collective-permute-start.11 = (bf16[32,1152]{1,0:T(8,128)(2,1)S(1)}, bf16[32,1152]{1,0:T(8,128)(2,1)S(1)}, u32[]{:S(2)}, u32[]{:S(2)}) collective-permute-start(bf16[32,1152]{1,0:T(8,128)(2,1)S(1)} %pad_maximum_fusion.3), channel_id=1, source_target_pairs={{0,4},{2,6},{4,0},{6,2},{8,12},{10,14},{12,8},{14,10},{16,20},{18,... | collective-permute-start | bytes 221192 | tf_op jit(solution)/shard_map/ppermute | solution.py:216
  27.6 4.4 %collective-permute-start.5 = (bf16[32,1152]{1,0:T(8,128)(2,1)S(1)}, bf16[32,1152]{1,0:T(8,128)(2,1)S(1)}, u32[]{:S(2)}, u32[]{:S(2)}) collective-permute-start(bf16[32,1152]{1,0:T(8,128)(2,1)S(1)} %pad_maximum_fusion.2), channel_id=1, source_target_pairs={{0,4},{2,6},{4,0},{6,2},{8,12},{10,14},{12,8},{14,10},{16,20},{18,... | collective-permute-start | bytes 221192 | tf_op jit(solution)/shard_map/ppermute | solution.py:216
  29.6 2.4 %collective-permute-start.13 = (bf16[64,1152]{1,0:T(8,128)(2,1)S(1)}, bf16[64,1152]{1,0:T(8,128)(2,1)S(1)}, u32[]{:S(2)}, u32[]{:S(2)}) collective-permute-start(bf16[64,1152]{1,0:T(8,128)(2,1)S(1)} %pad_maximum_fusion.1.refs_1_), channel_id=1, source_target_pairs={{0,2},{2,0},{4,6},{6,4},{8,10},{10,8},{12,14},{14,12},{16,18},{18,... | collective-permute-start | bytes 442376 | tf_op jit(solution)/shard_map/ppermute | solution.py:216
  31.9 1.4 %collective-permute-start.12 = (bf16[64,1152]{1,0:T(8,128)(2,1)S(1)}, bf16[64,1152]{1,0:T(8,128)(2,1)S(1)}, u32[]{:S(2)}, u32[]{:S(2)}) collective-permute-start(bf16[64,1152]{1,0:T(8,128)(2,1)S(1)} %pad_maximum_fusion.refs_0_), channel_id=1, source_target_pairs={{0,2},{2,0},{4,6},{6,4},{8,10},{10,8},{12,14},{14,12},{16,18},{18,... | collective-permute-start | bytes 442376 | tf_op jit(solution)/shard_map/ppermute | solution.py:216

commit v5 on v4

v5 whole, which is shorter than its diff:
```python
import functools
import math

import jax
import jax.numpy as jnp
from jax import lax
from jax.experimental import pallas as pl
from jax.experimental.pallas import tpu as pltpu
from jax.sharding import PartitionSpec as P

C = 32
LOW = 256
LANES = 128
VMEM_LIMIT = 48 * 1024 * 1024


def parity_sign(number, bit_count):
    shift = 1
    while shift < bit_count:
        shift *= 2
    while shift > 1:
        shift //= 2
        number = number ^ (number >> shift)
    return (1 - 2 * (number & 1)).astype(jnp.float32)


def partial_kernel(high_count, total_bits, parts, x_hbm, s_hbm, col_hbm, near_ref, far_ref, x_buf, s_buf, col_buf, low, high, sems):
    kept = col_hbm.shape[1]
    wide = x_hbm.shape[1] // parts
    me = lax.axis_index("feat")
    col_copy = pltpu.make_async_copy(col_hbm, col_buf, sems.at[parts])
    sign_copy = pltpu.make_async_copy(s_hbm, s_buf, sems.at[parts + 1])
    col_copy.start()
    sign_copy.start()
    copies = []
    for part in range(parts):
        cols = pl.ds(part * wide, wide)
        copies.append(pltpu.make_async_copy(x_hbm.at[:, cols], x_buf.at[:, cols], sems.at[part]))
        copies[-1].start()
    col_copy.wait()
    col = col_buf[...]
    index = lax.broadcasted_iota(jnp.int32, (16, kept), 0)
    inner = parity_sign(index & col, 4)
    outer = parity_sign(index & (col >> 4), 4)
    for row in range(LOW // 16):
        low[row * 16:(row + 1) * 16] = (inner * outer[row:row + 1]).astype(jnp.bfloat16)
    high_index = lax.broadcasted_iota(jnp.int32, high.shape, 0) + me * high_count
    high[...] = parity_sign(high_index & (col >> 8), total_bits - 8)
    sign_copy.wait()
    blocks = wide // LOW
    rows = x_hbm.shape[0]
    for part in range(parts):
        copies[part].wait()
        stack = []
        for block in range(part * blocks, (part + 1) * blocks):
            cols = slice(block * LOW, (block + 1) * LOW)
            stack.append(x_buf[:, cols] * s_buf[:, cols].astype(jnp.bfloat16))
        stack = jnp.concatenate(stack, axis=0)
        for group in range(kept // LOW):
            cols = slice(group * LOW, (group + 1) * LOW)
            products = jnp.dot(stack, low[:, cols], preferred_element_type=jnp.float32)
            total = None
            for at in range(blocks):
                row = part * blocks + at
                term = products[at * rows:(at + 1) * rows] * high[row:row + 1, cols]
                total = term if total is None else total + term
            for ref, span in ((near_ref, slice(0, near_ref.shape[0])), (far_ref, slice(near_ref.shape[0], rows))):
                if part > 0:
                    ref[:, cols] += total[span]
                else:
                    ref[:, cols] = total[span]


def partial_rows(features, signs, columns, feat_count, near):
    rows, width = features.shape
    kept = columns.shape[0]
    parts = max(1, width // 2048)
    high_count = width // LOW
    total_bits = (width * feat_count).bit_length() - 1
    return pl.pallas_call(
        functools.partial(partial_kernel, high_count, total_bits, parts),
        in_specs=[pl.BlockSpec(memory_space=pltpu.HBM)] * 3,
        out_specs=[pl.BlockSpec(memory_space=pltpu.VMEM)] * 2,
        out_shape=[jax.ShapeDtypeStruct((size, kept), jnp.float32) for size in (near, rows - near)],
        scratch_shapes=[
            pltpu.VMEM((rows, width), jnp.bfloat16),
            pltpu.VMEM((1, width), jnp.int32),
            pltpu.VMEM((1, kept), jnp.int32),
            pltpu.VMEM((LOW, kept), jnp.bfloat16),
            pltpu.VMEM((high_count, kept), jnp.float32),
            pltpu.SemaphoreType.DMA((parts + 2,)),
        ],
        compiler_params=pltpu.CompilerParams(vmem_limit_bytes=VMEM_LIMIT),
        cost_estimate=pl.CostEstimate(
            flops=2 * rows * width * kept, bytes_accessed=2 * rows * width + 4 * rows * kept, transcendentals=0
        ),
        name="partial_transform",
    )(*(
        pltpu.with_memory_space_constraint(operand, pltpu.HBM)
        for operand in (features, signs.reshape(1, width), columns.reshape(1, kept))
    ))


def gram_kernel(shard, group, factor, own0, got0, own1, got1, out_ref, rows, own, label):
    step = pl.program_id(0)
    kept = out_ref.shape[1]
    wide = group * shard
    steps = pl.num_programs(0)

    def load(ref, first):
        size = ref.shape[0]
        span = slice(first, first + size)
        rows[span] = ref[:, :kept]
        lane = lax.broadcasted_iota(jnp.int32, (size, wide), 1)
        named = ref[:, kept:kept + 1].astype(jnp.float32).astype(jnp.int32)
        label[span] = named - lane // shard

    @pl.when(step == 0)
    def _():
        core = lax.rem(lax.axis_index("feat"), 2)
        for this, pair in ((0, (own0, got1)), (1, (got0, own1))):
            @pl.when(core == this)
            def _():
                load(pair[0], 0)
                load(pair[1], own0.shape[0])
        first = lax.axis_index("feat") * shard
        source = lax.broadcasted_iota(jnp.int32, (kept, wide), 0)
        lane = lax.broadcasted_iota(jnp.int32, (kept, wide), 1)
        pick = jnp.where(source == first + (lane & (shard - 1)), 1.0, 0.0).astype(jnp.bfloat16)
        own[...] = jnp.dot(rows[...], pick, preferred_element_type=jnp.float32)

    first = (lax.axis_index("tok") * steps + step) * group
    chosen = jnp.where(label[...] == first, own[...], 0.0).astype(jnp.bfloat16)
    gram = lax.dot_general(chosen, rows[...], (((0,), (0,)), ((), ())), preferred_element_type=jnp.float32)
    out_ref[...] = gram * factor


def gram_blocks(pieces, concepts, shard, kept, factor):
    tokens = pieces[0].shape[0] + pieces[2].shape[0]
    group = max(1, min(concepts, LOW // shard))
    return pl.pallas_call(
        functools.partial(gram_kernel, shard, group, factor),
        grid=(concepts // group,),
        in_specs=[pl.BlockSpec(piece.shape, lambda i: (0, 0)) for piece in pieces],
        out_specs=pl.BlockSpec((group * shard, kept), lambda i: (i, 0)),
        out_shape=jax.ShapeDtypeStruct((concepts * shard, kept), jnp.float32),
        scratch_shapes=[
            pltpu.VMEM((tokens, kept), jnp.bfloat16),
            pltpu.VMEM((tokens, group * shard), jnp.float32),
            pltpu.VMEM((tokens, group * shard), jnp.int32),
        ],
        compiler_params=pltpu.CompilerParams(vmem_limit_bytes=VMEM_LIMIT),
        cost_estimate=pl.CostEstimate(
            flops=2 * tokens * concepts * shard * kept, bytes_accessed=4 * concepts * shard * kept, transcendentals=0
        ),
        name="gram",
    )(*pieces)


def encode(values, word_ref):
    kept = values.shape[1]
    half = values.shape[0] // 2
    top = jnp.max(jnp.abs(values), axis=1, keepdims=True)
    power = jnp.ceil(jnp.log2(jnp.maximum(top, 2.0 ** -100)))
    whole = jnp.round(values * jnp.exp2(15.0 - power))
    whole = jnp.clip(whole, -32767.0, 32767.0).astype(jnp.int32)
    power = jnp.broadcast_to(power, (values.shape[0], LANES)).astype(jnp.int32)
    for cols, code in ((slice(0, kept), whole), (slice(kept, kept + LANES), power)):
        word_ref[:, cols] = (code[:half] & 0xFFFF) | (code[half:] << 16)


def decode(word_ref):
    word = word_ref[...]
    code = jnp.concatenate([(word << 16) >> 16, word >> 16], axis=0).astype(jnp.float32)
    return code[:, :-LANES] * jnp.exp2(code[:, -LANES:-LANES + 1] - 15.0)


def on_core(core):
    return pl.when(lax.rem(lax.axis_index("feat"), 2) == core)


def both_cores(kernel):
    def combined(operands, *refs):
        results = (len(refs) - 2 * operands) // 2
        for core in range(2):
            taken = refs[core * operands:(core + 1) * operands]
            given = refs[2 * operands + core * results:2 * operands + (core + 1) * results]

            @pl.when(lax.rem(lax.axis_index("feat"), 2) == core)
            def _():
                kernel(*taken, *given)

    return combined


def first_step(keep_ref, got_ref, total_ref, word_ref):
    size = total_ref.shape[0]
    digit = lax.rem(lax.axis_index("feat") // 2, 2)

    def piece(at):
        span = pl.ds(pl.multiple_of(at * size, size), size)
        return keep_ref[span, :] + got_ref[span, :]

    total_ref[...] = piece(digit)
    encode(piece(1 - digit), word_ref)


def middle_step(total_ref, word_ref, sum_ref, out_ref):
    total = total_ref[...] + decode(word_ref)
    sum_ref[...] = total
    encode(total, out_ref)


def last_step(scale, total_ref, word_ref, label_ref, row_ref):
    total = total_ref[...] + decode(word_ref)
    kept = total.shape[1]
    row_ref[:, :kept] = (total * scale).astype(jnp.bfloat16)
    row_ref[:, kept:] = label_ref[...]


def local_call(step, name, chains, out_types):
    operands = len(chains[0])
    results = len(out_types[0])
    out = pl.pallas_call(
        functools.partial(both_cores(step), operands),
        out_shape=[*out_types[0], *out_types[1]],
        compiler_params=pltpu.CompilerParams(vmem_limit_bytes=VMEM_LIMIT),
        name=name,
    )(*chains[0], *chains[1])
    return [list(out[:results]), list(out[results:])]


def move(array, core, tok=0, feat=0):
    tok_count, feat_count = lax.axis_size("tok"), lax.axis_size("feat")
    pairs = [
        (f * tok_count + t, (f ^ feat) * tok_count + (t ^ tok))
        for f in range(core, feat_count, 2)
        for t in range(tok_count)
    ]
    return lax.ppermute(array, ("feat", "tok"), pairs)


def body(features, signs, columns, labels):
    rows, width = features.shape
    feat_count = lax.axis_size("feat")
    feat_index = lax.axis_index("feat")
    tok_count = lax.axis_size("tok")
    kept = columns.shape[0]
    shard = kept // feat_count
    scale = 1.0 / math.sqrt(width * feat_count)
    near = rows // 4

    partials = partial_rows(features, signs, columns, feat_count, near)
    chains, own_labels, out_types, row_types = [], [], [], []
    first = 0
    for core, keep in enumerate(partials):
        size = keep.shape[0] // 2
        chains.append([keep, move(keep, 1 - core, feat=1)])
        labels_at = first + (feat_index >> 1 & 1) * size
        label = lax.dynamic_slice_in_dim(labels, labels_at, size, 0).astype(jnp.bfloat16)
        own_labels.append(jnp.broadcast_to(label, (size, LANES)))
        out_types.append([
            jax.ShapeDtypeStruct((size, kept), jnp.float32),
            jax.ShapeDtypeStruct((size // 2, kept + LANES), jnp.int32),
        ])
        row_types.append([jax.ShapeDtypeStruct((size, kept + LANES), jnp.bfloat16)])
        first += 2 * size
    chains = local_call(first_step, "first_split", chains, out_types)
    chains = [[total, move(word, core, feat=2)] for core, (total, word) in enumerate(chains)]
    stride = 4
    while stride < feat_count:
        chains = local_call(middle_step, "add_encode", chains, out_types)
        chains = [[total, move(word, core, feat=stride)] for core, (total, word) in enumerate(chains)]
        stride *= 2
    chains = [[*chain, label] for chain, label in zip(chains, own_labels)]
    chains = local_call(functools.partial(last_step, scale), "sketch_rows", chains, row_types)
    pieces = []
    for core, (ours,) in enumerate(chains):
        stride = 2
        while stride < tok_count:
            ours = jnp.concatenate([ours, move(ours, core, tok=stride)], axis=0)
            stride *= 2
        received = [move(ours, core, tok=1, feat=2)] if tok_count > 1 else []
        received += [move(ours, core, feat=2)]
        received += [move(ours, core, tok=1)] if tok_count > 1 else []
        ours = jnp.concatenate([ours] + received, axis=0)
        pieces += [ours, move(ours, core, feat=1)]
    concepts = C // tok_count
    gram = gram_blocks(pieces, concepts, shard, kept, C / (rows * tok_count))
    return gram.reshape(concepts, shard, kept)


def solution(mesh):
    in_specs = (P("tok", "feat"), P("feat"), P(), P("tok", None))
    out_specs = P("tok", "feat", None)
    return jax.shard_map(body, mesh=mesh, in_specs=in_specs, out_specs=out_specs, check_vma=False)
```

time: 36.8 us -> 55.9 us (1.52)
  starting transfers between devices: 18 us -> 34.1 us
  waiting for transfers between devices: 9.72 us -> 12.7 us
    ppermute x14 -> x16, starting transfers between devices: 18 us -> 34.1 us  [move(): return lax.ppermute(array, ('feat', 'tok'), pairs)]
    ppermute x14 -> x16, waiting for transfers between devices: 9.72 us -> 12.7 us  [move(): return lax.ppermute(array, ('feat', 'tok'), pairs)]
    pallas_call x9 -> x5, Pallas kernels: 5.22 us -> 4.6 us  [the longest x1 4.02 us: partial_rows(): pl.pallas_call(functools.partial(partial_kernel, high_count, total_bits,...]
  transfers between devices with their start and end apart: 14 -> 16, of which waited for: 9 -> 6; matrix products, arithmetic and copies ran while one was open for 1% -> 0% of each run, Pallas kernels for 3% -> 0%
where the time goes in v5:
time: 55.9 us; the launch traced here: 55.5 us
  starting transfers between devices  34.1 us (61%)
  waiting for transfers between devices  12.7 us (23%)
  Pallas kernels  7.97 us (14%)
    ppermute x16, starting transfers between devices, move(): return lax.ppermute(array, ('feat', 'tok'), pairs)  34.1 us
    ppermute x16, waiting for transfers between devices, move(): return lax.ppermute(array, ('feat', 'tok'), pairs)  12.7 us
    pallas_call x1, Pallas kernels, partial_rows(): pl.pallas_call(functools.partial(partial_kernel, high_count, total_bits,...  4.02 us
    pallas_call x1, Pallas kernels, gram_blocks(): pl.pallas_call(functools.partial(gram_kernel, shard, group, factor), grid...  3.37 us
  transfers between devices with their start and end apart: 16, of which 6 were waited for; matrix products, arithmetic and copies ran while one was open for 0% of the time, Pallas kernels for 0%

profile of v5, /device:TPU:0, one launch (start us, length us, event | category | flops | bytes accessed | tf_op | source)
XLA Modules:
  0.0 55.5 jit_solution(10804280902345618360)
XLA Ops:
  0.0 4.0 %partial_transform.1 = (f32[32,1024]{1,0:T(8,128)S(1)}, f32[96,1024]{1,0:T(8,128)S(1)}) custom-call(bf16[128,8192]{1,0:T(8,128)(2,1)} %x_hbm.1, s32[1,8192]{1,0:T(1,128)} %bitcast.7, s32[1,1024]{1,0:T(1,128)} %bitcast.8), custom_call_target="tpu_custom_call" | custom-call | flops 2147483648 | bytes 2621440 | tf_op jit(solution)/shard_map/partial_transform/pallas_call | solution.py:80
  4.0 2.4 %collective-permute-start.1 = (f32[96,1024]{1,0:T(8,128)S(1)}, f32[96,1024]{1,0:T(8,128)S(1)}, u32[]{:S(2)}, u32[]{:S(2)}) collective-permute-start(f32[96,1024]{1,0:T(8,128)S(1)} %get-tuple-element.22.refs_2_), channel_id=1, source_target_pairs={{0,2},{1,3},{4,6},{5,7},{8,10},{9,11},{12,14},{13,15},{16,18},{17,... | collective-permute-start | bytes 1179656 | tf_op jit(solution)/shard_map/ppermute | solution.py:240
  6.4 1.3 %collective-permute-start = (f32[32,1024]{1,0:T(8,128)S(1)}, f32[32,1024]{1,0:T(8,128)S(1)}, u32[]{:S(2)}, u32[]{:S(2)}) collective-permute-start(f32[32,1024]{1,0:T(8,128)S(1)} %get-tuple-element.21.refs_0_), channel_id=1, source_target_pairs={{2,0},{3,1},{6,4},{7,5},{10,8},{11,9},{14,12},{15,13},{18,16},{19,... | collective-permute-start | bytes 393224 | tf_op jit(solution)/shard_map/ppermute | solution.py:240
  7.7 1.9 %collective-permute-done.refs_1_ = f32[32,1024]{1,0:T(8,128)S(1)} collective-permute-done((f32[32,1024]{1,0:T(8,128)S(1)}, f32[32,1024]{1,0:T(8,128)S(1)}, u32[]{:S(2)}, u32[]{:S(2)}) %collective-permute-start) | collective-permute-done | bytes 131104 | tf_op jit(solution)/shard_map/ppermute | solution.py:240
  9.8 0.7 %collective-permute-start.3 = (s32[24,1152]{1,0:T(8,128)S(1)}, s32[24,1152]{1,0:T(8,128)S(1)}, u32[]{:S(2)}, u32[]{:S(2)}) collective-permute-start(s32[24,1152]{1,0:T(8,128)S(1)} %get-tuple-element.26), channel_id=1, source_target_pairs={{2,6},{3,7},{6,2},{7,3},{10,14},{11,15},{14,10},{15,11},{18,22},{1... | collective-permute-start | bytes 331784 | tf_op jit(solution)/shard_map/ppermute | solution.py:240
  10.5 4.2 %collective-permute-start.2 = (s32[8,1152]{1,0:T(8,128)S(1)}, s32[8,1152]{1,0:T(8,128)S(1)}, u32[]{:S(2)}, u32[]{:S(2)}) collective-permute-start(s32[8,1152]{1,0:T(8,128)S(1)} %get-tuple-element.24), channel_id=1, source_target_pairs={{0,4},{1,5},{4,0},{5,1},{8,12},{9,13},{12,8},{13,9},{16,20},{17,21... | collective-permute-start | bytes 110600 | tf_op jit(solution)/shard_map/ppermute | solution.py:240
  14.7 1.9 %collective-permute-done.2.refs_1_ = s32[8,1152]{1,0:T(8,128)S(1)} collective-permute-done((s32[8,1152]{1,0:T(8,128)S(1)}, s32[8,1152]{1,0:T(8,128)S(1)}, u32[]{:S(2)}, u32[]{:S(2)}) %collective-permute-start.2) | collective-permute-done | bytes 36896 | tf_op jit(solution)/shard_map/ppermute | solution.py:240
  16.8 4.0 %collective-permute-start.4 = (s32[8,1152]{1,0:T(8,128)S(1)}, s32[8,1152]{1,0:T(8,128)S(1)}, u32[]{:S(2)}, u32[]{:S(2)}) collective-permute-start(s32[8,1152]{1,0:T(8,128)S(1)} %get-tuple-element.28), channel_id=1, source_target_pairs={{0,8},{1,9},{4,12},{5,13},{8,0},{9,1},{12,4},{13,5},{16,24},{17,25... | collective-permute-start | bytes 110600 | tf_op jit(solution)/shard_map/ppermute | solution.py:240
  20.8 0.7 %collective-permute-start.5 = (s32[24,1152]{1,0:T(8,128)S(1)}, s32[24,1152]{1,0:T(8,128)S(1)}, u32[]{:S(2)}, u32[]{:S(2)}) collective-permute-start(s32[24,1152]{1,0:T(8,128)S(1)} %get-tuple-element.30), channel_id=1, source_target_pairs={{2,10},{3,11},{6,14},{7,15},{10,2},{11,3},{14,6},{15,7},{18,26},{1... | collective-permute-start | bytes 331784 | tf_op jit(solution)/shard_map/ppermute | solution.py:240
  21.6 1.5 %collective-permute-done.4.refs_1_ = s32[8,1152]{1,0:T(8,128)S(1)} collective-permute-done((s32[8,1152]{1,0:T(8,128)S(1)}, s32[8,1152]{1,0:T(8,128)S(1)}, u32[]{:S(2)}, u32[]{:S(2)}) %collective-permute-start.4) | collective-permute-done | bytes 36896 | tf_op jit(solution)/shard_map/ppermute | solution.py:240
  23.3 4.7 %collective-permute-start.6 = (s32[8,1152]{1,0:T(8,128)S(1)}, s32[8,1152]{1,0:T(8,128)S(1)}, u32[]{:S(2)}, u32[]{:S(2)}) collective-permute-start(s32[8,1152]{1,0:T(8,128)S(1)} %get-tuple-element.32), channel_id=1, source_target_pairs={{0,16},{1,17},{4,20},{5,21},{8,24},{9,25},{12,28},{13,29},{16,0},{... | collective-permute-start | bytes 110600 | tf_op jit(solution)/shard_map/ppermute | solution.py:240
  28.0 0.7 %collective-permute-start.7 = (s32[24,1152]{1,0:T(8,128)S(1)}, s32[24,1152]{1,0:T(8,128)S(1)}, u32[]{:S(2)}, u32[]{:S(2)}) collective-permute-start(s32[24,1152]{1,0:T(8,128)S(1)} %get-tuple-element.34), channel_id=1, source_target_pairs={{2,18},{3,19},{6,22},{7,23},{10,26},{11,27},{14,30},{15,31},{18,2}... | collective-permute-start | bytes 331784 | tf_op jit(solution)/shard_map/ppermute | solution.py:240
  28.7 3.3 %collective-permute-done.6.refs_1_ = s32[8,1152]{1,0:T(8,128)S(1)} collective-permute-done((s32[8,1152]{1,0:T(8,128)S(1)}, s32[8,1152]{1,0:T(8,128)S(1)}, u32[]{:S(2)}, u32[]{:S(2)}) %collective-permute-start.6) | collective-permute-done | bytes 36896 | tf_op jit(solution)/shard_map/ppermute | solution.py:240
  32.3 3.5 %collective-permute-start.10 = (bf16[16,1152]{1,0:T(8,128)(2,1)S(1)}, bf16[16,1152]{1,0:T(8,128)(2,1)S(1)}, u32[]{:S(2)}, u32[]{:S(2)}) collective-permute-start(bf16[16,1152]{1,0:T(8,128)(2,1)S(1)} %get-tuple-element.35), channel_id=1, source_target_pairs={{0,1},{1,0},{4,5},{5,4},{8,9},{9,8},{12,13},{13,12},{16,17},{17,16... | collective-permute-start | bytes 110600 | tf_op jit(solution)/shard_map/ppermute | solution.py:240
  35.8 3.4 %collective-permute-start.9 = (bf16[16,1152]{1,0:T(8,128)(2,1)S(1)}, bf16[16,1152]{1,0:T(8,128)(2,1)S(1)}, u32[]{:S(2)}, u32[]{:S(2)}) collective-permute-start(bf16[16,1152]{1,0:T(8,128)(2,1)S(1)} %get-tuple-element.35), channel_id=1, source_target_pairs={{0,4},{1,5},{4,0},{5,1},{8,12},{9,13},{12,8},{13,9},{16,20},{17,21... | collective-permute-start | bytes 110600 | tf_op jit(solution)/shard_map/ppermute | solution.py:240
  39.2 2.3 %collective-permute-start.8 = (bf16[16,1152]{1,0:T(8,128)(2,1)S(1)}, bf16[16,1152]{1,0:T(8,128)(2,1)S(1)}, u32[]{:S(2)}, u32[]{:S(2)}) collective-permute-start(bf16[16,1152]{1,0:T(8,128)(2,1)S(1)} %get-tuple-element.35), channel_id=1, source_target_pairs={{0,5},{1,4},{4,1},{5,0},{8,13},{9,12},{12,9},{13,8},{16,21},{17,20... | collective-permute-start | bytes 110600 | tf_op jit(solution)/shard_map/ppermute | solution.py:240
  41.5 0.7 %collective-permute-start.14 = (bf16[48,1152]{1,0:T(8,128)(2,1)S(1)}, bf16[48,1152]{1,0:T(8,128)(2,1)S(1)}, u32[]{:S(2)}, u32[]{:S(2)}) collective-permute-start(bf16[48,1152]{1,0:T(8,128)(2,1)S(1)} %get-tuple-element.36), channel_id=1, source_target_pairs={{2,3},{3,2},{6,7},{7,6},{10,11},{11,10},{14,15},{15,14},{18,19},{1... | collective-permute-start | bytes 331784 | tf_op jit(solution)/shard_map/ppermute | solution.py:240
  42.2 0.7 %collective-permute-start.13 = (bf16[48,1152]{1,0:T(8,128)(2,1)S(1)}, bf16[48,1152]{1,0:T(8,128)(2,1)S(1)}, u32[]{:S(2)}, u32[]{:S(2)}) collective-permute-start(bf16[48,1152]{1,0:T(8,128)(2,1)S(1)} %get-tuple-element.36), channel_id=1, source_target_pairs={{2,6},{3,7},{6,2},{7,3},{10,14},{11,15},{14,10},{15,11},{18,22},{1... | collective-permute-start | bytes 331784 | tf_op jit(solution)/shard_map/ppermute | solution.py:240
  42.9 3.1 %collective-permute-done.8 = bf16[16,1152]{1,0:T(8,128)(2,1)S(1)} collective-permute-done((bf16[16,1152]{1,0:T(8,128)(2,1)S(1)}, bf16[16,1152]{1,0:T(8,128)(2,1)S(1)}, u32[]{:S(2)}, u32[]{:S(2)}) %collective-permute-start.8) | collective-permute-done | bytes 36896 | tf_op jit(solution)/shard_map/ppermute | solution.py:240
  45.9 0.7 %collective-permute-start.12 = (bf16[48,1152]{1,0:T(8,128)(2,1)S(1)}, bf16[48,1152]{1,0:T(8,128)(2,1)S(1)}, u32[]{:S(2)}, u32[]{:S(2)}) collective-permute-start(bf16[48,1152]{1,0:T(8,128)(2,1)S(1)} %get-tuple-element.36), channel_id=1, source_target_pairs={{2,7},{3,6},{6,3},{7,2},{10,15},{11,14},{14,11},{15,10},{18,23},{1... | collective-permute-start | bytes 331784 | tf_op jit(solution)/shard_map/ppermute | solution.py:240
  46.7 1.3 %collective-permute-start.15 = (bf16[192,1152]{1,0:T(8,128)(2,1)S(1)}, bf16[192,1152]{1,0:T(8,128)(2,1)S(1)}, u32[]{:S(2)}, u32[]{:S(2)}) collective-permute-start(bf16[192,1152]{1,0:T(8,128)(2,1)S(1)} %constant_dynamic-update-slice_fusion.4.own1), channel_id=1, source_target_pairs={{2,0},{3,1},{6,4},{7,5},{10,8},{11,9},{14,12},{15,13},{18,16},{19,... | collective-permute-start | bytes 1327112 | tf_op jit(solution)/shard_map/ppermute | solution.py:240
  48.1 3.1 %collective-permute-start.11 = (bf16[64,1152]{1,0:T(8,128)(2,1)S(1)}, bf16[64,1152]{1,0:T(8,128)(2,1)S(1)}, u32[]{:S(2)}, u32[]{:S(2)}) collective-permute-start(bf16[64,1152]{1,0:T(8,128)(2,1)S(1)} %constant_dynamic-update-slice_fusion.own0), channel_id=1, source_target_pairs={{0,2},{1,3},{4,6},{5,7},{8,10},{9,11},{12,14},{13,15},{16,18},{17,... | collective-permute-start | bytes 442376 | tf_op jit(solution)/shard_map/ppermute | solution.py:240
  51.1 1.0 %collective-permute-done.11.got0 = bf16[64,1152]{1,0:T(8,128)(2,1)S(1)} collective-permute-done((bf16[64,1152]{1,0:T(8,128)(2,1)S(1)}, bf16[64,1152]{1,0:T(8,128)(2,1)S(1)}, u32[]{:S(2)}, u32[]{:S(2)}) %collective-permute-start.11) | collective-permute-done | bytes 147488 | tf_op jit(solution)/shard_map/ppermute | solution.py:240
  52.1 3.4 %gram.1 = f32[1024,1024]{1,0:T(8,128)} custom-call(bf16[64,1152]{1,0:T(8,128)(2,1)S(1)} %constant_dynamic-update-slice_fusion.own0, bf16[64,1152]{1,0:T(8,128)(2,1)S(1)} %collective-permute-done.11.got0, bf16[192,1152]{1,0:T(8,128)(2,1)S(1)} %constant_dynamic-update-slice_fusion.4.own1, bf16[192,1152]{1,0:T(8,128)(2,1)S(1)} %collective-permute-done.15.got1), custom_call_target="tpu_custom_call" | custom-call | flops 536870912 | bytes 4194304 | tf_op jit(solution)/shard_map/gram/pallas_call | solution.py:141
  (28 shorter events, 1.0 us)
Async XLA Ops:
  0.0 21.5 %copy-start = (s32[128,1]{0,1:T(1,128)S(1)}, s32[128,1]{0,1:T(1,128)}, u32[]{:S(2)}) copy-start(s32[128,1]{0,1:T(1,128)} %param.7) | copy-start | bytes 1540
  4.0 5.6 %collective-permute-start.1 = (f32[96,1024]{1,0:T(8,128)S(1)}, f32[96,1024]{1,0:T(8,128)S(1)}, u32[]{:S(2)}, u32[]{:S(2)}) collective-permute-start(f32[96,1024]{1,0:T(8,128)S(1)} %get-tuple-element.22.refs_2_), channel_id=1, source_target_pairs={{0,2},{1,3},{4,6},{5,7},{8,10},{9,11},{12,14},{13,15},{16,18},{17,... | collective-permute-start | bytes 1179656 | tf_op jit(solution)/shard_map/ppermute | solution.py:240
  6.4 3.2 %collective-permute-start = (f32[32,1024]{1,0:T(8,128)S(1)}, f32[32,1024]{1,0:T(8,128)S(1)}, u32[]{:S(2)}, u32[]{:S(2)}) collective-permute-start(f32[32,1024]{1,0:T(8,128)S(1)} %get-tuple-element.21.refs_0_), channel_id=1, source_target_pairs={{2,0},{3,1},{6,4},{7,5},{10,8},{11,9},{14,12},{15,13},{18,16},{19,... | collective-permute-start | bytes 393224 | tf_op jit(solution)/shard_map/ppermute | solution.py:240
  9.8 6.8 %collective-permute-start.3 = (s32[24,1152]{1,0:T(8,128)S(1)}, s32[24,1152]{1,0:T(8,128)S(1)}, u32[]{:S(2)}, u32[]{:S(2)}) collective-permute-start(s32[24,1152]{1,0:T(8,128)S(1)} %get-tuple-element.26), channel_id=1, source_target_pairs={{2,6},{3,7},{6,2},{7,3},{10,14},{11,15},{14,10},{15,11},{18,22},{1... | collective-permute-start | bytes 331784 | tf_op jit(solution)/shard_map/ppermute | solution.py:240
  10.5 6.2 %collective-permute-start.2 = (s32[8,1152]{1,0:T(8,128)S(1)}, s32[8,1152]{1,0:T(8,128)S(1)}, u32[]{:S(2)}, u32[]{:S(2)}) collective-permute-start(s32[8,1152]{1,0:T(8,128)S(1)} %get-tuple-element.24), channel_id=1, source_target_pairs={{0,4},{1,5},{4,0},{5,1},{8,12},{9,13},{12,8},{13,9},{16,20},{17,21... | collective-permute-start | bytes 110600 | tf_op jit(solution)/shard_map/ppermute | solution.py:240
  16.8 6.3 %collective-permute-start.4 = (s32[8,1152]{1,0:T(8,128)S(1)}, s32[8,1152]{1,0:T(8,128)S(1)}, u32[]{:S(2)}, u32[]{:S(2)}) collective-permute-start(s32[8,1152]{1,0:T(8,128)S(1)} %get-tuple-element.28), channel_id=1, source_target_pairs={{0,8},{1,9},{4,12},{5,13},{8,0},{9,1},{12,4},{13,5},{16,24},{17,25... | collective-permute-start | bytes 110600 | tf_op jit(solution)/shard_map/ppermute | solution.py:240
  20.8 2.3 %collective-permute-start.5 = (s32[24,1152]{1,0:T(8,128)S(1)}, s32[24,1152]{1,0:T(8,128)S(1)}, u32[]{:S(2)}, u32[]{:S(2)}) collective-permute-start(s32[24,1152]{1,0:T(8,128)S(1)} %get-tuple-element.30), channel_id=1, source_target_pairs={{2,10},{3,11},{6,14},{7,15},{10,2},{11,3},{14,6},{15,7},{18,26},{1... | collective-permute-start | bytes 331784 | tf_op jit(solution)/shard_map/ppermute | solution.py:240
  23.3 8.7 %collective-permute-start.6 = (s32[8,1152]{1,0:T(8,128)S(1)}, s32[8,1152]{1,0:T(8,128)S(1)}, u32[]{:S(2)}, u32[]{:S(2)}) collective-permute-start(s32[8,1152]{1,0:T(8,128)S(1)} %get-tuple-element.32), channel_id=1, source_target_pairs={{0,16},{1,17},{4,20},{5,21},{8,24},{9,25},{12,28},{13,29},{16,0},{... | collective-permute-start | bytes 110600 | tf_op jit(solution)/shard_map/ppermute | solution.py:240
  28.0 4.1 %collective-permute-start.7 = (s32[24,1152]{1,0:T(8,128)S(1)}, s32[24,1152]{1,0:T(8,128)S(1)}, u32[]{:S(2)}, u32[]{:S(2)}) collective-permute-start(s32[24,1152]{1,0:T(8,128)S(1)} %get-tuple-element.34), channel_id=1, source_target_pairs={{2,18},{3,19},{6,22},{7,23},{10,26},{11,27},{14,30},{15,31},{18,2}... | collective-permute-start | bytes 331784 | tf_op jit(solution)/shard_map/ppermute | solution.py:240
  32.3 15.8 %collective-permute-start.10 = (bf16[16,1152]{1,0:T(8,128)(2,1)S(1)}, bf16[16,1152]{1,0:T(8,128)(2,1)S(1)}, u32[]{:S(2)}, u32[]{:S(2)}) collective-permute-start(bf16[16,1152]{1,0:T(8,128)(2,1)S(1)} %get-tuple-element.35), channel_id=1, source_target_pairs={{0,1},{1,0},{4,5},{5,4},{8,9},{9,8},{12,13},{13,12},{16,17},{17,16... | collective-permute-start | bytes 110600 | tf_op jit(solution)/shard_map/ppermute | solution.py:240
  35.8 12.2 %collective-permute-start.9 = (bf16[16,1152]{1,0:T(8,128)(2,1)S(1)}, bf16[16,1152]{1,0:T(8,128)(2,1)S(1)}, u32[]{:S(2)}, u32[]{:S(2)}) collective-permute-start(bf16[16,1152]{1,0:T(8,128)(2,1)S(1)} %get-tuple-element.35), channel_id=1, source_target_pairs={{0,4},{1,5},{4,0},{5,1},{8,12},{9,13},{12,8},{13,9},{16,20},{17,21... | collective-permute-start | bytes 110600 | tf_op jit(solution)/shard_map/ppermute | solution.py:240
  39.2 6.8 %collective-permute-start.8 = (bf16[16,1152]{1,0:T(8,128)(2,1)S(1)}, bf16[16,1152]{1,0:T(8,128)(2,1)S(1)}, u32[]{:S(2)}, u32[]{:S(2)}) collective-permute-start(bf16[16,1152]{1,0:T(8,128)(2,1)S(1)} %get-tuple-element.35), channel_id=1, source_target_pairs={{0,5},{1,4},{4,1},{5,0},{8,13},{9,12},{12,9},{13,8},{16,21},{17,20... | collective-permute-start | bytes 110600 | tf_op jit(solution)/shard_map/ppermute | solution.py:240
  41.5 5.2 %collective-permute-start.14 = (bf16[48,1152]{1,0:T(8,128)(2,1)S(1)}, bf16[48,1152]{1,0:T(8,128)(2,1)S(1)}, u32[]{:S(2)}, u32[]{:S(2)}) collective-permute-start(bf16[48,1152]{1,0:T(8,128)(2,1)S(1)} %get-tuple-element.36), channel_id=1, source_target_pairs={{2,3},{3,2},{6,7},{7,6},{10,11},{11,10},{14,15},{15,14},{18,19},{1... | collective-permute-start | bytes 331784 | tf_op jit(solution)/shard_map/ppermute | solution.py:240
  42.2 4.5 %collective-permute-start.13 = (bf16[48,1152]{1,0:T(8,128)(2,1)S(1)}, bf16[48,1152]{1,0:T(8,128)(2,1)S(1)}, u32[]{:S(2)}, u32[]{:S(2)}) collective-permute-start(bf16[48,1152]{1,0:T(8,128)(2,1)S(1)} %get-tuple-element.36), channel_id=1, source_target_pairs={{2,6},{3,7},{6,2},{7,3},{10,14},{11,15},{14,10},{15,11},{18,22},{1... | collective-permute-start | bytes 331784 | tf_op jit(solution)/shard_map/ppermute | solution.py:240
  45.9 0.7 %collective-permute-start.12 = (bf16[48,1152]{1,0:T(8,128)(2,1)S(1)}, bf16[48,1152]{1,0:T(8,128)(2,1)S(1)}, u32[]{:S(2)}, u32[]{:S(2)}) collective-permute-start(bf16[48,1152]{1,0:T(8,128)(2,1)S(1)} %get-tuple-element.36), channel_id=1, source_target_pairs={{2,7},{3,6},{6,3},{7,2},{10,15},{11,14},{14,11},{15,10},{18,23},{1... | collective-permute-start | bytes 331784 | tf_op jit(solution)/shard_map/ppermute | solution.py:240
  46.7 5.4 %collective-permute-start.15 = (bf16[192,1152]{1,0:T(8,128)(2,1)S(1)}, bf16[192,1152]{1,0:T(8,128)(2,1)S(1)}, u32[]{:S(2)}, u32[]{:S(2)}) collective-permute-start(bf16[192,1152]{1,0:T(8,128)(2,1)S(1)} %constant_dynamic-update-slice_fusion.4.own1), channel_id=1, source_target_pairs={{2,0},{3,1},{6,4},{7,5},{10,8},{11,9},{14,12},{15,13},{18,16},{19,... | collective-permute-start | bytes 1327112 | tf_op jit(solution)/shard_map/ppermute | solution.py:240
  48.1 4.1 %collective-permute-start.11 = (bf16[64,1152]{1,0:T(8,128)(2,1)S(1)}, bf16[64,1152]{1,0:T(8,128)(2,1)S(1)}, u32[]{:S(2)}, u32[]{:S(2)}) collective-permute-start(bf16[64,1152]{1,0:T(8,128)(2,1)S(1)} %constant_dynamic-update-slice_fusion.own0), channel_id=1, source_target_pairs={{0,2},{1,3},{4,6},{5,7},{8,10},{9,11},{12,14},{13,15},{16,18},{17,... | collective-permute-start | bytes 442376 | tf_op jit(solution)/shard_map/ppermute | solution.py:240

commit v6 on v3

--- a/solution.py
+++ b/solution.py
@@ -22,6 +22,14 @@
         shift //= 2
         number = number ^ (number >> shift)
     return (1 - 2 * (number & 1)).astype(jnp.float32)
+
+
+def own_half():
+    bits = lax.axis_index("feat") ^ lax.axis_index("tok")
+    total = bits & 1
+    for position in range(1, max(lax.axis_size("feat"), lax.axis_size("tok")).bit_length() - 1):
+        total = total ^ (bits >> position & 1)
+    return total
 
 
 def partial_kernel(high_count, total_bits, parts, x_hbm, s_hbm, col_hbm, send_ref, keep_ref, x_buf, s_buf, col_buf, low, high, acc, sems):
@@ -68,7 +76,7 @@
                 total = total + acc[:, cols]
             acc[:, cols] = total
     half = keep_ref.shape[0]
-    mine = lax.rem(me, 2)
+    mine = own_half()
     keep_ref[...] = acc[pl.ds(pl.multiple_of(mine * half, half), half), :]
     send_ref[...] = acc[pl.ds(pl.multiple_of((1 - mine) * half, half), half), :]
 
@@ -206,8 +214,14 @@
     )(*operands)
 
 
-def swap(array, axis, offset):
-    return lax.ppermute(array, axis, [(i, i ^ offset) for i in range(lax.axis_size(axis))])
+def swap(array, tok=0, feat=0):
+    tok_count, feat_count = lax.axis_size("tok"), lax.axis_size("feat")
+    pairs = [
+        (f * tok_count + t, (f ^ feat) * tok_count + (t ^ tok))
+        for f in range(feat_count)
+        for t in range(tok_count)
+    ]
+    return lax.ppermute(array, ("feat", "tok"), pairs)
 
 
 def body(features, signs, columns, labels):
@@ -222,22 +236,22 @@
     word_type = jax.ShapeDtypeStruct((size // 2, kept + LANES), jnp.int32)
     row_type = jax.ShapeDtypeStruct((size, kept + LANES), jnp.bfloat16)
 
-    first = (feat_index & 1) * (rows // 2) + (feat_index >> 1 & 1) * size
+    first = own_half() * (rows // 2) + (feat_index >> 1 & 1) * size
     own_labels = lax.dynamic_slice_in_dim(labels, first, size, 0).astype(jnp.bfloat16)
     own_labels = jnp.broadcast_to(own_labels, (size, LANES))
 
     send, keep = partial_halves(features, signs, columns, feat_count)
-    got = swap(send, "feat", 1)
+    got = swap(send, feat=1)
     total, word = local_call(
         functools.partial(first_kernel, 2), "first_split", keep, got, out_shape=[total_type, word_type]
     )
-    word = swap(word, "feat", 2)
+    word = swap(word, feat=3)
     stride = 4
     while stride < feat_count:
         total, word = local_call(
             middle_kernel, "add_encode", total, word, out_shape=[total_type, word_type]
         )
-        word = swap(word, "feat", stride)
+        word = swap(word, feat=stride | 1)
         stride *= 2
     scale = 1.0 / math.sqrt(width * feat_count)
     ours = local_call(
@@ -246,10 +260,10 @@
 
     stride = 1
     while stride < tok_count:
-        ours = jnp.concatenate([ours, swap(ours, "tok", stride)], axis=0)
+        ours = jnp.concatenate([ours, swap(ours, tok=stride, feat=1)], axis=0)
         stride *= 2
-    ours = jnp.concatenate([ours, swap(ours, "feat", 2)], axis=0)
-    theirs = swap(ours, "feat", 1)
+    ours = jnp.concatenate([ours, swap(ours, feat=3)], axis=0)
+    theirs = swap(ours, feat=1)
     concepts = C // tok_count
     gram = gram_blocks(ours, theirs, concepts, shard, kept, C / (rows * tok_count))
     return gram.reshape(concepts, shard, kept)

time: 36.5 us -> 37.9 us (1.038)
  starting transfers between devices: 12.1 us -> 13.9 us
    ppermute x7, starting transfers between devices: 12.1 us -> 13.9 us  [swap(): return lax.ppermute(array, ('feat', 'tok'), pairs)]
where the time goes in v6:
time: 37.9 us; the launch traced here: 37.8 us
  waiting for transfers between devices  15.7 us (41%)
  starting transfers between devices  13.9 us (37%)
  Pallas kernels  7.98 us (21%)
    ppermute x7, waiting for transfers between devices, swap(): return lax.ppermute(array, ('feat', 'tok'), pairs)  15.7 us
    ppermute x7, starting transfers between devices, swap(): return lax.ppermute(array, ('feat', 'tok'), pairs)  13.9 us
    pallas_call x1, Pallas kernels, partial_halves(): pl.pallas_call(functools.partial(partial_kernel, high_count, total_bits,...  4.06 us
    pallas_call x1, Pallas kernels, gram_blocks(): pl.pallas_call(functools.partial(gram_kernel, shard, group, factor), grid...  3.29 us
  transfers between devices with their start and end apart: 7, of which 7 were waited for; matrix products, arithmetic and copies ran while one was open for 0% of the time, Pallas kernels for 0%

profile of v6, /device:TPU:0, one launch (start us, length us, event | category | flops | bytes accessed | tf_op | source)
XLA Modules:
  0.0 37.8 jit_solution(9898367031370028260)
XLA Ops:
  0.0 0.0 copy-start
  0.0 4.1 %partial_transform.1 = (f32[64,1024]{1,0:T(8,128)S(1)}, f32[64,1024]{1,0:T(8,128)S(1)}) custom-call(bf16[128,8192]{1,0:T(8,128)(2,1)} %x_hbm.1, s32[1,8192]{1,0:T(1,128)} %bitcast.5, s32[1,1024]{1,0:T(1,128)} %bitcast.6), custom_call_target="tpu_custom_call" | custom-call | flops 2147483648 | bytes 2621440 | tf_op jit(solution)/shard_map/partial_transform/pallas_call | solution.py:91
  4.1 0.5 %collective-permute-start = (f32[64,1024]{1,0:T(8,128)S(1)}, f32[64,1024]{1,0:T(8,128)S(1)}, u32[]{:S(2)}, u32[]{:S(2)}) collective-permute-start(f32[64,1024]{1,0:T(8,128)S(1)} %get-tuple-element.14), channel_id=1, source_target_pairs={{0,2},{1,3},{2,0},{3,1},{4,6},{5,7},{6,4},{7,5},{8,10},{9,11},{10,... | collective-permute-start | bytes 786440 | tf_op jit(solution)/shard_map/ppermute | solution.py:224
  4.6 1.2 %collective-permute-done.got_ref = f32[64,1024]{1,0:T(8,128)S(1)} collective-permute-done((f32[64,1024]{1,0:T(8,128)S(1)}, f32[64,1024]{1,0:T(8,128)S(1)}, u32[]{:S(2)}, u32[]{:S(2)}) %collective-permute-start) | collective-permute-done | bytes 262176 | tf_op jit(solution)/shard_map/ppermute | solution.py:224
  5.7 0.1 first_split.1
  5.9 2.7 %collective-permute-start.1 = (s32[16,1152]{1,0:T(8,128)S(1)}, s32[16,1152]{1,0:T(8,128)S(1)}, u32[]{:S(2)}, u32[]{:S(2)}) collective-permute-start(s32[16,1152]{1,0:T(8,128)S(1)} %get-tuple-element.16), channel_id=1, source_target_pairs={{0,6},{1,7},{2,4},{3,5},{4,2},{5,3},{6,0},{7,1},{8,14},{9,15},{10,... | collective-permute-start | bytes 221192 | tf_op jit(solution)/shard_map/ppermute | solution.py:224
  8.6 2.3 %collective-permute-done.1.word_ref = s32[16,1152]{1,0:T(8,128)S(1)} collective-permute-done((s32[16,1152]{1,0:T(8,128)S(1)}, s32[16,1152]{1,0:T(8,128)S(1)}, u32[]{:S(2)}, u32[]{:S(2)}) %collective-permute-start.1) | collective-permute-done | bytes 73760 | tf_op jit(solution)/shard_map/ppermute | solution.py:224
  10.9 0.2 add_encode.2
  11.1 2.1 %collective-permute-start.2 = (s32[16,1152]{1,0:T(8,128)S(1)}, s32[16,1152]{1,0:T(8,128)S(1)}, u32[]{:S(2)}, u32[]{:S(2)}) collective-permute-start(s32[16,1152]{1,0:T(8,128)S(1)} %get-tuple-element.18), channel_id=1, source_target_pairs={{0,10},{1,11},{2,8},{3,9},{4,14},{5,15},{6,12},{7,13},{8,2},{9,3},... | collective-permute-start | bytes 221192 | tf_op jit(solution)/shard_map/ppermute | solution.py:224
  13.2 2.3 %collective-permute-done.2.word_ref = s32[16,1152]{1,0:T(8,128)S(1)} collective-permute-done((s32[16,1152]{1,0:T(8,128)S(1)}, s32[16,1152]{1,0:T(8,128)S(1)}, u32[]{:S(2)}, u32[]{:S(2)}) %collective-permute-start.2) | collective-permute-done | bytes 73760 | tf_op jit(solution)/shard_map/ppermute | solution.py:224
  15.5 0.2 add_encode.3
  15.7 3.0 %collective-permute-start.3 = (s32[16,1152]{1,0:T(8,128)S(1)}, s32[16,1152]{1,0:T(8,128)S(1)}, u32[]{:S(2)}, u32[]{:S(2)}) collective-permute-start(s32[16,1152]{1,0:T(8,128)S(1)} %get-tuple-element.20), channel_id=1, source_target_pairs={{0,18},{1,19},{2,16},{3,17},{4,22},{5,23},{6,20},{7,21},{8,26},{9,... | collective-permute-start | bytes 221192 | tf_op jit(solution)/shard_map/ppermute | solution.py:224
  18.7 0.0 copy-done
  18.7 0.1 convert_bitcast_fusion
  18.8 2.3 %collective-permute-done.3.word_ref = s32[16,1152]{1,0:T(8,128)S(1)} collective-permute-done((s32[16,1152]{1,0:T(8,128)S(1)}, s32[16,1152]{1,0:T(8,128)S(1)}, u32[]{:S(2)}, u32[]{:S(2)}) %collective-permute-start.3) | collective-permute-done | bytes 73760 | tf_op jit(solution)/shard_map/ppermute | solution.py:224
  21.0 0.1 broadcast_in_dim.8.label_ref
  21.1 0.1 sketch_rows.1
  21.2 3.4 %collective-permute-start.4 = (bf16[32,1152]{1,0:T(8,128)(2,1)S(1)}, bf16[32,1152]{1,0:T(8,128)(2,1)S(1)}, u32[]{:S(2)}, u32[]{:S(2)}) collective-permute-start(bf16[32,1152]{1,0:T(8,128)(2,1)S(1)} %sketch_rows.1), channel_id=1, source_target_pairs={{0,3},{1,2},{2,1},{3,0},{4,7},{5,6},{6,5},{7,4},{8,11},{9,10},{10,... | collective-permute-start | bytes 221192 | tf_op jit(solution)/shard_map/ppermute | solution.py:224
  24.6 2.3 %collective-permute-done.4 = bf16[32,1152]{1,0:T(8,128)(2,1)S(1)} collective-permute-done((bf16[32,1152]{1,0:T(8,128)(2,1)S(1)}, bf16[32,1152]{1,0:T(8,128)(2,1)S(1)}, u32[]{:S(2)}, u32[]{:S(2)}) %collective-permute-start.4) | collective-permute-done | bytes 73760 | tf_op jit(solution)/shard_map/ppermute | solution.py:224
  27.0 1.9 %collective-permute-start.5 = (bf16[64,1152]{1,0:T(8,128)(2,1)S(1)}, bf16[64,1152]{1,0:T(8,128)(2,1)S(1)}, u32[]{:S(2)}, u32[]{:S(2)}) collective-permute-start(bf16[64,1152]{1,0:T(8,128)(2,1)S(1)} %pad_maximum_fusion.1), channel_id=1, source_target_pairs={{0,6},{1,7},{2,4},{3,5},{4,2},{5,3},{6,0},{7,1},{8,14},{9,15},{10,... | collective-permute-start | bytes 442376 | tf_op jit(solution)/shard_map/ppermute | solution.py:224
  28.9 3.9 %collective-permute-done.5 = bf16[64,1152]{1,0:T(8,128)(2,1)S(1)} collective-permute-done((bf16[64,1152]{1,0:T(8,128)(2,1)S(1)}, bf16[64,1152]{1,0:T(8,128)(2,1)S(1)}, u32[]{:S(2)}, u32[]{:S(2)}) %collective-permute-start.5) | collective-permute-done | bytes 147488 | tf_op jit(solution)/shard_map/ppermute | solution.py:224
  32.8 0.4 collective-permute-start.6
  33.2 1.3 %collective-permute-done.6.b_ref = bf16[128,1152]{1,0:T(8,128)(2,1)S(1)} collective-permute-done((bf16[128,1152]{1,0:T(8,128)(2,1)S(1)}, bf16[128,1152]{1,0:T(8,128)(2,1)S(1)}, u32[]{:S(2)}, u32[]{:S(2)}) %collective-permute-start.6) | collective-permute-done | bytes 294944 | tf_op jit(solution)/shard_map/ppermute | solution.py:224
  34.5 3.3 %gram.1 = f32[1024,1024]{1,0:T(8,128)} custom-call(bf16[128,1152]{1,0:T(8,128)(2,1)S(1)} %pad_maximum_fusion.a_ref, bf16[128,1152]{1,0:T(8,128)(2,1)S(1)} %collective-permute-done.6.b_ref), custom_call_target="tpu_custom_call" | custom-call | flops 536870912 | bytes 4194304 | tf_op jit(solution)/shard_map/gram/pallas_call | solution.py:146
  (2 shorter events, 0.0 us)
Async XLA Ops:
  0.0 18.7 %copy-start = (s32[128,1]{0,1:T(1,128)S(1)}, s32[128,1]{0,1:T(1,128)}, u32[]{:S(2)}) copy-start(s32[128,1]{0,1:T(1,128)} %param.7) | copy-start | bytes 1540
  4.1 1.7 %collective-permute-start = (f32[64,1024]{1,0:T(8,128)S(1)}, f32[64,1024]{1,0:T(8,128)S(1)}, u32[]{:S(2)}, u32[]{:S(2)}) collective-permute-start(f32[64,1024]{1,0:T(8,128)S(1)} %get-tuple-element.14), channel_id=1, source_target_pairs={{0,2},{1,3},{2,0},{3,1},{4,6},{5,7},{6,4},{7,5},{8,10},{9,11},{10,... | collective-permute-start | bytes 786440 | tf_op jit(solution)/shard_map/ppermute | solution.py:224
  5.9 5.0 %collective-permute-start.1 = (s32[16,1152]{1,0:T(8,128)S(1)}, s32[16,1152]{1,0:T(8,128)S(1)}, u32[]{:S(2)}, u32[]{:S(2)}) collective-permute-start(s32[16,1152]{1,0:T(8,128)S(1)} %get-tuple-element.16), channel_id=1, source_target_pairs={{0,6},{1,7},{2,4},{3,5},{4,2},{5,3},{6,0},{7,1},{8,14},{9,15},{10,... | collective-permute-start | bytes 221192 | tf_op jit(solution)/shard_map/ppermute | solution.py:224
  11.1 4.4 %collective-permute-start.2 = (s32[16,1152]{1,0:T(8,128)S(1)}, s32[16,1152]{1,0:T(8,128)S(1)}, u32[]{:S(2)}, u32[]{:S(2)}) collective-permute-start(s32[16,1152]{1,0:T(8,128)S(1)} %get-tuple-element.18), channel_id=1, source_target_pairs={{0,10},{1,11},{2,8},{3,9},{4,14},{5,15},{6,12},{7,13},{8,2},{9,3},... | collective-permute-start | bytes 221192 | tf_op jit(solution)/shard_map/ppermute | solution.py:224
  15.7 5.3 %collective-permute-start.3 = (s32[16,1152]{1,0:T(8,128)S(1)}, s32[16,1152]{1,0:T(8,128)S(1)}, u32[]{:S(2)}, u32[]{:S(2)}) collective-permute-start(s32[16,1152]{1,0:T(8,128)S(1)} %get-tuple-element.20), channel_id=1, source_target_pairs={{0,18},{1,19},{2,16},{3,17},{4,22},{5,23},{6,20},{7,21},{8,26},{9,... | collective-permute-start | bytes 221192 | tf_op jit(solution)/shard_map/ppermute | solution.py:224
  21.2 5.7 %collective-permute-start.4 = (bf16[32,1152]{1,0:T(8,128)(2,1)S(1)}, bf16[32,1152]{1,0:T(8,128)(2,1)S(1)}, u32[]{:S(2)}, u32[]{:S(2)}) collective-permute-start(bf16[32,1152]{1,0:T(8,128)(2,1)S(1)} %sketch_rows.1), channel_id=1, source_target_pairs={{0,3},{1,2},{2,1},{3,0},{4,7},{5,6},{6,5},{7,4},{8,11},{9,10},{10,... | collective-permute-start | bytes 221192 | tf_op jit(solution)/shard_map/ppermute | solution.py:224
  27.0 5.9 %collective-permute-start.5 = (bf16[64,1152]{1,0:T(8,128)(2,1)S(1)}, bf16[64,1152]{1,0:T(8,128)(2,1)S(1)}, u32[]{:S(2)}, u32[]{:S(2)}) collective-permute-start(bf16[64,1152]{1,0:T(8,128)(2,1)S(1)} %pad_maximum_fusion.1), channel_id=1, source_target_pairs={{0,6},{1,7},{2,4},{3,5},{4,2},{5,3},{6,0},{7,1},{8,14},{9,15},{10,... | collective-permute-start | bytes 442376 | tf_op jit(solution)/shard_map/ppermute | solution.py:224
  32.8 1.6 %collective-permute-start.6 = (bf16[128,1152]{1,0:T(8,128)(2,1)S(1)}, bf16[128,1152]{1,0:T(8,128)(2,1)S(1)}, u32[]{:S(2)}, u32[]{:S(2)}) collective-permute-start(bf16[128,1152]{1,0:T(8,128)(2,1)S(1)} %pad_maximum_fusion.a_ref), channel_id=1, source_target_pairs={{0,2},{1,3},{2,0},{3,1},{4,6},{5,7},{6,4},{7,5},{8,10},{9,11},{10,... | collective-permute-start | bytes 884744 | tf_op jit(solution)/shard_map/ppermute | solution.py:224

commit v7 on v6

--- a/solution.py
+++ b/solution.py
@@ -22,14 +22,6 @@
         shift //= 2
         number = number ^ (number >> shift)
     return (1 - 2 * (number & 1)).astype(jnp.float32)
-
-
-def own_half():
-    bits = lax.axis_index("feat") ^ lax.axis_index("tok")
-    total = bits & 1
-    for position in range(1, max(lax.axis_size("feat"), lax.axis_size("tok")).bit_length() - 1):
-        total = total ^ (bits >> position & 1)
-    return total
 
 
 def partial_kernel(high_count, total_bits, parts, x_hbm, s_hbm, col_hbm, send_ref, keep_ref, x_buf, s_buf, col_buf, low, high, acc, sems):
@@ -76,7 +68,7 @@
                 total = total + acc[:, cols]
             acc[:, cols] = total
     half = keep_ref.shape[0]
-    mine = own_half()
+    mine = lax.rem(me, 2)
     keep_ref[...] = acc[pl.ds(pl.multiple_of(mine * half, half), half), :]
     send_ref[...] = acc[pl.ds(pl.multiple_of((1 - mine) * half, half), half), :]
 
@@ -180,7 +172,7 @@
     return code[:, :-LANES] * jnp.exp2(code[:, -LANES:-LANES + 1] - 15.0)
 
 
-def first_kernel(stride, keep_ref, got_ref, total_ref, word_ref):
+def first_kernel(stride, keep_ref, got_ref, total_ref, here_ref, there_ref):
     size = total_ref.shape[0]
     digit = lax.rem(lax.axis_index("feat") // stride, 2)
 
@@ -189,7 +181,14 @@
         return keep_ref[span, :] + got_ref[span, :]
 
     total_ref[...] = piece(digit)
-    encode(piece(1 - digit), word_ref)
+    encode(piece(digit), here_ref)
+    encode(piece(1 - digit), there_ref)
+
+
+def square_kernel(total_ref, x_ref, z_ref, both_ref, sum_ref, out_ref):
+    total = (total_ref[...] + decode(x_ref)) + (decode(z_ref) + decode(both_ref))
+    sum_ref[...] = total
+    encode(total, out_ref)
 
 
 def middle_kernel(total_ref, word_ref, sum_ref, out_ref):
@@ -236,33 +235,45 @@
     word_type = jax.ShapeDtypeStruct((size // 2, kept + LANES), jnp.int32)
     row_type = jax.ShapeDtypeStruct((size, kept + LANES), jnp.bfloat16)
 
-    first = own_half() * (rows // 2) + (feat_index >> 1 & 1) * size
+    first = (feat_index & 1) * (rows // 2) + (feat_index >> 1 & 1) * size
     own_labels = lax.dynamic_slice_in_dim(labels, first, size, 0).astype(jnp.bfloat16)
     own_labels = jnp.broadcast_to(own_labels, (size, LANES))
 
     send, keep = partial_halves(features, signs, columns, feat_count)
     got = swap(send, feat=1)
+    total, here, there = local_call(
+        functools.partial(first_kernel, 2), "first_split", keep, got, out_shape=[total_type, word_type, word_type]
+    )
     total, word = local_call(
-        functools.partial(first_kernel, 2), "first_split", keep, got, out_shape=[total_type, word_type]
+        square_kernel,
+        "add_square",
+        total,
+        swap(there, feat=2),
+        swap(here, feat=4),
+        swap(there, feat=6),
+        out_shape=[total_type, word_type],
     )
-    word = swap(word, feat=3)
-    stride = 4
+    word = swap(word, feat=8)
+    stride = 16
     while stride < feat_count:
         total, word = local_call(
             middle_kernel, "add_encode", total, word, out_shape=[total_type, word_type]
         )
-        word = swap(word, feat=stride | 1)
+        word = swap(word, feat=stride)
         stride *= 2
     scale = 1.0 / math.sqrt(width * feat_count)
     ours = local_call(
         functools.partial(last_kernel, scale), "sketch_rows", total, word, own_labels, out_shape=row_type
     )
 
-    stride = 1
+    stride = 2
     while stride < tok_count:
-        ours = jnp.concatenate([ours, swap(ours, tok=stride, feat=1)], axis=0)
+        ours = jnp.concatenate([ours, swap(ours, tok=stride)], axis=0)
         stride *= 2
-    ours = jnp.concatenate([ours, swap(ours, feat=3)], axis=0)
+    received = [swap(ours, tok=1, feat=2)] if tok_count > 1 else []
+    received += [swap(ours, feat=2)]
+    received += [swap(ours, tok=1)] if tok_count > 1 else []
+    ours = jnp.concatenate([ours] + received, axis=0)
     theirs = swap(ours, feat=1)
     concepts = C // tok_count
     gram = gram_blocks(ours, theirs, concepts, shard, kept, C / (rows * tok_count))

time: 37.9 us -> 34.9 us (0.921)
  starting transfers between devices: 13.9 us -> 11.4 us
  waiting for transfers between devices: 15.7 us -> 15.3 us
    ppermute x7 -> x9, starting transfers between devices: 13.9 us -> 11.4 us  [swap(): return lax.ppermute(array, ('feat', 'tok'), pairs)]
    ppermute x7 -> x9, waiting for transfers between devices: 15.7 us -> 15.3 us  [swap(): return lax.ppermute(array, ('feat', 'tok'), pairs)]
  transfers between devices with their start and end apart: 7 -> 9, of which waited for: 7 -> 9; matrix products, arithmetic and copies ran while one was open for 0% -> 0% of each run, Pallas kernels for 0% -> 0%
where the time goes in v7:
time: 34.9 us; the launch traced here: 34.8 us
  waiting for transfers between devices  15.3 us (44%)
  starting transfers between devices  11.4 us (33%)
  Pallas kernels  7.85 us (22%)
    ppermute x9, waiting for transfers between devices, swap(): return lax.ppermute(array, ('feat', 'tok'), pairs)  15.3 us
    ppermute x9, starting transfers between devices, swap(): return lax.ppermute(array, ('feat', 'tok'), pairs)  11.4 us
    pallas_call x1, Pallas kernels, partial_halves(): pl.pallas_call(functools.partial(partial_kernel, high_count, total_bits,...  4.11 us
    pallas_call x1, Pallas kernels, gram_blocks(): pl.pallas_call(functools.partial(gram_kernel, shard, group, factor), grid...  3.28 us
  transfers between devices with their start and end apart: 9, of which 9 were waited for; matrix products, arithmetic and copies ran while one was open for 0% of the time, Pallas kernels for 0%

profile of v7, /device:TPU:0, one launch (start us, length us, event | category | flops | bytes accessed | tf_op | source)
XLA Modules:
  0.0 34.8 jit_solution(15708048368677627407)
XLA Ops:
  0.0 4.1 %partial_transform.1 = (f32[64,1024]{1,0:T(8,128)S(1)}, f32[64,1024]{1,0:T(8,128)S(1)}) custom-call(bf16[128,8192]{1,0:T(8,128)(2,1)} %x_hbm.1, s32[1,8192]{1,0:T(1,128)} %bitcast.5, s32[1,1024]{1,0:T(1,128)} %bitcast.6), custom_call_target="tpu_custom_call" | custom-call | flops 2147483648 | bytes 2621440 | tf_op jit(solution)/shard_map/partial_transform/pallas_call | solution.py:83
  4.1 0.5 %collective-permute-start = (f32[64,1024]{1,0:T(8,128)S(1)}, f32[64,1024]{1,0:T(8,128)S(1)}, u32[]{:S(2)}, u32[]{:S(2)}) collective-permute-start(f32[64,1024]{1,0:T(8,128)S(1)} %get-tuple-element.13), channel_id=1, source_target_pairs={{0,2},{1,3},{2,0},{3,1},{4,6},{5,7},{6,4},{7,5},{8,10},{9,11},{10,... | collective-permute-start | bytes 786440 | tf_op jit(solution)/shard_map/ppermute | solution.py:223
  4.6 1.2 %collective-permute-done.got_ref = f32[64,1024]{1,0:T(8,128)S(1)} collective-permute-done((f32[64,1024]{1,0:T(8,128)S(1)}, f32[64,1024]{1,0:T(8,128)S(1)}, u32[]{:S(2)}, u32[]{:S(2)}) %collective-permute-start) | collective-permute-done | bytes 262176 | tf_op jit(solution)/shard_map/ppermute | solution.py:223
  5.8 0.1 first_split.1
  5.9 3.0 %collective-permute-start.2 = (s32[16,1152]{1,0:T(8,128)S(1)}, s32[16,1152]{1,0:T(8,128)S(1)}, u32[]{:S(2)}, u32[]{:S(2)}) collective-permute-start(s32[16,1152]{1,0:T(8,128)S(1)} %get-tuple-element.16), channel_id=1, source_target_pairs={{0,8},{1,9},{2,10},{3,11},{4,12},{5,13},{6,14},{7,15},{8,0},{9,1},... | collective-permute-start | bytes 221192 | tf_op jit(solution)/shard_map/ppermute | solution.py:223
  9.0 1.4 %collective-permute-start.3 = (s32[16,1152]{1,0:T(8,128)S(1)}, s32[16,1152]{1,0:T(8,128)S(1)}, u32[]{:S(2)}, u32[]{:S(2)}) collective-permute-start(s32[16,1152]{1,0:T(8,128)S(1)} %get-tuple-element.15), channel_id=1, source_target_pairs={{0,12},{1,13},{2,14},{3,15},{4,8},{5,9},{6,10},{7,11},{8,4},{9,5},... | collective-permute-start | bytes 221192 | tf_op jit(solution)/shard_map/ppermute | solution.py:223
  10.3 0.2 collective-permute-start.1
  10.5 1.0 %collective-permute-done.2.z_ref = s32[16,1152]{1,0:T(8,128)S(1)} collective-permute-done((s32[16,1152]{1,0:T(8,128)S(1)}, s32[16,1152]{1,0:T(8,128)S(1)}, u32[]{:S(2)}, u32[]{:S(2)}) %collective-permute-start.2) | collective-permute-done | bytes 73760 | tf_op jit(solution)/shard_map/ppermute | solution.py:223
  11.5 2.8 %collective-permute-done.3.both_ref = s32[16,1152]{1,0:T(8,128)S(1)} collective-permute-done((s32[16,1152]{1,0:T(8,128)S(1)}, s32[16,1152]{1,0:T(8,128)S(1)}, u32[]{:S(2)}, u32[]{:S(2)}) %collective-permute-start.3) | collective-permute-done | bytes 73760 | tf_op jit(solution)/shard_map/ppermute | solution.py:223
  14.4 1.2 %collective-permute-done.1.x_ref = s32[16,1152]{1,0:T(8,128)S(1)} collective-permute-done((s32[16,1152]{1,0:T(8,128)S(1)}, s32[16,1152]{1,0:T(8,128)S(1)}, u32[]{:S(2)}, u32[]{:S(2)}) %collective-permute-start.1) | collective-permute-done | bytes 73760 | tf_op jit(solution)/shard_map/ppermute | solution.py:223
  15.5 0.2 add_square.1
  15.8 2.7 %collective-permute-start.4 = (s32[16,1152]{1,0:T(8,128)S(1)}, s32[16,1152]{1,0:T(8,128)S(1)}, u32[]{:S(2)}, u32[]{:S(2)}) collective-permute-start(s32[16,1152]{1,0:T(8,128)S(1)} %get-tuple-element.18), channel_id=1, source_target_pairs={{0,16},{1,17},{2,18},{3,19},{4,20},{5,21},{6,22},{7,23},{8,24},{9,... | collective-permute-start | bytes 221192 | tf_op jit(solution)/shard_map/ppermute | solution.py:223
  18.4 0.1 convert_bitcast_fusion
  18.5 3.6 %collective-permute-done.4.word_ref = s32[16,1152]{1,0:T(8,128)S(1)} collective-permute-done((s32[16,1152]{1,0:T(8,128)S(1)}, s32[16,1152]{1,0:T(8,128)S(1)}, u32[]{:S(2)}, u32[]{:S(2)}) %collective-permute-start.4) | collective-permute-done | bytes 73760 | tf_op jit(solution)/shard_map/ppermute | solution.py:223
  22.1 0.1 broadcast_in_dim.8.label_ref
  22.2 0.1 sketch_rows.1
  22.3 1.6 %collective-permute-start.7 = (bf16[32,1152]{1,0:T(8,128)(2,1)S(1)}, bf16[32,1152]{1,0:T(8,128)(2,1)S(1)}, u32[]{:S(2)}, u32[]{:S(2)}) collective-permute-start(bf16[32,1152]{1,0:T(8,128)(2,1)S(1)} %sketch_rows.1), channel_id=1, source_target_pairs={{0,1},{1,0},{2,3},{3,2},{4,5},{5,4},{6,7},{7,6},{8,9},{9,8},{10,11... | collective-permute-start | bytes 221192 | tf_op jit(solution)/shard_map/ppermute | solution.py:223
  23.9 0.7 %collective-permute-start.6 = (bf16[32,1152]{1,0:T(8,128)(2,1)S(1)}, bf16[32,1152]{1,0:T(8,128)(2,1)S(1)}, u32[]{:S(2)}, u32[]{:S(2)}) collective-permute-start(bf16[32,1152]{1,0:T(8,128)(2,1)S(1)} %sketch_rows.1), channel_id=1, source_target_pairs={{0,4},{1,5},{2,6},{3,7},{4,0},{5,1},{6,2},{7,3},{8,12},{9,13},{10,... | collective-permute-start | bytes 221192 | tf_op jit(solution)/shard_map/ppermute | solution.py:223
  24.6 1.3 %collective-permute-start.5 = (bf16[32,1152]{1,0:T(8,128)(2,1)S(1)}, bf16[32,1152]{1,0:T(8,128)(2,1)S(1)}, u32[]{:S(2)}, u32[]{:S(2)}) collective-permute-start(bf16[32,1152]{1,0:T(8,128)(2,1)S(1)} %sketch_rows.1), channel_id=1, source_target_pairs={{0,5},{1,4},{2,7},{3,6},{4,1},{5,0},{6,3},{7,2},{8,13},{9,12},{10,... | collective-permute-start | bytes 221192 | tf_op jit(solution)/shard_map/ppermute | solution.py:223
  25.9 1.4 %collective-permute-done.7 = bf16[32,1152]{1,0:T(8,128)(2,1)S(1)} collective-permute-done((bf16[32,1152]{1,0:T(8,128)(2,1)S(1)}, bf16[32,1152]{1,0:T(8,128)(2,1)S(1)}, u32[]{:S(2)}, u32[]{:S(2)}) %collective-permute-start.7) | collective-permute-done | bytes 73760 | tf_op jit(solution)/shard_map/ppermute | solution.py:223
  27.2 1.0 %collective-permute-done.6 = bf16[32,1152]{1,0:T(8,128)(2,1)S(1)} collective-permute-done((bf16[32,1152]{1,0:T(8,128)(2,1)S(1)}, bf16[32,1152]{1,0:T(8,128)(2,1)S(1)}, u32[]{:S(2)}, u32[]{:S(2)}) %collective-permute-start.6) | collective-permute-done | bytes 73760 | tf_op jit(solution)/shard_map/ppermute | solution.py:223
  28.2 1.6 %collective-permute-done.5 = bf16[32,1152]{1,0:T(8,128)(2,1)S(1)} collective-permute-done((bf16[32,1152]{1,0:T(8,128)(2,1)S(1)}, bf16[32,1152]{1,0:T(8,128)(2,1)S(1)}, u32[]{:S(2)}, u32[]{:S(2)}) %collective-permute-start.5) | collective-permute-done | bytes 73760 | tf_op jit(solution)/shard_map/ppermute | solution.py:223
  29.9 1.6 %collective-permute-done.8.b_ref = bf16[128,1152]{1,0:T(8,128)(2,1)S(1)} collective-permute-done((bf16[128,1152]{1,0:T(8,128)(2,1)S(1)}, bf16[128,1152]{1,0:T(8,128)(2,1)S(1)}, u32[]{:S(2)}, u32[]{:S(2)}) %collective-permute-start.8) | collective-permute-done | bytes 294944 | tf_op jit(solution)/shard_map/ppermute | solution.py:223
  31.5 3.3 %gram.1 = f32[1024,1024]{1,0:T(8,128)} custom-call(bf16[128,1152]{1,0:T(8,128)(2,1)S(1)} %pad_maximum_fusion.a_ref, bf16[128,1152]{1,0:T(8,128)(2,1)S(1)} %collective-permute-done.8.b_ref), custom_call_target="tpu_custom_call" | custom-call | flops 536870912 | bytes 4194304 | tf_op jit(solution)/shard_map/gram/pallas_call | solution.py:138
  (4 shorter events, 0.1 us)
Async XLA Ops:
  0.0 18.4 %copy-start = (s32[128,1]{0,1:T(1,128)S(1)}, s32[128,1]{0,1:T(1,128)}, u32[]{:S(2)}) copy-start(s32[128,1]{0,1:T(1,128)} %param.7) | copy-start | bytes 1540
  4.1 1.7 %collective-permute-start = (f32[64,1024]{1,0:T(8,128)S(1)}, f32[64,1024]{1,0:T(8,128)S(1)}, u32[]{:S(2)}, u32[]{:S(2)}) collective-permute-start(f32[64,1024]{1,0:T(8,128)S(1)} %get-tuple-element.13), channel_id=1, source_target_pairs={{0,2},{1,3},{2,0},{3,1},{4,6},{5,7},{6,4},{7,5},{8,10},{9,11},{10,... | collective-permute-start | bytes 786440 | tf_op jit(solution)/shard_map/ppermute | solution.py:223
  5.9 5.6 %collective-permute-start.2 = (s32[16,1152]{1,0:T(8,128)S(1)}, s32[16,1152]{1,0:T(8,128)S(1)}, u32[]{:S(2)}, u32[]{:S(2)}) collective-permute-start(s32[16,1152]{1,0:T(8,128)S(1)} %get-tuple-element.16), channel_id=1, source_target_pairs={{0,8},{1,9},{2,10},{3,11},{4,12},{5,13},{6,14},{7,15},{8,0},{9,1},... | collective-permute-start | bytes 221192 | tf_op jit(solution)/shard_map/ppermute | solution.py:223
  9.0 5.4 %collective-permute-start.3 = (s32[16,1152]{1,0:T(8,128)S(1)}, s32[16,1152]{1,0:T(8,128)S(1)}, u32[]{:S(2)}, u32[]{:S(2)}) collective-permute-start(s32[16,1152]{1,0:T(8,128)S(1)} %get-tuple-element.15), channel_id=1, source_target_pairs={{0,12},{1,13},{2,14},{3,15},{4,8},{5,9},{6,10},{7,11},{8,4},{9,5},... | collective-permute-start | bytes 221192 | tf_op jit(solution)/shard_map/ppermute | solution.py:223
  10.3 5.2 %collective-permute-start.1 = (s32[16,1152]{1,0:T(8,128)S(1)}, s32[16,1152]{1,0:T(8,128)S(1)}, u32[]{:S(2)}, u32[]{:S(2)}) collective-permute-start(s32[16,1152]{1,0:T(8,128)S(1)} %get-tuple-element.15), channel_id=1, source_target_pairs={{0,4},{1,5},{2,6},{3,7},{4,0},{5,1},{6,2},{7,3},{8,12},{9,13},{10,... | collective-permute-start | bytes 221192 | tf_op jit(solution)/shard_map/ppermute | solution.py:223
  15.8 6.4 %collective-permute-start.4 = (s32[16,1152]{1,0:T(8,128)S(1)}, s32[16,1152]{1,0:T(8,128)S(1)}, u32[]{:S(2)}, u32[]{:S(2)}) collective-permute-start(s32[16,1152]{1,0:T(8,128)S(1)} %get-tuple-element.18), channel_id=1, source_target_pairs={{0,16},{1,17},{2,18},{3,19},{4,20},{5,21},{6,22},{7,23},{8,24},{9,... | collective-permute-start | bytes 221192 | tf_op jit(solution)/shard_map/ppermute | solution.py:223
  22.3 4.9 %collective-permute-start.7 = (bf16[32,1152]{1,0:T(8,128)(2,1)S(1)}, bf16[32,1152]{1,0:T(8,128)(2,1)S(1)}, u32[]{:S(2)}, u32[]{:S(2)}) collective-permute-start(bf16[32,1152]{1,0:T(8,128)(2,1)S(1)} %sketch_rows.1), channel_id=1, source_target_pairs={{0,1},{1,0},{2,3},{3,2},{4,5},{5,4},{6,7},{7,6},{8,9},{9,8},{10,11... | collective-permute-start | bytes 221192 | tf_op jit(solution)/shard_map/ppermute | solution.py:223
  23.9 4.4 %collective-permute-start.6 = (bf16[32,1152]{1,0:T(8,128)(2,1)S(1)}, bf16[32,1152]{1,0:T(8,128)(2,1)S(1)}, u32[]{:S(2)}, u32[]{:S(2)}) collective-permute-start(bf16[32,1152]{1,0:T(8,128)(2,1)S(1)} %sketch_rows.1), channel_id=1, source_target_pairs={{0,4},{1,5},{2,6},{3,7},{4,0},{5,1},{6,2},{7,3},{8,12},{9,13},{10,... | collective-permute-start | bytes 221192 | tf_op jit(solution)/shard_map/ppermute | solution.py:223
  24.6 5.3 %collective-permute-start.5 = (bf16[32,1152]{1,0:T(8,128)(2,1)S(1)}, bf16[32,1152]{1,0:T(8,128)(2,1)S(1)}, u32[]{:S(2)}, u32[]{:S(2)}) collective-permute-start(bf16[32,1152]{1,0:T(8,128)(2,1)S(1)} %sketch_rows.1), channel_id=1, source_target_pairs={{0,5},{1,4},{2,7},{3,6},{4,1},{5,0},{6,3},{7,2},{8,13},{9,12},{10,... | collective-permute-start | bytes 221192 | tf_op jit(solution)/shard_map/ppermute | solution.py:223
  29.8 1.6 %collective-permute-start.8 = (bf16[128,1152]{1,0:T(8,128)(2,1)S(1)}, bf16[128,1152]{1,0:T(8,128)(2,1)S(1)}, u32[]{:S(2)}, u32[]{:S(2)}) collective-permute-start(bf16[128,1152]{1,0:T(8,128)(2,1)S(1)} %pad_maximum_fusion.a_ref), channel_id=1, source_target_pairs={{0,2},{1,3},{2,0},{3,1},{4,6},{5,7},{6,4},{7,5},{8,10},{9,11},{10,... | collective-permute-start | bytes 884744 | tf_op jit(solution)/shard_map/ppermute | solution.py:223

commit v8 on v7

--- a/solution.py
+++ b/solution.py
@@ -105,53 +105,81 @@
     ))
 
 
-def gram_kernel(shard, group, factor, a_ref, b_ref, out_ref, rows, own, label):
-    step = pl.program_id(0)
-    kept = out_ref.shape[1]
+def mask_operands(shard, wide, factor, row_ref):
+    kept = row_ref.shape[1] - LANES
+    first = lax.axis_index("feat") * shard
+    start = pl.multiple_of(first // LANES * LANES, LANES)
+    window = row_ref[:, pl.ds(start, LANES)].astype(jnp.float32) * factor
+    window = pltpu.roll(window, lax.rem(LANES - (first - start), LANES), 1)
+    lane = lax.broadcasted_iota(jnp.int32, window.shape, 1)
+    own = jnp.where(lane < shard, window, 0.0)
+    step = shard
+    while step < LANES:
+        own = own + pltpu.roll(own, step, 1)
+        step *= 2
+    own = jnp.concatenate([own] * -(-wide // LANES), axis=1)[:, :wide]
+    named = row_ref[:, kept:kept + 1].astype(jnp.float32).astype(jnp.int32)
+    label = named - lax.broadcasted_iota(jnp.int32, own.shape, 1) // shard
+    return own, label
+
+
+def mask_kernel(shard, wide, factor, row_ref, own_ref, label_ref):
+    own_ref[...], label_ref[...] = mask_operands(shard, wide, factor, row_ref)
+
+
+def gram_kernel(shard, group, factor, ours, own_ref, label_ref, theirs, out_hbm, rows, blocks, sems):
+    kept = rows.shape[1]
+    half = ours.shape[0]
     wide = group * shard
-    steps = pl.num_programs(0)
-    half = a_ref.shape[0]
-
-    @pl.when(step == 0)
-    def _():
-        first = lax.axis_index("feat") * shard
-        source = lax.broadcasted_iota(jnp.int32, (kept, wide), 0)
-        lane = lax.broadcasted_iota(jnp.int32, (kept, wide), 1)
-        pick = jnp.where(source == first + (lane & (shard - 1)), 1.0, 0.0).astype(jnp.bfloat16)
-        lane = lax.broadcasted_iota(jnp.int32, (half, wide), 1)
-        for at, ref in enumerate((a_ref, b_ref)):
-            span = slice(at * half, (at + 1) * half)
-            rows[span] = ref[:, :kept]
-            named = ref[:, kept:kept + 1].astype(jnp.float32).astype(jnp.int32)
-            label[span] = named - lane // shard
-        own[...] = jnp.dot(rows[...], pick, preferred_element_type=jnp.float32)
-
-    first = (lax.axis_index("tok") * steps + step) * group
-    chosen = jnp.where(label[...] == first, own[...], 0.0).astype(jnp.bfloat16)
-    gram = lax.dot_general(chosen, rows[...], (((0,), (0,)), ((), ())), preferred_element_type=jnp.float32)
-    out_ref[...] = gram * factor
+    steps = blocks.shape[0]
+    rows[:half] = ours[:, :kept]
+    rows[half:] = theirs[:, :kept]
+    parts = ((own_ref[...], label_ref[...]), mask_operands(shard, wide, factor, theirs))
+    base = lax.axis_index("tok") * steps * group
+    copies = []
+    for step in range(steps):
+        chosen = jnp.concatenate(
+            [jnp.where(label == base + step * group, own, 0.0).astype(jnp.bfloat16) for own, label in parts], axis=0
+        )
+        blocks[step] = lax.dot_general(
+            chosen, rows[...], (((0,), (0,)), ((), ())), preferred_element_type=jnp.float32
+        )
+        copies.append(
+            pltpu.make_async_copy(blocks.at[step], out_hbm.at[pl.ds(step * wide, wide), :], sems.at[step])
+        )
+        copies[-1].start()
+    for copy in copies:
+        copy.wait()
 
 
 def gram_blocks(ours, theirs, concepts, shard, kept, factor):
-    tokens, lanes = ours.shape
+    tokens = ours.shape[0]
     group = max(1, min(concepts, LOW // shard))
+    wide = group * shard
+    steps = concepts // group
+    params = pltpu.CompilerParams(vmem_limit_bytes=VMEM_LIMIT)
+    own, label = pl.pallas_call(
+        functools.partial(mask_kernel, shard, wide, factor),
+        out_shape=[jax.ShapeDtypeStruct((tokens, wide), dtype) for dtype in (jnp.float32, jnp.int32)],
+        compiler_params=params,
+        name="mask_ours",
+    )(ours)
     return pl.pallas_call(
         functools.partial(gram_kernel, shard, group, factor),
-        grid=(concepts // group,),
-        in_specs=[pl.BlockSpec((tokens, lanes), lambda i: (0, 0))] * 2,
-        out_specs=pl.BlockSpec((group * shard, kept), lambda i: (i, 0)),
+        in_specs=[pl.BlockSpec(memory_space=pltpu.VMEM)] * 4,
+        out_specs=pl.BlockSpec(memory_space=pltpu.HBM),
         out_shape=jax.ShapeDtypeStruct((concepts * shard, kept), jnp.float32),
         scratch_shapes=[
             pltpu.VMEM((2 * tokens, kept), jnp.bfloat16),
-            pltpu.VMEM((2 * tokens, group * shard), jnp.float32),
-            pltpu.VMEM((2 * tokens, group * shard), jnp.int32),
+            pltpu.VMEM((steps, wide, kept), jnp.float32),
+            pltpu.SemaphoreType.DMA((steps,)),
         ],
-        compiler_params=pltpu.CompilerParams(vmem_limit_bytes=VMEM_LIMIT),
+        compiler_params=params,
         cost_estimate=pl.CostEstimate(
             flops=4 * tokens * concepts * shard * kept, bytes_accessed=4 * concepts * shard * kept, transcendentals=0
         ),
         name="gram",
-    )(ours, theirs)
+    )(ours, own, label, theirs)
 
 
 def encode(values, word_ref):
@@ -172,7 +200,7 @@
     return code[:, :-LANES] * jnp.exp2(code[:, -LANES:-LANES + 1] - 15.0)
 
 
-def first_kernel(stride, keep_ref, got_ref, total_ref, here_ref, there_ref):
+def first_kernel(stride, keep_ref, got_ref, total_ref, there_ref, here_ref, again_ref):
     size = total_ref.shape[0]
     digit = lax.rem(lax.axis_index("feat") // stride, 2)
 
@@ -181,11 +209,12 @@
         return keep_ref[span, :] + got_ref[span, :]
 
     total_ref[...] = piece(digit)
+    encode(piece(1 - digit), there_ref)
+    again_ref[...] = there_ref[...]
     encode(piece(digit), here_ref)
-    encode(piece(1 - digit), there_ref)
-
-
-def square_kernel(total_ref, x_ref, z_ref, both_ref, sum_ref, out_ref):
+
+
+def square_kernel(total_ref, both_ref, x_ref, z_ref, sum_ref, out_ref):
     total = (total_ref[...] + decode(x_ref)) + (decode(z_ref) + decode(both_ref))
     sum_ref[...] = total
     encode(total, out_ref)
@@ -241,16 +270,16 @@
 
     send, keep = partial_halves(features, signs, columns, feat_count)
     got = swap(send, feat=1)
-    total, here, there = local_call(
-        functools.partial(first_kernel, 2), "first_split", keep, got, out_shape=[total_type, word_type, word_type]
+    total, there, here, again = local_call(
+        functools.partial(first_kernel, 2), "first_split", keep, got, out_shape=[total_type, word_type, word_type, word_type]
     )
     total, word = local_call(
         square_kernel,
         "add_square",
         total,
+        swap(again, feat=6),
         swap(there, feat=2),
         swap(here, feat=4),
-        swap(there, feat=6),
         out_shape=[total_type, word_type],
     )
     word = swap(word, feat=8)

time: 34.9 us -> 33.9 us (0.971)
  Pallas kernels: 7.85 us -> 7.28 us
  waiting for transfers between devices: 15.3 us -> 14.8 us
    pallas_call x1 -> x2, Pallas kernels: 3.28 us -> 2.69 us  [the longest x1 2.52 us: gram_blocks(): pl.pallas_call(functools.partial(gram_kernel, shard, group, factor), in_s...]
    ppermute x9, waiting for transfers between devices: 15.3 us -> 14.8 us  [swap(): return lax.ppermute(array, ('feat', 'tok'), pairs)]
  transfers between devices with their start and end apart: 9 -> 9, of which waited for: 9 -> 9; matrix products, arithmetic and copies ran while one was open for 0% -> 0% of each run, Pallas kernels for 0% -> 1%
where the time goes in v8:
time: 33.9 us; the launch traced here: 33.7 us
  waiting for transfers between devices  14.8 us (44%)
  starting transfers between devices  11.4 us (34%)
  Pallas kernels  7.28 us (21%)
    ppermute x9, waiting for transfers between devices, swap(): return lax.ppermute(array, ('feat', 'tok'), pairs)  14.8 us
    ppermute x9, starting transfers between devices, swap(): return lax.ppermute(array, ('feat', 'tok'), pairs)  11.4 us
    pallas_call x1, Pallas kernels, partial_halves(): pl.pallas_call(functools.partial(partial_kernel, high_count, total_bits,...  4.11 us
    pallas_call x1, Pallas kernels, gram_blocks(): pl.pallas_call(functools.partial(gram_kernel, shard, group, factor), in_s...  2.52 us
  transfers between devices with their start and end apart: 9, of which 9 were waited for; matrix products, arithmetic and copies ran while one was open for 0% of the time, Pallas kernels for 1%

profile of v8, /device:TPU:0, one launch (start us, length us, event | category | flops | bytes accessed | tf_op | source)
XLA Modules:
  0.0 33.7 jit_solution(13266044456161618265)
XLA Ops:
  0.0 4.1 %partial_transform.1 = (f32[64,1024]{1,0:T(8,128)S(1)}, f32[64,1024]{1,0:T(8,128)S(1)}) custom-call(bf16[128,8192]{1,0:T(8,128)(2,1)} %x_hbm.1, s32[1,8192]{1,0:T(1,128)} %bitcast.5, s32[1,1024]{1,0:T(1,128)} %bitcast.6), custom_call_target="tpu_custom_call" | custom-call | flops 2147483648 | bytes 2621440 | tf_op jit(solution)/shard_map/partial_transform/pallas_call | solution.py:83
  4.1 0.5 %collective-permute-start = (f32[64,1024]{1,0:T(8,128)S(1)}, f32[64,1024]{1,0:T(8,128)S(1)}, u32[]{:S(2)}, u32[]{:S(2)}) collective-permute-start(f32[64,1024]{1,0:T(8,128)S(1)} %get-tuple-element.16), channel_id=1, source_target_pairs={{0,2},{1,3},{2,0},{3,1},{4,6},{5,7},{6,4},{7,5},{8,10},{9,11},{10,... | collective-permute-start | bytes 786440 | tf_op jit(solution)/shard_map/ppermute | solution.py:252
  4.6 1.2 %collective-permute-done.got_ref = f32[64,1024]{1,0:T(8,128)S(1)} collective-permute-done((f32[64,1024]{1,0:T(8,128)S(1)}, f32[64,1024]{1,0:T(8,128)S(1)}, u32[]{:S(2)}, u32[]{:S(2)}) %collective-permute-start) | collective-permute-done | bytes 262176 | tf_op jit(solution)/shard_map/ppermute | solution.py:252
  5.8 0.2 first_split.1
  6.0 3.9 %collective-permute-start.1 = (s32[16,1152]{1,0:T(8,128)S(1)}, s32[16,1152]{1,0:T(8,128)S(1)}, u32[]{:S(2)}, u32[]{:S(2)}) collective-permute-start(s32[16,1152]{1,0:T(8,128)S(1)} %get-tuple-element.18), channel_id=1, source_target_pairs={{0,12},{1,13},{2,14},{3,15},{4,8},{5,9},{6,10},{7,11},{8,4},{9,5},... | collective-permute-start | bytes 221192 | tf_op jit(solution)/shard_map/ppermute | solution.py:252
  9.9 0.5 %collective-permute-start.2 = (s32[16,1152]{1,0:T(8,128)S(1)}, s32[16,1152]{1,0:T(8,128)S(1)}, u32[]{:S(2)}, u32[]{:S(2)}) collective-permute-start(s32[16,1152]{1,0:T(8,128)S(1)} %get-tuple-element.19), channel_id=1, source_target_pairs={{0,4},{1,5},{2,6},{3,7},{4,0},{5,1},{6,2},{7,3},{8,12},{9,13},{10,... | collective-permute-start | bytes 221192 | tf_op jit(solution)/shard_map/ppermute | solution.py:252
  10.4 0.1 collective-permute-start.3
  10.6 2.0 %collective-permute-done.1.both_ref = s32[16,1152]{1,0:T(8,128)S(1)} collective-permute-done((s32[16,1152]{1,0:T(8,128)S(1)}, s32[16,1152]{1,0:T(8,128)S(1)}, u32[]{:S(2)}, u32[]{:S(2)}) %collective-permute-start.1) | collective-permute-done | bytes 73760 | tf_op jit(solution)/shard_map/ppermute | solution.py:252
  12.5 1.7 %collective-permute-done.2.x_ref = s32[16,1152]{1,0:T(8,128)S(1)} collective-permute-done((s32[16,1152]{1,0:T(8,128)S(1)}, s32[16,1152]{1,0:T(8,128)S(1)}, u32[]{:S(2)}, u32[]{:S(2)}) %collective-permute-start.2) | collective-permute-done | bytes 73760 | tf_op jit(solution)/shard_map/ppermute | solution.py:252
  14.3 0.5 %collective-permute-done.3.z_ref = s32[16,1152]{1,0:T(8,128)S(1)} collective-permute-done((s32[16,1152]{1,0:T(8,128)S(1)}, s32[16,1152]{1,0:T(8,128)S(1)}, u32[]{:S(2)}, u32[]{:S(2)}) %collective-permute-start.3) | collective-permute-done | bytes 73760 | tf_op jit(solution)/shard_map/ppermute | solution.py:252
  14.8 0.2 add_square.1
  15.0 2.7 %collective-permute-start.4 = (s32[16,1152]{1,0:T(8,128)S(1)}, s32[16,1152]{1,0:T(8,128)S(1)}, u32[]{:S(2)}, u32[]{:S(2)}) collective-permute-start(s32[16,1152]{1,0:T(8,128)S(1)} %get-tuple-element.22), channel_id=1, source_target_pairs={{0,16},{1,17},{2,18},{3,19},{4,20},{5,21},{6,22},{7,23},{8,24},{9,... | collective-permute-start | bytes 221192 | tf_op jit(solution)/shard_map/ppermute | solution.py:252
  17.7 0.1 convert_bitcast_fusion
  17.8 3.6 %collective-permute-done.4.word_ref = s32[16,1152]{1,0:T(8,128)S(1)} collective-permute-done((s32[16,1152]{1,0:T(8,128)S(1)}, s32[16,1152]{1,0:T(8,128)S(1)}, u32[]{:S(2)}, u32[]{:S(2)}) %collective-permute-start.4) | collective-permute-done | bytes 73760 | tf_op jit(solution)/shard_map/ppermute | solution.py:252
  21.5 0.1 sketch_rows.1
  21.6 1.6 %collective-permute-start.7 = (bf16[32,1152]{1,0:T(8,128)(2,1)S(1)}, bf16[32,1152]{1,0:T(8,128)(2,1)S(1)}, u32[]{:S(2)}, u32[]{:S(2)}) collective-permute-start(bf16[32,1152]{1,0:T(8,128)(2,1)S(1)} %sketch_rows.1), channel_id=1, source_target_pairs={{0,1},{1,0},{2,3},{3,2},{4,5},{5,4},{6,7},{7,6},{8,9},{9,8},{10,11... | collective-permute-start | bytes 221192 | tf_op jit(solution)/shard_map/ppermute | solution.py:252
  23.1 1.1 %collective-permute-start.6 = (bf16[32,1152]{1,0:T(8,128)(2,1)S(1)}, bf16[32,1152]{1,0:T(8,128)(2,1)S(1)}, u32[]{:S(2)}, u32[]{:S(2)}) collective-permute-start(bf16[32,1152]{1,0:T(8,128)(2,1)S(1)} %sketch_rows.1), channel_id=1, source_target_pairs={{0,4},{1,5},{2,6},{3,7},{4,0},{5,1},{6,2},{7,3},{8,12},{9,13},{10,... | collective-permute-start | bytes 221192 | tf_op jit(solution)/shard_map/ppermute | solution.py:252
  24.3 0.8 %collective-permute-start.5 = (bf16[32,1152]{1,0:T(8,128)(2,1)S(1)}, bf16[32,1152]{1,0:T(8,128)(2,1)S(1)}, u32[]{:S(2)}, u32[]{:S(2)}) collective-permute-start(bf16[32,1152]{1,0:T(8,128)(2,1)S(1)} %sketch_rows.1), channel_id=1, source_target_pairs={{0,5},{1,4},{2,7},{3,6},{4,1},{5,0},{6,3},{7,2},{8,13},{9,12},{10,... | collective-permute-start | bytes 221192 | tf_op jit(solution)/shard_map/ppermute | solution.py:252
  25.1 1.5 %collective-permute-done.7 = bf16[32,1152]{1,0:T(8,128)(2,1)S(1)} collective-permute-done((bf16[32,1152]{1,0:T(8,128)(2,1)S(1)}, bf16[32,1152]{1,0:T(8,128)(2,1)S(1)}, u32[]{:S(2)}, u32[]{:S(2)}) %collective-permute-start.7) | collective-permute-done | bytes 73760 | tf_op jit(solution)/shard_map/ppermute | solution.py:252
  26.6 0.9 %collective-permute-done.6 = bf16[32,1152]{1,0:T(8,128)(2,1)S(1)} collective-permute-done((bf16[32,1152]{1,0:T(8,128)(2,1)S(1)}, bf16[32,1152]{1,0:T(8,128)(2,1)S(1)}, u32[]{:S(2)}, u32[]{:S(2)}) %collective-permute-start.6) | collective-permute-done | bytes 73760 | tf_op jit(solution)/shard_map/ppermute | solution.py:252
  27.5 2.0 %collective-permute-done.5 = bf16[32,1152]{1,0:T(8,128)(2,1)S(1)} collective-permute-done((bf16[32,1152]{1,0:T(8,128)(2,1)S(1)}, bf16[32,1152]{1,0:T(8,128)(2,1)S(1)}, u32[]{:S(2)}, u32[]{:S(2)}) %collective-permute-start.5) | collective-permute-done | bytes 73760 | tf_op jit(solution)/shard_map/ppermute | solution.py:252
  29.6 0.2 mask_ours.1
  29.8 1.4 %collective-permute-done.8.theirs = bf16[128,1152]{1,0:T(8,128)(2,1)S(1)} collective-permute-done((bf16[128,1152]{1,0:T(8,128)(2,1)S(1)}, bf16[128,1152]{1,0:T(8,128)(2,1)S(1)}, u32[]{:S(2)}, u32[]{:S(2)}) %collective-permute-start.8) | collective-permute-done | bytes 294944 | tf_op jit(solution)/shard_map/ppermute | solution.py:252
  31.2 2.5 %gram.1 = f32[1024,1024]{1,0:T(8,128)} custom-call(bf16[128,1152]{1,0:T(8,128)(2,1)S(1)} %pad_maximum_fusion.row_ref.ours, f32[128,256]{1,0:T(8,128)S(1)} %get-tuple-element.23.own_ref, s32[128,256]{1,0:T(8,128)S(1)} %get-tuple-element.24.label_ref, bf16[128,1152]{1,0:T(8,128)(2,1)S(1)} %collective-permute-done.8.theirs), custom_call_target="tpu_custom_call" | custom-call | flops 536870912 | bytes 4194304 | tf_op jit(solution)/shard_map/gram/pallas_call | solution.py:167
  (5 shorter events, 0.2 us)
Async XLA Ops:
  0.0 17.7 %copy-start = (s32[128,1]{0,1:T(1,128)S(1)}, s32[128,1]{0,1:T(1,128)}, u32[]{:S(2)}) copy-start(s32[128,1]{0,1:T(1,128)} %param.7) | copy-start | bytes 1540
  4.1 1.7 %collective-permute-start = (f32[64,1024]{1,0:T(8,128)S(1)}, f32[64,1024]{1,0:T(8,128)S(1)}, u32[]{:S(2)}, u32[]{:S(2)}) collective-permute-start(f32[64,1024]{1,0:T(8,128)S(1)} %get-tuple-element.16), channel_id=1, source_target_pairs={{0,2},{1,3},{2,0},{3,1},{4,6},{5,7},{6,4},{7,5},{8,10},{9,11},{10,... | collective-permute-start | bytes 786440 | tf_op jit(solution)/shard_map/ppermute | solution.py:252
  6.0 6.6 %collective-permute-start.1 = (s32[16,1152]{1,0:T(8,128)S(1)}, s32[16,1152]{1,0:T(8,128)S(1)}, u32[]{:S(2)}, u32[]{:S(2)}) collective-permute-start(s32[16,1152]{1,0:T(8,128)S(1)} %get-tuple-element.18), channel_id=1, source_target_pairs={{0,12},{1,13},{2,14},{3,15},{4,8},{5,9},{6,10},{7,11},{8,4},{9,5},... | collective-permute-start | bytes 221192 | tf_op jit(solution)/shard_map/ppermute | solution.py:252
  9.9 4.4 %collective-permute-start.2 = (s32[16,1152]{1,0:T(8,128)S(1)}, s32[16,1152]{1,0:T(8,128)S(1)}, u32[]{:S(2)}, u32[]{:S(2)}) collective-permute-start(s32[16,1152]{1,0:T(8,128)S(1)} %get-tuple-element.19), channel_id=1, source_target_pairs={{0,4},{1,5},{2,6},{3,7},{4,0},{5,1},{6,2},{7,3},{8,12},{9,13},{10,... | collective-permute-start | bytes 221192 | tf_op jit(solution)/shard_map/ppermute | solution.py:252
  10.4 4.4 %collective-permute-start.3 = (s32[16,1152]{1,0:T(8,128)S(1)}, s32[16,1152]{1,0:T(8,128)S(1)}, u32[]{:S(2)}, u32[]{:S(2)}) collective-permute-start(s32[16,1152]{1,0:T(8,128)S(1)} %get-tuple-element.20), channel_id=1, source_target_pairs={{0,8},{1,9},{2,10},{3,11},{4,12},{5,13},{6,14},{7,15},{8,0},{9,1},... | collective-permute-start | bytes 221192 | tf_op jit(solution)/shard_map/ppermute | solution.py:252
  15.0 6.4 %collective-permute-start.4 = (s32[16,1152]{1,0:T(8,128)S(1)}, s32[16,1152]{1,0:T(8,128)S(1)}, u32[]{:S(2)}, u32[]{:S(2)}) collective-permute-start(s32[16,1152]{1,0:T(8,128)S(1)} %get-tuple-element.22), channel_id=1, source_target_pairs={{0,16},{1,17},{2,18},{3,19},{4,20},{5,21},{6,22},{7,23},{8,24},{9,... | collective-permute-start | bytes 221192 | tf_op jit(solution)/shard_map/ppermute | solution.py:252
  21.6 5.0 %collective-permute-start.7 = (bf16[32,1152]{1,0:T(8,128)(2,1)S(1)}, bf16[32,1152]{1,0:T(8,128)(2,1)S(1)}, u32[]{:S(2)}, u32[]{:S(2)}) collective-permute-start(bf16[32,1152]{1,0:T(8,128)(2,1)S(1)} %sketch_rows.1), channel_id=1, source_target_pairs={{0,1},{1,0},{2,3},{3,2},{4,5},{5,4},{6,7},{7,6},{8,9},{9,8},{10,11... | collective-permute-start | bytes 221192 | tf_op jit(solution)/shard_map/ppermute | solution.py:252
  23.1 4.4 %collective-permute-start.6 = (bf16[32,1152]{1,0:T(8,128)(2,1)S(1)}, bf16[32,1152]{1,0:T(8,128)(2,1)S(1)}, u32[]{:S(2)}, u32[]{:S(2)}) collective-permute-start(bf16[32,1152]{1,0:T(8,128)(2,1)S(1)} %sketch_rows.1), channel_id=1, source_target_pairs={{0,4},{1,5},{2,6},{3,7},{4,0},{5,1},{6,2},{7,3},{8,12},{9,13},{10,... | collective-permute-start | bytes 221192 | tf_op jit(solution)/shard_map/ppermute | solution.py:252
  24.3 5.3 %collective-permute-start.5 = (bf16[32,1152]{1,0:T(8,128)(2,1)S(1)}, bf16[32,1152]{1,0:T(8,128)(2,1)S(1)}, u32[]{:S(2)}, u32[]{:S(2)}) collective-permute-start(bf16[32,1152]{1,0:T(8,128)(2,1)S(1)} %sketch_rows.1), channel_id=1, source_target_pairs={{0,5},{1,4},{2,7},{3,6},{4,1},{5,0},{6,3},{7,2},{8,13},{9,12},{10,... | collective-permute-start | bytes 221192 | tf_op jit(solution)/shard_map/ppermute | solution.py:252
  29.5 1.6 %collective-permute-start.8 = (bf16[128,1152]{1,0:T(8,128)(2,1)S(1)}, bf16[128,1152]{1,0:T(8,128)(2,1)S(1)}, u32[]{:S(2)}, u32[]{:S(2)}) collective-permute-start(bf16[128,1152]{1,0:T(8,128)(2,1)S(1)} %pad_maximum_fusion.row_ref.ours), channel_id=1, source_target_pairs={{0,2},{1,3},{2,0},{3,1},{4,6},{5,7},{6,4},{7,5},{8,10},{9,11},{10,... | collective-permute-start | bytes 884744 | tf_op jit(solution)/shard_map/ppermute | solution.py:252

commit v9 on v8

--- a/solution.py
+++ b/solution.py
@@ -24,19 +24,45 @@
     return (1 - 2 * (number & 1)).astype(jnp.float32)
 
 
-def partial_kernel(high_count, total_bits, parts, x_hbm, s_hbm, col_hbm, send_ref, keep_ref, x_buf, s_buf, col_buf, low, high, acc, sems):
-    kept = col_hbm.shape[1]
+def add_products(x_ref, sign_ref, low, high, out_ref, part, wide):
+    rows, kept = out_ref.shape
+    blocks = wide // LOW
+    stack = []
+    for block in range(part * blocks, (part + 1) * blocks):
+        cols = slice(block * LOW, (block + 1) * LOW)
+        stack.append(x_ref[:, cols] * sign_ref[:, cols].astype(jnp.bfloat16))
+    stack = jnp.concatenate(stack, axis=0)
+    for group in range(kept // LOW):
+        cols = slice(group * LOW, (group + 1) * LOW)
+        products = jnp.dot(stack, low[:, cols], preferred_element_type=jnp.float32)
+        total = None
+        for at in range(blocks):
+            row = part * blocks + at
+            term = products[at * rows:(at + 1) * rows] * high[row:row + 1, cols]
+            total = term if total is None else total + term
+        if part > 0:
+            total = total + out_ref[:, cols]
+        out_ref[:, cols] = total
+
+
+def send_kernel(total_bits, parts, x_hbm, s_hbm, col_hbm, send_ref, x_keep, signs, low, high, x_buf, col_buf, sems):
+    half, kept = send_ref.shape
     wide = x_hbm.shape[1] // parts
     me = lax.axis_index("feat")
+    mine = lax.rem(me, 2)
     col_copy = pltpu.make_async_copy(col_hbm, col_buf, sems.at[parts])
-    sign_copy = pltpu.make_async_copy(s_hbm, s_buf, sems.at[parts + 1])
+    sign_copy = pltpu.make_async_copy(s_hbm, signs, sems.at[parts + 1])
     col_copy.start()
     sign_copy.start()
     copies = []
     for part in range(parts):
         cols = pl.ds(part * wide, wide)
-        copies.append(pltpu.make_async_copy(x_hbm.at[:, cols], x_buf.at[:, cols], sems.at[part]))
+        rows = pl.ds(pl.multiple_of((1 - mine) * half, half), half)
+        copies.append(pltpu.make_async_copy(x_hbm.at[rows, cols], x_buf.at[:, cols], sems.at[part]))
         copies[-1].start()
+    rows = pl.ds(pl.multiple_of(mine * half, half), half)
+    keep_copy = pltpu.make_async_copy(x_hbm.at[rows, :], x_keep, sems.at[parts + 2])
+    keep_copy.start()
     col_copy.wait()
     col = col_buf[...]
     index = lax.broadcasted_iota(jnp.int32, (16, kept), 0)
@@ -44,65 +70,64 @@
     outer = parity_sign(index & (col >> 4), 4)
     for row in range(LOW // 16):
         low[row * 16:(row + 1) * 16] = (inner * outer[row:row + 1]).astype(jnp.bfloat16)
-    high_index = lax.broadcasted_iota(jnp.int32, high.shape, 0) + me * high_count
+    high_index = lax.broadcasted_iota(jnp.int32, high.shape, 0) + me * high.shape[0]
     high[...] = parity_sign(high_index & (col >> 8), total_bits - 8)
     sign_copy.wait()
-    blocks = wide // LOW
-    rows = x_hbm.shape[0]
     for part in range(parts):
         copies[part].wait()
-        stack = []
-        for block in range(part * blocks, (part + 1) * blocks):
-            cols = slice(block * LOW, (block + 1) * LOW)
-            stack.append(x_buf[:, cols] * s_buf[:, cols].astype(jnp.bfloat16))
-        stack = jnp.concatenate(stack, axis=0)
-        for group in range(kept // LOW):
-            cols = slice(group * LOW, (group + 1) * LOW)
-            products = jnp.dot(stack, low[:, cols], preferred_element_type=jnp.float32)
-            total = None
-            for at in range(blocks):
-                row = part * blocks + at
-                term = products[at * rows:(at + 1) * rows] * high[row:row + 1, cols]
-                total = term if total is None else total + term
-            if part > 0:
-                total = total + acc[:, cols]
-            acc[:, cols] = total
-    half = keep_ref.shape[0]
-    mine = lax.rem(me, 2)
-    keep_ref[...] = acc[pl.ds(pl.multiple_of(mine * half, half), half), :]
-    send_ref[...] = acc[pl.ds(pl.multiple_of((1 - mine) * half, half), half), :]
+        add_products(x_buf, signs, low, high, send_ref, part, wide)
+    keep_copy.wait()
+
+
+def keep_kernel(parts, x_keep, signs, low, high, keep_ref):
+    wide = x_keep.shape[1] // parts
+    for part in range(parts):
+        add_products(x_keep, signs, low, high, keep_ref, part, wide)
 
 
 def partial_halves(features, signs, columns, feat_count):
     rows, width = features.shape
     kept = columns.shape[0]
     parts = max(1, width // 2048)
-    high_count = width // LOW
+    half = rows // 2
     total_bits = (width * feat_count).bit_length() - 1
-    half = jax.ShapeDtypeStruct((rows // 2, kept), jnp.float32)
-    return pl.pallas_call(
-        functools.partial(partial_kernel, high_count, total_bits, parts),
+    params = pltpu.CompilerParams(vmem_limit_bytes=VMEM_LIMIT)
+    cost = pl.CostEstimate(
+        flops=2 * half * width * kept, bytes_accessed=2 * rows * width + 4 * half * kept, transcendentals=0
+    )
+    total_type = jax.ShapeDtypeStruct((half, kept), jnp.float32)
+    send, *held = pl.pallas_call(
+        functools.partial(send_kernel, total_bits, parts),
         in_specs=[pl.BlockSpec(memory_space=pltpu.HBM)] * 3,
-        out_specs=[pl.BlockSpec(memory_space=pltpu.VMEM)] * 2,
-        out_shape=[half, half],
+        out_specs=[pl.BlockSpec(memory_space=pltpu.VMEM)] * 5,
+        out_shape=[
+            total_type,
+            jax.ShapeDtypeStruct((half, width), jnp.bfloat16),
+            jax.ShapeDtypeStruct((1, width), jnp.int32),
+            jax.ShapeDtypeStruct((LOW, kept), jnp.bfloat16),
+            jax.ShapeDtypeStruct((width // LOW, kept), jnp.float32),
+        ],
         scratch_shapes=[
-            pltpu.VMEM((rows, width), jnp.bfloat16),
-            pltpu.VMEM((1, width), jnp.int32),
+            pltpu.VMEM((half, width), jnp.bfloat16),
             pltpu.VMEM((1, kept), jnp.int32),
-            pltpu.VMEM((LOW, kept), jnp.bfloat16),
-            pltpu.VMEM((high_count, kept), jnp.float32),
-            pltpu.VMEM((rows, kept), jnp.float32),
-            pltpu.SemaphoreType.DMA((parts + 2,)),
+            pltpu.SemaphoreType.DMA((parts + 3,)),
         ],
-        compiler_params=pltpu.CompilerParams(vmem_limit_bytes=VMEM_LIMIT),
-        cost_estimate=pl.CostEstimate(
-            flops=2 * rows * width * kept, bytes_accessed=2 * rows * width + 4 * rows * kept, transcendentals=0
-        ),
-        name="partial_transform",
+        compiler_params=params,
+        cost_estimate=cost,
+        name="partial_sent",
     )(*(
         pltpu.with_memory_space_constraint(operand, pltpu.HBM)
         for operand in (features, signs.reshape(1, width), columns.reshape(1, kept))
     ))
+    got = swap(send, feat=1)
+    keep = pl.pallas_call(
+        functools.partial(keep_kernel, parts),
+        out_shape=total_type,
+        compiler_params=params,
+        cost_estimate=cost,
+        name="partial_kept",
+    )(*held)
+    return keep, got
 
 
 def mask_operands(shard, wide, factor, row_ref):
@@ -120,32 +145,34 @@
     own = jnp.concatenate([own] * -(-wide // LANES), axis=1)[:, :wide]
     named = row_ref[:, kept:kept + 1].astype(jnp.float32).astype(jnp.int32)
     label = named - lax.broadcasted_iota(jnp.int32, own.shape, 1) // shard
-    return own, label
+    return own.T, label.T
 
 
 def mask_kernel(shard, wide, factor, row_ref, own_ref, label_ref):
     own_ref[...], label_ref[...] = mask_operands(shard, wide, factor, row_ref)
 
 
-def gram_kernel(shard, group, factor, ours, own_ref, label_ref, theirs, out_hbm, rows, blocks, sems):
+def gram_kernel(shard, group, factor, ours, own_ref, label_ref, theirs, out_hbm, rows, chosen, blocks, sems):
     kept = rows.shape[1]
     half = ours.shape[0]
     wide = group * shard
-    steps = blocks.shape[0]
+    steps = chosen.shape[0] // wide
+    chunks = blocks.shape[0]
     rows[:half] = ours[:, :kept]
     rows[half:] = theirs[:, :kept]
     parts = ((own_ref[...], label_ref[...]), mask_operands(shard, wide, factor, theirs))
     base = lax.axis_index("tok") * steps * group
+    for step in range(steps):
+        for at, (own, label) in enumerate(parts):
+            masked = jnp.where(label == base + step * group, own, 0.0).astype(jnp.bfloat16)
+            chosen[step * wide:(step + 1) * wide, at * half:(at + 1) * half] = masked
     copies = []
-    for step in range(steps):
-        chosen = jnp.concatenate(
-            [jnp.where(label == base + step * group, own, 0.0).astype(jnp.bfloat16) for own, label in parts], axis=0
-        )
-        blocks[step] = lax.dot_general(
-            chosen, rows[...], (((0,), (0,)), ((), ())), preferred_element_type=jnp.float32
-        )
+    size = kept // chunks
+    for chunk in range(chunks):
+        cols = slice(chunk * size, (chunk + 1) * size)
+        blocks[chunk] = jnp.dot(chosen[...], rows[:, cols], preferred_element_type=jnp.float32)
         copies.append(
-            pltpu.make_async_copy(blocks.at[step], out_hbm.at[pl.ds(step * wide, wide), :], sems.at[step])
+            pltpu.make_async_copy(blocks.at[chunk], out_hbm.at[:, pl.ds(chunk * size, size)], sems.at[chunk])
         )
         copies[-1].start()
     for copy in copies:
@@ -156,11 +183,11 @@
     tokens = ours.shape[0]
     group = max(1, min(concepts, LOW // shard))
     wide = group * shard
-    steps = concepts // group
+    chunks = kept // LOW
     params = pltpu.CompilerParams(vmem_limit_bytes=VMEM_LIMIT)
     own, label = pl.pallas_call(
         functools.partial(mask_kernel, shard, wide, factor),
-        out_shape=[jax.ShapeDtypeStruct((tokens, wide), dtype) for dtype in (jnp.float32, jnp.int32)],
+        out_shape=[jax.ShapeDtypeStruct((wide, tokens), dtype) for dtype in (jnp.float32, jnp.int32)],
         compiler_params=params,
         name="mask_ours",
     )(ours)
@@ -171,8 +198,9 @@
         out_shape=jax.ShapeDtypeStruct((concepts * shard, kept), jnp.float32),
         scratch_shapes=[
             pltpu.VMEM((2 * tokens, kept), jnp.bfloat16),
-            pltpu.VMEM((steps, wide, kept), jnp.float32),
-            pltpu.SemaphoreType.DMA((steps,)),
+            pltpu.VMEM((concepts * shard, 2 * tokens), jnp.bfloat16),
+            pltpu.VMEM((chunks, concepts * shard, LOW), jnp.float32),
+            pltpu.SemaphoreType.DMA((chunks,)),
         ],
         compiler_params=params,
         cost_estimate=pl.CostEstimate(
@@ -226,11 +254,13 @@
     encode(total, out_ref)
 
 
-def last_kernel(scale, total_ref, word_ref, label_ref, row_ref):
+def last_kernel(scale, total_ref, word_ref, label_ref, *row_refs):
     total = total_ref[...] + decode(word_ref)
     kept = total.shape[1]
-    row_ref[:, :kept] = (total * scale).astype(jnp.bfloat16)
-    row_ref[:, kept:] = label_ref[...]
+    row = (total * scale).astype(jnp.bfloat16)
+    for row_ref in row_refs:
+        row_ref[:, :kept] = row
+        row_ref[:, kept:] = label_ref[...]
 
 
 def local_call(kernel, name, *operands, out_shape):
@@ -268,8 +298,7 @@
     own_labels = lax.dynamic_slice_in_dim(labels, first, size, 0).astype(jnp.bfloat16)
     own_labels = jnp.broadcast_to(own_labels, (size, LANES))
 
-    send, keep = partial_halves(features, signs, columns, feat_count)
-    got = swap(send, feat=1)
+    keep, got = partial_halves(features, signs, columns, feat_count)
     total, there, here, again = local_call(
         functools.partial(first_kernel, 2), "first_split", keep, got, out_shape=[total_type, word_type, word_type, word_type]
     )
@@ -291,18 +320,18 @@
         word = swap(word, feat=stride)
         stride *= 2
     scale = 1.0 / math.sqrt(width * feat_count)
-    ours = local_call(
-        functools.partial(last_kernel, scale), "sketch_rows", total, word, own_labels, out_shape=row_type
+    copies = local_call(
+        functools.partial(last_kernel, scale), "sketch_rows", total, word, own_labels, out_shape=[row_type] * 3
     )
 
     stride = 2
     while stride < tok_count:
-        ours = jnp.concatenate([ours, swap(ours, tok=stride)], axis=0)
+        copies = [jnp.concatenate([copies[0], swap(copies[0], tok=stride)], axis=0)] * 3
         stride *= 2
-    received = [swap(ours, tok=1, feat=2)] if tok_count > 1 else []
-    received += [swap(ours, feat=2)]
-    received += [swap(ours, tok=1)] if tok_count > 1 else []
-    ours = jnp.concatenate([ours] + received, axis=0)
+    received = [swap(copies[0], tok=1, feat=2)] if tok_count > 1 else []
+    received += [swap(copies[1], feat=2)]
+    received += [swap(copies[2], tok=1)] if tok_count > 1 else []
+    ours = jnp.concatenate([copies[0]] + received, axis=0)
     theirs = swap(ours, feat=1)
     concepts = C // tok_count
     gram = gram_blocks(ours, theirs, concepts, shard, kept, C / (rows * tok_count))

time: 33.9 us -> 32.3 us (0.953)
  waiting for transfers between devices: 14.8 us -> 13.2 us
    ppermute x9, waiting for transfers between devices: 14.8 us -> 13.2 us  [swap(): return lax.ppermute(array, ('feat', 'tok'), pairs)]
    pallas_call x1 -> x2, Pallas kernels: 4.11 us -> 4.11 us  [the longest x1 2.84 us: partial_halves(): pl.pallas_call(functools.partial(send_kernel, total_bits, parts), in_spec...]
  transfers between devices with their start and end apart: 9 -> 9, of which waited for: 9 -> 8; matrix products, arithmetic and copies ran while one was open for 0% -> 0% of each run, Pallas kernels for 1% -> 5%
where the time goes in v9:
time: 32.3 us; the launch traced here: 32.2 us
  waiting for transfers between devices  13.2 us (41%)
  starting transfers between devices  11.2 us (35%)
  Pallas kernels  7.54 us (23%)
    ppermute x9, waiting for transfers between devices, swap(): return lax.ppermute(array, ('feat', 'tok'), pairs)  13.2 us
    ppermute x9, starting transfers between devices, swap(): return lax.ppermute(array, ('feat', 'tok'), pairs)  11.2 us
    pallas_call x1, Pallas kernels, partial_halves(): pl.pallas_call(functools.partial(send_kernel, total_bits, parts), in_spec...  2.84 us
    pallas_call x1, Pallas kernels, gram_blocks(): pl.pallas_call(functools.partial(gram_kernel, shard, group, factor), in_s...  2.69 us
    pallas_call x1, Pallas kernels, partial_halves(): pl.pallas_call(functools.partial(keep_kernel, parts), out_shape=total_typ...  1.27 us
  transfers between devices with their start and end apart: 9, of which 8 were waited for; matrix products, arithmetic and copies ran while one was open for 0% of the time, Pallas kernels for 5%

profile of v9, /device:TPU:0, one launch (start us, length us, event | category | flops | bytes accessed | tf_op | source)
XLA Modules:
  0.0 32.2 jit_solution(8693990076384291871)
XLA Ops:
  0.0 2.8 %partial_sent.1 = (f32[64,1024]{1,0:T(8,128)S(1)}, bf16[64,8192]{1,0:T(8,128)(2,1)S(1)}, s32[1,8192]{1,0:T(1,128)S(1)}, bf16[256,1024]{1,0:T(8,128)(2,1)S(1)}, f32[32,1024]{1,0:T(8,128)S(1)}) custom-call(bf16[128,8192]{1,0:T(8,128)(2,1)} %x_hbm.1, s32[1,8192]{1,0:T(1,128)} %bitcast.5, s32[1,1024]{1,0:T(1,128)} %bitcast.6), custom_call_target="tpu_custom_call" | custom-call | flops 1073741824 | bytes 2359296 | tf_op jit(solution)/shard_map/partial_sent/pallas_call | solution.py:99
  2.9 0.5 %collective-permute-start = (f32[64,1024]{1,0:T(8,128)S(1)}, f32[64,1024]{1,0:T(8,128)S(1)}, u32[]{:S(2)}, u32[]{:S(2)}) collective-permute-start(f32[64,1024]{1,0:T(8,128)S(1)} %get-tuple-element.25), channel_id=1, source_target_pairs={{0,2},{1,3},{2,0},{3,1},{4,6},{5,7},{6,4},{7,5},{8,10},{9,11},{10,... | collective-permute-start | bytes 786440 | tf_op jit(solution)/shard_map/ppermute | solution.py:282
  3.4 1.3 %partial_kept.1.keep_ref = f32[64,1024]{1,0:T(8,128)S(1)} custom-call(bf16[64,8192]{1,0:T(8,128)(2,1)S(1)} %get-tuple-element.21.x_keep, s32[1,8192]{1,0:T(1,128)S(1)} %get-tuple-element.22.signs, bf16[256,1024]{1,0:T(8,128)(2,1)S(1)} %get-tuple-element.23.low, f32[32,1024]{1,0:T(8,128)S(1)} %get-tuple-element.24.high), custom_call_target="tpu_custom_call" | custom-call | flops 1073741824 | bytes 2359296 | tf_op jit(solution)/shard_map/partial_kept/pallas_call | solution.py:123
  4.7 0.2 first_split.1
  4.8 3.8 %collective-permute-start.1 = (s32[16,1152]{1,0:T(8,128)S(1)}, s32[16,1152]{1,0:T(8,128)S(1)}, u32[]{:S(2)}, u32[]{:S(2)}) collective-permute-start(s32[16,1152]{1,0:T(8,128)S(1)} %get-tuple-element.27), channel_id=1, source_target_pairs={{0,12},{1,13},{2,14},{3,15},{4,8},{5,9},{6,10},{7,11},{8,4},{9,5},... | collective-permute-start | bytes 221192 | tf_op jit(solution)/shard_map/ppermute | solution.py:282
  8.6 0.5 %collective-permute-start.2 = (s32[16,1152]{1,0:T(8,128)S(1)}, s32[16,1152]{1,0:T(8,128)S(1)}, u32[]{:S(2)}, u32[]{:S(2)}) collective-permute-start(s32[16,1152]{1,0:T(8,128)S(1)} %get-tuple-element.28), channel_id=1, source_target_pairs={{0,4},{1,5},{2,6},{3,7},{4,0},{5,1},{6,2},{7,3},{8,12},{9,13},{10,... | collective-permute-start | bytes 221192 | tf_op jit(solution)/shard_map/ppermute | solution.py:282
  9.2 0.1 collective-permute-start.3
  9.3 2.1 %collective-permute-done.1.both_ref = s32[16,1152]{1,0:T(8,128)S(1)} collective-permute-done((s32[16,1152]{1,0:T(8,128)S(1)}, s32[16,1152]{1,0:T(8,128)S(1)}, u32[]{:S(2)}, u32[]{:S(2)}) %collective-permute-start.1) | collective-permute-done | bytes 73760 | tf_op jit(solution)/shard_map/ppermute | solution.py:282
  11.4 1.6 %collective-permute-done.2.x_ref = s32[16,1152]{1,0:T(8,128)S(1)} collective-permute-done((s32[16,1152]{1,0:T(8,128)S(1)}, s32[16,1152]{1,0:T(8,128)S(1)}, u32[]{:S(2)}, u32[]{:S(2)}) %collective-permute-start.2) | collective-permute-done | bytes 73760 | tf_op jit(solution)/shard_map/ppermute | solution.py:282
  13.0 0.5 %collective-permute-done.3.z_ref = s32[16,1152]{1,0:T(8,128)S(1)} collective-permute-done((s32[16,1152]{1,0:T(8,128)S(1)}, s32[16,1152]{1,0:T(8,128)S(1)}, u32[]{:S(2)}, u32[]{:S(2)}) %collective-permute-start.3) | collective-permute-done | bytes 73760 | tf_op jit(solution)/shard_map/ppermute | solution.py:282
  13.5 0.2 add_square.1
  13.7 2.7 %collective-permute-start.4 = (s32[16,1152]{1,0:T(8,128)S(1)}, s32[16,1152]{1,0:T(8,128)S(1)}, u32[]{:S(2)}, u32[]{:S(2)}) collective-permute-start(s32[16,1152]{1,0:T(8,128)S(1)} %get-tuple-element.31), channel_id=1, source_target_pairs={{0,16},{1,17},{2,18},{3,19},{4,20},{5,21},{6,22},{7,23},{8,24},{9,... | collective-permute-start | bytes 221192 | tf_op jit(solution)/shard_map/ppermute | solution.py:282
  16.4 0.1 convert_bitcast_fusion
  16.5 3.8 %collective-permute-done.4.word_ref = s32[16,1152]{1,0:T(8,128)S(1)} collective-permute-done((s32[16,1152]{1,0:T(8,128)S(1)}, s32[16,1152]{1,0:T(8,128)S(1)}, u32[]{:S(2)}, u32[]{:S(2)}) %collective-permute-start.4) | collective-permute-done | bytes 73760 | tf_op jit(solution)/shard_map/ppermute | solution.py:282
  20.3 0.1 sketch_rows.1
  20.4 2.0 %collective-permute-start.5 = (bf16[32,1152]{1,0:T(8,128)(2,1)S(1)}, bf16[32,1152]{1,0:T(8,128)(2,1)S(1)}, u32[]{:S(2)}, u32[]{:S(2)}) collective-permute-start(bf16[32,1152]{1,0:T(8,128)(2,1)S(1)} %get-tuple-element.32), channel_id=1, source_target_pairs={{0,5},{1,4},{2,7},{3,6},{4,1},{5,0},{6,3},{7,2},{8,13},{9,12},{10,... | collective-permute-start | bytes 221192 | tf_op jit(solution)/shard_map/ppermute | solution.py:282
  22.4 1.1 %collective-permute-start.6 = (bf16[32,1152]{1,0:T(8,128)(2,1)S(1)}, bf16[32,1152]{1,0:T(8,128)(2,1)S(1)}, u32[]{:S(2)}, u32[]{:S(2)}) collective-permute-start(bf16[32,1152]{1,0:T(8,128)(2,1)S(1)} %get-tuple-element.33), channel_id=1, source_target_pairs={{0,4},{1,5},{2,6},{3,7},{4,0},{5,1},{6,2},{7,3},{8,12},{9,13},{10,... | collective-permute-start | bytes 221192 | tf_op jit(solution)/shard_map/ppermute | solution.py:282
  23.5 0.5 %collective-permute-start.7 = (bf16[32,1152]{1,0:T(8,128)(2,1)S(1)}, bf16[32,1152]{1,0:T(8,128)(2,1)S(1)}, u32[]{:S(2)}, u32[]{:S(2)}) collective-permute-start(bf16[32,1152]{1,0:T(8,128)(2,1)S(1)} %get-tuple-element.34), channel_id=1, source_target_pairs={{0,1},{1,0},{2,3},{3,2},{4,5},{5,4},{6,7},{7,6},{8,9},{9,8},{10,11... | collective-permute-start | bytes 221192 | tf_op jit(solution)/shard_map/ppermute | solution.py:282
  24.0 1.8 %collective-permute-done.5 = bf16[32,1152]{1,0:T(8,128)(2,1)S(1)} collective-permute-done((bf16[32,1152]{1,0:T(8,128)(2,1)S(1)}, bf16[32,1152]{1,0:T(8,128)(2,1)S(1)}, u32[]{:S(2)}, u32[]{:S(2)}) %collective-permute-start.5) | collective-permute-done | bytes 73760 | tf_op jit(solution)/shard_map/ppermute | solution.py:282
  25.8 1.0 %collective-permute-done.6 = bf16[32,1152]{1,0:T(8,128)(2,1)S(1)} collective-permute-done((bf16[32,1152]{1,0:T(8,128)(2,1)S(1)}, bf16[32,1152]{1,0:T(8,128)(2,1)S(1)}, u32[]{:S(2)}, u32[]{:S(2)}) %collective-permute-start.6) | collective-permute-done | bytes 73760 | tf_op jit(solution)/shard_map/ppermute | solution.py:282
  26.8 1.0 %collective-permute-done.7 = bf16[32,1152]{1,0:T(8,128)(2,1)S(1)} collective-permute-done((bf16[32,1152]{1,0:T(8,128)(2,1)S(1)}, bf16[32,1152]{1,0:T(8,128)(2,1)S(1)}, u32[]{:S(2)}, u32[]{:S(2)}) %collective-permute-start.7) | collective-permute-done | bytes 73760 | tf_op jit(solution)/shard_map/ppermute | solution.py:282
  27.9 0.3 mask_ours.1
  28.2 1.3 %collective-permute-done.8.theirs = bf16[128,1152]{1,0:T(8,128)(2,1)S(1)} collective-permute-done((bf16[128,1152]{1,0:T(8,128)(2,1)S(1)}, bf16[128,1152]{1,0:T(8,128)(2,1)S(1)}, u32[]{:S(2)}, u32[]{:S(2)}) %collective-permute-start.8) | collective-permute-done | bytes 294944 | tf_op jit(solution)/shard_map/ppermute | solution.py:282
  29.5 2.7 %gram.1 = f32[1024,1024]{1,0:T(8,128)} custom-call(bf16[128,1152]{1,0:T(8,128)(2,1)S(1)} %constant_dynamic-update-slice_fusion.row_ref.ours, f32[256,128]{1,0:T(8,128)S(1)} %get-tuple-element.35.own_ref, s32[256,128]{1,0:T(8,128)S(1)} %get-tuple-element.36.label_ref, bf16[128,1152]{1,0:T(8,128)(2,1)S(1)} %collective-permute-done.8.theirs), custom_call_target="tpu_custom_call" | custom-call | flops 536870912 | bytes 4194304 | tf_op jit(solution)/shard_map/gram/pallas_call | solution.py:194
  (9 shorter events, 0.2 us)
Async XLA Ops:
  0.0 16.4 %copy-start = (s32[128,1]{0,1:T(1,128)S(1)}, s32[128,1]{0,1:T(1,128)}, u32[]{:S(2)}) copy-start(s32[128,1]{0,1:T(1,128)} %param.7) | copy-start | bytes 1540
  2.9 1.8 %collective-permute-start = (f32[64,1024]{1,0:T(8,128)S(1)}, f32[64,1024]{1,0:T(8,128)S(1)}, u32[]{:S(2)}, u32[]{:S(2)}) collective-permute-start(f32[64,1024]{1,0:T(8,128)S(1)} %get-tuple-element.25), channel_id=1, source_target_pairs={{0,2},{1,3},{2,0},{3,1},{4,6},{5,7},{6,4},{7,5},{8,10},{9,11},{10,... | collective-permute-start | bytes 786440 | tf_op jit(solution)/shard_map/ppermute | solution.py:282
  4.8 6.5 %collective-permute-start.1 = (s32[16,1152]{1,0:T(8,128)S(1)}, s32[16,1152]{1,0:T(8,128)S(1)}, u32[]{:S(2)}, u32[]{:S(2)}) collective-permute-start(s32[16,1152]{1,0:T(8,128)S(1)} %get-tuple-element.27), channel_id=1, source_target_pairs={{0,12},{1,13},{2,14},{3,15},{4,8},{5,9},{6,10},{7,11},{8,4},{9,5},... | collective-permute-start | bytes 221192 | tf_op jit(solution)/shard_map/ppermute | solution.py:282
  8.6 4.4 %collective-permute-start.2 = (s32[16,1152]{1,0:T(8,128)S(1)}, s32[16,1152]{1,0:T(8,128)S(1)}, u32[]{:S(2)}, u32[]{:S(2)}) collective-permute-start(s32[16,1152]{1,0:T(8,128)S(1)} %get-tuple-element.28), channel_id=1, source_target_pairs={{0,4},{1,5},{2,6},{3,7},{4,0},{5,1},{6,2},{7,3},{8,12},{9,13},{10,... | collective-permute-start | bytes 221192 | tf_op jit(solution)/shard_map/ppermute | solution.py:282
  9.2 4.4 %collective-permute-start.3 = (s32[16,1152]{1,0:T(8,128)S(1)}, s32[16,1152]{1,0:T(8,128)S(1)}, u32[]{:S(2)}, u32[]{:S(2)}) collective-permute-start(s32[16,1152]{1,0:T(8,128)S(1)} %get-tuple-element.29), channel_id=1, source_target_pairs={{0,8},{1,9},{2,10},{3,11},{4,12},{5,13},{6,14},{7,15},{8,0},{9,1},... | collective-permute-start | bytes 221192 | tf_op jit(solution)/shard_map/ppermute | solution.py:282
  13.7 6.5 %collective-permute-start.4 = (s32[16,1152]{1,0:T(8,128)S(1)}, s32[16,1152]{1,0:T(8,128)S(1)}, u32[]{:S(2)}, u32[]{:S(2)}) collective-permute-start(s32[16,1152]{1,0:T(8,128)S(1)} %get-tuple-element.31), channel_id=1, source_target_pairs={{0,16},{1,17},{2,18},{3,19},{4,20},{5,21},{6,22},{7,23},{8,24},{9,... | collective-permute-start | bytes 221192 | tf_op jit(solution)/shard_map/ppermute | solution.py:282
  20.4 5.3 %collective-permute-start.5 = (bf16[32,1152]{1,0:T(8,128)(2,1)S(1)}, bf16[32,1152]{1,0:T(8,128)(2,1)S(1)}, u32[]{:S(2)}, u32[]{:S(2)}) collective-permute-start(bf16[32,1152]{1,0:T(8,128)(2,1)S(1)} %get-tuple-element.32), channel_id=1, source_target_pairs={{0,5},{1,4},{2,7},{3,6},{4,1},{5,0},{6,3},{7,2},{8,13},{9,12},{10,... | collective-permute-start | bytes 221192 | tf_op jit(solution)/shard_map/ppermute | solution.py:282
  22.4 4.4 %collective-permute-start.6 = (bf16[32,1152]{1,0:T(8,128)(2,1)S(1)}, bf16[32,1152]{1,0:T(8,128)(2,1)S(1)}, u32[]{:S(2)}, u32[]{:S(2)}) collective-permute-start(bf16[32,1152]{1,0:T(8,128)(2,1)S(1)} %get-tuple-element.33), channel_id=1, source_target_pairs={{0,4},{1,5},{2,6},{3,7},{4,0},{5,1},{6,2},{7,3},{8,12},{9,13},{10,... | collective-permute-start | bytes 221192 | tf_op jit(solution)/shard_map/ppermute | solution.py:282
  23.5 4.4 %collective-permute-start.7 = (bf16[32,1152]{1,0:T(8,128)(2,1)S(1)}, bf16[32,1152]{1,0:T(8,128)(2,1)S(1)}, u32[]{:S(2)}, u32[]{:S(2)}) collective-permute-start(bf16[32,1152]{1,0:T(8,128)(2,1)S(1)} %get-tuple-element.34), channel_id=1, source_target_pairs={{0,1},{1,0},{2,3},{3,2},{4,5},{5,4},{6,7},{7,6},{8,9},{9,8},{10,11... | collective-permute-start | bytes 221192 | tf_op jit(solution)/shard_map/ppermute | solution.py:282
  27.8 1.6 %collective-permute-start.8 = (bf16[128,1152]{1,0:T(8,128)(2,1)S(1)}, bf16[128,1152]{1,0:T(8,128)(2,1)S(1)}, u32[]{:S(2)}, u32[]{:S(2)}) collective-permute-start(bf16[128,1152]{1,0:T(8,128)(2,1)S(1)} %constant_dynamic-update-slice_fusion.row_ref.ours), channel_id=1, source_target_pairs={{0,2},{1,3},{2,0},{3,1},{4,6},{5,7},{6,4},{7,5},{8,10},{9,11},{10,... | collective-permute-start | bytes 884744 | tf_op jit(solution)/shard_map/ppermute | solution.py:282

commit v10 on v9

--- a/solution.py
+++ b/solution.py
@@ -130,105 +130,85 @@
     return keep, got
 
 
-def mask_operands(shard, wide, factor, row_ref):
-    kept = row_ref.shape[1] - LANES
+def gram_kernel(shard, group, factor, label_ref, *refs):
+    pieces, (out_hbm, rows, blocks, sems) = refs[:-4], refs[-4:]
+    steps, wide, _ = blocks.shape
+    place = 0
+    for piece in pieces:
+        rows[place:place + piece.shape[0]] = piece[...]
+        place += piece.shape[0]
     first = lax.axis_index("feat") * shard
     start = pl.multiple_of(first // LANES * LANES, LANES)
-    window = row_ref[:, pl.ds(start, LANES)].astype(jnp.float32) * factor
+    window = rows[:, pl.ds(start, LANES)].astype(jnp.float32) * factor
     window = pltpu.roll(window, lax.rem(LANES - (first - start), LANES), 1)
-    lane = lax.broadcasted_iota(jnp.int32, window.shape, 1)
-    own = jnp.where(lane < shard, window, 0.0)
-    step = shard
-    while step < LANES:
-        own = own + pltpu.roll(own, step, 1)
-        step *= 2
-    own = jnp.concatenate([own] * -(-wide // LANES), axis=1)[:, :wide]
-    named = row_ref[:, kept:kept + 1].astype(jnp.float32).astype(jnp.int32)
-    label = named - lax.broadcasted_iota(jnp.int32, own.shape, 1) // shard
-    return own.T, label.T
-
-
-def mask_kernel(shard, wide, factor, row_ref, own_ref, label_ref):
-    own_ref[...], label_ref[...] = mask_operands(shard, wide, factor, row_ref)
-
-
-def gram_kernel(shard, group, factor, ours, own_ref, label_ref, theirs, out_hbm, rows, chosen, blocks, sems):
-    kept = rows.shape[1]
-    half = ours.shape[0]
-    wide = group * shard
-    steps = chosen.shape[0] // wide
-    chunks = blocks.shape[0]
-    rows[:half] = ours[:, :kept]
-    rows[half:] = theirs[:, :kept]
-    parts = ((own_ref[...], label_ref[...]), mask_operands(shard, wide, factor, theirs))
+    own = jnp.concatenate([window.T[:shard]] * group, axis=0)
+    label = label_ref[...] - lax.broadcasted_iota(jnp.int32, own.shape, 0) // shard
     base = lax.axis_index("tok") * steps * group
+    copies = []
     for step in range(steps):
-        for at, (own, label) in enumerate(parts):
-            masked = jnp.where(label == base + step * group, own, 0.0).astype(jnp.bfloat16)
-            chosen[step * wide:(step + 1) * wide, at * half:(at + 1) * half] = masked
-    copies = []
-    size = kept // chunks
-    for chunk in range(chunks):
-        cols = slice(chunk * size, (chunk + 1) * size)
-        blocks[chunk] = jnp.dot(chosen[...], rows[:, cols], preferred_element_type=jnp.float32)
+        chosen = jnp.where(label == base + step * group, own, 0.0).astype(jnp.bfloat16)
+        blocks[step] = jnp.dot(chosen, rows[...], preferred_element_type=jnp.float32)
         copies.append(
-            pltpu.make_async_copy(blocks.at[chunk], out_hbm.at[:, pl.ds(chunk * size, size)], sems.at[chunk])
+            pltpu.make_async_copy(blocks.at[step], out_hbm.at[pl.ds(step * wide, wide), :], sems.at[step])
         )
         copies[-1].start()
     for copy in copies:
         copy.wait()
 
 
-def gram_blocks(ours, theirs, concepts, shard, kept, factor):
-    tokens = ours.shape[0]
+def gram_blocks(pieces, label_row, concepts, shard, factor):
+    tokens = sum(piece.shape[0] for piece in pieces)
+    kept = pieces[0].shape[1]
     group = max(1, min(concepts, LOW // shard))
     wide = group * shard
-    chunks = kept // LOW
-    params = pltpu.CompilerParams(vmem_limit_bytes=VMEM_LIMIT)
-    own, label = pl.pallas_call(
-        functools.partial(mask_kernel, shard, wide, factor),
-        out_shape=[jax.ShapeDtypeStruct((wide, tokens), dtype) for dtype in (jnp.float32, jnp.int32)],
-        compiler_params=params,
-        name="mask_ours",
-    )(ours)
+    steps = concepts // group
     return pl.pallas_call(
         functools.partial(gram_kernel, shard, group, factor),
-        in_specs=[pl.BlockSpec(memory_space=pltpu.VMEM)] * 4,
+        in_specs=[pl.BlockSpec(memory_space=pltpu.VMEM)] * (1 + len(pieces)),
         out_specs=pl.BlockSpec(memory_space=pltpu.HBM),
         out_shape=jax.ShapeDtypeStruct((concepts * shard, kept), jnp.float32),
         scratch_shapes=[
-            pltpu.VMEM((2 * tokens, kept), jnp.bfloat16),
-            pltpu.VMEM((concepts * shard, 2 * tokens), jnp.bfloat16),
-            pltpu.VMEM((chunks, concepts * shard, LOW), jnp.float32),
-            pltpu.SemaphoreType.DMA((chunks,)),
+            pltpu.VMEM((tokens, kept), jnp.bfloat16),
+            pltpu.VMEM((steps, wide, kept), jnp.float32),
+            pltpu.SemaphoreType.DMA((steps,)),
         ],
-        compiler_params=params,
+        compiler_params=pltpu.CompilerParams(vmem_limit_bytes=VMEM_LIMIT),
         cost_estimate=pl.CostEstimate(
-            flops=4 * tokens * concepts * shard * kept, bytes_accessed=4 * concepts * shard * kept, transcendentals=0
+            flops=2 * tokens * concepts * shard * kept, bytes_accessed=4 * concepts * shard * kept, transcendentals=0
         ),
         name="gram",
-    )(ours, own, label, theirs)
+    )(label_row, *pieces)
 
 
 def encode(values, word_ref):
-    kept = values.shape[1]
-    half = values.shape[0] // 2
+    size, kept = values.shape
+    half = size // 2
     top = jnp.max(jnp.abs(values), axis=1, keepdims=True)
     power = jnp.ceil(jnp.log2(jnp.maximum(top, 2.0 ** -100)))
     whole = jnp.round(values * jnp.exp2(15.0 - power))
     whole = jnp.clip(whole, -32767.0, 32767.0).astype(jnp.int32)
-    power = jnp.broadcast_to(power, (values.shape[0], LANES)).astype(jnp.int32)
-    for cols, code in ((slice(0, kept), whole), (slice(kept, kept + LANES), power)):
-        word_ref[:, cols] = (code[:half] & 0xFFFF) | (code[half:] << 16)
-
-
-def decode(word_ref):
-    word = word_ref[...]
+    word = (whole[:half] & 0xFFFF) | (whole[half:] << 16)
+    for column in range(kept // LANES):
+        word_ref[column * half:(column + 1) * half] = word[:, column * LANES:(column + 1) * LANES]
+    group = lax.broadcasted_iota(jnp.int32, (8, LANES), 1) // (LANES * 8 // size)
+    tile = jnp.zeros((8, LANES), jnp.int32)
+    for at in range(size // 8):
+        tile = jnp.where(group == at, power[at * 8:(at + 1) * 8].astype(jnp.int32), tile)
+    word_ref[kept // LANES * half:] = tile
+
+
+def decode(word_ref, size):
+    half = size // 2
+    columns = word_ref.shape[0] // half
+    word = jnp.concatenate([word_ref[at * half:(at + 1) * half] for at in range(columns)], axis=1)
     code = jnp.concatenate([(word << 16) >> 16, word >> 16], axis=0).astype(jnp.float32)
-    return code[:, :-LANES] * jnp.exp2(code[:, -LANES:-LANES + 1] - 15.0)
-
-
-def first_kernel(stride, keep_ref, got_ref, total_ref, there_ref, here_ref, again_ref):
+    tile = jnp.exp2(word_ref[columns * half:].astype(jnp.float32) - 15.0)
+    lanes = LANES * 8 // size
+    scale = jnp.concatenate([tile[:, at * lanes:at * lanes + 1] for at in range(size // 8)], axis=0)
+    return code * scale
+
+
+def first_kernel(stride, keep_ref, got_ref, label_ref, total_ref, there_ref, here_ref, again_ref, label_out):
     size = total_ref.shape[0]
     digit = lax.rem(lax.axis_index("feat") // stride, 2)
 
@@ -236,31 +216,47 @@
         span = pl.ds(pl.multiple_of(at * size, size), size)
         return keep_ref[span, :] + got_ref[span, :]
 
-    total_ref[...] = piece(digit)
     encode(piece(1 - digit), there_ref)
     again_ref[...] = there_ref[...]
-    encode(piece(digit), here_ref)
+    total = piece(digit)
+    total_ref[...] = total
+    encode(total, here_ref)
+    label_out[...] = label_ref[...]
 
 
 def square_kernel(total_ref, both_ref, x_ref, z_ref, sum_ref, out_ref):
-    total = (total_ref[...] + decode(x_ref)) + (decode(z_ref) + decode(both_ref))
+    size = total_ref.shape[0]
+    total = (total_ref[...] + decode(x_ref, size)) + (decode(z_ref, size) + decode(both_ref, size))
     sum_ref[...] = total
     encode(total, out_ref)
 
 
 def middle_kernel(total_ref, word_ref, sum_ref, out_ref):
-    total = total_ref[...] + decode(word_ref)
+    total = total_ref[...] + decode(word_ref, total_ref.shape[0])
     sum_ref[...] = total
     encode(total, out_ref)
 
 
-def last_kernel(scale, total_ref, word_ref, label_ref, *row_refs):
-    total = total_ref[...] + decode(word_ref)
-    kept = total.shape[1]
-    row = (total * scale).astype(jnp.bfloat16)
+def last_kernel(scale, blocks, total_ref, word_ref, *refs):
+    label_refs, (label_out, *row_refs) = refs[:-5], refs[-5:]
+    size = total_ref.shape[0]
+    row = ((total_ref[...] + decode(word_ref, size)) * scale).astype(jnp.bfloat16)
     for row_ref in row_refs:
-        row_ref[:, :kept] = row
-        row_ref[:, kept:] = label_ref[...]
+        row_ref[...] = row
+    core = lax.rem(lax.axis_index("feat"), 2)
+    digit = lax.rem(lax.axis_index("feat") // 2, 2)
+    groups = LANES // size
+    lane = lax.broadcasted_iota(jnp.int32, (8, LANES), 1)
+    for place in range(0, 2 * len(blocks), groups):
+        out = jnp.zeros((8, LANES), jnp.int32)
+        for at in range(groups):
+            half, (tok, x) = (place + at) // len(blocks), blocks[(place + at) % len(blocks)]
+            source = (core ^ half) * 2 * size + (digit ^ x) * size
+            moved = pltpu.roll(
+                jnp.broadcast_to(label_refs[tok][...], out.shape), lax.rem(at * size - source + LANES, LANES), 1
+            )
+            out = jnp.where(lane // size == at, moved, out)
+        label_out[:, place * size:(place + groups) * size] = out[:1]
 
 
 def local_call(kernel, name, *operands, out_shape):
@@ -291,50 +287,57 @@
     shard = kept // feat_count
     size = rows // 4
     total_type = jax.ShapeDtypeStruct((size, kept), jnp.float32)
-    word_type = jax.ShapeDtypeStruct((size // 2, kept + LANES), jnp.int32)
-    row_type = jax.ShapeDtypeStruct((size, kept + LANES), jnp.bfloat16)
-
-    first = (feat_index & 1) * (rows // 2) + (feat_index >> 1 & 1) * size
-    own_labels = lax.dynamic_slice_in_dim(labels, first, size, 0).astype(jnp.bfloat16)
-    own_labels = jnp.broadcast_to(own_labels, (size, LANES))
+    word_type = jax.ShapeDtypeStruct((kept // LANES * (size // 2) + 8, LANES), jnp.int32)
+    row_type = jax.ShapeDtypeStruct((size, kept), jnp.bfloat16)
+    label_type = jax.ShapeDtypeStruct((1, rows), jnp.int32)
 
     keep, got = partial_halves(features, signs, columns, feat_count)
-    total, there, here, again = local_call(
-        functools.partial(first_kernel, 2), "first_split", keep, got, out_shape=[total_type, word_type, word_type, word_type]
+    total, there, here, again, label = local_call(
+        functools.partial(first_kernel, 2),
+        "first_split",
+        keep,
+        got,
+        labels.reshape(1, rows),
+        out_shape=[total_type, word_type, word_type, word_type, label_type],
     )
+    both = swap(again, feat=6)
+    x_word = swap(there, feat=2)
+    z_word = swap(here, feat=4)
+    all_labels = [label] + [swap(label, tok=tok) for tok in range(1, tok_count)]
     total, word = local_call(
-        square_kernel,
-        "add_square",
-        total,
-        swap(again, feat=6),
-        swap(there, feat=2),
-        swap(here, feat=4),
-        out_shape=[total_type, word_type],
+        square_kernel, "add_square", total, both, x_word, z_word, out_shape=[total_type, word_type]
     )
     word = swap(word, feat=8)
     stride = 16
     while stride < feat_count:
-        total, word = local_call(
-            middle_kernel, "add_encode", total, word, out_shape=[total_type, word_type]
-        )
+        total, word = local_call(middle_kernel, "add_encode", total, word, out_shape=[total_type, word_type])
         word = swap(word, feat=stride)
         stride *= 2
-    scale = 1.0 / math.sqrt(width * feat_count)
-    copies = local_call(
-        functools.partial(last_kernel, scale), "sketch_rows", total, word, own_labels, out_shape=[row_type] * 3
-    )
-
+
+    blocks = [(0, 0)]
     stride = 2
     while stride < tok_count:
-        copies = [jnp.concatenate([copies[0], swap(copies[0], tok=stride)], axis=0)] * 3
+        blocks = blocks + [(tok ^ stride, x) for tok, x in blocks]
         stride *= 2
-    received = [swap(copies[0], tok=1, feat=2)] if tok_count > 1 else []
-    received += [swap(copies[1], feat=2)]
-    received += [swap(copies[2], tok=1)] if tok_count > 1 else []
-    ours = jnp.concatenate([copies[0]] + received, axis=0)
-    theirs = swap(ours, feat=1)
+    blocks = [(tok ^ flip, x) for flip, x in ((0, 0), (1, 1), (0, 1), (1, 0)) for tok, _ in blocks]
+    scale = 1.0 / math.sqrt(width * feat_count)
+    label_row, *copies = local_call(
+        functools.partial(last_kernel, scale, blocks),
+        "sketch_rows",
+        total,
+        word,
+        *all_labels,
+        out_shape=[jax.ShapeDtypeStruct((1, 2 * len(blocks) * size), jnp.int32)] + [row_type] * 4,
+    )
+    stride = 2
+    while stride < tok_count:
+        copies = [jnp.concatenate([copies[0], swap(copies[0], tok=stride)], axis=0)] * 4
+        stride *= 2
+    received = [swap(copies[0], tok=1, feat=2), swap(copies[1], feat=2), swap(copies[2], tok=1)]
+    ours = copies[3:] + received
+    theirs = [swap(block, feat=1) for block in ours]
     concepts = C // tok_count
-    gram = gram_blocks(ours, theirs, concepts, shard, kept, C / (rows * tok_count))
+    gram = gram_blocks(ours + theirs, label_row, concepts, shard, C / (rows * tok_count))
     return gram.reshape(concepts, shard, kept)
 
 

time: 32.3 us -> 31.4 us (0.972)
  waiting for transfers between devices: 13.2 us -> 11.3 us
  starting transfers between devices: 11.2 us -> 12.7 us
    ppermute x9 -> x13, waiting for transfers between devices: 13.2 us -> 11.3 us  [swap(): return lax.ppermute(array, ('feat', 'tok'), pairs)]
    ppermute x9 -> x13, starting transfers between devices: 11.2 us -> 12.7 us  [swap(): return lax.ppermute(array, ('feat', 'tok'), pairs)]
  transfers between devices with their start and end apart: 9 -> 13, of which waited for: 8 -> 10; matrix products, arithmetic and copies ran while one was open for 0% -> 0% of each run, Pallas kernels for 5% -> 4%
where the time goes in v10:
time: 31.4 us; the launch traced here: 31.3 us
  starting transfers between devices  12.7 us (40%)
  waiting for transfers between devices  11.3 us (36%)
  Pallas kernels  7.26 us (23%)
    ppermute x13, starting transfers between devices, swap(): return lax.ppermute(array, ('feat', 'tok'), pairs)  12.7 us
    ppermute x13, waiting for transfers between devices, swap(): return lax.ppermute(array, ('feat', 'tok'), pairs)  11.3 us
    pallas_call x1, Pallas kernels, partial_halves(): pl.pallas_call(functools.partial(send_kernel, total_bits, parts), in_spec...  2.86 us
    pallas_call x1, Pallas kernels, gram_blocks(): pl.pallas_call(functools.partial(gram_kernel, shard, group, factor), in_s...  2.49 us
    pallas_call x1, Pallas kernels, partial_halves(): pl.pallas_call(functools.partial(keep_kernel, parts), out_shape=total_typ...  1.3 us
  transfers between devices with their start and end apart: 13, of which 10 were waited for; matrix products, arithmetic and copies ran while one was open for 0% of the time, Pallas kernels for 4%

profile of v10, /device:TPU:0, one launch (start us, length us, event | category | flops | bytes accessed | tf_op | source)
XLA Modules:
  0.0 31.3 jit_solution(6405961034872452329)
XLA Ops:
  0.0 2.9 %partial_sent.1 = (f32[64,1024]{1,0:T(8,128)S(1)}, bf16[64,8192]{1,0:T(8,128)(2,1)S(1)}, s32[1,8192]{1,0:T(1,128)S(1)}, bf16[256,1024]{1,0:T(8,128)(2,1)S(1)}, f32[32,1024]{1,0:T(8,128)S(1)}) custom-call(bf16[128,8192]{1,0:T(8,128)(2,1)} %x_hbm.1, s32[1,8192]{1,0:T(1,128)} %bitcast.5, s32[1,1024]{1,0:T(1,128)} %bitcast.6), custom_call_target="tpu_custom_call" | custom-call | flops 1073741824 | bytes 2359296 | tf_op jit(solution)/shard_map/partial_sent/pallas_call | solution.py:99
  2.9 0.5 %collective-permute-start = (f32[64,1024]{1,0:T(8,128)S(1)}, f32[64,1024]{1,0:T(8,128)S(1)}, u32[]{:S(2)}, u32[]{:S(2)}) collective-permute-start(f32[64,1024]{1,0:T(8,128)S(1)} %get-tuple-element.26), channel_id=1, source_target_pairs={{0,2},{1,3},{2,0},{3,1},{4,6},{5,7},{6,4},{7,5},{8,10},{9,11},{10,... | collective-permute-start | bytes 786440 | tf_op jit(solution)/shard_map/ppermute | solution.py:278
  3.4 1.3 %partial_kept.1.keep_ref = f32[64,1024]{1,0:T(8,128)S(1)} custom-call(bf16[64,8192]{1,0:T(8,128)(2,1)S(1)} %get-tuple-element.22.x_keep, s32[1,8192]{1,0:T(1,128)S(1)} %get-tuple-element.23.signs, bf16[256,1024]{1,0:T(8,128)(2,1)S(1)} %get-tuple-element.24.low, f32[32,1024]{1,0:T(8,128)S(1)} %get-tuple-element.25.high), custom_call_target="tpu_custom_call" | custom-call | flops 1073741824 | bytes 2359296 | tf_op jit(solution)/shard_map/partial_kept/pallas_call | solution.py:123
  4.7 0.2 first_split.1
  4.9 3.8 %collective-permute-start.1 = (s32[136,128]{1,0:T(8,128)S(1)}, s32[136,128]{1,0:T(8,128)S(1)}, u32[]{:S(2)}, u32[]{:S(2)}) collective-permute-start(s32[136,128]{1,0:T(8,128)S(1)} %get-tuple-element.28), channel_id=1, source_target_pairs={{0,12},{1,13},{2,14},{3,15},{4,8},{5,9},{6,10},{7,11},{8,4},{9,5},... | collective-permute-start | bytes 208904 | tf_op jit(solution)/shard_map/ppermute | solution.py:278
  8.6 0.5 %collective-permute-start.2 = (s32[136,128]{1,0:T(8,128)S(1)}, s32[136,128]{1,0:T(8,128)S(1)}, u32[]{:S(2)}, u32[]{:S(2)}) collective-permute-start(s32[136,128]{1,0:T(8,128)S(1)} %get-tuple-element.29), channel_id=1, source_target_pairs={{0,4},{1,5},{2,6},{3,7},{4,0},{5,1},{6,2},{7,3},{8,12},{9,13},{10,... | collective-permute-start | bytes 208904 | tf_op jit(solution)/shard_map/ppermute | solution.py:278
  9.2 0.1 collective-permute-start.3
  9.3 2.0 %collective-permute-done.1.both_ref = s32[136,128]{1,0:T(8,128)S(1)} collective-permute-done((s32[136,128]{1,0:T(8,128)S(1)}, s32[136,128]{1,0:T(8,128)S(1)}, u32[]{:S(2)}, u32[]{:S(2)}) %collective-permute-start.1) | collective-permute-done | bytes 69664 | tf_op jit(solution)/shard_map/ppermute | solution.py:278
  11.3 1.7 %collective-permute-done.2.x_ref = s32[136,128]{1,0:T(8,128)S(1)} collective-permute-done((s32[136,128]{1,0:T(8,128)S(1)}, s32[136,128]{1,0:T(8,128)S(1)}, u32[]{:S(2)}, u32[]{:S(2)}) %collective-permute-start.2) | collective-permute-done | bytes 69664 | tf_op jit(solution)/shard_map/ppermute | solution.py:278
  13.0 0.5 %collective-permute-done.3.z_ref = s32[136,128]{1,0:T(8,128)S(1)} collective-permute-done((s32[136,128]{1,0:T(8,128)S(1)}, s32[136,128]{1,0:T(8,128)S(1)}, u32[]{:S(2)}, u32[]{:S(2)}) %collective-permute-start.3) | collective-permute-done | bytes 69664 | tf_op jit(solution)/shard_map/ppermute | solution.py:278
  13.5 0.3 add_square.1
  13.8 2.7 %collective-permute-start.4 = (s32[136,128]{1,0:T(8,128)S(1)}, s32[136,128]{1,0:T(8,128)S(1)}, u32[]{:S(2)}, u32[]{:S(2)}) collective-permute-start(s32[136,128]{1,0:T(8,128)S(1)} %get-tuple-element.32), channel_id=1, source_target_pairs={{0,16},{1,17},{2,18},{3,19},{4,20},{5,21},{6,22},{7,23},{8,24},{9,... | collective-permute-start | bytes 208904 | tf_op jit(solution)/shard_map/ppermute | solution.py:278
  16.4 1.5 %collective-permute-start.5 = (s32[1,128]{1,0:T(1,128)S(1)}, s32[1,128]{1,0:T(1,128)S(1)}, u32[]{:S(2)}, u32[]{:S(2)}) collective-permute-start(s32[1,128]{1,0:T(1,128)S(1)} %get-tuple-element.33.refs_0_), channel_id=1, source_target_pairs={{0,1},{1,0},{2,3},{3,2},{4,5},{5,4},{6,7},{7,6},{8,9},{9,8},{10,11... | collective-permute-start | bytes 1544 | tf_op jit(solution)/shard_map/ppermute | solution.py:278
  17.9 2.0 %collective-permute-done.5.refs_1_ = s32[1,128]{1,0:T(1,128)S(1)} collective-permute-done((s32[1,128]{1,0:T(1,128)S(1)}, s32[1,128]{1,0:T(1,128)S(1)}, u32[]{:S(2)}, u32[]{:S(2)}) %collective-permute-start.5) | collective-permute-done | bytes 544 | tf_op jit(solution)/shard_map/ppermute | solution.py:278
  20.0 0.2 sketch_rows.1
  20.2 2.4 %collective-permute-start.6 = (bf16[32,1024]{1,0:T(8,128)(2,1)S(1)}, bf16[32,1024]{1,0:T(8,128)(2,1)S(1)}, u32[]{:S(2)}, u32[]{:S(2)}) collective-permute-start(bf16[32,1024]{1,0:T(8,128)(2,1)S(1)} %get-tuple-element.36), channel_id=1, source_target_pairs={{0,5},{1,4},{2,7},{3,6},{4,1},{5,0},{6,3},{7,2},{8,13},{9,12},{10,... | collective-permute-start | bytes 196616 | tf_op jit(solution)/shard_map/ppermute | solution.py:278
  22.6 0.6 %collective-permute-start.7 = (bf16[32,1024]{1,0:T(8,128)(2,1)S(1)}, bf16[32,1024]{1,0:T(8,128)(2,1)S(1)}, u32[]{:S(2)}, u32[]{:S(2)}) collective-permute-start(bf16[32,1024]{1,0:T(8,128)(2,1)S(1)} %get-tuple-element.37), channel_id=1, source_target_pairs={{0,4},{1,5},{2,6},{3,7},{4,0},{5,1},{6,2},{7,3},{8,12},{9,13},{10,... | collective-permute-start | bytes 196616 | tf_op jit(solution)/shard_map/ppermute | solution.py:278
  23.3 0.5 %collective-permute-start.8 = (bf16[32,1024]{1,0:T(8,128)(2,1)S(1)}, bf16[32,1024]{1,0:T(8,128)(2,1)S(1)}, u32[]{:S(2)}, u32[]{:S(2)}) collective-permute-start(bf16[32,1024]{1,0:T(8,128)(2,1)S(1)} %get-tuple-element.38), channel_id=1, source_target_pairs={{0,1},{1,0},{2,3},{3,2},{4,5},{5,4},{6,7},{7,6},{8,9},{9,8},{10,11... | collective-permute-start | bytes 196616 | tf_op jit(solution)/shard_map/ppermute | solution.py:278
  23.8 1.7 %collective-permute-done.6.refs_1_ = bf16[32,1024]{1,0:T(8,128)(2,1)S(1)} collective-permute-done((bf16[32,1024]{1,0:T(8,128)(2,1)S(1)}, bf16[32,1024]{1,0:T(8,128)(2,1)S(1)}, u32[]{:S(2)}, u32[]{:S(2)}) %collective-permute-start.6) | collective-permute-done | bytes 65568 | tf_op jit(solution)/shard_map/ppermute | solution.py:278
  25.4 1.5 %collective-permute-done.7.refs_2_ = bf16[32,1024]{1,0:T(8,128)(2,1)S(1)} collective-permute-done((bf16[32,1024]{1,0:T(8,128)(2,1)S(1)}, bf16[32,1024]{1,0:T(8,128)(2,1)S(1)}, u32[]{:S(2)}, u32[]{:S(2)}) %collective-permute-start.7) | collective-permute-done | bytes 65568 | tf_op jit(solution)/shard_map/ppermute | solution.py:278
  26.9 0.6 %collective-permute-done.8.refs_3_ = bf16[32,1024]{1,0:T(8,128)(2,1)S(1)} collective-permute-done((bf16[32,1024]{1,0:T(8,128)(2,1)S(1)}, bf16[32,1024]{1,0:T(8,128)(2,1)S(1)}, u32[]{:S(2)}, u32[]{:S(2)}) %collective-permute-start.8) | collective-permute-done | bytes 65568 | tf_op jit(solution)/shard_map/ppermute | solution.py:278
  27.5 0.6 %collective-permute-done.11.refs_6_ = bf16[32,1024]{1,0:T(8,128)(2,1)S(1)} collective-permute-done((bf16[32,1024]{1,0:T(8,128)(2,1)S(1)}, bf16[32,1024]{1,0:T(8,128)(2,1)S(1)}, u32[]{:S(2)}, u32[]{:S(2)}) %collective-permute-start.11) | collective-permute-done | bytes 65568 | tf_op jit(solution)/shard_map/ppermute | solution.py:278
  28.2 0.6 %collective-permute-done.12.refs_7_ = bf16[32,1024]{1,0:T(8,128)(2,1)S(1)} collective-permute-done((bf16[32,1024]{1,0:T(8,128)(2,1)S(1)}, bf16[32,1024]{1,0:T(8,128)(2,1)S(1)}, u32[]{:S(2)}, u32[]{:S(2)}) %collective-permute-start.12) | collective-permute-done | bytes 65568 | tf_op jit(solution)/shard_map/ppermute | solution.py:278
  28.8 2.5 %gram.1 = f32[1024,1024]{1,0:T(8,128)} custom-call(s32[1,256]{1,0:T(1,128)S(1)} %get-tuple-element.34.label_ref, bf16[32,1024]{1,0:T(8,128)(2,1)S(1)} %get-tuple-element.35.refs_0_, bf16[32,1024]{1,0:T(8,128)(2,1)S(1)} %collective-permute-done.6.refs_1_, bf16[32,1024]{1,0:T(8,128)(2,1)S(1)} %collective-permute-done.7.refs_2_, ...), custom_call_target="tpu_custom_call" | custom-call | flops 536870912 | bytes 4194304 | tf_op jit(solution)/shard_map/gram/pallas_call | solution.py:165
  (10 shorter events, 0.1 us)
Async XLA Ops:
  0.0 4.7 %copy-start = (s32[128,1]{0,1:T(1,128)S(1)}, s32[128,1]{0,1:T(1,128)}, u32[]{:S(2)}) copy-start(s32[128,1]{0,1:T(1,128)} %param.7) | copy-start | bytes 1540
  2.9 1.8 %collective-permute-start = (f32[64,1024]{1,0:T(8,128)S(1)}, f32[64,1024]{1,0:T(8,128)S(1)}, u32[]{:S(2)}, u32[]{:S(2)}) collective-permute-start(f32[64,1024]{1,0:T(8,128)S(1)} %get-tuple-element.26), channel_id=1, source_target_pairs={{0,2},{1,3},{2,0},{3,1},{4,6},{5,7},{6,4},{7,5},{8,10},{9,11},{10,... | collective-permute-start | bytes 786440 | tf_op jit(solution)/shard_map/ppermute | solution.py:278
  4.9 6.4 %collective-permute-start.1 = (s32[136,128]{1,0:T(8,128)S(1)}, s32[136,128]{1,0:T(8,128)S(1)}, u32[]{:S(2)}, u32[]{:S(2)}) collective-permute-start(s32[136,128]{1,0:T(8,128)S(1)} %get-tuple-element.28), channel_id=1, source_target_pairs={{0,12},{1,13},{2,14},{3,15},{4,8},{5,9},{6,10},{7,11},{8,4},{9,5},... | collective-permute-start | bytes 208904 | tf_op jit(solution)/shard_map/ppermute | solution.py:278
  8.6 4.3 %collective-permute-start.2 = (s32[136,128]{1,0:T(8,128)S(1)}, s32[136,128]{1,0:T(8,128)S(1)}, u32[]{:S(2)}, u32[]{:S(2)}) collective-permute-start(s32[136,128]{1,0:T(8,128)S(1)} %get-tuple-element.29), channel_id=1, source_target_pairs={{0,4},{1,5},{2,6},{3,7},{4,0},{5,1},{6,2},{7,3},{8,12},{9,13},{10,... | collective-permute-start | bytes 208904 | tf_op jit(solution)/shard_map/ppermute | solution.py:278
  9.2 4.3 %collective-permute-start.3 = (s32[136,128]{1,0:T(8,128)S(1)}, s32[136,128]{1,0:T(8,128)S(1)}, u32[]{:S(2)}, u32[]{:S(2)}) collective-permute-start(s32[136,128]{1,0:T(8,128)S(1)} %get-tuple-element.30), channel_id=1, source_target_pairs={{0,8},{1,9},{2,10},{3,11},{4,12},{5,13},{6,14},{7,15},{8,0},{9,1},... | collective-permute-start | bytes 208904 | tf_op jit(solution)/shard_map/ppermute | solution.py:278
  13.8 6.3 %collective-permute-start.4 = (s32[136,128]{1,0:T(8,128)S(1)}, s32[136,128]{1,0:T(8,128)S(1)}, u32[]{:S(2)}, u32[]{:S(2)}) collective-permute-start(s32[136,128]{1,0:T(8,128)S(1)} %get-tuple-element.32), channel_id=1, source_target_pairs={{0,16},{1,17},{2,18},{3,19},{4,20},{5,21},{6,22},{7,23},{8,24},{9,... | collective-permute-start | bytes 208904 | tf_op jit(solution)/shard_map/ppermute | solution.py:278
  16.4 3.5 %collective-permute-start.5 = (s32[1,128]{1,0:T(1,128)S(1)}, s32[1,128]{1,0:T(1,128)S(1)}, u32[]{:S(2)}, u32[]{:S(2)}) collective-permute-start(s32[1,128]{1,0:T(1,128)S(1)} %get-tuple-element.33.refs_0_), channel_id=1, source_target_pairs={{0,1},{1,0},{2,3},{3,2},{4,5},{5,4},{6,7},{7,6},{8,9},{9,8},{10,11... | collective-permute-start | bytes 1544 | tf_op jit(solution)/shard_map/ppermute | solution.py:278
  20.2 5.2 %collective-permute-start.6 = (bf16[32,1024]{1,0:T(8,128)(2,1)S(1)}, bf16[32,1024]{1,0:T(8,128)(2,1)S(1)}, u32[]{:S(2)}, u32[]{:S(2)}) collective-permute-start(bf16[32,1024]{1,0:T(8,128)(2,1)S(1)} %get-tuple-element.36), channel_id=1, source_target_pairs={{0,5},{1,4},{2,7},{3,6},{4,1},{5,0},{6,3},{7,2},{8,13},{9,12},{10,... | collective-permute-start | bytes 196616 | tf_op jit(solution)/shard_map/ppermute | solution.py:278
  22.6 4.3 %collective-permute-start.7 = (bf16[32,1024]{1,0:T(8,128)(2,1)S(1)}, bf16[32,1024]{1,0:T(8,128)(2,1)S(1)}, u32[]{:S(2)}, u32[]{:S(2)}) collective-permute-start(bf16[32,1024]{1,0:T(8,128)(2,1)S(1)} %get-tuple-element.37), channel_id=1, source_target_pairs={{0,4},{1,5},{2,6},{3,7},{4,0},{5,1},{6,2},{7,3},{8,12},{9,13},{10,... | collective-permute-start | bytes 196616 | tf_op jit(solution)/shard_map/ppermute | solution.py:278
  23.3 4.3 %collective-permute-start.8 = (bf16[32,1024]{1,0:T(8,128)(2,1)S(1)}, bf16[32,1024]{1,0:T(8,128)(2,1)S(1)}, u32[]{:S(2)}, u32[]{:S(2)}) collective-permute-start(bf16[32,1024]{1,0:T(8,128)(2,1)S(1)} %get-tuple-element.38), channel_id=1, source_target_pairs={{0,1},{1,0},{2,3},{3,2},{4,5},{5,4},{6,7},{7,6},{8,9},{9,8},{10,11... | collective-permute-start | bytes 196616 | tf_op jit(solution)/shard_map/ppermute | solution.py:278
  23.8 3.8 %collective-permute-start.9 = (bf16[32,1024]{1,0:T(8,128)(2,1)S(1)}, bf16[32,1024]{1,0:T(8,128)(2,1)S(1)}, u32[]{:S(2)}, u32[]{:S(2)}) collective-permute-start(bf16[32,1024]{1,0:T(8,128)(2,1)S(1)} %get-tuple-element.35.refs_0_), channel_id=1, source_target_pairs={{0,2},{1,3},{2,0},{3,1},{4,6},{5,7},{6,4},{7,5},{8,10},{9,11},{10,... | collective-permute-start | bytes 196616 | tf_op jit(solution)/shard_map/ppermute | solution.py:278
  25.4 2.1 %collective-permute-start.10 = (bf16[32,1024]{1,0:T(8,128)(2,1)S(1)}, bf16[32,1024]{1,0:T(8,128)(2,1)S(1)}, u32[]{:S(2)}, u32[]{:S(2)}) collective-permute-start(bf16[32,1024]{1,0:T(8,128)(2,1)S(1)} %collective-permute-done.6.refs_1_), channel_id=1, source_target_pairs={{0,2},{1,3},{2,0},{3,1},{4,6},{5,7},{6,4},{7,5},{8,10},{9,11},{10,... | collective-permute-start | bytes 196616 | tf_op jit(solution)/shard_map/ppermute | solution.py:278
  26.9 1.3 %collective-permute-start.11 = (bf16[32,1024]{1,0:T(8,128)(2,1)S(1)}, bf16[32,1024]{1,0:T(8,128)(2,1)S(1)}, u32[]{:S(2)}, u32[]{:S(2)}) collective-permute-start(bf16[32,1024]{1,0:T(8,128)(2,1)S(1)} %collective-permute-done.7.refs_2_), channel_id=1, source_target_pairs={{0,2},{1,3},{2,0},{3,1},{4,6},{5,7},{6,4},{7,5},{8,10},{9,11},{10,... | collective-permute-start | bytes 196616 | tf_op jit(solution)/shard_map/ppermute | solution.py:278
  27.5 1.3 %collective-permute-start.12 = (bf16[32,1024]{1,0:T(8,128)(2,1)S(1)}, bf16[32,1024]{1,0:T(8,128)(2,1)S(1)}, u32[]{:S(2)}, u32[]{:S(2)}) collective-permute-start(bf16[32,1024]{1,0:T(8,128)(2,1)S(1)} %collective-permute-done.8.refs_3_), channel_id=1, source_target_pairs={{0,2},{1,3},{2,0},{3,1},{4,6},{5,7},{6,4},{7,5},{8,10},{9,11},{10,... | collective-permute-start | bytes 196616 | tf_op jit(solution)/shard_map/ppermute | solution.py:278

commit v11 on v10

--- a/solution.py
+++ b/solution.py
@@ -11,6 +11,7 @@
 C = 32
 LOW = 256
 LANES = 128
+SPLIT = 4
 VMEM_LIMIT = 48 * 1024 * 1024
 
 
@@ -62,7 +63,6 @@
         copies[-1].start()
     rows = pl.ds(pl.multiple_of(mine * half, half), half)
     keep_copy = pltpu.make_async_copy(x_hbm.at[rows, :], x_keep, sems.at[parts + 2])
-    keep_copy.start()
     col_copy.wait()
     col = col_buf[...]
     index = lax.broadcasted_iota(jnp.int32, (16, kept), 0)
@@ -75,6 +75,8 @@
     sign_copy.wait()
     for part in range(parts):
         copies[part].wait()
+        if part == 0:
+            keep_copy.start()
         add_products(x_buf, signs, low, high, send_ref, part, wide)
     keep_copy.wait()
 
@@ -148,10 +150,16 @@
     for step in range(steps):
         chosen = jnp.where(label == base + step * group, own, 0.0).astype(jnp.bfloat16)
         blocks[step] = jnp.dot(chosen, rows[...], preferred_element_type=jnp.float32)
-        copies.append(
-            pltpu.make_async_copy(blocks.at[step], out_hbm.at[pl.ds(step * wide, wide), :], sems.at[step])
-        )
-        copies[-1].start()
+        size = wide // SPLIT
+        for at in range(SPLIT):
+            copies.append(
+                pltpu.make_async_copy(
+                    blocks.at[step, pl.ds(at * size, size), :],
+                    out_hbm.at[pl.ds(step * wide + at * size, size), :],
+                    sems.at[step * SPLIT + at],
+                )
+            )
+            copies[-1].start()
     for copy in copies:
         copy.wait()
 
@@ -170,7 +178,7 @@
         scratch_shapes=[
             pltpu.VMEM((tokens, kept), jnp.bfloat16),
             pltpu.VMEM((steps, wide, kept), jnp.float32),
-            pltpu.SemaphoreType.DMA((steps,)),
+            pltpu.SemaphoreType.DMA((steps * SPLIT,)),
         ],
         compiler_params=pltpu.CompilerParams(vmem_limit_bytes=VMEM_LIMIT),
         cost_estimate=pl.CostEstimate(
@@ -208,7 +216,7 @@
     return code * scale
 
 
-def first_kernel(stride, keep_ref, got_ref, label_ref, total_ref, there_ref, here_ref, again_ref, label_out):
+def first_kernel(stride, keep_ref, got_ref, label_ref, total_ref, far_ref, even_ref, odd_ref, label_out):
     size = total_ref.shape[0]
     digit = lax.rem(lax.axis_index("feat") // stride, 2)
 
@@ -216,17 +224,22 @@
         span = pl.ds(pl.multiple_of(at * size, size), size)
         return keep_ref[span, :] + got_ref[span, :]
 
-    encode(piece(1 - digit), there_ref)
-    again_ref[...] = there_ref[...]
+    encode(piece(1 - digit), far_ref)
     total = piece(digit)
     total_ref[...] = total
-    encode(total, here_ref)
+    core = lax.rem(lax.axis_index("feat"), 2)
+    for this, there_ref, here_ref in ((0, even_ref, odd_ref), (1, odd_ref, even_ref)):
+        @pl.when(core == this)
+        def _():
+            there_ref[...] = far_ref[...]
+            encode(total, here_ref)
+
     label_out[...] = label_ref[...]
 
 
-def square_kernel(total_ref, both_ref, x_ref, z_ref, sum_ref, out_ref):
+def square_kernel(total_ref, far_ref, even_ref, odd_ref, sum_ref, out_ref):
     size = total_ref.shape[0]
-    total = (total_ref[...] + decode(x_ref, size)) + (decode(z_ref, size) + decode(both_ref, size))
+    total = (total_ref[...] + decode(far_ref, size)) + (decode(even_ref, size) + decode(odd_ref, size))
     sum_ref[...] = total
     encode(total, out_ref)
 
@@ -250,12 +263,12 @@
     for place in range(0, 2 * len(blocks), groups):
         out = jnp.zeros((8, LANES), jnp.int32)
         for at in range(groups):
-            half, (tok, x) = (place + at) // len(blocks), blocks[(place + at) % len(blocks)]
-            source = (core ^ half) * 2 * size + (digit ^ x) * size
-            moved = pltpu.roll(
-                jnp.broadcast_to(label_refs[tok][...], out.shape), lax.rem(at * size - source + LANES, LANES), 1
-            )
-            out = jnp.where(lane // size == at, moved, out)
+            half = core ^ ((place + at) // len(blocks))
+            for this, (tok, x) in enumerate(blocks[(place + at) % len(blocks)]):
+                source = half * 2 * size + (digit ^ x) * size
+                row = jnp.broadcast_to(label_refs[tok][...], out.shape)
+                moved = pltpu.roll(row, lax.rem(at * size - source + LANES, LANES), 1)
+                out = jnp.where((lane // size == at) & (half == this), moved, out)
         label_out[:, place * size:(place + groups) * size] = out[:1]
 
 
@@ -268,10 +281,11 @@
     )(*operands)
 
 
-def swap(array, tok=0, feat=0):
+def swap(array, tok=0, feat=0, odd=None):
     tok_count, feat_count = lax.axis_size("tok"), lax.axis_size("feat")
+    bits = ((tok, feat), odd or (tok, feat))
     pairs = [
-        (f * tok_count + t, (f ^ feat) * tok_count + (t ^ tok))
+        (f * tok_count + t, (f ^ bits[f & 1][1]) * tok_count + (t ^ bits[f & 1][0]))
         for f in range(feat_count)
         for t in range(tok_count)
     ]
@@ -292,7 +306,7 @@
     label_type = jax.ShapeDtypeStruct((1, rows), jnp.int32)
 
     keep, got = partial_halves(features, signs, columns, feat_count)
-    total, there, here, again, label = local_call(
+    total, far, even, odd, label = local_call(
         functools.partial(first_kernel, 2),
         "first_split",
         keep,
@@ -300,12 +314,12 @@
         labels.reshape(1, rows),
         out_shape=[total_type, word_type, word_type, word_type, label_type],
     )
-    both = swap(again, feat=6)
-    x_word = swap(there, feat=2)
-    z_word = swap(here, feat=4)
+    far = swap(far, feat=6)
+    even = swap(even, feat=2, odd=(0, 4))
+    odd = swap(odd, feat=4, odd=(0, 2))
     all_labels = [label] + [swap(label, tok=tok) for tok in range(1, tok_count)]
     total, word = local_call(
-        square_kernel, "add_square", total, both, x_word, z_word, out_shape=[total_type, word_type]
+        square_kernel, "add_square", total, far, even, odd, out_shape=[total_type, word_type]
     )
     word = swap(word, feat=8)
     stride = 16
@@ -319,7 +333,10 @@
     while stride < tok_count:
         blocks = blocks + [(tok ^ stride, x) for tok, x in blocks]
         stride *= 2
-    blocks = [(tok ^ flip, x) for flip, x in ((0, 0), (1, 1), (0, 1), (1, 0)) for tok, _ in blocks]
+    flips = (((0, 0), (1, 1), (0, 1), (1, 0)), ((0, 0), (1, 1), (1, 0), (0, 1)))
+    blocks = [
+        ((tok ^ even[0], even[1]), (tok ^ odd[0], odd[1])) for even, odd in zip(*flips) for tok, _ in blocks
+    ]
     scale = 1.0 / math.sqrt(width * feat_count)
     label_row, *copies = local_call(
         functools.partial(last_kernel, scale, blocks),
@@ -333,7 +350,11 @@
     while stride < tok_count:
         copies = [jnp.concatenate([copies[0], swap(copies[0], tok=stride)], axis=0)] * 4
         stride *= 2
-    received = [swap(copies[0], tok=1, feat=2), swap(copies[1], feat=2), swap(copies[2], tok=1)]
+    received = [
+        swap(copies[0], tok=1, feat=2),
+        swap(copies[1], feat=2, odd=(1, 0)),
+        swap(copies[2], tok=1, odd=(0, 2)),
+    ]
     ours = copies[3:] + received
     theirs = [swap(block, feat=1) for block in ours]
     concepts = C // tok_count

time: 31.4 us -> 31.7 us (level)
  no operation moved by 1% of the time
where the time goes in v11:
time: 31.7 us; the launch traced here: 31.6 us
  starting transfers between devices  12.7 us (40%)
  waiting for transfers between devices  11.4 us (36%)
  Pallas kernels  7.46 us (24%)
    ppermute x13, starting transfers between devices, swap(): return lax.ppermute(array, ('feat', 'tok'), pairs)  12.7 us
    ppermute x13, waiting for transfers between devices, swap(): return lax.ppermute(array, ('feat', 'tok'), pairs)  11.4 us
    pallas_call x1, Pallas kernels, partial_halves(): pl.pallas_call(functools.partial(send_kernel, total_bits, parts), in_spec...  2.86 us
    pallas_call x1, Pallas kernels, gram_blocks(): pl.pallas_call(functools.partial(gram_kernel, shard, group, factor), in_s...  2.59 us
    pallas_call x1, Pallas kernels, partial_halves(): pl.pallas_call(functools.partial(keep_kernel, parts), out_shape=total_typ...  1.3 us
    pallas_call x3, Pallas kernels, local_call(): pl.pallas_call(kernel, out_shape=out_shape, compiler_params=pltpu.Compile...  0.7 us
  transfers between devices with their start and end apart: 13, of which 10 were waited for; matrix products, arithmetic and copies ran while one was open for 0% of the time, Pallas kernels for 4%

profile of v11, /device:TPU:0, one launch (start us, length us, event | category | flops | bytes accessed | tf_op | source)
XLA Modules:
  0.0 31.6 jit_solution(12550530402022732002)
XLA Ops:
  0.0 2.9 %partial_sent.1 = (f32[64,1024]{1,0:T(8,128)S(1)}, bf16[64,8192]{1,0:T(8,128)(2,1)S(1)}, s32[1,8192]{1,0:T(1,128)S(1)}, bf16[256,1024]{1,0:T(8,128)(2,1)S(1)}, f32[32,1024]{1,0:T(8,128)S(1)}) custom-call(bf16[128,8192]{1,0:T(8,128)(2,1)} %x_hbm.1, s32[1,8192]{1,0:T(1,128)} %bitcast.5, s32[1,1024]{1,0:T(1,128)} %bitcast.6), custom_call_target="tpu_custom_call" | custom-call | flops 1073741824 | bytes 2359296 | tf_op jit(solution)/shard_map/partial_sent/pallas_call | solution.py:101
  2.9 0.5 %collective-permute-start = (f32[64,1024]{1,0:T(8,128)S(1)}, f32[64,1024]{1,0:T(8,128)S(1)}, u32[]{:S(2)}, u32[]{:S(2)}) collective-permute-start(f32[64,1024]{1,0:T(8,128)S(1)} %get-tuple-element.26), channel_id=1, source_target_pairs={{0,2},{1,3},{2,0},{3,1},{4,6},{5,7},{6,4},{7,5},{8,10},{9,11},{10,... | collective-permute-start | bytes 786440 | tf_op jit(solution)/shard_map/ppermute | solution.py:292
  3.4 1.3 %partial_kept.1.keep_ref = f32[64,1024]{1,0:T(8,128)S(1)} custom-call(bf16[64,8192]{1,0:T(8,128)(2,1)S(1)} %get-tuple-element.22.x_keep, s32[1,8192]{1,0:T(1,128)S(1)} %get-tuple-element.23.signs, bf16[256,1024]{1,0:T(8,128)(2,1)S(1)} %get-tuple-element.24.low, f32[32,1024]{1,0:T(8,128)S(1)} %get-tuple-element.25.high), custom_call_target="tpu_custom_call" | custom-call | flops 1073741824 | bytes 2359296 | tf_op jit(solution)/shard_map/partial_kept/pallas_call | solution.py:125
  4.7 0.3 first_split.1
  5.0 3.8 %collective-permute-start.1 = (s32[136,128]{1,0:T(8,128)S(1)}, s32[136,128]{1,0:T(8,128)S(1)}, u32[]{:S(2)}, u32[]{:S(2)}) collective-permute-start(s32[136,128]{1,0:T(8,128)S(1)} %get-tuple-element.28), channel_id=1, source_target_pairs={{0,12},{1,13},{2,14},{3,15},{4,8},{5,9},{6,10},{7,11},{8,4},{9,5},... | collective-permute-start | bytes 208904 | tf_op jit(solution)/shard_map/ppermute | solution.py:292
  8.8 0.5 %collective-permute-start.2 = (s32[136,128]{1,0:T(8,128)S(1)}, s32[136,128]{1,0:T(8,128)S(1)}, u32[]{:S(2)}, u32[]{:S(2)}) collective-permute-start(s32[136,128]{1,0:T(8,128)S(1)} %get-tuple-element.29), channel_id=1, source_target_pairs={{0,4},{1,5},{2,10},{3,11},{4,0},{5,1},{6,14},{7,15},{8,12},{9,13},... | collective-permute-start | bytes 208904 | tf_op jit(solution)/shard_map/ppermute | solution.py:292
  9.4 2.1 %collective-permute-done.1.far_ref = s32[136,128]{1,0:T(8,128)S(1)} collective-permute-done((s32[136,128]{1,0:T(8,128)S(1)}, s32[136,128]{1,0:T(8,128)S(1)}, u32[]{:S(2)}, u32[]{:S(2)}) %collective-permute-start.1) | collective-permute-done | bytes 69664 | tf_op jit(solution)/shard_map/ppermute | solution.py:292
  11.5 1.6 %collective-permute-done.2.even_ref = s32[136,128]{1,0:T(8,128)S(1)} collective-permute-done((s32[136,128]{1,0:T(8,128)S(1)}, s32[136,128]{1,0:T(8,128)S(1)}, u32[]{:S(2)}, u32[]{:S(2)}) %collective-permute-start.2) | collective-permute-done | bytes 69664 | tf_op jit(solution)/shard_map/ppermute | solution.py:292
  13.1 0.5 %collective-permute-done.3.odd_ref = s32[136,128]{1,0:T(8,128)S(1)} collective-permute-done((s32[136,128]{1,0:T(8,128)S(1)}, s32[136,128]{1,0:T(8,128)S(1)}, u32[]{:S(2)}, u32[]{:S(2)}) %collective-permute-start.3) | collective-permute-done | bytes 69664 | tf_op jit(solution)/shard_map/ppermute | solution.py:292
  13.6 0.3 add_square.1
  13.9 2.7 %collective-permute-start.4 = (s32[136,128]{1,0:T(8,128)S(1)}, s32[136,128]{1,0:T(8,128)S(1)}, u32[]{:S(2)}, u32[]{:S(2)}) collective-permute-start(s32[136,128]{1,0:T(8,128)S(1)} %get-tuple-element.32), channel_id=1, source_target_pairs={{0,16},{1,17},{2,18},{3,19},{4,20},{5,21},{6,22},{7,23},{8,24},{9,... | collective-permute-start | bytes 208904 | tf_op jit(solution)/shard_map/ppermute | solution.py:292
  16.5 1.5 %collective-permute-start.5 = (s32[1,128]{1,0:T(1,128)S(1)}, s32[1,128]{1,0:T(1,128)S(1)}, u32[]{:S(2)}, u32[]{:S(2)}) collective-permute-start(s32[1,128]{1,0:T(1,128)S(1)} %get-tuple-element.33.refs_0_), channel_id=1, source_target_pairs={{0,1},{1,0},{2,3},{3,2},{4,5},{5,4},{6,7},{7,6},{8,9},{9,8},{10,11... | collective-permute-start | bytes 1544 | tf_op jit(solution)/shard_map/ppermute | solution.py:292
  18.0 2.0 %collective-permute-done.5.refs_1_ = s32[1,128]{1,0:T(1,128)S(1)} collective-permute-done((s32[1,128]{1,0:T(1,128)S(1)}, s32[1,128]{1,0:T(1,128)S(1)}, u32[]{:S(2)}, u32[]{:S(2)}) %collective-permute-start.5) | collective-permute-done | bytes 544 | tf_op jit(solution)/shard_map/ppermute | solution.py:292
  20.1 0.2 collective-permute-done.4.word_ref
  20.3 0.2 sketch_rows.1
  20.4 2.5 %collective-permute-start.6 = (bf16[32,1024]{1,0:T(8,128)(2,1)S(1)}, bf16[32,1024]{1,0:T(8,128)(2,1)S(1)}, u32[]{:S(2)}, u32[]{:S(2)}) collective-permute-start(bf16[32,1024]{1,0:T(8,128)(2,1)S(1)} %get-tuple-element.36), channel_id=1, source_target_pairs={{0,5},{1,4},{2,7},{3,6},{4,1},{5,0},{6,3},{7,2},{8,13},{9,12},{10,... | collective-permute-start | bytes 196616 | tf_op jit(solution)/shard_map/ppermute | solution.py:292
  22.9 0.6 %collective-permute-start.7 = (bf16[32,1024]{1,0:T(8,128)(2,1)S(1)}, bf16[32,1024]{1,0:T(8,128)(2,1)S(1)}, u32[]{:S(2)}, u32[]{:S(2)}) collective-permute-start(bf16[32,1024]{1,0:T(8,128)(2,1)S(1)} %get-tuple-element.37), channel_id=1, source_target_pairs={{0,4},{1,5},{2,3},{3,2},{4,0},{5,1},{6,7},{7,6},{8,12},{9,13},{10,... | collective-permute-start | bytes 196616 | tf_op jit(solution)/shard_map/ppermute | solution.py:292
  23.5 0.5 %collective-permute-start.8 = (bf16[32,1024]{1,0:T(8,128)(2,1)S(1)}, bf16[32,1024]{1,0:T(8,128)(2,1)S(1)}, u32[]{:S(2)}, u32[]{:S(2)}) collective-permute-start(bf16[32,1024]{1,0:T(8,128)(2,1)S(1)} %get-tuple-element.38), channel_id=1, source_target_pairs={{0,1},{1,0},{2,6},{3,7},{4,5},{5,4},{6,2},{7,3},{8,9},{9,8},{10,14... | collective-permute-start | bytes 196616 | tf_op jit(solution)/shard_map/ppermute | solution.py:292
  24.0 1.7 %collective-permute-done.6.refs_1_ = bf16[32,1024]{1,0:T(8,128)(2,1)S(1)} collective-permute-done((bf16[32,1024]{1,0:T(8,128)(2,1)S(1)}, bf16[32,1024]{1,0:T(8,128)(2,1)S(1)}, u32[]{:S(2)}, u32[]{:S(2)}) %collective-permute-start.6) | collective-permute-done | bytes 65568 | tf_op jit(solution)/shard_map/ppermute | solution.py:292
  25.7 1.4 %collective-permute-done.7.refs_2_ = bf16[32,1024]{1,0:T(8,128)(2,1)S(1)} collective-permute-done((bf16[32,1024]{1,0:T(8,128)(2,1)S(1)}, bf16[32,1024]{1,0:T(8,128)(2,1)S(1)}, u32[]{:S(2)}, u32[]{:S(2)}) %collective-permute-start.7) | collective-permute-done | bytes 65568 | tf_op jit(solution)/shard_map/ppermute | solution.py:292
  27.2 0.6 %collective-permute-done.8.refs_3_ = bf16[32,1024]{1,0:T(8,128)(2,1)S(1)} collective-permute-done((bf16[32,1024]{1,0:T(8,128)(2,1)S(1)}, bf16[32,1024]{1,0:T(8,128)(2,1)S(1)}, u32[]{:S(2)}, u32[]{:S(2)}) %collective-permute-start.8) | collective-permute-done | bytes 65568 | tf_op jit(solution)/shard_map/ppermute | solution.py:292
  27.8 0.6 %collective-permute-done.11.refs_6_ = bf16[32,1024]{1,0:T(8,128)(2,1)S(1)} collective-permute-done((bf16[32,1024]{1,0:T(8,128)(2,1)S(1)}, bf16[32,1024]{1,0:T(8,128)(2,1)S(1)}, u32[]{:S(2)}, u32[]{:S(2)}) %collective-permute-start.11) | collective-permute-done | bytes 65568 | tf_op jit(solution)/shard_map/ppermute | solution.py:292
  28.4 0.6 %collective-permute-done.12.refs_7_ = bf16[32,1024]{1,0:T(8,128)(2,1)S(1)} collective-permute-done((bf16[32,1024]{1,0:T(8,128)(2,1)S(1)}, bf16[32,1024]{1,0:T(8,128)(2,1)S(1)}, u32[]{:S(2)}, u32[]{:S(2)}) %collective-permute-start.12) | collective-permute-done | bytes 65568 | tf_op jit(solution)/shard_map/ppermute | solution.py:292
  29.0 2.6 %gram.1 = f32[1024,1024]{1,0:T(8,128)} custom-call(s32[1,256]{1,0:T(1,128)S(1)} %get-tuple-element.34.label_ref, bf16[32,1024]{1,0:T(8,128)(2,1)S(1)} %get-tuple-element.35.refs_0_, bf16[32,1024]{1,0:T(8,128)(2,1)S(1)} %collective-permute-done.6.refs_1_, bf16[32,1024]{1,0:T(8,128)(2,1)S(1)} %collective-permute-done.7.refs_2_, ...), custom_call_target="tpu_custom_call" | custom-call | flops 536870912 | bytes 4194304 | tf_op jit(solution)/shard_map/gram/pallas_call | solution.py:173
  (10 shorter events, 0.1 us)
Async XLA Ops:
  0.0 4.7 %copy-start = (s32[128,1]{0,1:T(1,128)S(1)}, s32[128,1]{0,1:T(1,128)}, u32[]{:S(2)}) copy-start(s32[128,1]{0,1:T(1,128)} %param.7) | copy-start | bytes 1540
  2.9 1.8 %collective-permute-start = (f32[64,1024]{1,0:T(8,128)S(1)}, f32[64,1024]{1,0:T(8,128)S(1)}, u32[]{:S(2)}, u32[]{:S(2)}) collective-permute-start(f32[64,1024]{1,0:T(8,128)S(1)} %get-tuple-element.26), channel_id=1, source_target_pairs={{0,2},{1,3},{2,0},{3,1},{4,6},{5,7},{6,4},{7,5},{8,10},{9,11},{10,... | collective-permute-start | bytes 786440 | tf_op jit(solution)/shard_map/ppermute | solution.py:292
  5.0 6.5 %collective-permute-start.1 = (s32[136,128]{1,0:T(8,128)S(1)}, s32[136,128]{1,0:T(8,128)S(1)}, u32[]{:S(2)}, u32[]{:S(2)}) collective-permute-start(s32[136,128]{1,0:T(8,128)S(1)} %get-tuple-element.28), channel_id=1, source_target_pairs={{0,12},{1,13},{2,14},{3,15},{4,8},{5,9},{6,10},{7,11},{8,4},{9,5},... | collective-permute-start | bytes 208904 | tf_op jit(solution)/shard_map/ppermute | solution.py:292
  8.8 4.3 %collective-permute-start.2 = (s32[136,128]{1,0:T(8,128)S(1)}, s32[136,128]{1,0:T(8,128)S(1)}, u32[]{:S(2)}, u32[]{:S(2)}) collective-permute-start(s32[136,128]{1,0:T(8,128)S(1)} %get-tuple-element.29), channel_id=1, source_target_pairs={{0,4},{1,5},{2,10},{3,11},{4,0},{5,1},{6,14},{7,15},{8,12},{9,13},... | collective-permute-start | bytes 208904 | tf_op jit(solution)/shard_map/ppermute | solution.py:292
  9.3 4.3 %collective-permute-start.3 = (s32[136,128]{1,0:T(8,128)S(1)}, s32[136,128]{1,0:T(8,128)S(1)}, u32[]{:S(2)}, u32[]{:S(2)}) collective-permute-start(s32[136,128]{1,0:T(8,128)S(1)} %get-tuple-element.30), channel_id=1, source_target_pairs={{0,8},{1,9},{2,6},{3,7},{4,12},{5,13},{6,2},{7,3},{8,0},{9,1},{10,... | collective-permute-start | bytes 208904 | tf_op jit(solution)/shard_map/ppermute | solution.py:292
  13.9 6.4 %collective-permute-start.4 = (s32[136,128]{1,0:T(8,128)S(1)}, s32[136,128]{1,0:T(8,128)S(1)}, u32[]{:S(2)}, u32[]{:S(2)}) collective-permute-start(s32[136,128]{1,0:T(8,128)S(1)} %get-tuple-element.32), channel_id=1, source_target_pairs={{0,16},{1,17},{2,18},{3,19},{4,20},{5,21},{6,22},{7,23},{8,24},{9,... | collective-permute-start | bytes 208904 | tf_op jit(solution)/shard_map/ppermute | solution.py:292
  16.5 3.5 %collective-permute-start.5 = (s32[1,128]{1,0:T(1,128)S(1)}, s32[1,128]{1,0:T(1,128)S(1)}, u32[]{:S(2)}, u32[]{:S(2)}) collective-permute-start(s32[1,128]{1,0:T(1,128)S(1)} %get-tuple-element.33.refs_0_), channel_id=1, source_target_pairs={{0,1},{1,0},{2,3},{3,2},{4,5},{5,4},{6,7},{7,6},{8,9},{9,8},{10,11... | collective-permute-start | bytes 1544 | tf_op jit(solution)/shard_map/ppermute | solution.py:292
  20.4 5.3 %collective-permute-start.6 = (bf16[32,1024]{1,0:T(8,128)(2,1)S(1)}, bf16[32,1024]{1,0:T(8,128)(2,1)S(1)}, u32[]{:S(2)}, u32[]{:S(2)}) collective-permute-start(bf16[32,1024]{1,0:T(8,128)(2,1)S(1)} %get-tuple-element.36), channel_id=1, source_target_pairs={{0,5},{1,4},{2,7},{3,6},{4,1},{5,0},{6,3},{7,2},{8,13},{9,12},{10,... | collective-permute-start | bytes 196616 | tf_op jit(solution)/shard_map/ppermute | solution.py:292
  22.9 4.3 %collective-permute-start.7 = (bf16[32,1024]{1,0:T(8,128)(2,1)S(1)}, bf16[32,1024]{1,0:T(8,128)(2,1)S(1)}, u32[]{:S(2)}, u32[]{:S(2)}) collective-permute-start(bf16[32,1024]{1,0:T(8,128)(2,1)S(1)} %get-tuple-element.37), channel_id=1, source_target_pairs={{0,4},{1,5},{2,3},{3,2},{4,0},{5,1},{6,7},{7,6},{8,12},{9,13},{10,... | collective-permute-start | bytes 196616 | tf_op jit(solution)/shard_map/ppermute | solution.py:292
  23.5 4.3 %collective-permute-start.8 = (bf16[32,1024]{1,0:T(8,128)(2,1)S(1)}, bf16[32,1024]{1,0:T(8,128)(2,1)S(1)}, u32[]{:S(2)}, u32[]{:S(2)}) collective-permute-start(bf16[32,1024]{1,0:T(8,128)(2,1)S(1)} %get-tuple-element.38), channel_id=1, source_target_pairs={{0,1},{1,0},{2,6},{3,7},{4,5},{5,4},{6,2},{7,3},{8,9},{9,8},{10,14... | collective-permute-start | bytes 196616 | tf_op jit(solution)/shard_map/ppermute | solution.py:292
  24.0 3.8 %collective-permute-start.9 = (bf16[32,1024]{1,0:T(8,128)(2,1)S(1)}, bf16[32,1024]{1,0:T(8,128)(2,1)S(1)}, u32[]{:S(2)}, u32[]{:S(2)}) collective-permute-start(bf16[32,1024]{1,0:T(8,128)(2,1)S(1)} %get-tuple-element.35.refs_0_), channel_id=1, source_target_pairs={{0,2},{1,3},{2,0},{3,1},{4,6},{5,7},{6,4},{7,5},{8,10},{9,11},{10,... | collective-permute-start | bytes 196616 | tf_op jit(solution)/shard_map/ppermute | solution.py:292
  25.7 2.1 %collective-permute-start.10 = (bf16[32,1024]{1,0:T(8,128)(2,1)S(1)}, bf16[32,1024]{1,0:T(8,128)(2,1)S(1)}, u32[]{:S(2)}, u32[]{:S(2)}) collective-permute-start(bf16[32,1024]{1,0:T(8,128)(2,1)S(1)} %collective-permute-done.6.refs_1_), channel_id=1, source_target_pairs={{0,2},{1,3},{2,0},{3,1},{4,6},{5,7},{6,4},{7,5},{8,10},{9,11},{10,... | collective-permute-start | bytes 196616 | tf_op jit(solution)/shard_map/ppermute | solution.py:292
  27.2 1.3 %collective-permute-start.11 = (bf16[32,1024]{1,0:T(8,128)(2,1)S(1)}, bf16[32,1024]{1,0:T(8,128)(2,1)S(1)}, u32[]{:S(2)}, u32[]{:S(2)}) collective-permute-start(bf16[32,1024]{1,0:T(8,128)(2,1)S(1)} %collective-permute-done.7.refs_2_), channel_id=1, source_target_pairs={{0,2},{1,3},{2,0},{3,1},{4,6},{5,7},{6,4},{7,5},{8,10},{9,11},{10,... | collective-permute-start | bytes 196616 | tf_op jit(solution)/shard_map/ppermute | solution.py:292
  27.8 1.3 %collective-permute-start.12 = (bf16[32,1024]{1,0:T(8,128)(2,1)S(1)}, bf16[32,1024]{1,0:T(8,128)(2,1)S(1)}, u32[]{:S(2)}, u32[]{:S(2)}) collective-permute-start(bf16[32,1024]{1,0:T(8,128)(2,1)S(1)} %collective-permute-done.8.refs_3_), channel_id=1, source_target_pairs={{0,2},{1,3},{2,0},{3,1},{4,6},{5,7},{6,4},{7,5},{8,10},{9,11},{10,... | collective-permute-start | bytes 196616 | tf_op jit(solution)/shard_map/ppermute | solution.py:292

commit v12 on v10

--- a/solution.py
+++ b/solution.py
@@ -11,6 +11,7 @@
 C = 32
 LOW = 256
 LANES = 128
+DEPTH_BITS = 9
 VMEM_LIMIT = 48 * 1024 * 1024
 
 
@@ -26,10 +27,11 @@
 
 def add_products(x_ref, sign_ref, low, high, out_ref, part, wide):
     rows, kept = out_ref.shape
-    blocks = wide // LOW
+    depth = low.shape[0]
+    blocks = wide // depth
     stack = []
     for block in range(part * blocks, (part + 1) * blocks):
-        cols = slice(block * LOW, (block + 1) * LOW)
+        cols = slice(block * depth, (block + 1) * depth)
         stack.append(x_ref[:, cols] * sign_ref[:, cols].astype(jnp.bfloat16))
     stack = jnp.concatenate(stack, axis=0)
     for group in range(kept // LOW):
@@ -59,19 +61,20 @@
         cols = pl.ds(part * wide, wide)
         rows = pl.ds(pl.multiple_of((1 - mine) * half, half), half)
         copies.append(pltpu.make_async_copy(x_hbm.at[rows, cols], x_buf.at[:, cols], sems.at[part]))
-        copies[-1].start()
+        copies[-1].start(priority=part % 2)
     rows = pl.ds(pl.multiple_of(mine * half, half), half)
     keep_copy = pltpu.make_async_copy(x_hbm.at[rows, :], x_keep, sems.at[parts + 2])
-    keep_copy.start()
+    keep_copy.start(priority=1)
     col_copy.wait()
     col = col_buf[...]
     index = lax.broadcasted_iota(jnp.int32, (16, kept), 0)
     inner = parity_sign(index & col, 4)
-    outer = parity_sign(index & (col >> 4), 4)
-    for row in range(LOW // 16):
+    index = lax.broadcasted_iota(jnp.int32, (low.shape[0] // 16, kept), 0)
+    outer = parity_sign(index & (col >> 4), DEPTH_BITS - 4)
+    for row in range(low.shape[0] // 16):
         low[row * 16:(row + 1) * 16] = (inner * outer[row:row + 1]).astype(jnp.bfloat16)
     high_index = lax.broadcasted_iota(jnp.int32, high.shape, 0) + me * high.shape[0]
-    high[...] = parity_sign(high_index & (col >> 8), total_bits - 8)
+    high[...] = parity_sign(high_index & (col >> DEPTH_BITS), total_bits - DEPTH_BITS)
     sign_copy.wait()
     for part in range(parts):
         copies[part].wait()
@@ -104,8 +107,8 @@
             total_type,
             jax.ShapeDtypeStruct((half, width), jnp.bfloat16),
             jax.ShapeDtypeStruct((1, width), jnp.int32),
-            jax.ShapeDtypeStruct((LOW, kept), jnp.bfloat16),
-            jax.ShapeDtypeStruct((width // LOW, kept), jnp.float32),
+            jax.ShapeDtypeStruct((1 << DEPTH_BITS, kept), jnp.bfloat16),
+            jax.ShapeDtypeStruct((width >> DEPTH_BITS, kept), jnp.float32),
         ],
         scratch_shapes=[
             pltpu.VMEM((half, width), jnp.bfloat16),
@@ -148,10 +151,16 @@
     for step in range(steps):
         chosen = jnp.where(label == base + step * group, own, 0.0).astype(jnp.bfloat16)
         blocks[step] = jnp.dot(chosen, rows[...], preferred_element_type=jnp.float32)
-        copies.append(
-            pltpu.make_async_copy(blocks.at[step], out_hbm.at[pl.ds(step * wide, wide), :], sems.at[step])
-        )
-        copies[-1].start()
+        size = wide // 2
+        for at in range(2):
+            copies.append(
+                pltpu.make_async_copy(
+                    blocks.at[step, pl.ds(at * size, size), :],
+                    out_hbm.at[pl.ds(step * wide + at * size, size), :],
+                    sems.at[step * 2 + at],
+                )
+            )
+            copies[-1].start(priority=at)
     for copy in copies:
         copy.wait()
 
@@ -170,7 +179,7 @@
         scratch_shapes=[
             pltpu.VMEM((tokens, kept), jnp.bfloat16),
             pltpu.VMEM((steps, wide, kept), jnp.float32),
-            pltpu.SemaphoreType.DMA((steps,)),
+            pltpu.SemaphoreType.DMA((2 * steps,)),
         ],
         compiler_params=pltpu.CompilerParams(vmem_limit_bytes=VMEM_LIMIT),
         cost_estimate=pl.CostEstimate(
@@ -268,10 +277,11 @@
     )(*operands)
 
 
-def swap(array, tok=0, feat=0):
+def swap(array, tok=0, feat=0, odd=None):
     tok_count, feat_count = lax.axis_size("tok"), lax.axis_size("feat")
+    bits = (feat, odd or feat)
     pairs = [
-        (f * tok_count + t, (f ^ feat) * tok_count + (t ^ tok))
+        (f * tok_count + t, (f ^ bits[f & 1]) * tok_count + (t ^ tok))
         for f in range(feat_count)
         for t in range(tok_count)
     ]
@@ -300,14 +310,14 @@
         labels.reshape(1, rows),
         out_shape=[total_type, word_type, word_type, word_type, label_type],
     )
-    both = swap(again, feat=6)
+    both = swap(again, feat=6, odd=10)
     x_word = swap(there, feat=2)
-    z_word = swap(here, feat=4)
+    z_word = swap(here, feat=4, odd=8)
     all_labels = [label] + [swap(label, tok=tok) for tok in range(1, tok_count)]
     total, word = local_call(
         square_kernel, "add_square", total, both, x_word, z_word, out_shape=[total_type, word_type]
     )
-    word = swap(word, feat=8)
+    word = swap(word, feat=8, odd=4)
     stride = 16
     while stride < feat_count:
         total, word = local_call(middle_kernel, "add_encode", total, word, out_shape=[total_type, word_type])

time: 31.4 us -> 31.8 us (1.013)
    ppermute x13, starting transfers between devices: 12.7 us -> 13 us  [swap(): return lax.ppermute(array, ('feat', 'tok'), pairs)]
  transfers between devices with their start and end apart: 13 -> 13, of which waited for: 10 -> 8; matrix products, arithmetic and copies ran while one was open for 0% -> 0% of each run, Pallas kernels for 4% -> 4%
where the time goes in v12:
time: 31.8 us; the launch traced here: 31.7 us
  starting transfers between devices  13 us (41%)
  waiting for transfers between devices  11.3 us (36%)
  Pallas kernels  7.31 us (23%)
    ppermute x13, starting transfers between devices, swap(): return lax.ppermute(array, ('feat', 'tok'), pairs)  13 us
    ppermute x13, waiting for transfers between devices, swap(): return lax.ppermute(array, ('feat', 'tok'), pairs)  11.3 us
    pallas_call x1, Pallas kernels, partial_halves(): pl.pallas_call(functools.partial(send_kernel, total_bits, parts), in_spec...  2.86 us
    pallas_call x1, Pallas kernels, gram_blocks(): pl.pallas_call(functools.partial(gram_kernel, shard, group, factor), in_s...  2.53 us
    pallas_call x1, Pallas kernels, partial_halves(): pl.pallas_call(functools.partial(keep_kernel, parts), out_shape=total_typ...  1.32 us
  transfers between devices with their start and end apart: 13, of which 8 were waited for; matrix products, arithmetic and copies ran while one was open for 0% of the time, Pallas kernels for 4%

profile of v12, /device:TPU:0, one launch (start us, length us, event | category | flops | bytes accessed | tf_op | source)
XLA Modules:
  0.0 31.7 jit_solution(15513020562789551119)
XLA Ops:
  0.0 2.9 %partial_sent.1 = (f32[64,1024]{1,0:T(8,128)S(1)}, bf16[64,8192]{1,0:T(8,128)(2,1)S(1)}, s32[1,8192]{1,0:T(1,128)S(1)}, bf16[512,1024]{1,0:T(8,128)(2,1)S(1)}, f32[16,1024]{1,0:T(8,128)S(1)}) custom-call(bf16[128,8192]{1,0:T(8,128)(2,1)} %x_hbm.1, s32[1,8192]{1,0:T(1,128)} %bitcast.5, s32[1,1024]{1,0:T(1,128)} %bitcast.6), custom_call_target="tpu_custom_call" | custom-call | flops 1073741824 | bytes 2359296 | tf_op jit(solution)/shard_map/partial_sent/pallas_call | solution.py:102
  2.9 0.5 %collective-permute-start = (f32[64,1024]{1,0:T(8,128)S(1)}, f32[64,1024]{1,0:T(8,128)S(1)}, u32[]{:S(2)}, u32[]{:S(2)}) collective-permute-start(f32[64,1024]{1,0:T(8,128)S(1)} %get-tuple-element.26), channel_id=1, source_target_pairs={{0,2},{1,3},{2,0},{3,1},{4,6},{5,7},{6,4},{7,5},{8,10},{9,11},{10,... | collective-permute-start | bytes 786440 | tf_op jit(solution)/shard_map/ppermute | solution.py:288
  3.4 1.3 %partial_kept.1.keep_ref = f32[64,1024]{1,0:T(8,128)S(1)} custom-call(bf16[64,8192]{1,0:T(8,128)(2,1)S(1)} %get-tuple-element.22.x_keep, s32[1,8192]{1,0:T(1,128)S(1)} %get-tuple-element.23.signs, bf16[512,1024]{1,0:T(8,128)(2,1)S(1)} %get-tuple-element.24.low, f32[16,1024]{1,0:T(8,128)S(1)} %get-tuple-element.25.high), custom_call_target="tpu_custom_call" | custom-call | flops 1073741824 | bytes 2359296 | tf_op jit(solution)/shard_map/partial_kept/pallas_call | solution.py:126
  4.7 0.2 first_split.1
  4.9 3.7 %collective-permute-start.1 = (s32[136,128]{1,0:T(8,128)S(1)}, s32[136,128]{1,0:T(8,128)S(1)}, u32[]{:S(2)}, u32[]{:S(2)}) collective-permute-start(s32[136,128]{1,0:T(8,128)S(1)} %get-tuple-element.28), channel_id=1, source_target_pairs={{0,12},{1,13},{2,22},{3,23},{4,8},{5,9},{6,18},{7,19},{8,4},{9,5},... | collective-permute-start | bytes 208904 | tf_op jit(solution)/shard_map/ppermute | solution.py:288
  8.6 0.5 %collective-permute-start.2 = (s32[136,128]{1,0:T(8,128)S(1)}, s32[136,128]{1,0:T(8,128)S(1)}, u32[]{:S(2)}, u32[]{:S(2)}) collective-permute-start(s32[136,128]{1,0:T(8,128)S(1)} %get-tuple-element.29), channel_id=1, source_target_pairs={{0,4},{1,5},{2,6},{3,7},{4,0},{5,1},{6,2},{7,3},{8,12},{9,13},{10,... | collective-permute-start | bytes 208904 | tf_op jit(solution)/shard_map/ppermute | solution.py:288
  9.2 0.1 collective-permute-start.3
  9.3 1.7 %collective-permute-done.1.both_ref = s32[136,128]{1,0:T(8,128)S(1)} collective-permute-done((s32[136,128]{1,0:T(8,128)S(1)}, s32[136,128]{1,0:T(8,128)S(1)}, u32[]{:S(2)}, u32[]{:S(2)}) %collective-permute-start.1) | collective-permute-done | bytes 69664 | tf_op jit(solution)/shard_map/ppermute | solution.py:288
  10.9 2.6 %collective-permute-done.2.x_ref = s32[136,128]{1,0:T(8,128)S(1)} collective-permute-done((s32[136,128]{1,0:T(8,128)S(1)}, s32[136,128]{1,0:T(8,128)S(1)}, u32[]{:S(2)}, u32[]{:S(2)}) %collective-permute-start.2) | collective-permute-done | bytes 69664 | tf_op jit(solution)/shard_map/ppermute | solution.py:288
  13.6 0.0 collective-permute-done.3.z_ref
  13.6 0.3 add_square.1
  13.9 3.0 %collective-permute-start.4 = (s32[136,128]{1,0:T(8,128)S(1)}, s32[136,128]{1,0:T(8,128)S(1)}, u32[]{:S(2)}, u32[]{:S(2)}) collective-permute-start(s32[136,128]{1,0:T(8,128)S(1)} %get-tuple-element.32), channel_id=1, source_target_pairs={{0,16},{1,17},{2,10},{3,11},{4,20},{5,21},{6,14},{7,15},{8,24},{9,... | collective-permute-start | bytes 208904 | tf_op jit(solution)/shard_map/ppermute | solution.py:288
  16.9 1.5 %collective-permute-start.5 = (s32[1,128]{1,0:T(1,128)S(1)}, s32[1,128]{1,0:T(1,128)S(1)}, u32[]{:S(2)}, u32[]{:S(2)}) collective-permute-start(s32[1,128]{1,0:T(1,128)S(1)} %get-tuple-element.33.refs_0_), channel_id=1, source_target_pairs={{0,1},{1,0},{2,3},{3,2},{4,5},{5,4},{6,7},{7,6},{8,9},{9,8},{10,11... | collective-permute-start | bytes 1544 | tf_op jit(solution)/shard_map/ppermute | solution.py:288
  18.4 2.0 %collective-permute-done.5.refs_1_ = s32[1,128]{1,0:T(1,128)S(1)} collective-permute-done((s32[1,128]{1,0:T(1,128)S(1)}, s32[1,128]{1,0:T(1,128)S(1)}, u32[]{:S(2)}, u32[]{:S(2)}) %collective-permute-start.5) | collective-permute-done | bytes 544 | tf_op jit(solution)/shard_map/ppermute | solution.py:288
  20.4 0.2 sketch_rows.1
  20.6 2.5 %collective-permute-start.6 = (bf16[32,1024]{1,0:T(8,128)(2,1)S(1)}, bf16[32,1024]{1,0:T(8,128)(2,1)S(1)}, u32[]{:S(2)}, u32[]{:S(2)}) collective-permute-start(bf16[32,1024]{1,0:T(8,128)(2,1)S(1)} %get-tuple-element.36), channel_id=1, source_target_pairs={{0,5},{1,4},{2,7},{3,6},{4,1},{5,0},{6,3},{7,2},{8,13},{9,12},{10,... | collective-permute-start | bytes 196616 | tf_op jit(solution)/shard_map/ppermute | solution.py:288
  23.1 0.5 %collective-permute-start.7 = (bf16[32,1024]{1,0:T(8,128)(2,1)S(1)}, bf16[32,1024]{1,0:T(8,128)(2,1)S(1)}, u32[]{:S(2)}, u32[]{:S(2)}) collective-permute-start(bf16[32,1024]{1,0:T(8,128)(2,1)S(1)} %get-tuple-element.37), channel_id=1, source_target_pairs={{0,4},{1,5},{2,6},{3,7},{4,0},{5,1},{6,2},{7,3},{8,12},{9,13},{10,... | collective-permute-start | bytes 196616 | tf_op jit(solution)/shard_map/ppermute | solution.py:288
  23.6 0.5 %collective-permute-start.8 = (bf16[32,1024]{1,0:T(8,128)(2,1)S(1)}, bf16[32,1024]{1,0:T(8,128)(2,1)S(1)}, u32[]{:S(2)}, u32[]{:S(2)}) collective-permute-start(bf16[32,1024]{1,0:T(8,128)(2,1)S(1)} %get-tuple-element.38), channel_id=1, source_target_pairs={{0,1},{1,0},{2,3},{3,2},{4,5},{5,4},{6,7},{7,6},{8,9},{9,8},{10,11... | collective-permute-start | bytes 196616 | tf_op jit(solution)/shard_map/ppermute | solution.py:288
  24.1 1.7 %collective-permute-done.6.refs_1_ = bf16[32,1024]{1,0:T(8,128)(2,1)S(1)} collective-permute-done((bf16[32,1024]{1,0:T(8,128)(2,1)S(1)}, bf16[32,1024]{1,0:T(8,128)(2,1)S(1)}, u32[]{:S(2)}, u32[]{:S(2)}) %collective-permute-start.6) | collective-permute-done | bytes 65568 | tf_op jit(solution)/shard_map/ppermute | solution.py:288
  25.8 1.5 %collective-permute-done.7.refs_2_ = bf16[32,1024]{1,0:T(8,128)(2,1)S(1)} collective-permute-done((bf16[32,1024]{1,0:T(8,128)(2,1)S(1)}, bf16[32,1024]{1,0:T(8,128)(2,1)S(1)}, u32[]{:S(2)}, u32[]{:S(2)}) %collective-permute-start.7) | collective-permute-done | bytes 65568 | tf_op jit(solution)/shard_map/ppermute | solution.py:288
  27.4 0.5 %collective-permute-done.8.refs_3_ = bf16[32,1024]{1,0:T(8,128)(2,1)S(1)} collective-permute-done((bf16[32,1024]{1,0:T(8,128)(2,1)S(1)}, bf16[32,1024]{1,0:T(8,128)(2,1)S(1)}, u32[]{:S(2)}, u32[]{:S(2)}) %collective-permute-start.8) | collective-permute-done | bytes 65568 | tf_op jit(solution)/shard_map/ppermute | solution.py:288
  27.9 0.7 %collective-permute-done.11.refs_6_ = bf16[32,1024]{1,0:T(8,128)(2,1)S(1)} collective-permute-done((bf16[32,1024]{1,0:T(8,128)(2,1)S(1)}, bf16[32,1024]{1,0:T(8,128)(2,1)S(1)}, u32[]{:S(2)}, u32[]{:S(2)}) %collective-permute-start.11) | collective-permute-done | bytes 65568 | tf_op jit(solution)/shard_map/ppermute | solution.py:288
  28.6 0.5 %collective-permute-done.12.refs_7_ = bf16[32,1024]{1,0:T(8,128)(2,1)S(1)} collective-permute-done((bf16[32,1024]{1,0:T(8,128)(2,1)S(1)}, bf16[32,1024]{1,0:T(8,128)(2,1)S(1)}, u32[]{:S(2)}, u32[]{:S(2)}) %collective-permute-start.12) | collective-permute-done | bytes 65568 | tf_op jit(solution)/shard_map/ppermute | solution.py:288
  29.2 2.5 %gram.1 = f32[1024,1024]{1,0:T(8,128)} custom-call(s32[1,256]{1,0:T(1,128)S(1)} %get-tuple-element.34.label_ref, bf16[32,1024]{1,0:T(8,128)(2,1)S(1)} %get-tuple-element.35.refs_0_, bf16[32,1024]{1,0:T(8,128)(2,1)S(1)} %collective-permute-done.6.refs_1_, bf16[32,1024]{1,0:T(8,128)(2,1)S(1)} %collective-permute-done.7.refs_2_, ...), custom_call_target="tpu_custom_call" | custom-call | flops 536870912 | bytes 4194304 | tf_op jit(solution)/shard_map/gram/pallas_call | solution.py:174
  (10 shorter events, 0.0 us)
Async XLA Ops:
  0.0 4.7 %copy-start = (s32[128,1]{0,1:T(1,128)S(1)}, s32[128,1]{0,1:T(1,128)}, u32[]{:S(2)}) copy-start(s32[128,1]{0,1:T(1,128)} %param.7) | copy-start | bytes 1540
  2.9 1.8 %collective-permute-start = (f32[64,1024]{1,0:T(8,128)S(1)}, f32[64,1024]{1,0:T(8,128)S(1)}, u32[]{:S(2)}, u32[]{:S(2)}) collective-permute-start(f32[64,1024]{1,0:T(8,128)S(1)} %get-tuple-element.26), channel_id=1, source_target_pairs={{0,2},{1,3},{2,0},{3,1},{4,6},{5,7},{6,4},{7,5},{8,10},{9,11},{10,... | collective-permute-start | bytes 786440 | tf_op jit(solution)/shard_map/ppermute | solution.py:288
  4.9 6.0 %collective-permute-start.1 = (s32[136,128]{1,0:T(8,128)S(1)}, s32[136,128]{1,0:T(8,128)S(1)}, u32[]{:S(2)}, u32[]{:S(2)}) collective-permute-start(s32[136,128]{1,0:T(8,128)S(1)} %get-tuple-element.28), channel_id=1, source_target_pairs={{0,12},{1,13},{2,22},{3,23},{4,8},{5,9},{6,18},{7,19},{8,4},{9,5},... | collective-permute-start | bytes 208904 | tf_op jit(solution)/shard_map/ppermute | solution.py:288
  8.6 4.9 %collective-permute-start.2 = (s32[136,128]{1,0:T(8,128)S(1)}, s32[136,128]{1,0:T(8,128)S(1)}, u32[]{:S(2)}, u32[]{:S(2)}) collective-permute-start(s32[136,128]{1,0:T(8,128)S(1)} %get-tuple-element.29), channel_id=1, source_target_pairs={{0,4},{1,5},{2,6},{3,7},{4,0},{5,1},{6,2},{7,3},{8,12},{9,13},{10,... | collective-permute-start | bytes 208904 | tf_op jit(solution)/shard_map/ppermute | solution.py:288
  9.2 4.4 %collective-permute-start.3 = (s32[136,128]{1,0:T(8,128)S(1)}, s32[136,128]{1,0:T(8,128)S(1)}, u32[]{:S(2)}, u32[]{:S(2)}) collective-permute-start(s32[136,128]{1,0:T(8,128)S(1)} %get-tuple-element.30), channel_id=1, source_target_pairs={{0,8},{1,9},{2,18},{3,19},{4,12},{5,13},{6,22},{7,23},{8,0},{9,1},... | collective-permute-start | bytes 208904 | tf_op jit(solution)/shard_map/ppermute | solution.py:288
  13.9 6.6 %collective-permute-start.4 = (s32[136,128]{1,0:T(8,128)S(1)}, s32[136,128]{1,0:T(8,128)S(1)}, u32[]{:S(2)}, u32[]{:S(2)}) collective-permute-start(s32[136,128]{1,0:T(8,128)S(1)} %get-tuple-element.32), channel_id=1, source_target_pairs={{0,16},{1,17},{2,10},{3,11},{4,20},{5,21},{6,14},{7,15},{8,24},{9,... | collective-permute-start | bytes 208904 | tf_op jit(solution)/shard_map/ppermute | solution.py:288
  16.9 3.5 %collective-permute-start.5 = (s32[1,128]{1,0:T(1,128)S(1)}, s32[1,128]{1,0:T(1,128)S(1)}, u32[]{:S(2)}, u32[]{:S(2)}) collective-permute-start(s32[1,128]{1,0:T(1,128)S(1)} %get-tuple-element.33.refs_0_), channel_id=1, source_target_pairs={{0,1},{1,0},{2,3},{3,2},{4,5},{5,4},{6,7},{7,6},{8,9},{9,8},{10,11... | collective-permute-start | bytes 1544 | tf_op jit(solution)/shard_map/ppermute | solution.py:288
  20.6 5.2 %collective-permute-start.6 = (bf16[32,1024]{1,0:T(8,128)(2,1)S(1)}, bf16[32,1024]{1,0:T(8,128)(2,1)S(1)}, u32[]{:S(2)}, u32[]{:S(2)}) collective-permute-start(bf16[32,1024]{1,0:T(8,128)(2,1)S(1)} %get-tuple-element.36), channel_id=1, source_target_pairs={{0,5},{1,4},{2,7},{3,6},{4,1},{5,0},{6,3},{7,2},{8,13},{9,12},{10,... | collective-permute-start | bytes 196616 | tf_op jit(solution)/shard_map/ppermute | solution.py:288
  23.1 4.3 %collective-permute-start.7 = (bf16[32,1024]{1,0:T(8,128)(2,1)S(1)}, bf16[32,1024]{1,0:T(8,128)(2,1)S(1)}, u32[]{:S(2)}, u32[]{:S(2)}) collective-permute-start(bf16[32,1024]{1,0:T(8,128)(2,1)S(1)} %get-tuple-element.37), channel_id=1, source_target_pairs={{0,4},{1,5},{2,6},{3,7},{4,0},{5,1},{6,2},{7,3},{8,12},{9,13},{10,... | collective-permute-start | bytes 196616 | tf_op jit(solution)/shard_map/ppermute | solution.py:288
  23.6 4.3 %collective-permute-start.8 = (bf16[32,1024]{1,0:T(8,128)(2,1)S(1)}, bf16[32,1024]{1,0:T(8,128)(2,1)S(1)}, u32[]{:S(2)}, u32[]{:S(2)}) collective-permute-start(bf16[32,1024]{1,0:T(8,128)(2,1)S(1)} %get-tuple-element.38), channel_id=1, source_target_pairs={{0,1},{1,0},{2,3},{3,2},{4,5},{5,4},{6,7},{7,6},{8,9},{9,8},{10,11... | collective-permute-start | bytes 196616 | tf_op jit(solution)/shard_map/ppermute | solution.py:288
  24.1 3.8 %collective-permute-start.9 = (bf16[32,1024]{1,0:T(8,128)(2,1)S(1)}, bf16[32,1024]{1,0:T(8,128)(2,1)S(1)}, u32[]{:S(2)}, u32[]{:S(2)}) collective-permute-start(bf16[32,1024]{1,0:T(8,128)(2,1)S(1)} %get-tuple-element.35.refs_0_), channel_id=1, source_target_pairs={{0,2},{1,3},{2,0},{3,1},{4,6},{5,7},{6,4},{7,5},{8,10},{9,11},{10,... | collective-permute-start | bytes 196616 | tf_op jit(solution)/shard_map/ppermute | solution.py:288
  25.8 2.1 %collective-permute-start.10 = (bf16[32,1024]{1,0:T(8,128)(2,1)S(1)}, bf16[32,1024]{1,0:T(8,128)(2,1)S(1)}, u32[]{:S(2)}, u32[]{:S(2)}) collective-permute-start(bf16[32,1024]{1,0:T(8,128)(2,1)S(1)} %collective-permute-done.6.refs_1_), channel_id=1, source_target_pairs={{0,2},{1,3},{2,0},{3,1},{4,6},{5,7},{6,4},{7,5},{8,10},{9,11},{10,... | collective-permute-start | bytes 196616 | tf_op jit(solution)/shard_map/ppermute | solution.py:288
  27.4 1.3 %collective-permute-start.11 = (bf16[32,1024]{1,0:T(8,128)(2,1)S(1)}, bf16[32,1024]{1,0:T(8,128)(2,1)S(1)}, u32[]{:S(2)}, u32[]{:S(2)}) collective-permute-start(bf16[32,1024]{1,0:T(8,128)(2,1)S(1)} %collective-permute-done.7.refs_2_), channel_id=1, source_target_pairs={{0,2},{1,3},{2,0},{3,1},{4,6},{5,7},{6,4},{7,5},{8,10},{9,11},{10,... | collective-permute-start | bytes 196616 | tf_op jit(solution)/shard_map/ppermute | solution.py:288
  27.9 1.3 %collective-permute-start.12 = (bf16[32,1024]{1,0:T(8,128)(2,1)S(1)}, bf16[32,1024]{1,0:T(8,128)(2,1)S(1)}, u32[]{:S(2)}, u32[]{:S(2)}) collective-permute-start(bf16[32,1024]{1,0:T(8,128)(2,1)S(1)} %collective-permute-done.8.refs_3_), channel_id=1, source_target_pairs={{0,2},{1,3},{2,0},{3,1},{4,6},{5,7},{6,4},{7,5},{8,10},{9,11},{10,... | collective-permute-start | bytes 196616 | tf_op jit(solution)/shard_map/ppermute | solution.py:288

commit v13 on v10

--- a/solution.py
+++ b/solution.py
@@ -238,7 +238,7 @@
 
 
 def last_kernel(scale, blocks, total_ref, word_ref, *refs):
-    label_refs, (label_out, *row_refs) = refs[:-5], refs[-5:]
+    label_refs, (label_out, *row_refs) = refs[:-6], refs[-6:]
     size = total_ref.shape[0]
     row = ((total_ref[...] + decode(word_ref, size)) * scale).astype(jnp.bfloat16)
     for row_ref in row_refs:
@@ -327,15 +327,16 @@
         total,
         word,
         *all_labels,
-        out_shape=[jax.ShapeDtypeStruct((1, 2 * len(blocks) * size), jnp.int32)] + [row_type] * 4,
+        out_shape=[jax.ShapeDtypeStruct((1, 2 * len(blocks) * size), jnp.int32)] + [row_type] * 5,
     )
     stride = 2
     while stride < tok_count:
-        copies = [jnp.concatenate([copies[0], swap(copies[0], tok=stride)], axis=0)] * 4
+        copies = [jnp.concatenate([copies[0], swap(copies[0], tok=stride)], axis=0)] * 5
         stride *= 2
     received = [swap(copies[0], tok=1, feat=2), swap(copies[1], feat=2), swap(copies[2], tok=1)]
-    ours = copies[3:] + received
-    theirs = [swap(block, feat=1) for block in ours]
+    last = swap(copies[3], tok=1, feat=1)
+    ours = copies[4:] + received
+    theirs = [swap(block, feat=1) for block in ours[:3]] + [last]
     concepts = C // tok_count
     gram = gram_blocks(ours + theirs, label_row, concepts, shard, C / (rows * tok_count))
     return gram.reshape(concepts, shard, kept)

time: 31.4 us -> 30.9 us (0.984)
  waiting for transfers between devices: 11.3 us -> 9.05 us
  starting transfers between devices: 12.7 us -> 14.3 us
    ppermute x13, waiting for transfers between devices: 11.3 us -> 9.05 us  [swap(): return lax.ppermute(array, ('feat', 'tok'), pairs)]
    ppermute x13, starting transfers between devices: 12.7 us -> 14.3 us  [swap(): return lax.ppermute(array, ('feat', 'tok'), pairs)]
  transfers between devices with their start and end apart: 13 -> 13, of which waited for: 10 -> 7; matrix products, arithmetic and copies ran while one was open for 0% -> 0% of each run, Pallas kernels for 4% -> 4%
where the time goes in v13:
time: 30.9 us; the launch traced here: 30.7 us
  starting transfers between devices  14.3 us (46%)
  waiting for transfers between devices  9.05 us (29%)
  Pallas kernels  7.26 us (23%)
    ppermute x13, starting transfers between devices, swap(): return lax.ppermute(array, ('feat', 'tok'), pairs)  14.3 us
    ppermute x13, waiting for transfers between devices, swap(): return lax.ppermute(array, ('feat', 'tok'), pairs)  9.05 us
    pallas_call x1, Pallas kernels, partial_halves(): pl.pallas_call(functools.partial(send_kernel, total_bits, parts), in_spec...  2.86 us
    pallas_call x1, Pallas kernels, gram_blocks(): pl.pallas_call(functools.partial(gram_kernel, shard, group, factor), in_s...  2.5 us
    pallas_call x1, Pallas kernels, partial_halves(): pl.pallas_call(functools.partial(keep_kernel, parts), out_shape=total_typ...  1.3 us
  transfers between devices with their start and end apart: 13, of which 7 were waited for; matrix products, arithmetic and copies ran while one was open for 0% of the time, Pallas kernels for 4%

profile of v13, /device:TPU:0, one launch (start us, length us, event | category | flops | bytes accessed | tf_op | source)
XLA Modules:
  0.0 30.7 jit_solution(11616217634904091648)
XLA Ops:
  0.0 2.9 %partial_sent.1 = (f32[64,1024]{1,0:T(8,128)S(1)}, bf16[64,8192]{1,0:T(8,128)(2,1)S(1)}, s32[1,8192]{1,0:T(1,128)S(1)}, bf16[256,1024]{1,0:T(8,128)(2,1)S(1)}, f32[32,1024]{1,0:T(8,128)S(1)}) custom-call(bf16[128,8192]{1,0:T(8,128)(2,1)} %x_hbm.1, s32[1,8192]{1,0:T(1,128)} %bitcast.5, s32[1,1024]{1,0:T(1,128)} %bitcast.6), custom_call_target="tpu_custom_call" | custom-call | flops 1073741824 | bytes 2359296 | tf_op jit(solution)/shard_map/partial_sent/pallas_call | solution.py:99
  2.9 0.5 %collective-permute-start = (f32[64,1024]{1,0:T(8,128)S(1)}, f32[64,1024]{1,0:T(8,128)S(1)}, u32[]{:S(2)}, u32[]{:S(2)}) collective-permute-start(f32[64,1024]{1,0:T(8,128)S(1)} %get-tuple-element.27), channel_id=1, source_target_pairs={{0,2},{1,3},{2,0},{3,1},{4,6},{5,7},{6,4},{7,5},{8,10},{9,11},{10,... | collective-permute-start | bytes 786440 | tf_op jit(solution)/shard_map/ppermute | solution.py:278
  3.4 1.3 %partial_kept.1.keep_ref = f32[64,1024]{1,0:T(8,128)S(1)} custom-call(bf16[64,8192]{1,0:T(8,128)(2,1)S(1)} %get-tuple-element.23.x_keep, s32[1,8192]{1,0:T(1,128)S(1)} %get-tuple-element.24.signs, bf16[256,1024]{1,0:T(8,128)(2,1)S(1)} %get-tuple-element.25.low, f32[32,1024]{1,0:T(8,128)S(1)} %get-tuple-element.26.high), custom_call_target="tpu_custom_call" | custom-call | flops 1073741824 | bytes 2359296 | tf_op jit(solution)/shard_map/partial_kept/pallas_call | solution.py:123
  4.7 0.2 first_split.1
  4.9 3.8 %collective-permute-start.1 = (s32[136,128]{1,0:T(8,128)S(1)}, s32[136,128]{1,0:T(8,128)S(1)}, u32[]{:S(2)}, u32[]{:S(2)}) collective-permute-start(s32[136,128]{1,0:T(8,128)S(1)} %get-tuple-element.29), channel_id=1, source_target_pairs={{0,12},{1,13},{2,14},{3,15},{4,8},{5,9},{6,10},{7,11},{8,4},{9,5},... | collective-permute-start | bytes 208904 | tf_op jit(solution)/shard_map/ppermute | solution.py:278
  8.6 0.5 %collective-permute-start.2 = (s32[136,128]{1,0:T(8,128)S(1)}, s32[136,128]{1,0:T(8,128)S(1)}, u32[]{:S(2)}, u32[]{:S(2)}) collective-permute-start(s32[136,128]{1,0:T(8,128)S(1)} %get-tuple-element.30), channel_id=1, source_target_pairs={{0,4},{1,5},{2,6},{3,7},{4,0},{5,1},{6,2},{7,3},{8,12},{9,13},{10,... | collective-permute-start | bytes 208904 | tf_op jit(solution)/shard_map/ppermute | solution.py:278
  9.2 0.1 collective-permute-start.3
  9.3 2.0 %collective-permute-done.1.both_ref = s32[136,128]{1,0:T(8,128)S(1)} collective-permute-done((s32[136,128]{1,0:T(8,128)S(1)}, s32[136,128]{1,0:T(8,128)S(1)}, u32[]{:S(2)}, u32[]{:S(2)}) %collective-permute-start.1) | collective-permute-done | bytes 69664 | tf_op jit(solution)/shard_map/ppermute | solution.py:278
  11.3 1.7 %collective-permute-done.2.x_ref = s32[136,128]{1,0:T(8,128)S(1)} collective-permute-done((s32[136,128]{1,0:T(8,128)S(1)}, s32[136,128]{1,0:T(8,128)S(1)}, u32[]{:S(2)}, u32[]{:S(2)}) %collective-permute-start.2) | collective-permute-done | bytes 69664 | tf_op jit(solution)/shard_map/ppermute | solution.py:278
  13.0 0.5 %collective-permute-done.3.z_ref = s32[136,128]{1,0:T(8,128)S(1)} collective-permute-done((s32[136,128]{1,0:T(8,128)S(1)}, s32[136,128]{1,0:T(8,128)S(1)}, u32[]{:S(2)}, u32[]{:S(2)}) %collective-permute-start.3) | collective-permute-done | bytes 69664 | tf_op jit(solution)/shard_map/ppermute | solution.py:278
  13.5 0.3 add_square.1
  13.8 2.7 %collective-permute-start.4 = (s32[136,128]{1,0:T(8,128)S(1)}, s32[136,128]{1,0:T(8,128)S(1)}, u32[]{:S(2)}, u32[]{:S(2)}) collective-permute-start(s32[136,128]{1,0:T(8,128)S(1)} %get-tuple-element.33), channel_id=1, source_target_pairs={{0,16},{1,17},{2,18},{3,19},{4,20},{5,21},{6,22},{7,23},{8,24},{9,... | collective-permute-start | bytes 208904 | tf_op jit(solution)/shard_map/ppermute | solution.py:278
  16.4 1.5 %collective-permute-start.5 = (s32[1,128]{1,0:T(1,128)S(1)}, s32[1,128]{1,0:T(1,128)S(1)}, u32[]{:S(2)}, u32[]{:S(2)}) collective-permute-start(s32[1,128]{1,0:T(1,128)S(1)} %get-tuple-element.34.refs_0_), channel_id=1, source_target_pairs={{0,1},{1,0},{2,3},{3,2},{4,5},{5,4},{6,7},{7,6},{8,9},{9,8},{10,11... | collective-permute-start | bytes 1544 | tf_op jit(solution)/shard_map/ppermute | solution.py:278
  17.9 2.0 %collective-permute-done.5.refs_1_ = s32[1,128]{1,0:T(1,128)S(1)} collective-permute-done((s32[1,128]{1,0:T(1,128)S(1)}, s32[1,128]{1,0:T(1,128)S(1)}, u32[]{:S(2)}, u32[]{:S(2)}) %collective-permute-start.5) | collective-permute-done | bytes 544 | tf_op jit(solution)/shard_map/ppermute | solution.py:278
  20.0 0.1 collective-permute-done.4.word_ref
  20.0 0.2 sketch_rows.1
  20.2 2.4 %collective-permute-start.6 = (bf16[32,1024]{1,0:T(8,128)(2,1)S(1)}, bf16[32,1024]{1,0:T(8,128)(2,1)S(1)}, u32[]{:S(2)}, u32[]{:S(2)}) collective-permute-start(bf16[32,1024]{1,0:T(8,128)(2,1)S(1)} %get-tuple-element.37), channel_id=1, source_target_pairs={{0,5},{1,4},{2,7},{3,6},{4,1},{5,0},{6,3},{7,2},{8,13},{9,12},{10,... | collective-permute-start | bytes 196616 | tf_op jit(solution)/shard_map/ppermute | solution.py:278
  22.6 0.6 %collective-permute-start.7 = (bf16[32,1024]{1,0:T(8,128)(2,1)S(1)}, bf16[32,1024]{1,0:T(8,128)(2,1)S(1)}, u32[]{:S(2)}, u32[]{:S(2)}) collective-permute-start(bf16[32,1024]{1,0:T(8,128)(2,1)S(1)} %get-tuple-element.38), channel_id=1, source_target_pairs={{0,4},{1,5},{2,6},{3,7},{4,0},{5,1},{6,2},{7,3},{8,12},{9,13},{10,... | collective-permute-start | bytes 196616 | tf_op jit(solution)/shard_map/ppermute | solution.py:278
  23.3 0.5 %collective-permute-start.8 = (bf16[32,1024]{1,0:T(8,128)(2,1)S(1)}, bf16[32,1024]{1,0:T(8,128)(2,1)S(1)}, u32[]{:S(2)}, u32[]{:S(2)}) collective-permute-start(bf16[32,1024]{1,0:T(8,128)(2,1)S(1)} %get-tuple-element.39), channel_id=1, source_target_pairs={{0,1},{1,0},{2,3},{3,2},{4,5},{5,4},{6,7},{7,6},{8,9},{9,8},{10,11... | collective-permute-start | bytes 196616 | tf_op jit(solution)/shard_map/ppermute | solution.py:278
  23.8 1.6 %collective-permute-start.9 = (bf16[32,1024]{1,0:T(8,128)(2,1)S(1)}, bf16[32,1024]{1,0:T(8,128)(2,1)S(1)}, u32[]{:S(2)}, u32[]{:S(2)}) collective-permute-start(bf16[32,1024]{1,0:T(8,128)(2,1)S(1)} %get-tuple-element.36.refs_0_), channel_id=1, source_target_pairs={{0,2},{1,3},{2,0},{3,1},{4,6},{5,7},{6,4},{7,5},{8,10},{9,11},{10,... | collective-permute-start | bytes 196616 | tf_op jit(solution)/shard_map/ppermute | solution.py:278
  25.4 0.0 collective-permute-done.6.refs_1_
  25.4 1.5 %collective-permute-done.7.refs_2_ = bf16[32,1024]{1,0:T(8,128)(2,1)S(1)} collective-permute-done((bf16[32,1024]{1,0:T(8,128)(2,1)S(1)}, bf16[32,1024]{1,0:T(8,128)(2,1)S(1)}, u32[]{:S(2)}, u32[]{:S(2)}) %collective-permute-start.7) | collective-permute-done | bytes 65568 | tf_op jit(solution)/shard_map/ppermute | solution.py:278
  26.9 1.2 %collective-permute-done.8.refs_3_ = bf16[32,1024]{1,0:T(8,128)(2,1)S(1)} collective-permute-done((bf16[32,1024]{1,0:T(8,128)(2,1)S(1)}, bf16[32,1024]{1,0:T(8,128)(2,1)S(1)}, u32[]{:S(2)}, u32[]{:S(2)}) %collective-permute-start.8) | collective-permute-done | bytes 65568 | tf_op jit(solution)/shard_map/ppermute | solution.py:278
  28.2 2.5 %gram.1 = f32[1024,1024]{1,0:T(8,128)} custom-call(s32[1,256]{1,0:T(1,128)S(1)} %get-tuple-element.35.label_ref, bf16[32,1024]{1,0:T(8,128)(2,1)S(1)} %get-tuple-element.36.refs_0_, bf16[32,1024]{1,0:T(8,128)(2,1)S(1)} %collective-permute-done.6.refs_1_, bf16[32,1024]{1,0:T(8,128)(2,1)S(1)} %collective-permute-done.7.refs_2_, ...), custom_call_target="tpu_custom_call" | custom-call | flops 536870912 | bytes 4194304 | tf_op jit(solution)/shard_map/gram/pallas_call | solution.py:165
  (10 shorter events, 0.0 us)
Async XLA Ops:
  0.0 4.7 %copy-start = (s32[128,1]{0,1:T(1,128)S(1)}, s32[128,1]{0,1:T(1,128)}, u32[]{:S(2)}) copy-start(s32[128,1]{0,1:T(1,128)} %param.7) | copy-start | bytes 1540
  2.9 1.8 %collective-permute-start = (f32[64,1024]{1,0:T(8,128)S(1)}, f32[64,1024]{1,0:T(8,128)S(1)}, u32[]{:S(2)}, u32[]{:S(2)}) collective-permute-start(f32[64,1024]{1,0:T(8,128)S(1)} %get-tuple-element.27), channel_id=1, source_target_pairs={{0,2},{1,3},{2,0},{3,1},{4,6},{5,7},{6,4},{7,5},{8,10},{9,11},{10,... | collective-permute-start | bytes 786440 | tf_op jit(solution)/shard_map/ppermute | solution.py:278
  4.9 6.4 %collective-permute-start.1 = (s32[136,128]{1,0:T(8,128)S(1)}, s32[136,128]{1,0:T(8,128)S(1)}, u32[]{:S(2)}, u32[]{:S(2)}) collective-permute-start(s32[136,128]{1,0:T(8,128)S(1)} %get-tuple-element.29), channel_id=1, source_target_pairs={{0,12},{1,13},{2,14},{3,15},{4,8},{5,9},{6,10},{7,11},{8,4},{9,5},... | collective-permute-start | bytes 208904 | tf_op jit(solution)/shard_map/ppermute | solution.py:278
  8.6 4.3 %collective-permute-start.2 = (s32[136,128]{1,0:T(8,128)S(1)}, s32[136,128]{1,0:T(8,128)S(1)}, u32[]{:S(2)}, u32[]{:S(2)}) collective-permute-start(s32[136,128]{1,0:T(8,128)S(1)} %get-tuple-element.30), channel_id=1, source_target_pairs={{0,4},{1,5},{2,6},{3,7},{4,0},{5,1},{6,2},{7,3},{8,12},{9,13},{10,... | collective-permute-start | bytes 208904 | tf_op jit(solution)/shard_map/ppermute | solution.py:278
  9.2 4.3 %collective-permute-start.3 = (s32[136,128]{1,0:T(8,128)S(1)}, s32[136,128]{1,0:T(8,128)S(1)}, u32[]{:S(2)}, u32[]{:S(2)}) collective-permute-start(s32[136,128]{1,0:T(8,128)S(1)} %get-tuple-element.31), channel_id=1, source_target_pairs={{0,8},{1,9},{2,10},{3,11},{4,12},{5,13},{6,14},{7,15},{8,0},{9,1},... | collective-permute-start | bytes 208904 | tf_op jit(solution)/shard_map/ppermute | solution.py:278
  13.8 6.3 %collective-permute-start.4 = (s32[136,128]{1,0:T(8,128)S(1)}, s32[136,128]{1,0:T(8,128)S(1)}, u32[]{:S(2)}, u32[]{:S(2)}) collective-permute-start(s32[136,128]{1,0:T(8,128)S(1)} %get-tuple-element.33), channel_id=1, source_target_pairs={{0,16},{1,17},{2,18},{3,19},{4,20},{5,21},{6,22},{7,23},{8,24},{9,... | collective-permute-start | bytes 208904 | tf_op jit(solution)/shard_map/ppermute | solution.py:278
  16.4 3.5 %collective-permute-start.5 = (s32[1,128]{1,0:T(1,128)S(1)}, s32[1,128]{1,0:T(1,128)S(1)}, u32[]{:S(2)}, u32[]{:S(2)}) collective-permute-start(s32[1,128]{1,0:T(1,128)S(1)} %get-tuple-element.34.refs_0_), channel_id=1, source_target_pairs={{0,1},{1,0},{2,3},{3,2},{4,5},{5,4},{6,7},{7,6},{8,9},{9,8},{10,11... | collective-permute-start | bytes 1544 | tf_op jit(solution)/shard_map/ppermute | solution.py:278
  20.2 5.2 %collective-permute-start.6 = (bf16[32,1024]{1,0:T(8,128)(2,1)S(1)}, bf16[32,1024]{1,0:T(8,128)(2,1)S(1)}, u32[]{:S(2)}, u32[]{:S(2)}) collective-permute-start(bf16[32,1024]{1,0:T(8,128)(2,1)S(1)} %get-tuple-element.37), channel_id=1, source_target_pairs={{0,5},{1,4},{2,7},{3,6},{4,1},{5,0},{6,3},{7,2},{8,13},{9,12},{10,... | collective-permute-start | bytes 196616 | tf_op jit(solution)/shard_map/ppermute | solution.py:278
  22.6 4.3 %collective-permute-start.7 = (bf16[32,1024]{1,0:T(8,128)(2,1)S(1)}, bf16[32,1024]{1,0:T(8,128)(2,1)S(1)}, u32[]{:S(2)}, u32[]{:S(2)}) collective-permute-start(bf16[32,1024]{1,0:T(8,128)(2,1)S(1)} %get-tuple-element.38), channel_id=1, source_target_pairs={{0,4},{1,5},{2,6},{3,7},{4,0},{5,1},{6,2},{7,3},{8,12},{9,13},{10,... | collective-permute-start | bytes 196616 | tf_op jit(solution)/shard_map/ppermute | solution.py:278
  23.3 4.9 %collective-permute-start.8 = (bf16[32,1024]{1,0:T(8,128)(2,1)S(1)}, bf16[32,1024]{1,0:T(8,128)(2,1)S(1)}, u32[]{:S(2)}, u32[]{:S(2)}) collective-permute-start(bf16[32,1024]{1,0:T(8,128)(2,1)S(1)} %get-tuple-element.39), channel_id=1, source_target_pairs={{0,1},{1,0},{2,3},{3,2},{4,5},{5,4},{6,7},{7,6},{8,9},{9,8},{10,11... | collective-permute-start | bytes 196616 | tf_op jit(solution)/shard_map/ppermute | solution.py:278
  23.8 4.4 %collective-permute-start.12 = (bf16[32,1024]{1,0:T(8,128)(2,1)S(1)}, bf16[32,1024]{1,0:T(8,128)(2,1)S(1)}, u32[]{:S(2)}, u32[]{:S(2)}) collective-permute-start(bf16[32,1024]{1,0:T(8,128)(2,1)S(1)} %get-tuple-element.40), channel_id=1, source_target_pairs={{0,3},{1,2},{2,1},{3,0},{4,7},{5,6},{6,5},{7,4},{8,11},{9,10},{10,... | collective-permute-start | bytes 196616 | tf_op jit(solution)/shard_map/ppermute | solution.py:278
  23.8 4.4 %collective-permute-start.9 = (bf16[32,1024]{1,0:T(8,128)(2,1)S(1)}, bf16[32,1024]{1,0:T(8,128)(2,1)S(1)}, u32[]{:S(2)}, u32[]{:S(2)}) collective-permute-start(bf16[32,1024]{1,0:T(8,128)(2,1)S(1)} %get-tuple-element.36.refs_0_), channel_id=1, source_target_pairs={{0,2},{1,3},{2,0},{3,1},{4,6},{5,7},{6,4},{7,5},{8,10},{9,11},{10,... | collective-permute-start | bytes 196616 | tf_op jit(solution)/shard_map/ppermute | solution.py:278
  25.4 2.7 %collective-permute-start.10 = (bf16[32,1024]{1,0:T(8,128)(2,1)S(1)}, bf16[32,1024]{1,0:T(8,128)(2,1)S(1)}, u32[]{:S(2)}, u32[]{:S(2)}) collective-permute-start(bf16[32,1024]{1,0:T(8,128)(2,1)S(1)} %collective-permute-done.6.refs_1_), channel_id=1, source_target_pairs={{0,2},{1,3},{2,0},{3,1},{4,6},{5,7},{6,4},{7,5},{8,10},{9,11},{10,... | collective-permute-start | bytes 196616 | tf_op jit(solution)/shard_map/ppermute | solution.py:278
  26.9 1.3 %collective-permute-start.11 = (bf16[32,1024]{1,0:T(8,128)(2,1)S(1)}, bf16[32,1024]{1,0:T(8,128)(2,1)S(1)}, u32[]{:S(2)}, u32[]{:S(2)}) collective-permute-start(bf16[32,1024]{1,0:T(8,128)(2,1)S(1)} %collective-permute-done.7.refs_2_), channel_id=1, source_target_pairs={{0,2},{1,3},{2,0},{3,1},{4,6},{5,7},{6,4},{7,5},{8,10},{9,11},{10,... | collective-permute-start | bytes 196616 | tf_op jit(solution)/shard_map/ppermute | solution.py:278

commit v14 on v13

--- a/solution.py
+++ b/solution.py
@@ -333,10 +333,11 @@
     while stride < tok_count:
         copies = [jnp.concatenate([copies[0], swap(copies[0], tok=stride)], axis=0)] * 5
         stride *= 2
-    received = [swap(copies[0], tok=1, feat=2), swap(copies[1], feat=2), swap(copies[2], tok=1)]
-    last = swap(copies[3], tok=1, feat=1)
+    far = swap(copies[0], tok=1, feat=2)
+    crossed = swap(copies[1], tok=1, feat=1)
+    received = [far, swap(copies[2], feat=2), swap(copies[3], tok=1)]
     ours = copies[4:] + received
-    theirs = [swap(block, feat=1) for block in ours[:3]] + [last]
+    theirs = [swap(block, feat=1) for block in ours[:3]] + [crossed]
     concepts = C // tok_count
     gram = gram_blocks(ours + theirs, label_row, concepts, shard, C / (rows * tok_count))
     return gram.reshape(concepts, shard, kept)

time: 30.9 us -> 30.9 us (level)
  no operation moved by 1% of the time
where the time goes in v14:
time: 30.9 us; the launch traced here: 30.7 us
  starting transfers between devices  14.3 us (46%)
  waiting for transfers between devices  9.05 us (29%)
  Pallas kernels  7.26 us (23%)
    ppermute x13, starting transfers between devices, swap(): return lax.ppermute(array, ('feat', 'tok'), pairs)  14.3 us
    ppermute x13, waiting for transfers between devices, swap(): return lax.ppermute(array, ('feat', 'tok'), pairs)  9.05 us
    pallas_call x1, Pallas kernels, partial_halves(): pl.pallas_call(functools.partial(send_kernel, total_bits, parts), in_spec...  2.86 us
    pallas_call x1, Pallas kernels, gram_blocks(): pl.pallas_call(functools.partial(gram_kernel, shard, group, factor), in_s...  2.5 us
    pallas_call x1, Pallas kernels, partial_halves(): pl.pallas_call(functools.partial(keep_kernel, parts), out_shape=total_typ...  1.3 us
  transfers between devices with their start and end apart: 13, of which 7 were waited for; matrix products, arithmetic and copies ran while one was open for 0% of the time, Pallas kernels for 4%

profile of v14, /device:TPU:0, one launch (start us, length us, event | category | flops | bytes accessed | tf_op | source)
XLA Modules:
  0.0 30.7 jit_solution(5079360588577180882)
XLA Ops:
  0.0 2.9 %partial_sent.1 = (f32[64,1024]{1,0:T(8,128)S(1)}, bf16[64,8192]{1,0:T(8,128)(2,1)S(1)}, s32[1,8192]{1,0:T(1,128)S(1)}, bf16[256,1024]{1,0:T(8,128)(2,1)S(1)}, f32[32,1024]{1,0:T(8,128)S(1)}) custom-call(bf16[128,8192]{1,0:T(8,128)(2,1)} %x_hbm.1, s32[1,8192]{1,0:T(1,128)} %bitcast.5, s32[1,1024]{1,0:T(1,128)} %bitcast.6), custom_call_target="tpu_custom_call" | custom-call | flops 1073741824 | bytes 2359296 | tf_op jit(solution)/shard_map/partial_sent/pallas_call | solution.py:99
  2.9 0.5 %collective-permute-start = (f32[64,1024]{1,0:T(8,128)S(1)}, f32[64,1024]{1,0:T(8,128)S(1)}, u32[]{:S(2)}, u32[]{:S(2)}) collective-permute-start(f32[64,1024]{1,0:T(8,128)S(1)} %get-tuple-element.27), channel_id=1, source_target_pairs={{0,2},{1,3},{2,0},{3,1},{4,6},{5,7},{6,4},{7,5},{8,10},{9,11},{10,... | collective-permute-start | bytes 786440 | tf_op jit(solution)/shard_map/ppermute | solution.py:278
  3.4 1.3 %partial_kept.1.keep_ref = f32[64,1024]{1,0:T(8,128)S(1)} custom-call(bf16[64,8192]{1,0:T(8,128)(2,1)S(1)} %get-tuple-element.23.x_keep, s32[1,8192]{1,0:T(1,128)S(1)} %get-tuple-element.24.signs, bf16[256,1024]{1,0:T(8,128)(2,1)S(1)} %get-tuple-element.25.low, f32[32,1024]{1,0:T(8,128)S(1)} %get-tuple-element.26.high), custom_call_target="tpu_custom_call" | custom-call | flops 1073741824 | bytes 2359296 | tf_op jit(solution)/shard_map/partial_kept/pallas_call | solution.py:123
  4.7 0.2 first_split.1
  4.9 3.8 %collective-permute-start.1 = (s32[136,128]{1,0:T(8,128)S(1)}, s32[136,128]{1,0:T(8,128)S(1)}, u32[]{:S(2)}, u32[]{:S(2)}) collective-permute-start(s32[136,128]{1,0:T(8,128)S(1)} %get-tuple-element.29), channel_id=1, source_target_pairs={{0,12},{1,13},{2,14},{3,15},{4,8},{5,9},{6,10},{7,11},{8,4},{9,5},... | collective-permute-start | bytes 208904 | tf_op jit(solution)/shard_map/ppermute | solution.py:278
  8.6 0.5 %collective-permute-start.2 = (s32[136,128]{1,0:T(8,128)S(1)}, s32[136,128]{1,0:T(8,128)S(1)}, u32[]{:S(2)}, u32[]{:S(2)}) collective-permute-start(s32[136,128]{1,0:T(8,128)S(1)} %get-tuple-element.30), channel_id=1, source_target_pairs={{0,4},{1,5},{2,6},{3,7},{4,0},{5,1},{6,2},{7,3},{8,12},{9,13},{10,... | collective-permute-start | bytes 208904 | tf_op jit(solution)/shard_map/ppermute | solution.py:278
  9.2 0.1 collective-permute-start.3
  9.3 2.0 %collective-permute-done.1.both_ref = s32[136,128]{1,0:T(8,128)S(1)} collective-permute-done((s32[136,128]{1,0:T(8,128)S(1)}, s32[136,128]{1,0:T(8,128)S(1)}, u32[]{:S(2)}, u32[]{:S(2)}) %collective-permute-start.1) | collective-permute-done | bytes 69664 | tf_op jit(solution)/shard_map/ppermute | solution.py:278
  11.3 1.7 %collective-permute-done.2.x_ref = s32[136,128]{1,0:T(8,128)S(1)} collective-permute-done((s32[136,128]{1,0:T(8,128)S(1)}, s32[136,128]{1,0:T(8,128)S(1)}, u32[]{:S(2)}, u32[]{:S(2)}) %collective-permute-start.2) | collective-permute-done | bytes 69664 | tf_op jit(solution)/shard_map/ppermute | solution.py:278
  13.0 0.5 %collective-permute-done.3.z_ref = s32[136,128]{1,0:T(8,128)S(1)} collective-permute-done((s32[136,128]{1,0:T(8,128)S(1)}, s32[136,128]{1,0:T(8,128)S(1)}, u32[]{:S(2)}, u32[]{:S(2)}) %collective-permute-start.3) | collective-permute-done | bytes 69664 | tf_op jit(solution)/shard_map/ppermute | solution.py:278
  13.5 0.3 add_square.1
  13.8 2.7 %collective-permute-start.4 = (s32[136,128]{1,0:T(8,128)S(1)}, s32[136,128]{1,0:T(8,128)S(1)}, u32[]{:S(2)}, u32[]{:S(2)}) collective-permute-start(s32[136,128]{1,0:T(8,128)S(1)} %get-tuple-element.33), channel_id=1, source_target_pairs={{0,16},{1,17},{2,18},{3,19},{4,20},{5,21},{6,22},{7,23},{8,24},{9,... | collective-permute-start | bytes 208904 | tf_op jit(solution)/shard_map/ppermute | solution.py:278
  16.4 1.5 %collective-permute-start.5 = (s32[1,128]{1,0:T(1,128)S(1)}, s32[1,128]{1,0:T(1,128)S(1)}, u32[]{:S(2)}, u32[]{:S(2)}) collective-permute-start(s32[1,128]{1,0:T(1,128)S(1)} %get-tuple-element.34.refs_0_), channel_id=1, source_target_pairs={{0,1},{1,0},{2,3},{3,2},{4,5},{5,4},{6,7},{7,6},{8,9},{9,8},{10,11... | collective-permute-start | bytes 1544 | tf_op jit(solution)/shard_map/ppermute | solution.py:278
  17.9 2.0 %collective-permute-done.5.refs_1_ = s32[1,128]{1,0:T(1,128)S(1)} collective-permute-done((s32[1,128]{1,0:T(1,128)S(1)}, s32[1,128]{1,0:T(1,128)S(1)}, u32[]{:S(2)}, u32[]{:S(2)}) %collective-permute-start.5) | collective-permute-done | bytes 544 | tf_op jit(solution)/shard_map/ppermute | solution.py:278
  20.0 0.1 collective-permute-done.4.word_ref
  20.0 0.2 sketch_rows.1
  20.2 2.4 %collective-permute-start.6 = (bf16[32,1024]{1,0:T(8,128)(2,1)S(1)}, bf16[32,1024]{1,0:T(8,128)(2,1)S(1)}, u32[]{:S(2)}, u32[]{:S(2)}) collective-permute-start(bf16[32,1024]{1,0:T(8,128)(2,1)S(1)} %get-tuple-element.37), channel_id=1, source_target_pairs={{0,5},{1,4},{2,7},{3,6},{4,1},{5,0},{6,3},{7,2},{8,13},{9,12},{10,... | collective-permute-start | bytes 196616 | tf_op jit(solution)/shard_map/ppermute | solution.py:278
  22.6 0.6 %collective-permute-start.7 = (bf16[32,1024]{1,0:T(8,128)(2,1)S(1)}, bf16[32,1024]{1,0:T(8,128)(2,1)S(1)}, u32[]{:S(2)}, u32[]{:S(2)}) collective-permute-start(bf16[32,1024]{1,0:T(8,128)(2,1)S(1)} %get-tuple-element.38), channel_id=1, source_target_pairs={{0,4},{1,5},{2,6},{3,7},{4,0},{5,1},{6,2},{7,3},{8,12},{9,13},{10,... | collective-permute-start | bytes 196616 | tf_op jit(solution)/shard_map/ppermute | solution.py:278
  23.3 0.5 %collective-permute-start.8 = (bf16[32,1024]{1,0:T(8,128)(2,1)S(1)}, bf16[32,1024]{1,0:T(8,128)(2,1)S(1)}, u32[]{:S(2)}, u32[]{:S(2)}) collective-permute-start(bf16[32,1024]{1,0:T(8,128)(2,1)S(1)} %get-tuple-element.39), channel_id=1, source_target_pairs={{0,1},{1,0},{2,3},{3,2},{4,5},{5,4},{6,7},{7,6},{8,9},{9,8},{10,11... | collective-permute-start | bytes 196616 | tf_op jit(solution)/shard_map/ppermute | solution.py:278
  23.8 1.6 %collective-permute-start.9 = (bf16[32,1024]{1,0:T(8,128)(2,1)S(1)}, bf16[32,1024]{1,0:T(8,128)(2,1)S(1)}, u32[]{:S(2)}, u32[]{:S(2)}) collective-permute-start(bf16[32,1024]{1,0:T(8,128)(2,1)S(1)} %get-tuple-element.36.refs_0_), channel_id=1, source_target_pairs={{0,2},{1,3},{2,0},{3,1},{4,6},{5,7},{6,4},{7,5},{8,10},{9,11},{10,... | collective-permute-start | bytes 196616 | tf_op jit(solution)/shard_map/ppermute | solution.py:278
  25.4 0.0 collective-permute-done.6.refs_1_
  25.4 1.5 %collective-permute-done.7.refs_2_ = bf16[32,1024]{1,0:T(8,128)(2,1)S(1)} collective-permute-done((bf16[32,1024]{1,0:T(8,128)(2,1)S(1)}, bf16[32,1024]{1,0:T(8,128)(2,1)S(1)}, u32[]{:S(2)}, u32[]{:S(2)}) %collective-permute-start.7) | collective-permute-done | bytes 65568 | tf_op jit(solution)/shard_map/ppermute | solution.py:278
  26.9 1.2 %collective-permute-done.8.refs_3_ = bf16[32,1024]{1,0:T(8,128)(2,1)S(1)} collective-permute-done((bf16[32,1024]{1,0:T(8,128)(2,1)S(1)}, bf16[32,1024]{1,0:T(8,128)(2,1)S(1)}, u32[]{:S(2)}, u32[]{:S(2)}) %collective-permute-start.8) | collective-permute-done | bytes 65568 | tf_op jit(solution)/shard_map/ppermute | solution.py:278
  28.2 2.5 %gram.1 = f32[1024,1024]{1,0:T(8,128)} custom-call(s32[1,256]{1,0:T(1,128)S(1)} %get-tuple-element.35.label_ref, bf16[32,1024]{1,0:T(8,128)(2,1)S(1)} %get-tuple-element.36.refs_0_, bf16[32,1024]{1,0:T(8,128)(2,1)S(1)} %collective-permute-done.6.refs_1_, bf16[32,1024]{1,0:T(8,128)(2,1)S(1)} %collective-permute-done.7.refs_2_, ...), custom_call_target="tpu_custom_call" | custom-call | flops 536870912 | bytes 4194304 | tf_op jit(solution)/shard_map/gram/pallas_call | solution.py:165
  (10 shorter events, 0.0 us)
Async XLA Ops:
  0.0 4.7 %copy-start = (s32[128,1]{0,1:T(1,128)S(1)}, s32[128,1]{0,1:T(1,128)}, u32[]{:S(2)}) copy-start(s32[128,1]{0,1:T(1,128)} %param.7) | copy-start | bytes 1540
  2.9 1.8 %collective-permute-start = (f32[64,1024]{1,0:T(8,128)S(1)}, f32[64,1024]{1,0:T(8,128)S(1)}, u32[]{:S(2)}, u32[]{:S(2)}) collective-permute-start(f32[64,1024]{1,0:T(8,128)S(1)} %get-tuple-element.27), channel_id=1, source_target_pairs={{0,2},{1,3},{2,0},{3,1},{4,6},{5,7},{6,4},{7,5},{8,10},{9,11},{10,... | collective-permute-start | bytes 786440 | tf_op jit(solution)/shard_map/ppermute | solution.py:278
  4.9 6.4 %collective-permute-start.1 = (s32[136,128]{1,0:T(8,128)S(1)}, s32[136,128]{1,0:T(8,128)S(1)}, u32[]{:S(2)}, u32[]{:S(2)}) collective-permute-start(s32[136,128]{1,0:T(8,128)S(1)} %get-tuple-element.29), channel_id=1, source_target_pairs={{0,12},{1,13},{2,14},{3,15},{4,8},{5,9},{6,10},{7,11},{8,4},{9,5},... | collective-permute-start | bytes 208904 | tf_op jit(solution)/shard_map/ppermute | solution.py:278
  8.6 4.3 %collective-permute-start.2 = (s32[136,128]{1,0:T(8,128)S(1)}, s32[136,128]{1,0:T(8,128)S(1)}, u32[]{:S(2)}, u32[]{:S(2)}) collective-permute-start(s32[136,128]{1,0:T(8,128)S(1)} %get-tuple-element.30), channel_id=1, source_target_pairs={{0,4},{1,5},{2,6},{3,7},{4,0},{5,1},{6,2},{7,3},{8,12},{9,13},{10,... | collective-permute-start | bytes 208904 | tf_op jit(solution)/shard_map/ppermute | solution.py:278
  9.2 4.3 %collective-permute-start.3 = (s32[136,128]{1,0:T(8,128)S(1)}, s32[136,128]{1,0:T(8,128)S(1)}, u32[]{:S(2)}, u32[]{:S(2)}) collective-permute-start(s32[136,128]{1,0:T(8,128)S(1)} %get-tuple-element.31), channel_id=1, source_target_pairs={{0,8},{1,9},{2,10},{3,11},{4,12},{5,13},{6,14},{7,15},{8,0},{9,1},... | collective-permute-start | bytes 208904 | tf_op jit(solution)/shard_map/ppermute | solution.py:278
  13.8 6.3 %collective-permute-start.4 = (s32[136,128]{1,0:T(8,128)S(1)}, s32[136,128]{1,0:T(8,128)S(1)}, u32[]{:S(2)}, u32[]{:S(2)}) collective-permute-start(s32[136,128]{1,0:T(8,128)S(1)} %get-tuple-element.33), channel_id=1, source_target_pairs={{0,16},{1,17},{2,18},{3,19},{4,20},{5,21},{6,22},{7,23},{8,24},{9,... | collective-permute-start | bytes 208904 | tf_op jit(solution)/shard_map/ppermute | solution.py:278
  16.4 3.5 %collective-permute-start.5 = (s32[1,128]{1,0:T(1,128)S(1)}, s32[1,128]{1,0:T(1,128)S(1)}, u32[]{:S(2)}, u32[]{:S(2)}) collective-permute-start(s32[1,128]{1,0:T(1,128)S(1)} %get-tuple-element.34.refs_0_), channel_id=1, source_target_pairs={{0,1},{1,0},{2,3},{3,2},{4,5},{5,4},{6,7},{7,6},{8,9},{9,8},{10,11... | collective-permute-start | bytes 1544 | tf_op jit(solution)/shard_map/ppermute | solution.py:278
  20.2 5.2 %collective-permute-start.6 = (bf16[32,1024]{1,0:T(8,128)(2,1)S(1)}, bf16[32,1024]{1,0:T(8,128)(2,1)S(1)}, u32[]{:S(2)}, u32[]{:S(2)}) collective-permute-start(bf16[32,1024]{1,0:T(8,128)(2,1)S(1)} %get-tuple-element.37), channel_id=1, source_target_pairs={{0,5},{1,4},{2,7},{3,6},{4,1},{5,0},{6,3},{7,2},{8,13},{9,12},{10,... | collective-permute-start | bytes 196616 | tf_op jit(solution)/shard_map/ppermute | solution.py:278
  22.6 4.3 %collective-permute-start.7 = (bf16[32,1024]{1,0:T(8,128)(2,1)S(1)}, bf16[32,1024]{1,0:T(8,128)(2,1)S(1)}, u32[]{:S(2)}, u32[]{:S(2)}) collective-permute-start(bf16[32,1024]{1,0:T(8,128)(2,1)S(1)} %get-tuple-element.38), channel_id=1, source_target_pairs={{0,4},{1,5},{2,6},{3,7},{4,0},{5,1},{6,2},{7,3},{8,12},{9,13},{10,... | collective-permute-start | bytes 196616 | tf_op jit(solution)/shard_map/ppermute | solution.py:278
  23.3 4.9 %collective-permute-start.8 = (bf16[32,1024]{1,0:T(8,128)(2,1)S(1)}, bf16[32,1024]{1,0:T(8,128)(2,1)S(1)}, u32[]{:S(2)}, u32[]{:S(2)}) collective-permute-start(bf16[32,1024]{1,0:T(8,128)(2,1)S(1)} %get-tuple-element.39), channel_id=1, source_target_pairs={{0,1},{1,0},{2,3},{3,2},{4,5},{5,4},{6,7},{7,6},{8,9},{9,8},{10,11... | collective-permute-start | bytes 196616 | tf_op jit(solution)/shard_map/ppermute | solution.py:278
  23.8 4.4 %collective-permute-start.12 = (bf16[32,1024]{1,0:T(8,128)(2,1)S(1)}, bf16[32,1024]{1,0:T(8,128)(2,1)S(1)}, u32[]{:S(2)}, u32[]{:S(2)}) collective-permute-start(bf16[32,1024]{1,0:T(8,128)(2,1)S(1)} %get-tuple-element.40), channel_id=1, source_target_pairs={{0,3},{1,2},{2,1},{3,0},{4,7},{5,6},{6,5},{7,4},{8,11},{9,10},{10,... | collective-permute-start | bytes 196616 | tf_op jit(solution)/shard_map/ppermute | solution.py:278
  23.8 4.4 %collective-permute-start.9 = (bf16[32,1024]{1,0:T(8,128)(2,1)S(1)}, bf16[32,1024]{1,0:T(8,128)(2,1)S(1)}, u32[]{:S(2)}, u32[]{:S(2)}) collective-permute-start(bf16[32,1024]{1,0:T(8,128)(2,1)S(1)} %get-tuple-element.36.refs_0_), channel_id=1, source_target_pairs={{0,2},{1,3},{2,0},{3,1},{4,6},{5,7},{6,4},{7,5},{8,10},{9,11},{10,... | collective-permute-start | bytes 196616 | tf_op jit(solution)/shard_map/ppermute | solution.py:278
  25.4 2.7 %collective-permute-start.10 = (bf16[32,1024]{1,0:T(8,128)(2,1)S(1)}, bf16[32,1024]{1,0:T(8,128)(2,1)S(1)}, u32[]{:S(2)}, u32[]{:S(2)}) collective-permute-start(bf16[32,1024]{1,0:T(8,128)(2,1)S(1)} %collective-permute-done.6.refs_1_), channel_id=1, source_target_pairs={{0,2},{1,3},{2,0},{3,1},{4,6},{5,7},{6,4},{7,5},{8,10},{9,11},{10,... | collective-permute-start | bytes 196616 | tf_op jit(solution)/shard_map/ppermute | solution.py:278
  26.9 1.3 %collective-permute-start.11 = (bf16[32,1024]{1,0:T(8,128)(2,1)S(1)}, bf16[32,1024]{1,0:T(8,128)(2,1)S(1)}, u32[]{:S(2)}, u32[]{:S(2)}) collective-permute-start(bf16[32,1024]{1,0:T(8,128)(2,1)S(1)} %collective-permute-done.7.refs_2_), channel_id=1, source_target_pairs={{0,2},{1,3},{2,0},{3,1},{4,6},{5,7},{6,4},{7,5},{8,10},{9,11},{10,... | collective-permute-start | bytes 196616 | tf_op jit(solution)/shard_map/ppermute | solution.py:278

commit v15 on v13

--- a/solution.py
+++ b/solution.py
@@ -247,10 +247,9 @@
     digit = lax.rem(lax.axis_index("feat") // 2, 2)
     groups = LANES // size
     lane = lax.broadcasted_iota(jnp.int32, (8, LANES), 1)
-    for place in range(0, 2 * len(blocks), groups):
+    for place in range(0, len(blocks), groups):
         out = jnp.zeros((8, LANES), jnp.int32)
-        for at in range(groups):
-            half, (tok, x) = (place + at) // len(blocks), blocks[(place + at) % len(blocks)]
+        for at, (half, tok, x) in enumerate(blocks[place:place + groups]):
             source = (core ^ half) * 2 * size + (digit ^ x) * size
             moved = pltpu.roll(
                 jnp.broadcast_to(label_refs[tok][...], out.shape), lax.rem(at * size - source + LANES, LANES), 1
@@ -314,12 +313,13 @@
         word = swap(word, feat=stride)
         stride *= 2
 
-    blocks = [(0, 0)]
+    toks = [0]
     stride = 2
     while stride < tok_count:
-        blocks = blocks + [(tok ^ stride, x) for tok, x in blocks]
+        toks = toks + [tok ^ stride for tok in toks]
         stride *= 2
-    blocks = [(tok ^ flip, x) for flip, x in ((0, 0), (1, 1), (0, 1), (1, 0)) for tok, _ in blocks]
+    order = [(0, 1, 1), (1, 1, 0), (0, 0, 1), (0, 1, 0), (0, 0, 0), (1, 1, 1), (1, 0, 1), (1, 0, 0)]
+    blocks = [(core, tok ^ flip, x) for core, flip, x in order for tok in toks]
     scale = 1.0 / math.sqrt(width * feat_count)
     label_row, *copies = local_call(
         functools.partial(last_kernel, scale, blocks),
@@ -327,18 +327,19 @@
         total,
         word,
         *all_labels,
-        out_shape=[jax.ShapeDtypeStruct((1, 2 * len(blocks) * size), jnp.int32)] + [row_type] * 5,
+        out_shape=[jax.ShapeDtypeStruct((1, len(blocks) * size), jnp.int32)] + [row_type] * 5,
     )
     stride = 2
     while stride < tok_count:
         copies = [jnp.concatenate([copies[0], swap(copies[0], tok=stride)], axis=0)] * 5
         stride *= 2
-    received = [swap(copies[0], tok=1, feat=2), swap(copies[1], feat=2), swap(copies[2], tok=1)]
-    last = swap(copies[3], tok=1, feat=1)
-    ours = copies[4:] + received
-    theirs = [swap(block, feat=1) for block in ours[:3]] + [last]
+    far, crossed, beside, across, own = [
+        swap(copy, tok=tok, feat=2 * x + core) if core + tok + x else copy
+        for copy, (core, tok, x) in zip(copies, order)
+    ]
+    pieces = [far, crossed, beside, across, own] + [swap(block, feat=1) for block in (far, beside, own)]
     concepts = C // tok_count
-    gram = gram_blocks(ours + theirs, label_row, concepts, shard, C / (rows * tok_count))
+    gram = gram_blocks(pieces, label_row, concepts, shard, C / (rows * tok_count))
     return gram.reshape(concepts, shard, kept)
 
 

time: 30.9 us -> 30.9 us (level)
  waiting for transfers between devices: 9.05 us -> 9.37 us
    ppermute x13, waiting for transfers between devices: 9.05 us -> 9.37 us  [swap(): return lax.ppermute(array, ('feat', 'tok'), pairs)]
  transfers between devices with their start and end apart: 13 -> 13, of which waited for: 7 -> 9; matrix products, arithmetic and copies ran while one was open for 0% -> 0% of each run, Pallas kernels for 4% -> 4%
where the time goes in v15:
time: 30.9 us; the launch traced here: 30.7 us
  starting transfers between devices  14 us (45%)
  waiting for transfers between devices  9.37 us (30%)
  Pallas kernels  7.27 us (24%)
    ppermute x13, starting transfers between devices, swap(): return lax.ppermute(array, ('feat', 'tok'), pairs)  14 us
    ppermute x13, waiting for transfers between devices, swap(): return lax.ppermute(array, ('feat', 'tok'), pairs)  9.37 us
    pallas_call x1, Pallas kernels, partial_halves(): pl.pallas_call(functools.partial(send_kernel, total_bits, parts), in_spec...  2.86 us
    pallas_call x1, Pallas kernels, gram_blocks(): pl.pallas_call(functools.partial(gram_kernel, shard, group, factor), in_s...  2.51 us
    pallas_call x1, Pallas kernels, partial_halves(): pl.pallas_call(functools.partial(keep_kernel, parts), out_shape=total_typ...  1.3 us
  transfers between devices with their start and end apart: 13, of which 9 were waited for; matrix products, arithmetic and copies ran while one was open for 0% of the time, Pallas kernels for 4%

profile of v15, /device:TPU:0, one launch (start us, length us, event | category | flops | bytes accessed | tf_op | source)
XLA Modules:
  0.0 30.7 jit_solution(5497015222760501944)
XLA Ops:
  0.0 2.9 %partial_sent.1 = (f32[64,1024]{1,0:T(8,128)S(1)}, bf16[64,8192]{1,0:T(8,128)(2,1)S(1)}, s32[1,8192]{1,0:T(1,128)S(1)}, bf16[256,1024]{1,0:T(8,128)(2,1)S(1)}, f32[32,1024]{1,0:T(8,128)S(1)}) custom-call(bf16[128,8192]{1,0:T(8,128)(2,1)} %x_hbm.1, s32[1,8192]{1,0:T(1,128)} %bitcast.5, s32[1,1024]{1,0:T(1,128)} %bitcast.6), custom_call_target="tpu_custom_call" | custom-call | flops 1073741824 | bytes 2359296 | tf_op jit(solution)/shard_map/partial_sent/pallas_call | solution.py:99
  2.9 0.5 %collective-permute-start = (f32[64,1024]{1,0:T(8,128)S(1)}, f32[64,1024]{1,0:T(8,128)S(1)}, u32[]{:S(2)}, u32[]{:S(2)}) collective-permute-start(f32[64,1024]{1,0:T(8,128)S(1)} %get-tuple-element.27), channel_id=1, source_target_pairs={{0,2},{1,3},{2,0},{3,1},{4,6},{5,7},{6,4},{7,5},{8,10},{9,11},{10,... | collective-permute-start | bytes 786440 | tf_op jit(solution)/shard_map/ppermute | solution.py:277
  3.4 1.3 %partial_kept.1.keep_ref = f32[64,1024]{1,0:T(8,128)S(1)} custom-call(bf16[64,8192]{1,0:T(8,128)(2,1)S(1)} %get-tuple-element.23.x_keep, s32[1,8192]{1,0:T(1,128)S(1)} %get-tuple-element.24.signs, bf16[256,1024]{1,0:T(8,128)(2,1)S(1)} %get-tuple-element.25.low, f32[32,1024]{1,0:T(8,128)S(1)} %get-tuple-element.26.high), custom_call_target="tpu_custom_call" | custom-call | flops 1073741824 | bytes 2359296 | tf_op jit(solution)/shard_map/partial_kept/pallas_call | solution.py:123
  4.7 0.2 first_split.1
  4.9 3.8 %collective-permute-start.1 = (s32[136,128]{1,0:T(8,128)S(1)}, s32[136,128]{1,0:T(8,128)S(1)}, u32[]{:S(2)}, u32[]{:S(2)}) collective-permute-start(s32[136,128]{1,0:T(8,128)S(1)} %get-tuple-element.29), channel_id=1, source_target_pairs={{0,12},{1,13},{2,14},{3,15},{4,8},{5,9},{6,10},{7,11},{8,4},{9,5},... | collective-permute-start | bytes 208904 | tf_op jit(solution)/shard_map/ppermute | solution.py:277
  8.6 0.5 %collective-permute-start.2 = (s32[136,128]{1,0:T(8,128)S(1)}, s32[136,128]{1,0:T(8,128)S(1)}, u32[]{:S(2)}, u32[]{:S(2)}) collective-permute-start(s32[136,128]{1,0:T(8,128)S(1)} %get-tuple-element.30), channel_id=1, source_target_pairs={{0,4},{1,5},{2,6},{3,7},{4,0},{5,1},{6,2},{7,3},{8,12},{9,13},{10,... | collective-permute-start | bytes 208904 | tf_op jit(solution)/shard_map/ppermute | solution.py:277
  9.2 0.1 collective-permute-start.3
  9.3 2.0 %collective-permute-done.1.both_ref = s32[136,128]{1,0:T(8,128)S(1)} collective-permute-done((s32[136,128]{1,0:T(8,128)S(1)}, s32[136,128]{1,0:T(8,128)S(1)}, u32[]{:S(2)}, u32[]{:S(2)}) %collective-permute-start.1) | collective-permute-done | bytes 69664 | tf_op jit(solution)/shard_map/ppermute | solution.py:277
  11.3 1.7 %collective-permute-done.2.x_ref = s32[136,128]{1,0:T(8,128)S(1)} collective-permute-done((s32[136,128]{1,0:T(8,128)S(1)}, s32[136,128]{1,0:T(8,128)S(1)}, u32[]{:S(2)}, u32[]{:S(2)}) %collective-permute-start.2) | collective-permute-done | bytes 69664 | tf_op jit(solution)/shard_map/ppermute | solution.py:277
  13.0 0.5 %collective-permute-done.3.z_ref = s32[136,128]{1,0:T(8,128)S(1)} collective-permute-done((s32[136,128]{1,0:T(8,128)S(1)}, s32[136,128]{1,0:T(8,128)S(1)}, u32[]{:S(2)}, u32[]{:S(2)}) %collective-permute-start.3) | collective-permute-done | bytes 69664 | tf_op jit(solution)/shard_map/ppermute | solution.py:277
  13.5 0.3 add_square.1
  13.8 2.7 %collective-permute-start.4 = (s32[136,128]{1,0:T(8,128)S(1)}, s32[136,128]{1,0:T(8,128)S(1)}, u32[]{:S(2)}, u32[]{:S(2)}) collective-permute-start(s32[136,128]{1,0:T(8,128)S(1)} %get-tuple-element.33), channel_id=1, source_target_pairs={{0,16},{1,17},{2,18},{3,19},{4,20},{5,21},{6,22},{7,23},{8,24},{9,... | collective-permute-start | bytes 208904 | tf_op jit(solution)/shard_map/ppermute | solution.py:277
  16.4 1.5 %collective-permute-start.5 = (s32[1,128]{1,0:T(1,128)S(1)}, s32[1,128]{1,0:T(1,128)S(1)}, u32[]{:S(2)}, u32[]{:S(2)}) collective-permute-start(s32[1,128]{1,0:T(1,128)S(1)} %get-tuple-element.34.refs_0_), channel_id=1, source_target_pairs={{0,1},{1,0},{2,3},{3,2},{4,5},{5,4},{6,7},{7,6},{8,9},{9,8},{10,11... | collective-permute-start | bytes 1544 | tf_op jit(solution)/shard_map/ppermute | solution.py:277
  17.9 2.0 %collective-permute-done.5.refs_1_ = s32[1,128]{1,0:T(1,128)S(1)} collective-permute-done((s32[1,128]{1,0:T(1,128)S(1)}, s32[1,128]{1,0:T(1,128)S(1)}, u32[]{:S(2)}, u32[]{:S(2)}) %collective-permute-start.5) | collective-permute-done | bytes 544 | tf_op jit(solution)/shard_map/ppermute | solution.py:277
  20.0 0.2 sketch_rows.1
  20.2 2.4 %collective-permute-start.6 = (bf16[32,1024]{1,0:T(8,128)(2,1)S(1)}, bf16[32,1024]{1,0:T(8,128)(2,1)S(1)}, u32[]{:S(2)}, u32[]{:S(2)}) collective-permute-start(bf16[32,1024]{1,0:T(8,128)(2,1)S(1)} %get-tuple-element.36), channel_id=1, source_target_pairs={{0,5},{1,4},{2,7},{3,6},{4,1},{5,0},{6,3},{7,2},{8,13},{9,12},{10,... | collective-permute-start | bytes 196616 | tf_op jit(solution)/shard_map/ppermute | solution.py:277
  22.6 0.6 %collective-permute-start.8 = (bf16[32,1024]{1,0:T(8,128)(2,1)S(1)}, bf16[32,1024]{1,0:T(8,128)(2,1)S(1)}, u32[]{:S(2)}, u32[]{:S(2)}) collective-permute-start(bf16[32,1024]{1,0:T(8,128)(2,1)S(1)} %get-tuple-element.38), channel_id=1, source_target_pairs={{0,4},{1,5},{2,6},{3,7},{4,0},{5,1},{6,2},{7,3},{8,12},{9,13},{10,... | collective-permute-start | bytes 196616 | tf_op jit(solution)/shard_map/ppermute | solution.py:277
  23.3 0.5 %collective-permute-start.9 = (bf16[32,1024]{1,0:T(8,128)(2,1)S(1)}, bf16[32,1024]{1,0:T(8,128)(2,1)S(1)}, u32[]{:S(2)}, u32[]{:S(2)}) collective-permute-start(bf16[32,1024]{1,0:T(8,128)(2,1)S(1)} %get-tuple-element.39), channel_id=1, source_target_pairs={{0,1},{1,0},{2,3},{3,2},{4,5},{5,4},{6,7},{7,6},{8,9},{9,8},{10,11... | collective-permute-start | bytes 196616 | tf_op jit(solution)/shard_map/ppermute | solution.py:277
  23.8 1.3 %collective-permute-start.12 = (bf16[32,1024]{1,0:T(8,128)(2,1)S(1)}, bf16[32,1024]{1,0:T(8,128)(2,1)S(1)}, u32[]{:S(2)}, u32[]{:S(2)}) collective-permute-start(bf16[32,1024]{1,0:T(8,128)(2,1)S(1)} %get-tuple-element.40.refs_4_), channel_id=1, source_target_pairs={{0,2},{1,3},{2,0},{3,1},{4,6},{5,7},{6,4},{7,5},{8,10},{9,11},{10,... | collective-permute-start | bytes 196616 | tf_op jit(solution)/shard_map/ppermute | solution.py:277
  25.1 0.3 %collective-permute-done.6.refs_0_ = bf16[32,1024]{1,0:T(8,128)(2,1)S(1)} collective-permute-done((bf16[32,1024]{1,0:T(8,128)(2,1)S(1)}, bf16[32,1024]{1,0:T(8,128)(2,1)S(1)}, u32[]{:S(2)}, u32[]{:S(2)}) %collective-permute-start.6) | collective-permute-done | bytes 65568 | tf_op jit(solution)/shard_map/ppermute | solution.py:277
  25.4 1.5 %collective-permute-done.8.refs_2_ = bf16[32,1024]{1,0:T(8,128)(2,1)S(1)} collective-permute-done((bf16[32,1024]{1,0:T(8,128)(2,1)S(1)}, bf16[32,1024]{1,0:T(8,128)(2,1)S(1)}, u32[]{:S(2)}, u32[]{:S(2)}) %collective-permute-start.8) | collective-permute-done | bytes 65568 | tf_op jit(solution)/shard_map/ppermute | solution.py:277
  26.9 0.2 collective-permute-done.7.refs_1_
  27.1 1.1 %collective-permute-done.9.refs_3_ = bf16[32,1024]{1,0:T(8,128)(2,1)S(1)} collective-permute-done((bf16[32,1024]{1,0:T(8,128)(2,1)S(1)}, bf16[32,1024]{1,0:T(8,128)(2,1)S(1)}, u32[]{:S(2)}, u32[]{:S(2)}) %collective-permute-start.9) | collective-permute-done | bytes 65568 | tf_op jit(solution)/shard_map/ppermute | solution.py:277
  28.2 2.5 %gram.1 = f32[1024,1024]{1,0:T(8,128)} custom-call(s32[1,256]{1,0:T(1,128)S(1)} %get-tuple-element.35.label_ref, bf16[32,1024]{1,0:T(8,128)(2,1)S(1)} %collective-permute-done.6.refs_0_, bf16[32,1024]{1,0:T(8,128)(2,1)S(1)} %collective-permute-done.7.refs_1_, bf16[32,1024]{1,0:T(8,128)(2,1)S(1)} %collective-permute-done.8.refs_2_, ...), custom_call_target="tpu_custom_call" | custom-call | flops 536870912 | bytes 4194304 | tf_op jit(solution)/shard_map/gram/pallas_call | solution.py:165
  (10 shorter events, 0.1 us)
Async XLA Ops:
  0.0 4.7 %copy-start = (s32[128,1]{0,1:T(1,128)S(1)}, s32[128,1]{0,1:T(1,128)}, u32[]{:S(2)}) copy-start(s32[128,1]{0,1:T(1,128)} %param.7) | copy-start | bytes 1540
  2.9 1.8 %collective-permute-start = (f32[64,1024]{1,0:T(8,128)S(1)}, f32[64,1024]{1,0:T(8,128)S(1)}, u32[]{:S(2)}, u32[]{:S(2)}) collective-permute-start(f32[64,1024]{1,0:T(8,128)S(1)} %get-tuple-element.27), channel_id=1, source_target_pairs={{0,2},{1,3},{2,0},{3,1},{4,6},{5,7},{6,4},{7,5},{8,10},{9,11},{10,... | collective-permute-start | bytes 786440 | tf_op jit(solution)/shard_map/ppermute | solution.py:277
  4.9 6.4 %collective-permute-start.1 = (s32[136,128]{1,0:T(8,128)S(1)}, s32[136,128]{1,0:T(8,128)S(1)}, u32[]{:S(2)}, u32[]{:S(2)}) collective-permute-start(s32[136,128]{1,0:T(8,128)S(1)} %get-tuple-element.29), channel_id=1, source_target_pairs={{0,12},{1,13},{2,14},{3,15},{4,8},{5,9},{6,10},{7,11},{8,4},{9,5},... | collective-permute-start | bytes 208904 | tf_op jit(solution)/shard_map/ppermute | solution.py:277
  8.6 4.3 %collective-permute-start.2 = (s32[136,128]{1,0:T(8,128)S(1)}, s32[136,128]{1,0:T(8,128)S(1)}, u32[]{:S(2)}, u32[]{:S(2)}) collective-permute-start(s32[136,128]{1,0:T(8,128)S(1)} %get-tuple-element.30), channel_id=1, source_target_pairs={{0,4},{1,5},{2,6},{3,7},{4,0},{5,1},{6,2},{7,3},{8,12},{9,13},{10,... | collective-permute-start | bytes 208904 | tf_op jit(solution)/shard_map/ppermute | solution.py:277
  9.2 4.3 %collective-permute-start.3 = (s32[136,128]{1,0:T(8,128)S(1)}, s32[136,128]{1,0:T(8,128)S(1)}, u32[]{:S(2)}, u32[]{:S(2)}) collective-permute-start(s32[136,128]{1,0:T(8,128)S(1)} %get-tuple-element.31), channel_id=1, source_target_pairs={{0,8},{1,9},{2,10},{3,11},{4,12},{5,13},{6,14},{7,15},{8,0},{9,1},... | collective-permute-start | bytes 208904 | tf_op jit(solution)/shard_map/ppermute | solution.py:277
  13.8 6.3 %collective-permute-start.4 = (s32[136,128]{1,0:T(8,128)S(1)}, s32[136,128]{1,0:T(8,128)S(1)}, u32[]{:S(2)}, u32[]{:S(2)}) collective-permute-start(s32[136,128]{1,0:T(8,128)S(1)} %get-tuple-element.33), channel_id=1, source_target_pairs={{0,16},{1,17},{2,18},{3,19},{4,20},{5,21},{6,22},{7,23},{8,24},{9,... | collective-permute-start | bytes 208904 | tf_op jit(solution)/shard_map/ppermute | solution.py:277
  16.4 3.5 %collective-permute-start.5 = (s32[1,128]{1,0:T(1,128)S(1)}, s32[1,128]{1,0:T(1,128)S(1)}, u32[]{:S(2)}, u32[]{:S(2)}) collective-permute-start(s32[1,128]{1,0:T(1,128)S(1)} %get-tuple-element.34.refs_0_), channel_id=1, source_target_pairs={{0,1},{1,0},{2,3},{3,2},{4,5},{5,4},{6,7},{7,6},{8,9},{9,8},{10,11... | collective-permute-start | bytes 1544 | tf_op jit(solution)/shard_map/ppermute | solution.py:277
  20.2 5.2 %collective-permute-start.6 = (bf16[32,1024]{1,0:T(8,128)(2,1)S(1)}, bf16[32,1024]{1,0:T(8,128)(2,1)S(1)}, u32[]{:S(2)}, u32[]{:S(2)}) collective-permute-start(bf16[32,1024]{1,0:T(8,128)(2,1)S(1)} %get-tuple-element.36), channel_id=1, source_target_pairs={{0,5},{1,4},{2,7},{3,6},{4,1},{5,0},{6,3},{7,2},{8,13},{9,12},{10,... | collective-permute-start | bytes 196616 | tf_op jit(solution)/shard_map/ppermute | solution.py:277
  22.6 4.3 %collective-permute-start.8 = (bf16[32,1024]{1,0:T(8,128)(2,1)S(1)}, bf16[32,1024]{1,0:T(8,128)(2,1)S(1)}, u32[]{:S(2)}, u32[]{:S(2)}) collective-permute-start(bf16[32,1024]{1,0:T(8,128)(2,1)S(1)} %get-tuple-element.38), channel_id=1, source_target_pairs={{0,4},{1,5},{2,6},{3,7},{4,0},{5,1},{6,2},{7,3},{8,12},{9,13},{10,... | collective-permute-start | bytes 196616 | tf_op jit(solution)/shard_map/ppermute | solution.py:277
  23.3 3.8 %collective-permute-start.7 = (bf16[32,1024]{1,0:T(8,128)(2,1)S(1)}, bf16[32,1024]{1,0:T(8,128)(2,1)S(1)}, u32[]{:S(2)}, u32[]{:S(2)}) collective-permute-start(bf16[32,1024]{1,0:T(8,128)(2,1)S(1)} %get-tuple-element.37), channel_id=1, source_target_pairs={{0,3},{1,2},{2,1},{3,0},{4,7},{5,6},{6,5},{7,4},{8,11},{9,10},{10,... | collective-permute-start | bytes 196616 | tf_op jit(solution)/shard_map/ppermute | solution.py:277
  23.3 4.9 %collective-permute-start.9 = (bf16[32,1024]{1,0:T(8,128)(2,1)S(1)}, bf16[32,1024]{1,0:T(8,128)(2,1)S(1)}, u32[]{:S(2)}, u32[]{:S(2)}) collective-permute-start(bf16[32,1024]{1,0:T(8,128)(2,1)S(1)} %get-tuple-element.39), channel_id=1, source_target_pairs={{0,1},{1,0},{2,3},{3,2},{4,5},{5,4},{6,7},{7,6},{8,9},{9,8},{10,11... | collective-permute-start | bytes 196616 | tf_op jit(solution)/shard_map/ppermute | solution.py:277
  23.8 4.4 %collective-permute-start.12 = (bf16[32,1024]{1,0:T(8,128)(2,1)S(1)}, bf16[32,1024]{1,0:T(8,128)(2,1)S(1)}, u32[]{:S(2)}, u32[]{:S(2)}) collective-permute-start(bf16[32,1024]{1,0:T(8,128)(2,1)S(1)} %get-tuple-element.40.refs_4_), channel_id=1, source_target_pairs={{0,2},{1,3},{2,0},{3,1},{4,6},{5,7},{6,4},{7,5},{8,10},{9,11},{10,... | collective-permute-start | bytes 196616 | tf_op jit(solution)/shard_map/ppermute | solution.py:277
  25.4 2.8 %collective-permute-start.10 = (bf16[32,1024]{1,0:T(8,128)(2,1)S(1)}, bf16[32,1024]{1,0:T(8,128)(2,1)S(1)}, u32[]{:S(2)}, u32[]{:S(2)}) collective-permute-start(bf16[32,1024]{1,0:T(8,128)(2,1)S(1)} %collective-permute-done.6.refs_0_), channel_id=1, source_target_pairs={{0,2},{1,3},{2,0},{3,1},{4,6},{5,7},{6,4},{7,5},{8,10},{9,11},{10,... | collective-permute-start | bytes 196616 | tf_op jit(solution)/shard_map/ppermute | solution.py:277
  26.9 1.3 %collective-permute-start.11 = (bf16[32,1024]{1,0:T(8,128)(2,1)S(1)}, bf16[32,1024]{1,0:T(8,128)(2,1)S(1)}, u32[]{:S(2)}, u32[]{:S(2)}) collective-permute-start(bf16[32,1024]{1,0:T(8,128)(2,1)S(1)} %collective-permute-done.8.refs_2_), channel_id=1, source_target_pairs={{0,2},{1,3},{2,0},{3,1},{4,6},{5,7},{6,4},{7,5},{8,10},{9,11},{10,... | collective-permute-start | bytes 196616 | tf_op jit(solution)/shard_map/ppermute | solution.py:277

commit v16 on v13

--- a/solution.py
+++ b/solution.py
@@ -59,10 +59,9 @@
         cols = pl.ds(part * wide, wide)
         rows = pl.ds(pl.multiple_of((1 - mine) * half, half), half)
         copies.append(pltpu.make_async_copy(x_hbm.at[rows, cols], x_buf.at[:, cols], sems.at[part]))
-        copies[-1].start()
+    copies[0].start()
     rows = pl.ds(pl.multiple_of(mine * half, half), half)
-    keep_copy = pltpu.make_async_copy(x_hbm.at[rows, :], x_keep, sems.at[parts + 2])
-    keep_copy.start()
+    copies.append(pltpu.make_async_copy(x_hbm.at[rows, :], x_keep, sems.at[parts + 2]))
     col_copy.wait()
     col = col_buf[...]
     index = lax.broadcasted_iota(jnp.int32, (16, kept), 0)
@@ -75,8 +74,9 @@
     sign_copy.wait()
     for part in range(parts):
         copies[part].wait()
+        copies[part + 1].start()
         add_products(x_buf, signs, low, high, send_ref, part, wide)
-    keep_copy.wait()
+    copies[parts].wait()
 
 
 def keep_kernel(parts, x_keep, signs, low, high, keep_ref):
@@ -146,12 +146,19 @@
     base = lax.axis_index("tok") * steps * group
     copies = []
     for step in range(steps):
-        chosen = jnp.where(label == base + step * group, own, 0.0).astype(jnp.bfloat16)
-        blocks[step] = jnp.dot(chosen, rows[...], preferred_element_type=jnp.float32)
-        copies.append(
-            pltpu.make_async_copy(blocks.at[step], out_hbm.at[pl.ds(step * wide, wide), :], sems.at[step])
-        )
-        copies[-1].start()
+        for span in ((0, shard), (shard, wide)) if step == 0 and wide > shard else ((0, wide),):
+            part = slice(*span)
+            chosen = jnp.where(label[part] == base + step * group, own[part], 0.0).astype(jnp.bfloat16)
+            blocks[step, part] = jnp.dot(chosen, rows[...], preferred_element_type=jnp.float32)
+            size = span[1] - span[0]
+            copies.append(
+                pltpu.make_async_copy(
+                    blocks.at[step, pl.ds(span[0], size), :],
+                    out_hbm.at[pl.ds(step * wide + span[0], size), :],
+                    sems.at[len(copies)],
+                )
+            )
+            copies[-1].start()
     for copy in copies:
         copy.wait()
 
@@ -170,7 +177,7 @@
         scratch_shapes=[
             pltpu.VMEM((tokens, kept), jnp.bfloat16),
             pltpu.VMEM((steps, wide, kept), jnp.float32),
-            pltpu.SemaphoreType.DMA((steps,)),
+            pltpu.SemaphoreType.DMA((steps + 1,)),
         ],
         compiler_params=pltpu.CompilerParams(vmem_limit_bytes=VMEM_LIMIT),
         cost_estimate=pl.CostEstimate(

time: 30.9 us -> 33.3 us (1.078)
  Pallas kernels: 7.26 us -> 9.51 us
    pallas_call x1, Pallas kernels: 2.86 us -> 5.13 us  [partial_halves(): pl.pallas_call(functools.partial(send_kernel, total_bits, parts), in_spec...]
where the time goes in v16:
time: 33.3 us; the launch traced here: 32.9 us
  starting transfers between devices  14.3 us (43%)
  Pallas kernels  9.51 us (29%)
  waiting for transfers between devices  9.07 us (27%)
    ppermute x13, starting transfers between devices, swap(): return lax.ppermute(array, ('feat', 'tok'), pairs)  14.3 us
    ppermute x13, waiting for transfers between devices, swap(): return lax.ppermute(array, ('feat', 'tok'), pairs)  9.07 us
    pallas_call x1, Pallas kernels, partial_halves(): pl.pallas_call(functools.partial(send_kernel, total_bits, parts), in_spec...  5.13 us
    pallas_call x1, Pallas kernels, gram_blocks(): pl.pallas_call(functools.partial(gram_kernel, shard, group, factor), in_s...  2.48 us
    pallas_call x1, Pallas kernels, partial_halves(): pl.pallas_call(functools.partial(keep_kernel, parts), out_shape=total_typ...  1.29 us
  transfers between devices with their start and end apart: 13, of which 7 were waited for; matrix products, arithmetic and copies ran while one was open for 0% of the time, Pallas kernels for 4%

profile of v16, /device:TPU:0, one launch (start us, length us, event | category | flops | bytes accessed | tf_op | source)
XLA Modules:
  0.0 32.9 jit_solution(16449351164237671435)
XLA Ops:
  0.0 5.1 %partial_sent.1 = (f32[64,1024]{1,0:T(8,128)S(1)}, bf16[64,8192]{1,0:T(8,128)(2,1)S(1)}, s32[1,8192]{1,0:T(1,128)S(1)}, bf16[256,1024]{1,0:T(8,128)(2,1)S(1)}, f32[32,1024]{1,0:T(8,128)S(1)}) custom-call(bf16[128,8192]{1,0:T(8,128)(2,1)} %x_hbm.1, s32[1,8192]{1,0:T(1,128)} %bitcast.5, s32[1,1024]{1,0:T(1,128)} %bitcast.6), custom_call_target="tpu_custom_call" | custom-call | flops 1073741824 | bytes 2359296 | tf_op jit(solution)/shard_map/partial_sent/pallas_call | solution.py:99
  5.1 0.5 %collective-permute-start = (f32[64,1024]{1,0:T(8,128)S(1)}, f32[64,1024]{1,0:T(8,128)S(1)}, u32[]{:S(2)}, u32[]{:S(2)}) collective-permute-start(f32[64,1024]{1,0:T(8,128)S(1)} %get-tuple-element.27), channel_id=1, source_target_pairs={{0,2},{1,3},{2,0},{3,1},{4,6},{5,7},{6,4},{7,5},{8,10},{9,11},{10,... | collective-permute-start | bytes 786440 | tf_op jit(solution)/shard_map/ppermute | solution.py:285
  5.7 1.3 %partial_kept.1.keep_ref = f32[64,1024]{1,0:T(8,128)S(1)} custom-call(bf16[64,8192]{1,0:T(8,128)(2,1)S(1)} %get-tuple-element.23.x_keep, s32[1,8192]{1,0:T(1,128)S(1)} %get-tuple-element.24.signs, bf16[256,1024]{1,0:T(8,128)(2,1)S(1)} %get-tuple-element.25.low, f32[32,1024]{1,0:T(8,128)S(1)} %get-tuple-element.26.high), custom_call_target="tpu_custom_call" | custom-call | flops 1073741824 | bytes 2359296 | tf_op jit(solution)/shard_map/partial_kept/pallas_call | solution.py:123
  7.0 0.2 first_split.1
  7.2 3.8 %collective-permute-start.1 = (s32[136,128]{1,0:T(8,128)S(1)}, s32[136,128]{1,0:T(8,128)S(1)}, u32[]{:S(2)}, u32[]{:S(2)}) collective-permute-start(s32[136,128]{1,0:T(8,128)S(1)} %get-tuple-element.29), channel_id=1, source_target_pairs={{0,12},{1,13},{2,14},{3,15},{4,8},{5,9},{6,10},{7,11},{8,4},{9,5},... | collective-permute-start | bytes 208904 | tf_op jit(solution)/shard_map/ppermute | solution.py:285
  10.9 0.5 %collective-permute-start.2 = (s32[136,128]{1,0:T(8,128)S(1)}, s32[136,128]{1,0:T(8,128)S(1)}, u32[]{:S(2)}, u32[]{:S(2)}) collective-permute-start(s32[136,128]{1,0:T(8,128)S(1)} %get-tuple-element.30), channel_id=1, source_target_pairs={{0,4},{1,5},{2,6},{3,7},{4,0},{5,1},{6,2},{7,3},{8,12},{9,13},{10,... | collective-permute-start | bytes 208904 | tf_op jit(solution)/shard_map/ppermute | solution.py:285
  11.4 0.1 collective-permute-start.3
  11.6 2.0 %collective-permute-done.1.both_ref = s32[136,128]{1,0:T(8,128)S(1)} collective-permute-done((s32[136,128]{1,0:T(8,128)S(1)}, s32[136,128]{1,0:T(8,128)S(1)}, u32[]{:S(2)}, u32[]{:S(2)}) %collective-permute-start.1) | collective-permute-done | bytes 69664 | tf_op jit(solution)/shard_map/ppermute | solution.py:285
  13.6 1.6 %collective-permute-done.2.x_ref = s32[136,128]{1,0:T(8,128)S(1)} collective-permute-done((s32[136,128]{1,0:T(8,128)S(1)}, s32[136,128]{1,0:T(8,128)S(1)}, u32[]{:S(2)}, u32[]{:S(2)}) %collective-permute-start.2) | collective-permute-done | bytes 69664 | tf_op jit(solution)/shard_map/ppermute | solution.py:285
  15.2 0.5 %collective-permute-done.3.z_ref = s32[136,128]{1,0:T(8,128)S(1)} collective-permute-done((s32[136,128]{1,0:T(8,128)S(1)}, s32[136,128]{1,0:T(8,128)S(1)}, u32[]{:S(2)}, u32[]{:S(2)}) %collective-permute-start.3) | collective-permute-done | bytes 69664 | tf_op jit(solution)/shard_map/ppermute | solution.py:285
  15.8 0.3 add_square.1
  16.0 2.7 %collective-permute-start.4 = (s32[136,128]{1,0:T(8,128)S(1)}, s32[136,128]{1,0:T(8,128)S(1)}, u32[]{:S(2)}, u32[]{:S(2)}) collective-permute-start(s32[136,128]{1,0:T(8,128)S(1)} %get-tuple-element.33), channel_id=1, source_target_pairs={{0,16},{1,17},{2,18},{3,19},{4,20},{5,21},{6,22},{7,23},{8,24},{9,... | collective-permute-start | bytes 208904 | tf_op jit(solution)/shard_map/ppermute | solution.py:285
  18.7 1.5 %collective-permute-start.5 = (s32[1,128]{1,0:T(1,128)S(1)}, s32[1,128]{1,0:T(1,128)S(1)}, u32[]{:S(2)}, u32[]{:S(2)}) collective-permute-start(s32[1,128]{1,0:T(1,128)S(1)} %get-tuple-element.34.refs_0_), channel_id=1, source_target_pairs={{0,1},{1,0},{2,3},{3,2},{4,5},{5,4},{6,7},{7,6},{8,9},{9,8},{10,11... | collective-permute-start | bytes 1544 | tf_op jit(solution)/shard_map/ppermute | solution.py:285
  20.2 2.0 %collective-permute-done.5.refs_1_ = s32[1,128]{1,0:T(1,128)S(1)} collective-permute-done((s32[1,128]{1,0:T(1,128)S(1)}, s32[1,128]{1,0:T(1,128)S(1)}, u32[]{:S(2)}, u32[]{:S(2)}) %collective-permute-start.5) | collective-permute-done | bytes 544 | tf_op jit(solution)/shard_map/ppermute | solution.py:285
  22.2 0.1 collective-permute-done.4.word_ref
  22.3 0.2 sketch_rows.1
  22.5 2.4 %collective-permute-start.6 = (bf16[32,1024]{1,0:T(8,128)(2,1)S(1)}, bf16[32,1024]{1,0:T(8,128)(2,1)S(1)}, u32[]{:S(2)}, u32[]{:S(2)}) collective-permute-start(bf16[32,1024]{1,0:T(8,128)(2,1)S(1)} %get-tuple-element.37), channel_id=1, source_target_pairs={{0,5},{1,4},{2,7},{3,6},{4,1},{5,0},{6,3},{7,2},{8,13},{9,12},{10,... | collective-permute-start | bytes 196616 | tf_op jit(solution)/shard_map/ppermute | solution.py:285
  24.9 0.6 %collective-permute-start.7 = (bf16[32,1024]{1,0:T(8,128)(2,1)S(1)}, bf16[32,1024]{1,0:T(8,128)(2,1)S(1)}, u32[]{:S(2)}, u32[]{:S(2)}) collective-permute-start(bf16[32,1024]{1,0:T(8,128)(2,1)S(1)} %get-tuple-element.38), channel_id=1, source_target_pairs={{0,4},{1,5},{2,6},{3,7},{4,0},{5,1},{6,2},{7,3},{8,12},{9,13},{10,... | collective-permute-start | bytes 196616 | tf_op jit(solution)/shard_map/ppermute | solution.py:285
  25.5 0.5 %collective-permute-start.8 = (bf16[32,1024]{1,0:T(8,128)(2,1)S(1)}, bf16[32,1024]{1,0:T(8,128)(2,1)S(1)}, u32[]{:S(2)}, u32[]{:S(2)}) collective-permute-start(bf16[32,1024]{1,0:T(8,128)(2,1)S(1)} %get-tuple-element.39), channel_id=1, source_target_pairs={{0,1},{1,0},{2,3},{3,2},{4,5},{5,4},{6,7},{7,6},{8,9},{9,8},{10,11... | collective-permute-start | bytes 196616 | tf_op jit(solution)/shard_map/ppermute | solution.py:285
  26.0 1.6 %collective-permute-start.9 = (bf16[32,1024]{1,0:T(8,128)(2,1)S(1)}, bf16[32,1024]{1,0:T(8,128)(2,1)S(1)}, u32[]{:S(2)}, u32[]{:S(2)}) collective-permute-start(bf16[32,1024]{1,0:T(8,128)(2,1)S(1)} %get-tuple-element.36.refs_0_), channel_id=1, source_target_pairs={{0,2},{1,3},{2,0},{3,1},{4,6},{5,7},{6,4},{7,5},{8,10},{9,11},{10,... | collective-permute-start | bytes 196616 | tf_op jit(solution)/shard_map/ppermute | solution.py:285
  27.7 0.0 collective-permute-done.6.refs_1_
  27.7 1.5 %collective-permute-done.7.refs_2_ = bf16[32,1024]{1,0:T(8,128)(2,1)S(1)} collective-permute-done((bf16[32,1024]{1,0:T(8,128)(2,1)S(1)}, bf16[32,1024]{1,0:T(8,128)(2,1)S(1)}, u32[]{:S(2)}, u32[]{:S(2)}) %collective-permute-start.7) | collective-permute-done | bytes 65568 | tf_op jit(solution)/shard_map/ppermute | solution.py:285
  29.2 1.2 %collective-permute-done.8.refs_3_ = bf16[32,1024]{1,0:T(8,128)(2,1)S(1)} collective-permute-done((bf16[32,1024]{1,0:T(8,128)(2,1)S(1)}, bf16[32,1024]{1,0:T(8,128)(2,1)S(1)}, u32[]{:S(2)}, u32[]{:S(2)}) %collective-permute-start.8) | collective-permute-done | bytes 65568 | tf_op jit(solution)/shard_map/ppermute | solution.py:285
  30.5 2.5 %gram.1 = f32[1024,1024]{1,0:T(8,128)} custom-call(s32[1,256]{1,0:T(1,128)S(1)} %get-tuple-element.35.label_ref, bf16[32,1024]{1,0:T(8,128)(2,1)S(1)} %get-tuple-element.36.refs_0_, bf16[32,1024]{1,0:T(8,128)(2,1)S(1)} %collective-permute-done.6.refs_1_, bf16[32,1024]{1,0:T(8,128)(2,1)S(1)} %collective-permute-done.7.refs_2_, ...), custom_call_target="tpu_custom_call" | custom-call | flops 536870912 | bytes 4194304 | tf_op jit(solution)/shard_map/gram/pallas_call | solution.py:172
  (10 shorter events, 0.0 us)
Async XLA Ops:
  0.0 7.0 %copy-start = (s32[128,1]{0,1:T(1,128)S(1)}, s32[128,1]{0,1:T(1,128)}, u32[]{:S(2)}) copy-start(s32[128,1]{0,1:T(1,128)} %param.7) | copy-start | bytes 1540
  5.1 1.8 %collective-permute-start = (f32[64,1024]{1,0:T(8,128)S(1)}, f32[64,1024]{1,0:T(8,128)S(1)}, u32[]{:S(2)}, u32[]{:S(2)}) collective-permute-start(f32[64,1024]{1,0:T(8,128)S(1)} %get-tuple-element.27), channel_id=1, source_target_pairs={{0,2},{1,3},{2,0},{3,1},{4,6},{5,7},{6,4},{7,5},{8,10},{9,11},{10,... | collective-permute-start | bytes 786440 | tf_op jit(solution)/shard_map/ppermute | solution.py:285
  7.2 6.4 %collective-permute-start.1 = (s32[136,128]{1,0:T(8,128)S(1)}, s32[136,128]{1,0:T(8,128)S(1)}, u32[]{:S(2)}, u32[]{:S(2)}) collective-permute-start(s32[136,128]{1,0:T(8,128)S(1)} %get-tuple-element.29), channel_id=1, source_target_pairs={{0,12},{1,13},{2,14},{3,15},{4,8},{5,9},{6,10},{7,11},{8,4},{9,5},... | collective-permute-start | bytes 208904 | tf_op jit(solution)/shard_map/ppermute | solution.py:285
  10.9 4.3 %collective-permute-start.2 = (s32[136,128]{1,0:T(8,128)S(1)}, s32[136,128]{1,0:T(8,128)S(1)}, u32[]{:S(2)}, u32[]{:S(2)}) collective-permute-start(s32[136,128]{1,0:T(8,128)S(1)} %get-tuple-element.30), channel_id=1, source_target_pairs={{0,4},{1,5},{2,6},{3,7},{4,0},{5,1},{6,2},{7,3},{8,12},{9,13},{10,... | collective-permute-start | bytes 208904 | tf_op jit(solution)/shard_map/ppermute | solution.py:285
  11.4 4.3 %collective-permute-start.3 = (s32[136,128]{1,0:T(8,128)S(1)}, s32[136,128]{1,0:T(8,128)S(1)}, u32[]{:S(2)}, u32[]{:S(2)}) collective-permute-start(s32[136,128]{1,0:T(8,128)S(1)} %get-tuple-element.31), channel_id=1, source_target_pairs={{0,8},{1,9},{2,10},{3,11},{4,12},{5,13},{6,14},{7,15},{8,0},{9,1},... | collective-permute-start | bytes 208904 | tf_op jit(solution)/shard_map/ppermute | solution.py:285
  16.0 6.3 %collective-permute-start.4 = (s32[136,128]{1,0:T(8,128)S(1)}, s32[136,128]{1,0:T(8,128)S(1)}, u32[]{:S(2)}, u32[]{:S(2)}) collective-permute-start(s32[136,128]{1,0:T(8,128)S(1)} %get-tuple-element.33), channel_id=1, source_target_pairs={{0,16},{1,17},{2,18},{3,19},{4,20},{5,21},{6,22},{7,23},{8,24},{9,... | collective-permute-start | bytes 208904 | tf_op jit(solution)/shard_map/ppermute | solution.py:285
  18.7 3.5 %collective-permute-start.5 = (s32[1,128]{1,0:T(1,128)S(1)}, s32[1,128]{1,0:T(1,128)S(1)}, u32[]{:S(2)}, u32[]{:S(2)}) collective-permute-start(s32[1,128]{1,0:T(1,128)S(1)} %get-tuple-element.34.refs_0_), channel_id=1, source_target_pairs={{0,1},{1,0},{2,3},{3,2},{4,5},{5,4},{6,7},{7,6},{8,9},{9,8},{10,11... | collective-permute-start | bytes 1544 | tf_op jit(solution)/shard_map/ppermute | solution.py:285
  22.5 5.2 %collective-permute-start.6 = (bf16[32,1024]{1,0:T(8,128)(2,1)S(1)}, bf16[32,1024]{1,0:T(8,128)(2,1)S(1)}, u32[]{:S(2)}, u32[]{:S(2)}) collective-permute-start(bf16[32,1024]{1,0:T(8,128)(2,1)S(1)} %get-tuple-element.37), channel_id=1, source_target_pairs={{0,5},{1,4},{2,7},{3,6},{4,1},{5,0},{6,3},{7,2},{8,13},{9,12},{10,... | collective-permute-start | bytes 196616 | tf_op jit(solution)/shard_map/ppermute | solution.py:285
  24.9 4.3 %collective-permute-start.7 = (bf16[32,1024]{1,0:T(8,128)(2,1)S(1)}, bf16[32,1024]{1,0:T(8,128)(2,1)S(1)}, u32[]{:S(2)}, u32[]{:S(2)}) collective-permute-start(bf16[32,1024]{1,0:T(8,128)(2,1)S(1)} %get-tuple-element.38), channel_id=1, source_target_pairs={{0,4},{1,5},{2,6},{3,7},{4,0},{5,1},{6,2},{7,3},{8,12},{9,13},{10,... | collective-permute-start | bytes 196616 | tf_op jit(solution)/shard_map/ppermute | solution.py:285
  25.5 4.9 %collective-permute-start.8 = (bf16[32,1024]{1,0:T(8,128)(2,1)S(1)}, bf16[32,1024]{1,0:T(8,128)(2,1)S(1)}, u32[]{:S(2)}, u32[]{:S(2)}) collective-permute-start(bf16[32,1024]{1,0:T(8,128)(2,1)S(1)} %get-tuple-element.39), channel_id=1, source_target_pairs={{0,1},{1,0},{2,3},{3,2},{4,5},{5,4},{6,7},{7,6},{8,9},{9,8},{10,11... | collective-permute-start | bytes 196616 | tf_op jit(solution)/shard_map/ppermute | solution.py:285
  26.0 4.4 %collective-permute-start.12 = (bf16[32,1024]{1,0:T(8,128)(2,1)S(1)}, bf16[32,1024]{1,0:T(8,128)(2,1)S(1)}, u32[]{:S(2)}, u32[]{:S(2)}) collective-permute-start(bf16[32,1024]{1,0:T(8,128)(2,1)S(1)} %get-tuple-element.40), channel_id=1, source_target_pairs={{0,3},{1,2},{2,1},{3,0},{4,7},{5,6},{6,5},{7,4},{8,11},{9,10},{10,... | collective-permute-start | bytes 196616 | tf_op jit(solution)/shard_map/ppermute | solution.py:285
  26.0 4.4 %collective-permute-start.9 = (bf16[32,1024]{1,0:T(8,128)(2,1)S(1)}, bf16[32,1024]{1,0:T(8,128)(2,1)S(1)}, u32[]{:S(2)}, u32[]{:S(2)}) collective-permute-start(bf16[32,1024]{1,0:T(8,128)(2,1)S(1)} %get-tuple-element.36.refs_0_), channel_id=1, source_target_pairs={{0,2},{1,3},{2,0},{3,1},{4,6},{5,7},{6,4},{7,5},{8,10},{9,11},{10,... | collective-permute-start | bytes 196616 | tf_op jit(solution)/shard_map/ppermute | solution.py:285
  27.7 2.7 %collective-permute-start.10 = (bf16[32,1024]{1,0:T(8,128)(2,1)S(1)}, bf16[32,1024]{1,0:T(8,128)(2,1)S(1)}, u32[]{:S(2)}, u32[]{:S(2)}) collective-permute-start(bf16[32,1024]{1,0:T(8,128)(2,1)S(1)} %collective-permute-done.6.refs_1_), channel_id=1, source_target_pairs={{0,2},{1,3},{2,0},{3,1},{4,6},{5,7},{6,4},{7,5},{8,10},{9,11},{10,... | collective-permute-start | bytes 196616 | tf_op jit(solution)/shard_map/ppermute | solution.py:285
  29.2 1.3 %collective-permute-start.11 = (bf16[32,1024]{1,0:T(8,128)(2,1)S(1)}, bf16[32,1024]{1,0:T(8,128)(2,1)S(1)}, u32[]{:S(2)}, u32[]{:S(2)}) collective-permute-start(bf16[32,1024]{1,0:T(8,128)(2,1)S(1)} %collective-permute-done.7.refs_2_), channel_id=1, source_target_pairs={{0,2},{1,3},{2,0},{3,1},{4,6},{5,7},{6,4},{7,5},{8,10},{9,11},{10,... | collective-permute-start | bytes 196616 | tf_op jit(solution)/shard_map/ppermute | solution.py:285

commit v17 on v13

--- a/solution.py
+++ b/solution.py
@@ -24,7 +24,7 @@
     return (1 - 2 * (number & 1)).astype(jnp.float32)
 
 
-def add_products(x_ref, sign_ref, low, high, out_ref, part, wide):
+def add_products(x_ref, sign_ref, low, high, out_ref, part, wide, make_tables=None):
     rows, kept = out_ref.shape
     blocks = wide // LOW
     stack = []
@@ -34,6 +34,8 @@
     stack = jnp.concatenate(stack, axis=0)
     for group in range(kept // LOW):
         cols = slice(group * LOW, (group + 1) * LOW)
+        if make_tables is not None:
+            make_tables(cols)
         products = jnp.dot(stack, low[:, cols], preferred_element_type=jnp.float32)
         total = None
         for at in range(blocks):
@@ -63,19 +65,22 @@
     rows = pl.ds(pl.multiple_of(mine * half, half), half)
     keep_copy = pltpu.make_async_copy(x_hbm.at[rows, :], x_keep, sems.at[parts + 2])
     keep_copy.start()
+
+    def make_tables(cols):
+        col = col_buf[:, cols]
+        index = lax.broadcasted_iota(jnp.int32, (16, LOW), 0)
+        inner = parity_sign(index & col, 4)
+        outer = parity_sign(index & (col >> 4), 4)
+        for row in range(LOW // 16):
+            low[row * 16:(row + 1) * 16, cols] = (inner * outer[row:row + 1]).astype(jnp.bfloat16)
+        index = lax.broadcasted_iota(jnp.int32, (high.shape[0], LOW), 0) + me * high.shape[0]
+        high[:, cols] = parity_sign(index & (col >> 8), total_bits - 8)
+
     col_copy.wait()
-    col = col_buf[...]
-    index = lax.broadcasted_iota(jnp.int32, (16, kept), 0)
-    inner = parity_sign(index & col, 4)
-    outer = parity_sign(index & (col >> 4), 4)
-    for row in range(LOW // 16):
-        low[row * 16:(row + 1) * 16] = (inner * outer[row:row + 1]).astype(jnp.bfloat16)
-    high_index = lax.broadcasted_iota(jnp.int32, high.shape, 0) + me * high.shape[0]
-    high[...] = parity_sign(high_index & (col >> 8), total_bits - 8)
     sign_copy.wait()
     for part in range(parts):
         copies[part].wait()
-        add_products(x_buf, signs, low, high, send_ref, part, wide)
+        add_products(x_buf, signs, low, high, send_ref, part, wide, make_tables if part == 0 else None)
     keep_copy.wait()
 
 
@@ -132,7 +137,7 @@
 
 def gram_kernel(shard, group, factor, label_ref, *refs):
     pieces, (out_hbm, rows, blocks, sems) = refs[:-4], refs[-4:]
-    steps, wide, _ = blocks.shape
+    steps, wide, kept = blocks.shape
     place = 0
     for piece in pieces:
         rows[place:place + piece.shape[0]] = piece[...]
@@ -147,11 +152,18 @@
     copies = []
     for step in range(steps):
         chosen = jnp.where(label == base + step * group, own, 0.0).astype(jnp.bfloat16)
-        blocks[step] = jnp.dot(chosen, rows[...], preferred_element_type=jnp.float32)
-        copies.append(
-            pltpu.make_async_copy(blocks.at[step], out_hbm.at[pl.ds(step * wide, wide), :], sems.at[step])
-        )
-        copies[-1].start()
+        size = kept if step < steps - 1 else LOW
+        for first in range(0, kept, size):
+            cols = slice(first, first + size)
+            blocks[step, :, cols] = jnp.dot(chosen, rows[:, cols], preferred_element_type=jnp.float32)
+            copies.append(
+                pltpu.make_async_copy(
+                    blocks.at[step, :, pl.ds(first, size)],
+                    out_hbm.at[pl.ds(step * wide, wide), pl.ds(first, size)],
+                    sems.at[len(copies)],
+                )
+            )
+            copies[-1].start()
     for copy in copies:
         copy.wait()
 
@@ -170,7 +182,7 @@
         scratch_shapes=[
             pltpu.VMEM((tokens, kept), jnp.bfloat16),
             pltpu.VMEM((steps, wide, kept), jnp.float32),
-            pltpu.SemaphoreType.DMA((steps,)),
+            pltpu.SemaphoreType.DMA((steps - 1 + kept // LOW,)),
         ],
         compiler_params=pltpu.CompilerParams(vmem_limit_bytes=VMEM_LIMIT),
         cost_estimate=pl.CostEstimate(

time: 30.9 us -> 30.9 us (level)
  no operation moved by 1% of the time
where the time goes in v17:
time: 30.9 us; the launch traced here: 30.7 us
  starting transfers between devices  14.3 us (46%)
  waiting for transfers between devices  9.08 us (29%)
  Pallas kernels  7.31 us (24%)
    ppermute x13, starting transfers between devices, swap(): return lax.ppermute(array, ('feat', 'tok'), pairs)  14.3 us
    ppermute x13, waiting for transfers between devices, swap(): return lax.ppermute(array, ('feat', 'tok'), pairs)  9.08 us
    pallas_call x1, Pallas kernels, partial_halves(): pl.pallas_call(functools.partial(send_kernel, total_bits, parts), in_spec...  2.89 us
    pallas_call x1, Pallas kernels, gram_blocks(): pl.pallas_call(functools.partial(gram_kernel, shard, group, factor), in_s...  2.52 us
    pallas_call x1, Pallas kernels, partial_halves(): pl.pallas_call(functools.partial(keep_kernel, parts), out_shape=total_typ...  1.3 us
  transfers between devices with their start and end apart: 13, of which 7 were waited for; matrix products, arithmetic and copies ran while one was open for 0% of the time, Pallas kernels for 4%

profile of v17, /device:TPU:0, one launch (start us, length us, event | category | flops | bytes accessed | tf_op | source)
XLA Modules:
  0.0 30.7 jit_solution(9829419772984491516)
XLA Ops:
  0.0 2.9 %partial_sent.1 = (f32[64,1024]{1,0:T(8,128)S(1)}, bf16[64,8192]{1,0:T(8,128)(2,1)S(1)}, s32[1,8192]{1,0:T(1,128)S(1)}, bf16[256,1024]{1,0:T(8,128)(2,1)S(1)}, f32[32,1024]{1,0:T(8,128)S(1)}) custom-call(bf16[128,8192]{1,0:T(8,128)(2,1)} %x_hbm.1, s32[1,8192]{1,0:T(1,128)} %bitcast.5, s32[1,1024]{1,0:T(1,128)} %bitcast.6), custom_call_target="tpu_custom_call" | custom-call | flops 1073741824 | bytes 2359296 | tf_op jit(solution)/shard_map/partial_sent/pallas_call | solution.py:104
  2.9 0.5 %collective-permute-start = (f32[64,1024]{1,0:T(8,128)S(1)}, f32[64,1024]{1,0:T(8,128)S(1)}, u32[]{:S(2)}, u32[]{:S(2)}) collective-permute-start(f32[64,1024]{1,0:T(8,128)S(1)} %get-tuple-element.27), channel_id=1, source_target_pairs={{0,2},{1,3},{2,0},{3,1},{4,6},{5,7},{6,4},{7,5},{8,10},{9,11},{10,... | collective-permute-start | bytes 786440 | tf_op jit(solution)/shard_map/ppermute | solution.py:290
  3.4 1.3 %partial_kept.1.keep_ref = f32[64,1024]{1,0:T(8,128)S(1)} custom-call(bf16[64,8192]{1,0:T(8,128)(2,1)S(1)} %get-tuple-element.23.x_keep, s32[1,8192]{1,0:T(1,128)S(1)} %get-tuple-element.24.signs, bf16[256,1024]{1,0:T(8,128)(2,1)S(1)} %get-tuple-element.25.low, f32[32,1024]{1,0:T(8,128)S(1)} %get-tuple-element.26.high), custom_call_target="tpu_custom_call" | custom-call | flops 1073741824 | bytes 2359296 | tf_op jit(solution)/shard_map/partial_kept/pallas_call | solution.py:128
  4.7 0.2 first_split.1
  4.9 3.8 %collective-permute-start.1 = (s32[136,128]{1,0:T(8,128)S(1)}, s32[136,128]{1,0:T(8,128)S(1)}, u32[]{:S(2)}, u32[]{:S(2)}) collective-permute-start(s32[136,128]{1,0:T(8,128)S(1)} %get-tuple-element.29), channel_id=1, source_target_pairs={{0,12},{1,13},{2,14},{3,15},{4,8},{5,9},{6,10},{7,11},{8,4},{9,5},... | collective-permute-start | bytes 208904 | tf_op jit(solution)/shard_map/ppermute | solution.py:290
  8.7 0.5 %collective-permute-start.2 = (s32[136,128]{1,0:T(8,128)S(1)}, s32[136,128]{1,0:T(8,128)S(1)}, u32[]{:S(2)}, u32[]{:S(2)}) collective-permute-start(s32[136,128]{1,0:T(8,128)S(1)} %get-tuple-element.30), channel_id=1, source_target_pairs={{0,4},{1,5},{2,6},{3,7},{4,0},{5,1},{6,2},{7,3},{8,12},{9,13},{10,... | collective-permute-start | bytes 208904 | tf_op jit(solution)/shard_map/ppermute | solution.py:290
  9.2 0.1 collective-permute-start.3
  9.3 2.0 %collective-permute-done.1.both_ref = s32[136,128]{1,0:T(8,128)S(1)} collective-permute-done((s32[136,128]{1,0:T(8,128)S(1)}, s32[136,128]{1,0:T(8,128)S(1)}, u32[]{:S(2)}, u32[]{:S(2)}) %collective-permute-start.1) | collective-permute-done | bytes 69664 | tf_op jit(solution)/shard_map/ppermute | solution.py:290
  11.3 1.7 %collective-permute-done.2.x_ref = s32[136,128]{1,0:T(8,128)S(1)} collective-permute-done((s32[136,128]{1,0:T(8,128)S(1)}, s32[136,128]{1,0:T(8,128)S(1)}, u32[]{:S(2)}, u32[]{:S(2)}) %collective-permute-start.2) | collective-permute-done | bytes 69664 | tf_op jit(solution)/shard_map/ppermute | solution.py:290
  13.0 0.5 %collective-permute-done.3.z_ref = s32[136,128]{1,0:T(8,128)S(1)} collective-permute-done((s32[136,128]{1,0:T(8,128)S(1)}, s32[136,128]{1,0:T(8,128)S(1)}, u32[]{:S(2)}, u32[]{:S(2)}) %collective-permute-start.3) | collective-permute-done | bytes 69664 | tf_op jit(solution)/shard_map/ppermute | solution.py:290
  13.5 0.3 add_square.1
  13.8 2.7 %collective-permute-start.4 = (s32[136,128]{1,0:T(8,128)S(1)}, s32[136,128]{1,0:T(8,128)S(1)}, u32[]{:S(2)}, u32[]{:S(2)}) collective-permute-start(s32[136,128]{1,0:T(8,128)S(1)} %get-tuple-element.33), channel_id=1, source_target_pairs={{0,16},{1,17},{2,18},{3,19},{4,20},{5,21},{6,22},{7,23},{8,24},{9,... | collective-permute-start | bytes 208904 | tf_op jit(solution)/shard_map/ppermute | solution.py:290
  16.5 1.5 %collective-permute-start.5 = (s32[1,128]{1,0:T(1,128)S(1)}, s32[1,128]{1,0:T(1,128)S(1)}, u32[]{:S(2)}, u32[]{:S(2)}) collective-permute-start(s32[1,128]{1,0:T(1,128)S(1)} %get-tuple-element.34.refs_0_), channel_id=1, source_target_pairs={{0,1},{1,0},{2,3},{3,2},{4,5},{5,4},{6,7},{7,6},{8,9},{9,8},{10,11... | collective-permute-start | bytes 1544 | tf_op jit(solution)/shard_map/ppermute | solution.py:290
  18.0 2.0 %collective-permute-done.5.refs_1_ = s32[1,128]{1,0:T(1,128)S(1)} collective-permute-done((s32[1,128]{1,0:T(1,128)S(1)}, s32[1,128]{1,0:T(1,128)S(1)}, u32[]{:S(2)}, u32[]{:S(2)}) %collective-permute-start.5) | collective-permute-done | bytes 544 | tf_op jit(solution)/shard_map/ppermute | solution.py:290
  20.0 0.1 collective-permute-done.4.word_ref
  20.1 0.2 sketch_rows.1
  20.2 2.4 %collective-permute-start.6 = (bf16[32,1024]{1,0:T(8,128)(2,1)S(1)}, bf16[32,1024]{1,0:T(8,128)(2,1)S(1)}, u32[]{:S(2)}, u32[]{:S(2)}) collective-permute-start(bf16[32,1024]{1,0:T(8,128)(2,1)S(1)} %get-tuple-element.37), channel_id=1, source_target_pairs={{0,5},{1,4},{2,7},{3,6},{4,1},{5,0},{6,3},{7,2},{8,13},{9,12},{10,... | collective-permute-start | bytes 196616 | tf_op jit(solution)/shard_map/ppermute | solution.py:290
  22.7 0.6 %collective-permute-start.7 = (bf16[32,1024]{1,0:T(8,128)(2,1)S(1)}, bf16[32,1024]{1,0:T(8,128)(2,1)S(1)}, u32[]{:S(2)}, u32[]{:S(2)}) collective-permute-start(bf16[32,1024]{1,0:T(8,128)(2,1)S(1)} %get-tuple-element.38), channel_id=1, source_target_pairs={{0,4},{1,5},{2,6},{3,7},{4,0},{5,1},{6,2},{7,3},{8,12},{9,13},{10,... | collective-permute-start | bytes 196616 | tf_op jit(solution)/shard_map/ppermute | solution.py:290
  23.3 0.5 %collective-permute-start.8 = (bf16[32,1024]{1,0:T(8,128)(2,1)S(1)}, bf16[32,1024]{1,0:T(8,128)(2,1)S(1)}, u32[]{:S(2)}, u32[]{:S(2)}) collective-permute-start(bf16[32,1024]{1,0:T(8,128)(2,1)S(1)} %get-tuple-element.39), channel_id=1, source_target_pairs={{0,1},{1,0},{2,3},{3,2},{4,5},{5,4},{6,7},{7,6},{8,9},{9,8},{10,11... | collective-permute-start | bytes 196616 | tf_op jit(solution)/shard_map/ppermute | solution.py:290
  23.8 1.6 %collective-permute-start.9 = (bf16[32,1024]{1,0:T(8,128)(2,1)S(1)}, bf16[32,1024]{1,0:T(8,128)(2,1)S(1)}, u32[]{:S(2)}, u32[]{:S(2)}) collective-permute-start(bf16[32,1024]{1,0:T(8,128)(2,1)S(1)} %get-tuple-element.36.refs_0_), channel_id=1, source_target_pairs={{0,2},{1,3},{2,0},{3,1},{4,6},{5,7},{6,4},{7,5},{8,10},{9,11},{10,... | collective-permute-start | bytes 196616 | tf_op jit(solution)/shard_map/ppermute | solution.py:290
  25.4 0.0 collective-permute-done.6.refs_1_
  25.5 1.5 %collective-permute-done.7.refs_2_ = bf16[32,1024]{1,0:T(8,128)(2,1)S(1)} collective-permute-done((bf16[32,1024]{1,0:T(8,128)(2,1)S(1)}, bf16[32,1024]{1,0:T(8,128)(2,1)S(1)}, u32[]{:S(2)}, u32[]{:S(2)}) %collective-permute-start.7) | collective-permute-done | bytes 65568 | tf_op jit(solution)/shard_map/ppermute | solution.py:290
  26.9 1.2 %collective-permute-done.8.refs_3_ = bf16[32,1024]{1,0:T(8,128)(2,1)S(1)} collective-permute-done((bf16[32,1024]{1,0:T(8,128)(2,1)S(1)}, bf16[32,1024]{1,0:T(8,128)(2,1)S(1)}, u32[]{:S(2)}, u32[]{:S(2)}) %collective-permute-start.8) | collective-permute-done | bytes 65568 | tf_op jit(solution)/shard_map/ppermute | solution.py:290
  28.2 2.5 %gram.1 = f32[1024,1024]{1,0:T(8,128)} custom-call(s32[1,256]{1,0:T(1,128)S(1)} %get-tuple-element.35.label_ref, bf16[32,1024]{1,0:T(8,128)(2,1)S(1)} %get-tuple-element.36.refs_0_, bf16[32,1024]{1,0:T(8,128)(2,1)S(1)} %collective-permute-done.6.refs_1_, bf16[32,1024]{1,0:T(8,128)(2,1)S(1)} %collective-permute-done.7.refs_2_, ...), custom_call_target="tpu_custom_call" | custom-call | flops 536870912 | bytes 4194304 | tf_op jit(solution)/shard_map/gram/pallas_call | solution.py:177
  (10 shorter events, 0.0 us)
Async XLA Ops:
  0.0 4.7 %copy-start = (s32[128,1]{0,1:T(1,128)S(1)}, s32[128,1]{0,1:T(1,128)}, u32[]{:S(2)}) copy-start(s32[128,1]{0,1:T(1,128)} %param.7) | copy-start | bytes 1540
  2.9 1.8 %collective-permute-start = (f32[64,1024]{1,0:T(8,128)S(1)}, f32[64,1024]{1,0:T(8,128)S(1)}, u32[]{:S(2)}, u32[]{:S(2)}) collective-permute-start(f32[64,1024]{1,0:T(8,128)S(1)} %get-tuple-element.27), channel_id=1, source_target_pairs={{0,2},{1,3},{2,0},{3,1},{4,6},{5,7},{6,4},{7,5},{8,10},{9,11},{10,... | collective-permute-start | bytes 786440 | tf_op jit(solution)/shard_map/ppermute | solution.py:290
  4.9 6.4 %collective-permute-start.1 = (s32[136,128]{1,0:T(8,128)S(1)}, s32[136,128]{1,0:T(8,128)S(1)}, u32[]{:S(2)}, u32[]{:S(2)}) collective-permute-start(s32[136,128]{1,0:T(8,128)S(1)} %get-tuple-element.29), channel_id=1, source_target_pairs={{0,12},{1,13},{2,14},{3,15},{4,8},{5,9},{6,10},{7,11},{8,4},{9,5},... | collective-permute-start | bytes 208904 | tf_op jit(solution)/shard_map/ppermute | solution.py:290
  8.7 4.3 %collective-permute-start.2 = (s32[136,128]{1,0:T(8,128)S(1)}, s32[136,128]{1,0:T(8,128)S(1)}, u32[]{:S(2)}, u32[]{:S(2)}) collective-permute-start(s32[136,128]{1,0:T(8,128)S(1)} %get-tuple-element.30), channel_id=1, source_target_pairs={{0,4},{1,5},{2,6},{3,7},{4,0},{5,1},{6,2},{7,3},{8,12},{9,13},{10,... | collective-permute-start | bytes 208904 | tf_op jit(solution)/shard_map/ppermute | solution.py:290
  9.2 4.3 %collective-permute-start.3 = (s32[136,128]{1,0:T(8,128)S(1)}, s32[136,128]{1,0:T(8,128)S(1)}, u32[]{:S(2)}, u32[]{:S(2)}) collective-permute-start(s32[136,128]{1,0:T(8,128)S(1)} %get-tuple-element.31), channel_id=1, source_target_pairs={{0,8},{1,9},{2,10},{3,11},{4,12},{5,13},{6,14},{7,15},{8,0},{9,1},... | collective-permute-start | bytes 208904 | tf_op jit(solution)/shard_map/ppermute | solution.py:290
  13.8 6.3 %collective-permute-start.4 = (s32[136,128]{1,0:T(8,128)S(1)}, s32[136,128]{1,0:T(8,128)S(1)}, u32[]{:S(2)}, u32[]{:S(2)}) collective-permute-start(s32[136,128]{1,0:T(8,128)S(1)} %get-tuple-element.33), channel_id=1, source_target_pairs={{0,16},{1,17},{2,18},{3,19},{4,20},{5,21},{6,22},{7,23},{8,24},{9,... | collective-permute-start | bytes 208904 | tf_op jit(solution)/shard_map/ppermute | solution.py:290
  16.5 3.5 %collective-permute-start.5 = (s32[1,128]{1,0:T(1,128)S(1)}, s32[1,128]{1,0:T(1,128)S(1)}, u32[]{:S(2)}, u32[]{:S(2)}) collective-permute-start(s32[1,128]{1,0:T(1,128)S(1)} %get-tuple-element.34.refs_0_), channel_id=1, source_target_pairs={{0,1},{1,0},{2,3},{3,2},{4,5},{5,4},{6,7},{7,6},{8,9},{9,8},{10,11... | collective-permute-start | bytes 1544 | tf_op jit(solution)/shard_map/ppermute | solution.py:290
  20.2 5.2 %collective-permute-start.6 = (bf16[32,1024]{1,0:T(8,128)(2,1)S(1)}, bf16[32,1024]{1,0:T(8,128)(2,1)S(1)}, u32[]{:S(2)}, u32[]{:S(2)}) collective-permute-start(bf16[32,1024]{1,0:T(8,128)(2,1)S(1)} %get-tuple-element.37), channel_id=1, source_target_pairs={{0,5},{1,4},{2,7},{3,6},{4,1},{5,0},{6,3},{7,2},{8,13},{9,12},{10,... | collective-permute-start | bytes 196616 | tf_op jit(solution)/shard_map/ppermute | solution.py:290
  22.7 4.3 %collective-permute-start.7 = (bf16[32,1024]{1,0:T(8,128)(2,1)S(1)}, bf16[32,1024]{1,0:T(8,128)(2,1)S(1)}, u32[]{:S(2)}, u32[]{:S(2)}) collective-permute-start(bf16[32,1024]{1,0:T(8,128)(2,1)S(1)} %get-tuple-element.38), channel_id=1, source_target_pairs={{0,4},{1,5},{2,6},{3,7},{4,0},{5,1},{6,2},{7,3},{8,12},{9,13},{10,... | collective-permute-start | bytes 196616 | tf_op jit(solution)/shard_map/ppermute | solution.py:290
  23.3 4.9 %collective-permute-start.8 = (bf16[32,1024]{1,0:T(8,128)(2,1)S(1)}, bf16[32,1024]{1,0:T(8,128)(2,1)S(1)}, u32[]{:S(2)}, u32[]{:S(2)}) collective-permute-start(bf16[32,1024]{1,0:T(8,128)(2,1)S(1)} %get-tuple-element.39), channel_id=1, source_target_pairs={{0,1},{1,0},{2,3},{3,2},{4,5},{5,4},{6,7},{7,6},{8,9},{9,8},{10,11... | collective-permute-start | bytes 196616 | tf_op jit(solution)/shard_map/ppermute | solution.py:290
  23.8 4.4 %collective-permute-start.12 = (bf16[32,1024]{1,0:T(8,128)(2,1)S(1)}, bf16[32,1024]{1,0:T(8,128)(2,1)S(1)}, u32[]{:S(2)}, u32[]{:S(2)}) collective-permute-start(bf16[32,1024]{1,0:T(8,128)(2,1)S(1)} %get-tuple-element.40), channel_id=1, source_target_pairs={{0,3},{1,2},{2,1},{3,0},{4,7},{5,6},{6,5},{7,4},{8,11},{9,10},{10,... | collective-permute-start | bytes 196616 | tf_op jit(solution)/shard_map/ppermute | solution.py:290
  23.8 4.4 %collective-permute-start.9 = (bf16[32,1024]{1,0:T(8,128)(2,1)S(1)}, bf16[32,1024]{1,0:T(8,128)(2,1)S(1)}, u32[]{:S(2)}, u32[]{:S(2)}) collective-permute-start(bf16[32,1024]{1,0:T(8,128)(2,1)S(1)} %get-tuple-element.36.refs_0_), channel_id=1, source_target_pairs={{0,2},{1,3},{2,0},{3,1},{4,6},{5,7},{6,4},{7,5},{8,10},{9,11},{10,... | collective-permute-start | bytes 196616 | tf_op jit(solution)/shard_map/ppermute | solution.py:290
  25.5 2.7 %collective-permute-start.10 = (bf16[32,1024]{1,0:T(8,128)(2,1)S(1)}, bf16[32,1024]{1,0:T(8,128)(2,1)S(1)}, u32[]{:S(2)}, u32[]{:S(2)}) collective-permute-start(bf16[32,1024]{1,0:T(8,128)(2,1)S(1)} %collective-permute-done.6.refs_1_), channel_id=1, source_target_pairs={{0,2},{1,3},{2,0},{3,1},{4,6},{5,7},{6,4},{7,5},{8,10},{9,11},{10,... | collective-permute-start | bytes 196616 | tf_op jit(solution)/shard_map/ppermute | solution.py:290
  26.9 1.3 %collective-permute-start.11 = (bf16[32,1024]{1,0:T(8,128)(2,1)S(1)}, bf16[32,1024]{1,0:T(8,128)(2,1)S(1)}, u32[]{:S(2)}, u32[]{:S(2)}) collective-permute-start(bf16[32,1024]{1,0:T(8,128)(2,1)S(1)} %collective-permute-done.7.refs_2_), channel_id=1, source_target_pairs={{0,2},{1,3},{2,0},{3,1},{4,6},{5,7},{6,4},{7,5},{8,10},{9,11},{10,... | collective-permute-start | bytes 196616 | tf_op jit(solution)/shard_map/ppermute | solution.py:290

commit v18 on v13

--- a/solution.py
+++ b/solution.py
@@ -224,7 +224,7 @@
     label_out[...] = label_ref[...]
 
 
-def square_kernel(total_ref, both_ref, x_ref, z_ref, sum_ref, out_ref):
+def square_kernel(total_ref, both_ref, z_ref, x_ref, sum_ref, out_ref):
     size = total_ref.shape[0]
     total = (total_ref[...] + decode(x_ref, size)) + (decode(z_ref, size) + decode(both_ref, size))
     sum_ref[...] = total
@@ -268,10 +268,11 @@
     )(*operands)
 
 
-def swap(array, tok=0, feat=0):
+def swap(array, tok=0, feat=0, odd=None):
     tok_count, feat_count = lax.axis_size("tok"), lax.axis_size("feat")
+    bits = (feat, odd or feat)
     pairs = [
-        (f * tok_count + t, (f ^ feat) * tok_count + (t ^ tok))
+        (f * tok_count + t, (f ^ bits[f & 1]) * tok_count + (t ^ tok))
         for f in range(feat_count)
         for t in range(tok_count)
     ]
@@ -300,14 +301,14 @@
         labels.reshape(1, rows),
         out_shape=[total_type, word_type, word_type, word_type, label_type],
     )
-    both = swap(again, feat=6)
+    both = swap(again, feat=10, odd=6)
+    z_word = swap(here, feat=8, odd=4)
     x_word = swap(there, feat=2)
-    z_word = swap(here, feat=4)
     all_labels = [label] + [swap(label, tok=tok) for tok in range(1, tok_count)]
     total, word = local_call(
-        square_kernel, "add_square", total, both, x_word, z_word, out_shape=[total_type, word_type]
+        square_kernel, "add_square", total, both, z_word, x_word, out_shape=[total_type, word_type]
     )
-    word = swap(word, feat=8)
+    word = swap(word, feat=4, odd=8)
     stride = 16
     while stride < feat_count:
         total, word = local_call(middle_kernel, "add_encode", total, word, out_shape=[total_type, word_type])

time: 30.9 us -> 31.2 us (level)
  transfers between devices with their start and end apart: 13 -> 13, of which waited for: 7 -> 5; matrix products, arithmetic and copies ran while one was open for 0% -> 0% of each run, Pallas kernels for 4% -> 4%
where the time goes in v18:
time: 31.2 us; the launch traced here: 31 us
  starting transfers between devices  14.3 us (46%)
  waiting for transfers between devices  9.35 us (30%)
  Pallas kernels  7.28 us (23%)
    ppermute x13, starting transfers between devices, swap(): return lax.ppermute(array, ('feat', 'tok'), pairs)  14.3 us
    ppermute x13, waiting for transfers between devices, swap(): return lax.ppermute(array, ('feat', 'tok'), pairs)  9.35 us
    pallas_call x1, Pallas kernels, partial_halves(): pl.pallas_call(functools.partial(send_kernel, total_bits, parts), in_spec...  2.86 us
    pallas_call x1, Pallas kernels, gram_blocks(): pl.pallas_call(functools.partial(gram_kernel, shard, group, factor), in_s...  2.51 us
    pallas_call x1, Pallas kernels, partial_halves(): pl.pallas_call(functools.partial(keep_kernel, parts), out_shape=total_typ...  1.3 us
  transfers between devices with their start and end apart: 13, of which 5 were waited for; matrix products, arithmetic and copies ran while one was open for 0% of the time, Pallas kernels for 4%

profile of v18, /device:TPU:0, one launch (start us, length us, event | category | flops | bytes accessed | tf_op | source)
XLA Modules:
  0.0 31.0 jit_solution(11390127316750805197)
XLA Ops:
  0.0 2.9 %partial_sent.1 = (f32[64,1024]{1,0:T(8,128)S(1)}, bf16[64,8192]{1,0:T(8,128)(2,1)S(1)}, s32[1,8192]{1,0:T(1,128)S(1)}, bf16[256,1024]{1,0:T(8,128)(2,1)S(1)}, f32[32,1024]{1,0:T(8,128)S(1)}) custom-call(bf16[128,8192]{1,0:T(8,128)(2,1)} %x_hbm.1, s32[1,8192]{1,0:T(1,128)} %bitcast.5, s32[1,1024]{1,0:T(1,128)} %bitcast.6), custom_call_target="tpu_custom_call" | custom-call | flops 1073741824 | bytes 2359296 | tf_op jit(solution)/shard_map/partial_sent/pallas_call | solution.py:99
  2.9 0.5 %collective-permute-start = (f32[64,1024]{1,0:T(8,128)S(1)}, f32[64,1024]{1,0:T(8,128)S(1)}, u32[]{:S(2)}, u32[]{:S(2)}) collective-permute-start(f32[64,1024]{1,0:T(8,128)S(1)} %get-tuple-element.27), channel_id=1, source_target_pairs={{0,2},{1,3},{2,0},{3,1},{4,6},{5,7},{6,4},{7,5},{8,10},{9,11},{10,... | collective-permute-start | bytes 786440 | tf_op jit(solution)/shard_map/ppermute | solution.py:279
  3.4 1.3 %partial_kept.1.keep_ref = f32[64,1024]{1,0:T(8,128)S(1)} custom-call(bf16[64,8192]{1,0:T(8,128)(2,1)S(1)} %get-tuple-element.23.x_keep, s32[1,8192]{1,0:T(1,128)S(1)} %get-tuple-element.24.signs, bf16[256,1024]{1,0:T(8,128)(2,1)S(1)} %get-tuple-element.25.low, f32[32,1024]{1,0:T(8,128)S(1)} %get-tuple-element.26.high), custom_call_target="tpu_custom_call" | custom-call | flops 1073741824 | bytes 2359296 | tf_op jit(solution)/shard_map/partial_kept/pallas_call | solution.py:123
  4.7 0.2 first_split.1
  4.9 4.8 %collective-permute-start.1 = (s32[136,128]{1,0:T(8,128)S(1)}, s32[136,128]{1,0:T(8,128)S(1)}, u32[]{:S(2)}, u32[]{:S(2)}) collective-permute-start(s32[136,128]{1,0:T(8,128)S(1)} %get-tuple-element.29), channel_id=1, source_target_pairs={{0,20},{1,21},{2,14},{3,15},{4,16},{5,17},{6,10},{7,11},{8,28},{9,... | collective-permute-start | bytes 208904 | tf_op jit(solution)/shard_map/ppermute | solution.py:279
  9.6 0.3 %collective-permute-start.2 = (s32[136,128]{1,0:T(8,128)S(1)}, s32[136,128]{1,0:T(8,128)S(1)}, u32[]{:S(2)}, u32[]{:S(2)}) collective-permute-start(s32[136,128]{1,0:T(8,128)S(1)} %get-tuple-element.30), channel_id=1, source_target_pairs={{0,16},{1,17},{2,10},{3,11},{4,20},{5,21},{6,14},{7,15},{8,24},{9,... | collective-permute-start | bytes 208904 | tf_op jit(solution)/shard_map/ppermute | solution.py:279
  10.0 0.3 collective-permute-start.3
  10.3 1.7 %collective-permute-done.1.both_ref = s32[136,128]{1,0:T(8,128)S(1)} collective-permute-done((s32[136,128]{1,0:T(8,128)S(1)}, s32[136,128]{1,0:T(8,128)S(1)}, u32[]{:S(2)}, u32[]{:S(2)}) %collective-permute-start.1) | collective-permute-done | bytes 69664 | tf_op jit(solution)/shard_map/ppermute | solution.py:279
  12.0 2.8 %collective-permute-done.2.z_ref = s32[136,128]{1,0:T(8,128)S(1)} collective-permute-done((s32[136,128]{1,0:T(8,128)S(1)}, s32[136,128]{1,0:T(8,128)S(1)}, u32[]{:S(2)}, u32[]{:S(2)}) %collective-permute-start.2) | collective-permute-done | bytes 69664 | tf_op jit(solution)/shard_map/ppermute | solution.py:279
  14.9 0.3 add_square.1
  15.1 1.6 %collective-permute-start.4 = (s32[136,128]{1,0:T(8,128)S(1)}, s32[136,128]{1,0:T(8,128)S(1)}, u32[]{:S(2)}, u32[]{:S(2)}) collective-permute-start(s32[136,128]{1,0:T(8,128)S(1)} %get-tuple-element.33), channel_id=1, source_target_pairs={{0,8},{1,9},{2,18},{3,19},{4,12},{5,13},{6,22},{7,23},{8,0},{9,1},... | collective-permute-start | bytes 208904 | tf_op jit(solution)/shard_map/ppermute | solution.py:279
  16.8 1.5 %collective-permute-start.5 = (s32[1,128]{1,0:T(1,128)S(1)}, s32[1,128]{1,0:T(1,128)S(1)}, u32[]{:S(2)}, u32[]{:S(2)}) collective-permute-start(s32[1,128]{1,0:T(1,128)S(1)} %get-tuple-element.34.refs_0_), channel_id=1, source_target_pairs={{0,1},{1,0},{2,3},{3,2},{4,5},{5,4},{6,7},{7,6},{8,9},{9,8},{10,11... | collective-permute-start | bytes 1544 | tf_op jit(solution)/shard_map/ppermute | solution.py:279
  18.3 2.0 %collective-permute-done.5.refs_1_ = s32[1,128]{1,0:T(1,128)S(1)} collective-permute-done((s32[1,128]{1,0:T(1,128)S(1)}, s32[1,128]{1,0:T(1,128)S(1)}, u32[]{:S(2)}, u32[]{:S(2)}) %collective-permute-start.5) | collective-permute-done | bytes 544 | tf_op jit(solution)/shard_map/ppermute | solution.py:279
  20.3 0.2 sketch_rows.1
  20.5 1.6 %collective-permute-start.6 = (bf16[32,1024]{1,0:T(8,128)(2,1)S(1)}, bf16[32,1024]{1,0:T(8,128)(2,1)S(1)}, u32[]{:S(2)}, u32[]{:S(2)}) collective-permute-start(bf16[32,1024]{1,0:T(8,128)(2,1)S(1)} %get-tuple-element.37), channel_id=1, source_target_pairs={{0,5},{1,4},{2,7},{3,6},{4,1},{5,0},{6,3},{7,2},{8,13},{9,12},{10,... | collective-permute-start | bytes 196616 | tf_op jit(solution)/shard_map/ppermute | solution.py:279
  22.1 1.5 %collective-permute-start.7 = (bf16[32,1024]{1,0:T(8,128)(2,1)S(1)}, bf16[32,1024]{1,0:T(8,128)(2,1)S(1)}, u32[]{:S(2)}, u32[]{:S(2)}) collective-permute-start(bf16[32,1024]{1,0:T(8,128)(2,1)S(1)} %get-tuple-element.38), channel_id=1, source_target_pairs={{0,4},{1,5},{2,6},{3,7},{4,0},{5,1},{6,2},{7,3},{8,12},{9,13},{10,... | collective-permute-start | bytes 196616 | tf_op jit(solution)/shard_map/ppermute | solution.py:279
  23.5 0.5 %collective-permute-start.8 = (bf16[32,1024]{1,0:T(8,128)(2,1)S(1)}, bf16[32,1024]{1,0:T(8,128)(2,1)S(1)}, u32[]{:S(2)}, u32[]{:S(2)}) collective-permute-start(bf16[32,1024]{1,0:T(8,128)(2,1)S(1)} %get-tuple-element.39), channel_id=1, source_target_pairs={{0,1},{1,0},{2,3},{3,2},{4,5},{5,4},{6,7},{7,6},{8,9},{9,8},{10,11... | collective-permute-start | bytes 196616 | tf_op jit(solution)/shard_map/ppermute | solution.py:279
  24.1 0.0 collective-permute-start.12
  24.1 1.6 %collective-permute-start.9 = (bf16[32,1024]{1,0:T(8,128)(2,1)S(1)}, bf16[32,1024]{1,0:T(8,128)(2,1)S(1)}, u32[]{:S(2)}, u32[]{:S(2)}) collective-permute-start(bf16[32,1024]{1,0:T(8,128)(2,1)S(1)} %get-tuple-element.36.refs_0_), channel_id=1, source_target_pairs={{0,2},{1,3},{2,0},{3,1},{4,6},{5,7},{6,4},{7,5},{8,10},{9,11},{10,... | collective-permute-start | bytes 196616 | tf_op jit(solution)/shard_map/ppermute | solution.py:279
  25.7 0.0 collective-permute-done.6.refs_1_
  25.7 0.8 %collective-permute-done.7.refs_2_ = bf16[32,1024]{1,0:T(8,128)(2,1)S(1)} collective-permute-done((bf16[32,1024]{1,0:T(8,128)(2,1)S(1)}, bf16[32,1024]{1,0:T(8,128)(2,1)S(1)}, u32[]{:S(2)}, u32[]{:S(2)}) %collective-permute-start.7) | collective-permute-done | bytes 65568 | tf_op jit(solution)/shard_map/ppermute | solution.py:279
  26.5 0.0 collective-permute-start.11
  26.5 2.0 %collective-permute-done.8.refs_3_ = bf16[32,1024]{1,0:T(8,128)(2,1)S(1)} collective-permute-done((bf16[32,1024]{1,0:T(8,128)(2,1)S(1)}, bf16[32,1024]{1,0:T(8,128)(2,1)S(1)}, u32[]{:S(2)}, u32[]{:S(2)}) %collective-permute-start.8) | collective-permute-done | bytes 65568 | tf_op jit(solution)/shard_map/ppermute | solution.py:279
  28.5 2.5 %gram.1 = f32[1024,1024]{1,0:T(8,128)} custom-call(s32[1,256]{1,0:T(1,128)S(1)} %get-tuple-element.35.label_ref, bf16[32,1024]{1,0:T(8,128)(2,1)S(1)} %get-tuple-element.36.refs_0_, bf16[32,1024]{1,0:T(8,128)(2,1)S(1)} %collective-permute-done.6.refs_1_, bf16[32,1024]{1,0:T(8,128)(2,1)S(1)} %collective-permute-done.7.refs_2_, ...), custom_call_target="tpu_custom_call" | custom-call | flops 536870912 | bytes 4194304 | tf_op jit(solution)/shard_map/gram/pallas_call | solution.py:165
  (10 shorter events, 0.0 us)
Async XLA Ops:
  0.0 4.7 %copy-start = (s32[128,1]{0,1:T(1,128)S(1)}, s32[128,1]{0,1:T(1,128)}, u32[]{:S(2)}) copy-start(s32[128,1]{0,1:T(1,128)} %param.7) | copy-start | bytes 1540
  2.9 1.8 %collective-permute-start = (f32[64,1024]{1,0:T(8,128)S(1)}, f32[64,1024]{1,0:T(8,128)S(1)}, u32[]{:S(2)}, u32[]{:S(2)}) collective-permute-start(f32[64,1024]{1,0:T(8,128)S(1)} %get-tuple-element.27), channel_id=1, source_target_pairs={{0,2},{1,3},{2,0},{3,1},{4,6},{5,7},{6,4},{7,5},{8,10},{9,11},{10,... | collective-permute-start | bytes 786440 | tf_op jit(solution)/shard_map/ppermute | solution.py:279
  4.9 7.1 %collective-permute-start.1 = (s32[136,128]{1,0:T(8,128)S(1)}, s32[136,128]{1,0:T(8,128)S(1)}, u32[]{:S(2)}, u32[]{:S(2)}) collective-permute-start(s32[136,128]{1,0:T(8,128)S(1)} %get-tuple-element.29), channel_id=1, source_target_pairs={{0,20},{1,21},{2,14},{3,15},{4,16},{5,17},{6,10},{7,11},{8,28},{9,... | collective-permute-start | bytes 208904 | tf_op jit(solution)/shard_map/ppermute | solution.py:279
  9.6 5.2 %collective-permute-start.2 = (s32[136,128]{1,0:T(8,128)S(1)}, s32[136,128]{1,0:T(8,128)S(1)}, u32[]{:S(2)}, u32[]{:S(2)}) collective-permute-start(s32[136,128]{1,0:T(8,128)S(1)} %get-tuple-element.30), channel_id=1, source_target_pairs={{0,16},{1,17},{2,10},{3,11},{4,20},{5,21},{6,14},{7,15},{8,24},{9,... | collective-permute-start | bytes 208904 | tf_op jit(solution)/shard_map/ppermute | solution.py:279
  10.0 4.9 %collective-permute-start.3 = (s32[136,128]{1,0:T(8,128)S(1)}, s32[136,128]{1,0:T(8,128)S(1)}, u32[]{:S(2)}, u32[]{:S(2)}) collective-permute-start(s32[136,128]{1,0:T(8,128)S(1)} %get-tuple-element.31), channel_id=1, source_target_pairs={{0,4},{1,5},{2,6},{3,7},{4,0},{5,1},{6,2},{7,3},{8,12},{9,13},{10,... | collective-permute-start | bytes 208904 | tf_op jit(solution)/shard_map/ppermute | solution.py:279
  15.1 5.2 %collective-permute-start.4 = (s32[136,128]{1,0:T(8,128)S(1)}, s32[136,128]{1,0:T(8,128)S(1)}, u32[]{:S(2)}, u32[]{:S(2)}) collective-permute-start(s32[136,128]{1,0:T(8,128)S(1)} %get-tuple-element.33), channel_id=1, source_target_pairs={{0,8},{1,9},{2,18},{3,19},{4,12},{5,13},{6,22},{7,23},{8,0},{9,1},... | collective-permute-start | bytes 208904 | tf_op jit(solution)/shard_map/ppermute | solution.py:279
  16.8 3.5 %collective-permute-start.5 = (s32[1,128]{1,0:T(1,128)S(1)}, s32[1,128]{1,0:T(1,128)S(1)}, u32[]{:S(2)}, u32[]{:S(2)}) collective-permute-start(s32[1,128]{1,0:T(1,128)S(1)} %get-tuple-element.34.refs_0_), channel_id=1, source_target_pairs={{0,1},{1,0},{2,3},{3,2},{4,5},{5,4},{6,7},{7,6},{8,9},{9,8},{10,11... | collective-permute-start | bytes 1544 | tf_op jit(solution)/shard_map/ppermute | solution.py:279
  20.5 5.2 %collective-permute-start.6 = (bf16[32,1024]{1,0:T(8,128)(2,1)S(1)}, bf16[32,1024]{1,0:T(8,128)(2,1)S(1)}, u32[]{:S(2)}, u32[]{:S(2)}) collective-permute-start(bf16[32,1024]{1,0:T(8,128)(2,1)S(1)} %get-tuple-element.37), channel_id=1, source_target_pairs={{0,5},{1,4},{2,7},{3,6},{4,1},{5,0},{6,3},{7,2},{8,13},{9,12},{10,... | collective-permute-start | bytes 196616 | tf_op jit(solution)/shard_map/ppermute | solution.py:279
  22.1 4.4 %collective-permute-start.7 = (bf16[32,1024]{1,0:T(8,128)(2,1)S(1)}, bf16[32,1024]{1,0:T(8,128)(2,1)S(1)}, u32[]{:S(2)}, u32[]{:S(2)}) collective-permute-start(bf16[32,1024]{1,0:T(8,128)(2,1)S(1)} %get-tuple-element.38), channel_id=1, source_target_pairs={{0,4},{1,5},{2,6},{3,7},{4,0},{5,1},{6,2},{7,3},{8,12},{9,13},{10,... | collective-permute-start | bytes 196616 | tf_op jit(solution)/shard_map/ppermute | solution.py:279
  23.5 4.9 %collective-permute-start.8 = (bf16[32,1024]{1,0:T(8,128)(2,1)S(1)}, bf16[32,1024]{1,0:T(8,128)(2,1)S(1)}, u32[]{:S(2)}, u32[]{:S(2)}) collective-permute-start(bf16[32,1024]{1,0:T(8,128)(2,1)S(1)} %get-tuple-element.39), channel_id=1, source_target_pairs={{0,1},{1,0},{2,3},{3,2},{4,5},{5,4},{6,7},{7,6},{8,9},{9,8},{10,11... | collective-permute-start | bytes 196616 | tf_op jit(solution)/shard_map/ppermute | solution.py:279
  24.1 4.4 %collective-permute-start.12 = (bf16[32,1024]{1,0:T(8,128)(2,1)S(1)}, bf16[32,1024]{1,0:T(8,128)(2,1)S(1)}, u32[]{:S(2)}, u32[]{:S(2)}) collective-permute-start(bf16[32,1024]{1,0:T(8,128)(2,1)S(1)} %get-tuple-element.40), channel_id=1, source_target_pairs={{0,3},{1,2},{2,1},{3,0},{4,7},{5,6},{6,5},{7,4},{8,11},{9,10},{10,... | collective-permute-start | bytes 196616 | tf_op jit(solution)/shard_map/ppermute | solution.py:279
  24.1 4.4 %collective-permute-start.9 = (bf16[32,1024]{1,0:T(8,128)(2,1)S(1)}, bf16[32,1024]{1,0:T(8,128)(2,1)S(1)}, u32[]{:S(2)}, u32[]{:S(2)}) collective-permute-start(bf16[32,1024]{1,0:T(8,128)(2,1)S(1)} %get-tuple-element.36.refs_0_), channel_id=1, source_target_pairs={{0,2},{1,3},{2,0},{3,1},{4,6},{5,7},{6,4},{7,5},{8,10},{9,11},{10,... | collective-permute-start | bytes 196616 | tf_op jit(solution)/shard_map/ppermute | solution.py:279
  25.7 2.7 %collective-permute-start.10 = (bf16[32,1024]{1,0:T(8,128)(2,1)S(1)}, bf16[32,1024]{1,0:T(8,128)(2,1)S(1)}, u32[]{:S(2)}, u32[]{:S(2)}) collective-permute-start(bf16[32,1024]{1,0:T(8,128)(2,1)S(1)} %collective-permute-done.6.refs_1_), channel_id=1, source_target_pairs={{0,2},{1,3},{2,0},{3,1},{4,6},{5,7},{6,4},{7,5},{8,10},{9,11},{10,... | collective-permute-start | bytes 196616 | tf_op jit(solution)/shard_map/ppermute | solution.py:279
  26.5 2.0 %collective-permute-start.11 = (bf16[32,1024]{1,0:T(8,128)(2,1)S(1)}, bf16[32,1024]{1,0:T(8,128)(2,1)S(1)}, u32[]{:S(2)}, u32[]{:S(2)}) collective-permute-start(bf16[32,1024]{1,0:T(8,128)(2,1)S(1)} %collective-permute-done.7.refs_2_), channel_id=1, source_target_pairs={{0,2},{1,3},{2,0},{3,1},{4,6},{5,7},{6,4},{7,5},{8,10},{9,11},{10,... | collective-permute-start | bytes 196616 | tf_op jit(solution)/shard_map/ppermute | solution.py:279

commit v19 on v18

--- a/solution.py
+++ b/solution.py
@@ -130,19 +130,20 @@
     return keep, got
 
 
-def gram_kernel(shard, group, factor, label_ref, *refs):
+def gram_kernel(shard, group, factor, *refs):
     pieces, (out_hbm, rows, blocks, sems) = refs[:-4], refs[-4:]
-    steps, wide, _ = blocks.shape
+    steps, wide, kept = blocks.shape
     place = 0
     for piece in pieces:
-        rows[place:place + piece.shape[0]] = piece[...]
+        rows[place:place + piece.shape[0]] = piece[:, :kept]
         place += piece.shape[0]
     first = lax.axis_index("feat") * shard
     start = pl.multiple_of(first // LANES * LANES, LANES)
     window = rows[:, pl.ds(start, LANES)].astype(jnp.float32) * factor
     window = pltpu.roll(window, lax.rem(LANES - (first - start), LANES), 1)
     own = jnp.concatenate([window.T[:shard]] * group, axis=0)
-    label = label_ref[...] - lax.broadcasted_iota(jnp.int32, own.shape, 0) // shard
+    named = jnp.concatenate([piece[:, kept:].astype(jnp.float32) for piece in pieces], axis=0).T[:1]
+    label = named.astype(jnp.int32) - lax.broadcasted_iota(jnp.int32, own.shape, 0) // shard
     base = lax.axis_index("tok") * steps * group
     copies = []
     for step in range(steps):
@@ -156,15 +157,15 @@
         copy.wait()
 
 
-def gram_blocks(pieces, label_row, concepts, shard, factor):
+def gram_blocks(pieces, concepts, shard, factor):
     tokens = sum(piece.shape[0] for piece in pieces)
-    kept = pieces[0].shape[1]
+    kept = pieces[0].shape[1] - LANES
     group = max(1, min(concepts, LOW // shard))
     wide = group * shard
     steps = concepts // group
     return pl.pallas_call(
         functools.partial(gram_kernel, shard, group, factor),
-        in_specs=[pl.BlockSpec(memory_space=pltpu.VMEM)] * (1 + len(pieces)),
+        in_specs=[pl.BlockSpec(memory_space=pltpu.VMEM)] * len(pieces),
         out_specs=pl.BlockSpec(memory_space=pltpu.HBM),
         out_shape=jax.ShapeDtypeStruct((concepts * shard, kept), jnp.float32),
         scratch_shapes=[
@@ -177,7 +178,7 @@
             flops=2 * tokens * concepts * shard * kept, bytes_accessed=4 * concepts * shard * kept, transcendentals=0
         ),
         name="gram",
-    )(label_row, *pieces)
+    )(*pieces)
 
 
 def encode(values, word_ref):
@@ -208,7 +209,7 @@
     return code * scale
 
 
-def first_kernel(stride, keep_ref, got_ref, label_ref, total_ref, there_ref, here_ref, again_ref, label_out):
+def first_kernel(stride, keep_ref, got_ref, total_ref, there_ref, here_ref, again_ref):
     size = total_ref.shape[0]
     digit = lax.rem(lax.axis_index("feat") // stride, 2)
 
@@ -221,7 +222,6 @@
     total = piece(digit)
     total_ref[...] = total
     encode(total, here_ref)
-    label_out[...] = label_ref[...]
 
 
 def square_kernel(total_ref, both_ref, z_ref, x_ref, sum_ref, out_ref):
@@ -237,26 +237,17 @@
     encode(total, out_ref)
 
 
-def last_kernel(scale, blocks, total_ref, word_ref, *refs):
-    label_refs, (label_out, *row_refs) = refs[:-6], refs[-6:]
-    size = total_ref.shape[0]
+def last_kernel(scale, total_ref, word_ref, label_ref, *row_refs):
+    size, kept = total_ref.shape
     row = ((total_ref[...] + decode(word_ref, size)) * scale).astype(jnp.bfloat16)
+    me = lax.axis_index("feat")
+    first = lax.rem(me, 2) * 2 * size + lax.rem(me // 2, 2) * size
+    label = jnp.broadcast_to(label_ref[...].astype(jnp.float32), (8, LANES))
+    label = pltpu.roll(label, lax.rem(LANES - first, LANES), 1)
+    label = jnp.broadcast_to(label[:1], (LANES, LANES)).T[:size].astype(jnp.bfloat16)
     for row_ref in row_refs:
-        row_ref[...] = row
-    core = lax.rem(lax.axis_index("feat"), 2)
-    digit = lax.rem(lax.axis_index("feat") // 2, 2)
-    groups = LANES // size
-    lane = lax.broadcasted_iota(jnp.int32, (8, LANES), 1)
-    for place in range(0, 2 * len(blocks), groups):
-        out = jnp.zeros((8, LANES), jnp.int32)
-        for at in range(groups):
-            half, (tok, x) = (place + at) // len(blocks), blocks[(place + at) % len(blocks)]
-            source = (core ^ half) * 2 * size + (digit ^ x) * size
-            moved = pltpu.roll(
-                jnp.broadcast_to(label_refs[tok][...], out.shape), lax.rem(at * size - source + LANES, LANES), 1
-            )
-            out = jnp.where(lane // size == at, moved, out)
-        label_out[:, place * size:(place + groups) * size] = out[:1]
+        row_ref[:, :kept] = row
+        row_ref[:, kept:] = label
 
 
 def local_call(kernel, name, *operands, out_shape):
@@ -282,29 +273,25 @@
 def body(features, signs, columns, labels):
     rows, width = features.shape
     feat_count = lax.axis_size("feat")
-    feat_index = lax.axis_index("feat")
     tok_count = lax.axis_size("tok")
     kept = columns.shape[0]
     shard = kept // feat_count
     size = rows // 4
     total_type = jax.ShapeDtypeStruct((size, kept), jnp.float32)
     word_type = jax.ShapeDtypeStruct((kept // LANES * (size // 2) + 8, LANES), jnp.int32)
-    row_type = jax.ShapeDtypeStruct((size, kept), jnp.bfloat16)
-    label_type = jax.ShapeDtypeStruct((1, rows), jnp.int32)
+    row_type = jax.ShapeDtypeStruct((size, kept + LANES), jnp.bfloat16)
 
     keep, got = partial_halves(features, signs, columns, feat_count)
-    total, there, here, again, label = local_call(
+    total, there, here, again = local_call(
         functools.partial(first_kernel, 2),
         "first_split",
         keep,
         got,
-        labels.reshape(1, rows),
-        out_shape=[total_type, word_type, word_type, word_type, label_type],
+        out_shape=[total_type, word_type, word_type, word_type],
     )
     both = swap(again, feat=10, odd=6)
     z_word = swap(here, feat=8, odd=4)
     x_word = swap(there, feat=2)
-    all_labels = [label] + [swap(label, tok=tok) for tok in range(1, tok_count)]
     total, word = local_call(
         square_kernel, "add_square", total, both, z_word, x_word, out_shape=[total_type, word_type]
     )
@@ -315,31 +302,26 @@
         word = swap(word, feat=stride)
         stride *= 2
 
-    blocks = [(0, 0)]
-    stride = 2
-    while stride < tok_count:
-        blocks = blocks + [(tok ^ stride, x) for tok, x in blocks]
-        stride *= 2
-    blocks = [(tok ^ flip, x) for flip, x in ((0, 0), (1, 1), (0, 1), (1, 0)) for tok, _ in blocks]
     scale = 1.0 / math.sqrt(width * feat_count)
-    label_row, *copies = local_call(
-        functools.partial(last_kernel, scale, blocks),
+    own, *copies = local_call(
+        functools.partial(last_kernel, scale),
         "sketch_rows",
         total,
         word,
-        *all_labels,
-        out_shape=[jax.ShapeDtypeStruct((1, 2 * len(blocks) * size), jnp.int32)] + [row_type] * 5,
+        labels.reshape(1, rows),
+        out_shape=[row_type] * 5,
     )
     stride = 2
     while stride < tok_count:
-        copies = [jnp.concatenate([copies[0], swap(copies[0], tok=stride)], axis=0)] * 5
+        copies = [jnp.concatenate([copies[0], swap(copies[0], tok=stride)], axis=0)] * 4
+        own = copies[0]
         stride *= 2
     received = [swap(copies[0], tok=1, feat=2), swap(copies[1], feat=2), swap(copies[2], tok=1)]
     last = swap(copies[3], tok=1, feat=1)
-    ours = copies[4:] + received
+    ours = [own] + received
     theirs = [swap(block, feat=1) for block in ours[:3]] + [last]
     concepts = C // tok_count
-    gram = gram_blocks(ours + theirs, label_row, concepts, shard, C / (rows * tok_count))
+    gram = gram_blocks(ours + theirs, concepts, shard, C / (rows * tok_count))
     return gram.reshape(concepts, shard, kept)
 
 

time: 31.2 us -> 30.6 us (0.981)
  starting transfers between devices: 14.3 us -> 12.8 us
  waiting for transfers between devices: 9.35 us -> 10.2 us
    ppermute x13 -> x12, starting transfers between devices: 14.3 us -> 12.8 us  [swap(): return lax.ppermute(array, ('feat', 'tok'), pairs)]
    ppermute x13 -> x12, waiting for transfers between devices: 9.35 us -> 10.2 us  [swap(): return lax.ppermute(array, ('feat', 'tok'), pairs)]
  transfers between devices with their start and end apart: 13 -> 12, of which waited for: 5 -> 6; matrix products, arithmetic and copies ran while one was open for 0% -> 0% of each run, Pallas kernels for 4% -> 4%
where the time goes in v19:
time: 30.6 us; the launch traced here: 30.3 us
  starting transfers between devices  12.8 us (42%)
  waiting for transfers between devices  10.2 us (33%)
  Pallas kernels  7.28 us (24%)
    ppermute x12, starting transfers between devices, swap(): return lax.ppermute(array, ('feat', 'tok'), pairs)  12.8 us
    ppermute x12, waiting for transfers between devices, swap(): return lax.ppermute(array, ('feat', 'tok'), pairs)  10.2 us
    pallas_call x1, Pallas kernels, partial_halves(): pl.pallas_call(functools.partial(send_kernel, total_bits, parts), in_spec...  2.86 us
    pallas_call x1, Pallas kernels, gram_blocks(): pl.pallas_call(functools.partial(gram_kernel, shard, group, factor), in_s...  2.49 us
    pallas_call x1, Pallas kernels, partial_halves(): pl.pallas_call(functools.partial(keep_kernel, parts), out_shape=total_typ...  1.3 us
    pallas_call x3, Pallas kernels, local_call(): pl.pallas_call(kernel, out_shape=out_shape, compiler_params=pltpu.Compile...  0.62 us
  transfers between devices with their start and end apart: 12, of which 6 were waited for; matrix products, arithmetic and copies ran while one was open for 0% of the time, Pallas kernels for 4%

profile of v19, /device:TPU:0, one launch (start us, length us, event | category | flops | bytes accessed | tf_op | source)
XLA Modules:
  0.0 30.3 jit_solution(1638851937034448081)
XLA Ops:
  0.0 2.9 %partial_sent.1 = (f32[64,1024]{1,0:T(8,128)S(1)}, bf16[64,8192]{1,0:T(8,128)(2,1)S(1)}, s32[1,8192]{1,0:T(1,128)S(1)}, bf16[256,1024]{1,0:T(8,128)(2,1)S(1)}, f32[32,1024]{1,0:T(8,128)S(1)}) custom-call(bf16[128,8192]{1,0:T(8,128)(2,1)} %x_hbm.1, s32[1,8192]{1,0:T(1,128)} %bitcast.5, s32[1,1024]{1,0:T(1,128)} %bitcast.6), custom_call_target="tpu_custom_call" | custom-call | flops 1073741824 | bytes 2359296 | tf_op jit(solution)/shard_map/partial_sent/pallas_call | solution.py:99
  2.9 0.5 %collective-permute-start = (f32[64,1024]{1,0:T(8,128)S(1)}, f32[64,1024]{1,0:T(8,128)S(1)}, u32[]{:S(2)}, u32[]{:S(2)}) collective-permute-start(f32[64,1024]{1,0:T(8,128)S(1)} %get-tuple-element.25), channel_id=1, source_target_pairs={{0,2},{1,3},{2,0},{3,1},{4,6},{5,7},{6,4},{7,5},{8,10},{9,11},{10,... | collective-permute-start | bytes 786440 | tf_op jit(solution)/shard_map/ppermute | solution.py:270
  3.4 1.3 %partial_kept.1.keep_ref = f32[64,1024]{1,0:T(8,128)S(1)} custom-call(bf16[64,8192]{1,0:T(8,128)(2,1)S(1)} %get-tuple-element.21.x_keep, s32[1,8192]{1,0:T(1,128)S(1)} %get-tuple-element.22.signs, bf16[256,1024]{1,0:T(8,128)(2,1)S(1)} %get-tuple-element.23.low, f32[32,1024]{1,0:T(8,128)S(1)} %get-tuple-element.24.high), custom_call_target="tpu_custom_call" | custom-call | flops 1073741824 | bytes 2359296 | tf_op jit(solution)/shard_map/partial_kept/pallas_call | solution.py:123
  4.7 0.0 collective-permute-done.got_ref
  4.7 0.2 first_split.1
  4.9 4.8 %collective-permute-start.1 = (s32[136,128]{1,0:T(8,128)S(1)}, s32[136,128]{1,0:T(8,128)S(1)}, u32[]{:S(2)}, u32[]{:S(2)}) collective-permute-start(s32[136,128]{1,0:T(8,128)S(1)} %get-tuple-element.27), channel_id=1, source_target_pairs={{0,20},{1,21},{2,14},{3,15},{4,16},{5,17},{6,10},{7,11},{8,28},{9,... | collective-permute-start | bytes 208904 | tf_op jit(solution)/shard_map/ppermute | solution.py:270
  9.6 0.3 %collective-permute-start.2 = (s32[136,128]{1,0:T(8,128)S(1)}, s32[136,128]{1,0:T(8,128)S(1)}, u32[]{:S(2)}, u32[]{:S(2)}) collective-permute-start(s32[136,128]{1,0:T(8,128)S(1)} %get-tuple-element.28), channel_id=1, source_target_pairs={{0,16},{1,17},{2,10},{3,11},{4,20},{5,21},{6,14},{7,15},{8,24},{9,... | collective-permute-start | bytes 208904 | tf_op jit(solution)/shard_map/ppermute | solution.py:270
  10.0 0.3 collective-permute-start.3
  10.3 1.7 %collective-permute-done.1.both_ref = s32[136,128]{1,0:T(8,128)S(1)} collective-permute-done((s32[136,128]{1,0:T(8,128)S(1)}, s32[136,128]{1,0:T(8,128)S(1)}, u32[]{:S(2)}, u32[]{:S(2)}) %collective-permute-start.1) | collective-permute-done | bytes 69664 | tf_op jit(solution)/shard_map/ppermute | solution.py:270
  12.0 2.8 %collective-permute-done.2.z_ref = s32[136,128]{1,0:T(8,128)S(1)} collective-permute-done((s32[136,128]{1,0:T(8,128)S(1)}, s32[136,128]{1,0:T(8,128)S(1)}, u32[]{:S(2)}, u32[]{:S(2)}) %collective-permute-start.2) | collective-permute-done | bytes 69664 | tf_op jit(solution)/shard_map/ppermute | solution.py:270
  14.9 0.0 collective-permute-done.3.x_ref
  14.9 0.3 add_square.1
  15.1 1.6 %collective-permute-start.4 = (s32[136,128]{1,0:T(8,128)S(1)}, s32[136,128]{1,0:T(8,128)S(1)}, u32[]{:S(2)}, u32[]{:S(2)}) collective-permute-start(s32[136,128]{1,0:T(8,128)S(1)} %get-tuple-element.31), channel_id=1, source_target_pairs={{0,8},{1,9},{2,18},{3,19},{4,12},{5,13},{6,22},{7,23},{8,0},{9,1},... | collective-permute-start | bytes 208904 | tf_op jit(solution)/shard_map/ppermute | solution.py:270
  16.8 2.7 %collective-permute-done.4.word_ref = s32[136,128]{1,0:T(8,128)S(1)} collective-permute-done((s32[136,128]{1,0:T(8,128)S(1)}, s32[136,128]{1,0:T(8,128)S(1)}, u32[]{:S(2)}, u32[]{:S(2)}) %collective-permute-start.4) | collective-permute-done | bytes 69664 | tf_op jit(solution)/shard_map/ppermute | solution.py:270
  19.5 0.2 sketch_rows.1
  19.7 1.6 %collective-permute-start.5 = (bf16[32,1152]{1,0:T(8,128)(2,1)S(1)}, bf16[32,1152]{1,0:T(8,128)(2,1)S(1)}, u32[]{:S(2)}, u32[]{:S(2)}) collective-permute-start(bf16[32,1152]{1,0:T(8,128)(2,1)S(1)} %get-tuple-element.33), channel_id=1, source_target_pairs={{0,5},{1,4},{2,7},{3,6},{4,1},{5,0},{6,3},{7,2},{8,13},{9,12},{10,... | collective-permute-start | bytes 221192 | tf_op jit(solution)/shard_map/ppermute | solution.py:270
  21.3 1.5 %collective-permute-start.6 = (bf16[32,1152]{1,0:T(8,128)(2,1)S(1)}, bf16[32,1152]{1,0:T(8,128)(2,1)S(1)}, u32[]{:S(2)}, u32[]{:S(2)}) collective-permute-start(bf16[32,1152]{1,0:T(8,128)(2,1)S(1)} %get-tuple-element.34), channel_id=1, source_target_pairs={{0,4},{1,5},{2,6},{3,7},{4,0},{5,1},{6,2},{7,3},{8,12},{9,13},{10,... | collective-permute-start | bytes 221192 | tf_op jit(solution)/shard_map/ppermute | solution.py:270
  22.8 0.5 %collective-permute-start.7 = (bf16[32,1152]{1,0:T(8,128)(2,1)S(1)}, bf16[32,1152]{1,0:T(8,128)(2,1)S(1)}, u32[]{:S(2)}, u32[]{:S(2)}) collective-permute-start(bf16[32,1152]{1,0:T(8,128)(2,1)S(1)} %get-tuple-element.35), channel_id=1, source_target_pairs={{0,1},{1,0},{2,3},{3,2},{4,5},{5,4},{6,7},{7,6},{8,9},{9,8},{10,11... | collective-permute-start | bytes 221192 | tf_op jit(solution)/shard_map/ppermute | solution.py:270
  23.3 1.6 %collective-permute-start.8 = (bf16[32,1152]{1,0:T(8,128)(2,1)S(1)}, bf16[32,1152]{1,0:T(8,128)(2,1)S(1)}, u32[]{:S(2)}, u32[]{:S(2)}) collective-permute-start(bf16[32,1152]{1,0:T(8,128)(2,1)S(1)} %get-tuple-element.32.refs_0_), channel_id=1, source_target_pairs={{0,2},{1,3},{2,0},{3,1},{4,6},{5,7},{6,4},{7,5},{8,10},{9,11},{10,... | collective-permute-start | bytes 221192 | tf_op jit(solution)/shard_map/ppermute | solution.py:270
  24.9 0.1 collective-permute-done.5.refs_1_
  25.0 0.0 collective-permute-start.9
  25.0 0.8 %collective-permute-done.6.refs_2_ = bf16[32,1152]{1,0:T(8,128)(2,1)S(1)} collective-permute-done((bf16[32,1152]{1,0:T(8,128)(2,1)S(1)}, bf16[32,1152]{1,0:T(8,128)(2,1)S(1)}, u32[]{:S(2)}, u32[]{:S(2)}) %collective-permute-start.6) | collective-permute-done | bytes 73760 | tf_op jit(solution)/shard_map/ppermute | solution.py:270
  25.9 1.9 %collective-permute-done.7.refs_3_ = bf16[32,1152]{1,0:T(8,128)(2,1)S(1)} collective-permute-done((bf16[32,1152]{1,0:T(8,128)(2,1)S(1)}, bf16[32,1152]{1,0:T(8,128)(2,1)S(1)}, u32[]{:S(2)}, u32[]{:S(2)}) %collective-permute-start.7) | collective-permute-done | bytes 73760 | tf_op jit(solution)/shard_map/ppermute | solution.py:270
  27.8 2.5 %gram.1 = f32[1024,1024]{1,0:T(8,128)} custom-call(bf16[32,1152]{1,0:T(8,128)(2,1)S(1)} %get-tuple-element.32.refs_0_, bf16[32,1152]{1,0:T(8,128)(2,1)S(1)} %collective-permute-done.5.refs_1_, bf16[32,1152]{1,0:T(8,128)(2,1)S(1)} %collective-permute-done.6.refs_2_, bf16[32,1152]{1,0:T(8,128)(2,1)S(1)} %collective-permute-done.7.refs_3_, ...), custom_call_target="tpu_custom_call" | custom-call | flops 536870912 | bytes 4194304 | tf_op jit(solution)/shard_map/gram/pallas_call | solution.py:166
  (8 shorter events, 0.0 us)
Async XLA Ops:
  0.0 19.5 %copy-start = (s32[128,1]{0,1:T(1,128)S(1)}, s32[128,1]{0,1:T(1,128)}, u32[]{:S(2)}) copy-start(s32[128,1]{0,1:T(1,128)} %param.7) | copy-start | bytes 1540
  2.9 1.8 %collective-permute-start = (f32[64,1024]{1,0:T(8,128)S(1)}, f32[64,1024]{1,0:T(8,128)S(1)}, u32[]{:S(2)}, u32[]{:S(2)}) collective-permute-start(f32[64,1024]{1,0:T(8,128)S(1)} %get-tuple-element.25), channel_id=1, source_target_pairs={{0,2},{1,3},{2,0},{3,1},{4,6},{5,7},{6,4},{7,5},{8,10},{9,11},{10,... | collective-permute-start | bytes 786440 | tf_op jit(solution)/shard_map/ppermute | solution.py:270
  4.9 7.1 %collective-permute-start.1 = (s32[136,128]{1,0:T(8,128)S(1)}, s32[136,128]{1,0:T(8,128)S(1)}, u32[]{:S(2)}, u32[]{:S(2)}) collective-permute-start(s32[136,128]{1,0:T(8,128)S(1)} %get-tuple-element.27), channel_id=1, source_target_pairs={{0,20},{1,21},{2,14},{3,15},{4,16},{5,17},{6,10},{7,11},{8,28},{9,... | collective-permute-start | bytes 208904 | tf_op jit(solution)/shard_map/ppermute | solution.py:270
  9.6 5.2 %collective-permute-start.2 = (s32[136,128]{1,0:T(8,128)S(1)}, s32[136,128]{1,0:T(8,128)S(1)}, u32[]{:S(2)}, u32[]{:S(2)}) collective-permute-start(s32[136,128]{1,0:T(8,128)S(1)} %get-tuple-element.28), channel_id=1, source_target_pairs={{0,16},{1,17},{2,10},{3,11},{4,20},{5,21},{6,14},{7,15},{8,24},{9,... | collective-permute-start | bytes 208904 | tf_op jit(solution)/shard_map/ppermute | solution.py:270
  10.0 4.9 %collective-permute-start.3 = (s32[136,128]{1,0:T(8,128)S(1)}, s32[136,128]{1,0:T(8,128)S(1)}, u32[]{:S(2)}, u32[]{:S(2)}) collective-permute-start(s32[136,128]{1,0:T(8,128)S(1)} %get-tuple-element.29), channel_id=1, source_target_pairs={{0,4},{1,5},{2,6},{3,7},{4,0},{5,1},{6,2},{7,3},{8,12},{9,13},{10,... | collective-permute-start | bytes 208904 | tf_op jit(solution)/shard_map/ppermute | solution.py:270
  15.1 4.4 %collective-permute-start.4 = (s32[136,128]{1,0:T(8,128)S(1)}, s32[136,128]{1,0:T(8,128)S(1)}, u32[]{:S(2)}, u32[]{:S(2)}) collective-permute-start(s32[136,128]{1,0:T(8,128)S(1)} %get-tuple-element.31), channel_id=1, source_target_pairs={{0,8},{1,9},{2,18},{3,19},{4,12},{5,13},{6,22},{7,23},{8,0},{9,1},... | collective-permute-start | bytes 208904 | tf_op jit(solution)/shard_map/ppermute | solution.py:270
  19.7 5.3 %collective-permute-start.5 = (bf16[32,1152]{1,0:T(8,128)(2,1)S(1)}, bf16[32,1152]{1,0:T(8,128)(2,1)S(1)}, u32[]{:S(2)}, u32[]{:S(2)}) collective-permute-start(bf16[32,1152]{1,0:T(8,128)(2,1)S(1)} %get-tuple-element.33), channel_id=1, source_target_pairs={{0,5},{1,4},{2,7},{3,6},{4,1},{5,0},{6,3},{7,2},{8,13},{9,12},{10,... | collective-permute-start | bytes 221192 | tf_op jit(solution)/shard_map/ppermute | solution.py:270
  21.3 4.6 %collective-permute-start.6 = (bf16[32,1152]{1,0:T(8,128)(2,1)S(1)}, bf16[32,1152]{1,0:T(8,128)(2,1)S(1)}, u32[]{:S(2)}, u32[]{:S(2)}) collective-permute-start(bf16[32,1152]{1,0:T(8,128)(2,1)S(1)} %get-tuple-element.34), channel_id=1, source_target_pairs={{0,4},{1,5},{2,6},{3,7},{4,0},{5,1},{6,2},{7,3},{8,12},{9,13},{10,... | collective-permute-start | bytes 221192 | tf_op jit(solution)/shard_map/ppermute | solution.py:270
  22.8 5.1 %collective-permute-start.7 = (bf16[32,1152]{1,0:T(8,128)(2,1)S(1)}, bf16[32,1152]{1,0:T(8,128)(2,1)S(1)}, u32[]{:S(2)}, u32[]{:S(2)}) collective-permute-start(bf16[32,1152]{1,0:T(8,128)(2,1)S(1)} %get-tuple-element.35), channel_id=1, source_target_pairs={{0,1},{1,0},{2,3},{3,2},{4,5},{5,4},{6,7},{7,6},{8,9},{9,8},{10,11... | collective-permute-start | bytes 221192 | tf_op jit(solution)/shard_map/ppermute | solution.py:270
  23.3 4.6 %collective-permute-start.11 = (bf16[32,1152]{1,0:T(8,128)(2,1)S(1)}, bf16[32,1152]{1,0:T(8,128)(2,1)S(1)}, u32[]{:S(2)}, u32[]{:S(2)}) collective-permute-start(bf16[32,1152]{1,0:T(8,128)(2,1)S(1)} %get-tuple-element.36), channel_id=1, source_target_pairs={{0,3},{1,2},{2,1},{3,0},{4,7},{5,6},{6,5},{7,4},{8,11},{9,10},{10,... | collective-permute-start | bytes 221192 | tf_op jit(solution)/shard_map/ppermute | solution.py:270
  23.3 4.6 %collective-permute-start.8 = (bf16[32,1152]{1,0:T(8,128)(2,1)S(1)}, bf16[32,1152]{1,0:T(8,128)(2,1)S(1)}, u32[]{:S(2)}, u32[]{:S(2)}) collective-permute-start(bf16[32,1152]{1,0:T(8,128)(2,1)S(1)} %get-tuple-element.32.refs_0_), channel_id=1, source_target_pairs={{0,2},{1,3},{2,0},{3,1},{4,6},{5,7},{6,4},{7,5},{8,10},{9,11},{10,... | collective-permute-start | bytes 221192 | tf_op jit(solution)/shard_map/ppermute | solution.py:270
  25.0 2.8 %collective-permute-start.9 = (bf16[32,1152]{1,0:T(8,128)(2,1)S(1)}, bf16[32,1152]{1,0:T(8,128)(2,1)S(1)}, u32[]{:S(2)}, u32[]{:S(2)}) collective-permute-start(bf16[32,1152]{1,0:T(8,128)(2,1)S(1)} %collective-permute-done.5.refs_1_), channel_id=1, source_target_pairs={{0,2},{1,3},{2,0},{3,1},{4,6},{5,7},{6,4},{7,5},{8,10},{9,11},{10,... | collective-permute-start | bytes 221192 | tf_op jit(solution)/shard_map/ppermute | solution.py:270
  25.9 2.0 %collective-permute-start.10 = (bf16[32,1152]{1,0:T(8,128)(2,1)S(1)}, bf16[32,1152]{1,0:T(8,128)(2,1)S(1)}, u32[]{:S(2)}, u32[]{:S(2)}) collective-permute-start(bf16[32,1152]{1,0:T(8,128)(2,1)S(1)} %collective-permute-done.6.refs_2_), channel_id=1, source_target_pairs={{0,2},{1,3},{2,0},{3,1},{4,6},{5,7},{6,4},{7,5},{8,10},{9,11},{10,... | collective-permute-start | bytes 221192 | tf_op jit(solution)/shard_map/ppermute | solution.py:270

commit v20 on v19

--- a/solution.py
+++ b/solution.py
@@ -119,7 +119,7 @@
         pltpu.with_memory_space_constraint(operand, pltpu.HBM)
         for operand in (features, signs.reshape(1, width), columns.reshape(1, kept))
     ))
-    got = swap(send, feat=1)
+    got = swap(send, (0, 1))
     keep = pl.pallas_call(
         functools.partial(keep_kernel, parts),
         out_shape=total_type,
@@ -259,11 +259,11 @@
     )(*operands)
 
 
-def swap(array, tok=0, feat=0, odd=None):
+def swap(array, even, odd=None):
     tok_count, feat_count = lax.axis_size("tok"), lax.axis_size("feat")
-    bits = (feat, odd or feat)
+    bits = (even, odd or even)
     pairs = [
-        (f * tok_count + t, (f ^ bits[f & 1]) * tok_count + (t ^ tok))
+        (f * tok_count + t, (f ^ bits[f & 1][1]) * tok_count + (t ^ bits[f & 1][0]))
         for f in range(feat_count)
         for t in range(tok_count)
     ]
@@ -289,17 +289,17 @@
         got,
         out_shape=[total_type, word_type, word_type, word_type],
     )
-    both = swap(again, feat=10, odd=6)
-    z_word = swap(here, feat=8, odd=4)
-    x_word = swap(there, feat=2)
+    both = swap(again, (0, 10), (0, 6))
+    z_word = swap(here, (0, 8), (0, 4))
+    x_word = swap(there, (0, 2))
     total, word = local_call(
         square_kernel, "add_square", total, both, z_word, x_word, out_shape=[total_type, word_type]
     )
-    word = swap(word, feat=4, odd=8)
+    word = swap(word, (0, 4), (0, 8))
     stride = 16
     while stride < feat_count:
         total, word = local_call(middle_kernel, "add_encode", total, word, out_shape=[total_type, word_type])
-        word = swap(word, feat=stride)
+        word = swap(word, (0, stride))
         stride *= 2
 
     scale = 1.0 / math.sqrt(width * feat_count)
@@ -313,15 +313,16 @@
     )
     stride = 2
     while stride < tok_count:
-        copies = [jnp.concatenate([copies[0], swap(copies[0], tok=stride)], axis=0)] * 4
+        copies = [jnp.concatenate([copies[0], swap(copies[0], (stride, 0))], axis=0)] * 4
         own = copies[0]
         stride *= 2
-    received = [swap(copies[0], tok=1, feat=2), swap(copies[1], feat=2), swap(copies[2], tok=1)]
-    last = swap(copies[3], tok=1, feat=1)
-    ours = [own] + received
-    theirs = [swap(block, feat=1) for block in ours[:3]] + [last]
+    far = swap(copies[0], (1, 2))
+    second = swap(copies[1], (0, 2), (1, 0))
+    third = swap(copies[2], (1, 0), (0, 2))
+    crossed = swap(copies[3], (1, 1), (0, 3))
+    pieces = [own, far, second, third] + [swap(block, (0, 1)) for block in (own, far, second)] + [crossed]
     concepts = C // tok_count
-    gram = gram_blocks(ours + theirs, concepts, shard, C / (rows * tok_count))
+    gram = gram_blocks(pieces, concepts, shard, C / (rows * tok_count))
     return gram.reshape(concepts, shard, kept)
 
 

time: 30.6 us -> 29.9 us (0.977)
  starting transfers between devices: 12.8 us -> 11.8 us
    ppermute x12, starting transfers between devices: 12.8 us -> 11.8 us  [swap(): return lax.ppermute(array, ('feat', 'tok'), pairs)]
where the time goes in v20:
time: 29.9 us; the launch traced here: 29.6 us
  starting transfers between devices  11.8 us (39%)
  waiting for transfers between devices  10.5 us (35%)
  Pallas kernels  7.27 us (24%)
    ppermute x12, starting transfers between devices, swap(): return lax.ppermute(array, ('feat', 'tok'), pairs)  11.8 us
    ppermute x12, waiting for transfers between devices, swap(): return lax.ppermute(array, ('feat', 'tok'), pairs)  10.5 us
    pallas_call x1, Pallas kernels, partial_halves(): pl.pallas_call(functools.partial(send_kernel, total_bits, parts), in_spec...  2.86 us
    pallas_call x1, Pallas kernels, gram_blocks(): pl.pallas_call(functools.partial(gram_kernel, shard, group, factor), in_s...  2.49 us
    pallas_call x1, Pallas kernels, partial_halves(): pl.pallas_call(functools.partial(keep_kernel, parts), out_shape=total_typ...  1.3 us
    pallas_call x3, Pallas kernels, local_call(): pl.pallas_call(kernel, out_shape=out_shape, compiler_params=pltpu.Compile...  0.62 us
  transfers between devices with their start and end apart: 12, of which 6 were waited for; matrix products, arithmetic and copies ran while one was open for 0% of the time, Pallas kernels for 4%

profile of v20, /device:TPU:0, one launch (start us, length us, event | category | flops | bytes accessed | tf_op | source)
XLA Modules:
  0.0 29.6 jit_solution(2206598075397423194)
XLA Ops:
  0.0 2.9 %partial_sent.1 = (f32[64,1024]{1,0:T(8,128)S(1)}, bf16[64,8192]{1,0:T(8,128)(2,1)S(1)}, s32[1,8192]{1,0:T(1,128)S(1)}, bf16[256,1024]{1,0:T(8,128)(2,1)S(1)}, f32[32,1024]{1,0:T(8,128)S(1)}) custom-call(bf16[128,8192]{1,0:T(8,128)(2,1)} %x_hbm.1, s32[1,8192]{1,0:T(1,128)} %bitcast.5, s32[1,1024]{1,0:T(1,128)} %bitcast.6), custom_call_target="tpu_custom_call" | custom-call | flops 1073741824 | bytes 2359296 | tf_op jit(solution)/shard_map/partial_sent/pallas_call | solution.py:99
  2.9 0.5 %collective-permute-start = (f32[64,1024]{1,0:T(8,128)S(1)}, f32[64,1024]{1,0:T(8,128)S(1)}, u32[]{:S(2)}, u32[]{:S(2)}) collective-permute-start(f32[64,1024]{1,0:T(8,128)S(1)} %get-tuple-element.25), channel_id=1, source_target_pairs={{0,2},{1,3},{2,0},{3,1},{4,6},{5,7},{6,4},{7,5},{8,10},{9,11},{10,... | collective-permute-start | bytes 786440 | tf_op jit(solution)/shard_map/ppermute | solution.py:270
  3.4 1.3 %partial_kept.1.keep_ref = f32[64,1024]{1,0:T(8,128)S(1)} custom-call(bf16[64,8192]{1,0:T(8,128)(2,1)S(1)} %get-tuple-element.21.x_keep, s32[1,8192]{1,0:T(1,128)S(1)} %get-tuple-element.22.signs, bf16[256,1024]{1,0:T(8,128)(2,1)S(1)} %get-tuple-element.23.low, f32[32,1024]{1,0:T(8,128)S(1)} %get-tuple-element.24.high), custom_call_target="tpu_custom_call" | custom-call | flops 1073741824 | bytes 2359296 | tf_op jit(solution)/shard_map/partial_kept/pallas_call | solution.py:123
  4.7 0.0 collective-permute-done.got_ref
  4.7 0.2 first_split.1
  4.9 4.8 %collective-permute-start.1 = (s32[136,128]{1,0:T(8,128)S(1)}, s32[136,128]{1,0:T(8,128)S(1)}, u32[]{:S(2)}, u32[]{:S(2)}) collective-permute-start(s32[136,128]{1,0:T(8,128)S(1)} %get-tuple-element.27), channel_id=1, source_target_pairs={{0,20},{1,21},{2,14},{3,15},{4,16},{5,17},{6,10},{7,11},{8,28},{9,... | collective-permute-start | bytes 208904 | tf_op jit(solution)/shard_map/ppermute | solution.py:270
  9.6 0.3 %collective-permute-start.2 = (s32[136,128]{1,0:T(8,128)S(1)}, s32[136,128]{1,0:T(8,128)S(1)}, u32[]{:S(2)}, u32[]{:S(2)}) collective-permute-start(s32[136,128]{1,0:T(8,128)S(1)} %get-tuple-element.28), channel_id=1, source_target_pairs={{0,16},{1,17},{2,10},{3,11},{4,20},{5,21},{6,14},{7,15},{8,24},{9,... | collective-permute-start | bytes 208904 | tf_op jit(solution)/shard_map/ppermute | solution.py:270
  10.0 0.3 %collective-permute-start.3 = (s32[136,128]{1,0:T(8,128)S(1)}, s32[136,128]{1,0:T(8,128)S(1)}, u32[]{:S(2)}, u32[]{:S(2)}) collective-permute-start(s32[136,128]{1,0:T(8,128)S(1)} %get-tuple-element.29), channel_id=1, source_target_pairs={{0,4},{1,5},{2,6},{3,7},{4,0},{5,1},{6,2},{7,3},{8,12},{9,13},{10,... | collective-permute-start | bytes 208904 | tf_op jit(solution)/shard_map/ppermute | solution.py:270
  10.3 1.7 %collective-permute-done.1.both_ref = s32[136,128]{1,0:T(8,128)S(1)} collective-permute-done((s32[136,128]{1,0:T(8,128)S(1)}, s32[136,128]{1,0:T(8,128)S(1)}, u32[]{:S(2)}, u32[]{:S(2)}) %collective-permute-start.1) | collective-permute-done | bytes 69664 | tf_op jit(solution)/shard_map/ppermute | solution.py:270
  12.0 2.8 %collective-permute-done.2.z_ref = s32[136,128]{1,0:T(8,128)S(1)} collective-permute-done((s32[136,128]{1,0:T(8,128)S(1)}, s32[136,128]{1,0:T(8,128)S(1)}, u32[]{:S(2)}, u32[]{:S(2)}) %collective-permute-start.2) | collective-permute-done | bytes 69664 | tf_op jit(solution)/shard_map/ppermute | solution.py:270
  14.9 0.0 collective-permute-done.3.x_ref
  14.9 0.3 add_square.1
  15.1 1.6 %collective-permute-start.4 = (s32[136,128]{1,0:T(8,128)S(1)}, s32[136,128]{1,0:T(8,128)S(1)}, u32[]{:S(2)}, u32[]{:S(2)}) collective-permute-start(s32[136,128]{1,0:T(8,128)S(1)} %get-tuple-element.31), channel_id=1, source_target_pairs={{0,8},{1,9},{2,18},{3,19},{4,12},{5,13},{6,22},{7,23},{8,0},{9,1},... | collective-permute-start | bytes 208904 | tf_op jit(solution)/shard_map/ppermute | solution.py:270
  16.8 2.7 %collective-permute-done.4.word_ref = s32[136,128]{1,0:T(8,128)S(1)} collective-permute-done((s32[136,128]{1,0:T(8,128)S(1)}, s32[136,128]{1,0:T(8,128)S(1)}, u32[]{:S(2)}, u32[]{:S(2)}) %collective-permute-start.4) | collective-permute-done | bytes 69664 | tf_op jit(solution)/shard_map/ppermute | solution.py:270
  19.5 0.2 sketch_rows.1
  19.7 1.6 %collective-permute-start.5 = (bf16[32,1152]{1,0:T(8,128)(2,1)S(1)}, bf16[32,1152]{1,0:T(8,128)(2,1)S(1)}, u32[]{:S(2)}, u32[]{:S(2)}) collective-permute-start(bf16[32,1152]{1,0:T(8,128)(2,1)S(1)} %get-tuple-element.33), channel_id=1, source_target_pairs={{0,5},{1,4},{2,7},{3,6},{4,1},{5,0},{6,3},{7,2},{8,13},{9,12},{10,... | collective-permute-start | bytes 221192 | tf_op jit(solution)/shard_map/ppermute | solution.py:270
  21.3 1.5 %collective-permute-start.6 = (bf16[32,1152]{1,0:T(8,128)(2,1)S(1)}, bf16[32,1152]{1,0:T(8,128)(2,1)S(1)}, u32[]{:S(2)}, u32[]{:S(2)}) collective-permute-start(bf16[32,1152]{1,0:T(8,128)(2,1)S(1)} %get-tuple-element.34), channel_id=1, source_target_pairs={{0,4},{1,5},{2,3},{3,2},{4,0},{5,1},{6,7},{7,6},{8,12},{9,13},{10,... | collective-permute-start | bytes 221192 | tf_op jit(solution)/shard_map/ppermute | solution.py:270
  22.8 0.5 %collective-permute-start.7 = (bf16[32,1152]{1,0:T(8,128)(2,1)S(1)}, bf16[32,1152]{1,0:T(8,128)(2,1)S(1)}, u32[]{:S(2)}, u32[]{:S(2)}) collective-permute-start(bf16[32,1152]{1,0:T(8,128)(2,1)S(1)} %get-tuple-element.35), channel_id=1, source_target_pairs={{0,1},{1,0},{2,6},{3,7},{4,5},{5,4},{6,2},{7,3},{8,9},{9,8},{10,14... | collective-permute-start | bytes 221192 | tf_op jit(solution)/shard_map/ppermute | solution.py:270
  23.3 0.7 %collective-permute-start.8 = (bf16[32,1152]{1,0:T(8,128)(2,1)S(1)}, bf16[32,1152]{1,0:T(8,128)(2,1)S(1)}, u32[]{:S(2)}, u32[]{:S(2)}) collective-permute-start(bf16[32,1152]{1,0:T(8,128)(2,1)S(1)} %get-tuple-element.32.refs_0_), channel_id=1, source_target_pairs={{0,2},{1,3},{2,0},{3,1},{4,6},{5,7},{6,4},{7,5},{8,10},{9,11},{10,... | collective-permute-start | bytes 221192 | tf_op jit(solution)/shard_map/ppermute | solution.py:270
  23.9 1.1 %collective-permute-done.5.refs_1_ = bf16[32,1152]{1,0:T(8,128)(2,1)S(1)} collective-permute-done((bf16[32,1152]{1,0:T(8,128)(2,1)S(1)}, bf16[32,1152]{1,0:T(8,128)(2,1)S(1)}, u32[]{:S(2)}, u32[]{:S(2)}) %collective-permute-start.5) | collective-permute-done | bytes 73760 | tf_op jit(solution)/shard_map/ppermute | solution.py:270
  25.0 0.8 %collective-permute-done.6.refs_2_ = bf16[32,1152]{1,0:T(8,128)(2,1)S(1)} collective-permute-done((bf16[32,1152]{1,0:T(8,128)(2,1)S(1)}, bf16[32,1152]{1,0:T(8,128)(2,1)S(1)}, u32[]{:S(2)}, u32[]{:S(2)}) %collective-permute-start.6) | collective-permute-done | bytes 73760 | tf_op jit(solution)/shard_map/ppermute | solution.py:270
  25.9 1.2 %collective-permute-done.7.refs_3_ = bf16[32,1152]{1,0:T(8,128)(2,1)S(1)} collective-permute-done((bf16[32,1152]{1,0:T(8,128)(2,1)S(1)}, bf16[32,1152]{1,0:T(8,128)(2,1)S(1)}, u32[]{:S(2)}, u32[]{:S(2)}) %collective-permute-start.7) | collective-permute-done | bytes 73760 | tf_op jit(solution)/shard_map/ppermute | solution.py:270
  27.1 0.0 collective-permute-done.10.refs_6_
  27.1 2.5 %gram.1 = f32[1024,1024]{1,0:T(8,128)} custom-call(bf16[32,1152]{1,0:T(8,128)(2,1)S(1)} %get-tuple-element.32.refs_0_, bf16[32,1152]{1,0:T(8,128)(2,1)S(1)} %collective-permute-done.5.refs_1_, bf16[32,1152]{1,0:T(8,128)(2,1)S(1)} %collective-permute-done.6.refs_2_, bf16[32,1152]{1,0:T(8,128)(2,1)S(1)} %collective-permute-done.7.refs_3_, ...), custom_call_target="tpu_custom_call" | custom-call | flops 536870912 | bytes 4194304 | tf_op jit(solution)/shard_map/gram/pallas_call | solution.py:166
  (8 shorter events, 0.0 us)
Async XLA Ops:
  0.0 19.5 %copy-start = (s32[128,1]{0,1:T(1,128)S(1)}, s32[128,1]{0,1:T(1,128)}, u32[]{:S(2)}) copy-start(s32[128,1]{0,1:T(1,128)} %param.7) | copy-start | bytes 1540
  2.9 1.8 %collective-permute-start = (f32[64,1024]{1,0:T(8,128)S(1)}, f32[64,1024]{1,0:T(8,128)S(1)}, u32[]{:S(2)}, u32[]{:S(2)}) collective-permute-start(f32[64,1024]{1,0:T(8,128)S(1)} %get-tuple-element.25), channel_id=1, source_target_pairs={{0,2},{1,3},{2,0},{3,1},{4,6},{5,7},{6,4},{7,5},{8,10},{9,11},{10,... | collective-permute-start | bytes 786440 | tf_op jit(solution)/shard_map/ppermute | solution.py:270
  4.9 7.1 %collective-permute-start.1 = (s32[136,128]{1,0:T(8,128)S(1)}, s32[136,128]{1,0:T(8,128)S(1)}, u32[]{:S(2)}, u32[]{:S(2)}) collective-permute-start(s32[136,128]{1,0:T(8,128)S(1)} %get-tuple-element.27), channel_id=1, source_target_pairs={{0,20},{1,21},{2,14},{3,15},{4,16},{5,17},{6,10},{7,11},{8,28},{9,... | collective-permute-start | bytes 208904 | tf_op jit(solution)/shard_map/ppermute | solution.py:270
  9.6 5.2 %collective-permute-start.2 = (s32[136,128]{1,0:T(8,128)S(1)}, s32[136,128]{1,0:T(8,128)S(1)}, u32[]{:S(2)}, u32[]{:S(2)}) collective-permute-start(s32[136,128]{1,0:T(8,128)S(1)} %get-tuple-element.28), channel_id=1, source_target_pairs={{0,16},{1,17},{2,10},{3,11},{4,20},{5,21},{6,14},{7,15},{8,24},{9,... | collective-permute-start | bytes 208904 | tf_op jit(solution)/shard_map/ppermute | solution.py:270
  10.0 4.9 %collective-permute-start.3 = (s32[136,128]{1,0:T(8,128)S(1)}, s32[136,128]{1,0:T(8,128)S(1)}, u32[]{:S(2)}, u32[]{:S(2)}) collective-permute-start(s32[136,128]{1,0:T(8,128)S(1)} %get-tuple-element.29), channel_id=1, source_target_pairs={{0,4},{1,5},{2,6},{3,7},{4,0},{5,1},{6,2},{7,3},{8,12},{9,13},{10,... | collective-permute-start | bytes 208904 | tf_op jit(solution)/shard_map/ppermute | solution.py:270
  15.1 4.4 %collective-permute-start.4 = (s32[136,128]{1,0:T(8,128)S(1)}, s32[136,128]{1,0:T(8,128)S(1)}, u32[]{:S(2)}, u32[]{:S(2)}) collective-permute-start(s32[136,128]{1,0:T(8,128)S(1)} %get-tuple-element.31), channel_id=1, source_target_pairs={{0,8},{1,9},{2,18},{3,19},{4,12},{5,13},{6,22},{7,23},{8,0},{9,1},... | collective-permute-start | bytes 208904 | tf_op jit(solution)/shard_map/ppermute | solution.py:270
  19.7 5.3 %collective-permute-start.5 = (bf16[32,1152]{1,0:T(8,128)(2,1)S(1)}, bf16[32,1152]{1,0:T(8,128)(2,1)S(1)}, u32[]{:S(2)}, u32[]{:S(2)}) collective-permute-start(bf16[32,1152]{1,0:T(8,128)(2,1)S(1)} %get-tuple-element.33), channel_id=1, source_target_pairs={{0,5},{1,4},{2,7},{3,6},{4,1},{5,0},{6,3},{7,2},{8,13},{9,12},{10,... | collective-permute-start | bytes 221192 | tf_op jit(solution)/shard_map/ppermute | solution.py:270
  21.3 4.6 %collective-permute-start.6 = (bf16[32,1152]{1,0:T(8,128)(2,1)S(1)}, bf16[32,1152]{1,0:T(8,128)(2,1)S(1)}, u32[]{:S(2)}, u32[]{:S(2)}) collective-permute-start(bf16[32,1152]{1,0:T(8,128)(2,1)S(1)} %get-tuple-element.34), channel_id=1, source_target_pairs={{0,4},{1,5},{2,3},{3,2},{4,0},{5,1},{6,7},{7,6},{8,12},{9,13},{10,... | collective-permute-start | bytes 221192 | tf_op jit(solution)/shard_map/ppermute | solution.py:270
  22.8 4.4 %collective-permute-start.7 = (bf16[32,1152]{1,0:T(8,128)(2,1)S(1)}, bf16[32,1152]{1,0:T(8,128)(2,1)S(1)}, u32[]{:S(2)}, u32[]{:S(2)}) collective-permute-start(bf16[32,1152]{1,0:T(8,128)(2,1)S(1)} %get-tuple-element.35), channel_id=1, source_target_pairs={{0,1},{1,0},{2,6},{3,7},{4,5},{5,4},{6,2},{7,3},{8,9},{9,8},{10,14... | collective-permute-start | bytes 221192 | tf_op jit(solution)/shard_map/ppermute | solution.py:270
  23.3 3.9 %collective-permute-start.11 = (bf16[32,1152]{1,0:T(8,128)(2,1)S(1)}, bf16[32,1152]{1,0:T(8,128)(2,1)S(1)}, u32[]{:S(2)}, u32[]{:S(2)}) collective-permute-start(bf16[32,1152]{1,0:T(8,128)(2,1)S(1)} %get-tuple-element.36), channel_id=1, source_target_pairs={{0,3},{1,2},{2,4},{3,5},{4,7},{5,6},{6,0},{7,1},{8,11},{9,10},{10,... | collective-permute-start | bytes 221192 | tf_op jit(solution)/shard_map/ppermute | solution.py:270
  23.3 3.9 %collective-permute-start.8 = (bf16[32,1152]{1,0:T(8,128)(2,1)S(1)}, bf16[32,1152]{1,0:T(8,128)(2,1)S(1)}, u32[]{:S(2)}, u32[]{:S(2)}) collective-permute-start(bf16[32,1152]{1,0:T(8,128)(2,1)S(1)} %get-tuple-element.32.refs_0_), channel_id=1, source_target_pairs={{0,2},{1,3},{2,0},{3,1},{4,6},{5,7},{6,4},{7,5},{8,10},{9,11},{10,... | collective-permute-start | bytes 221192 | tf_op jit(solution)/shard_map/ppermute | solution.py:270
  25.0 2.1 %collective-permute-start.9 = (bf16[32,1152]{1,0:T(8,128)(2,1)S(1)}, bf16[32,1152]{1,0:T(8,128)(2,1)S(1)}, u32[]{:S(2)}, u32[]{:S(2)}) collective-permute-start(bf16[32,1152]{1,0:T(8,128)(2,1)S(1)} %collective-permute-done.5.refs_1_), channel_id=1, source_target_pairs={{0,2},{1,3},{2,0},{3,1},{4,6},{5,7},{6,4},{7,5},{8,10},{9,11},{10,... | collective-permute-start | bytes 221192 | tf_op jit(solution)/shard_map/ppermute | solution.py:270
  25.9 1.3 %collective-permute-start.10 = (bf16[32,1152]{1,0:T(8,128)(2,1)S(1)}, bf16[32,1152]{1,0:T(8,128)(2,1)S(1)}, u32[]{:S(2)}, u32[]{:S(2)}) collective-permute-start(bf16[32,1152]{1,0:T(8,128)(2,1)S(1)} %collective-permute-done.6.refs_2_), channel_id=1, source_target_pairs={{0,2},{1,3},{2,0},{3,1},{4,6},{5,7},{6,4},{7,5},{8,10},{9,11},{10,... | collective-permute-start | bytes 221192 | tf_op jit(solution)/shard_map/ppermute | solution.py:270

commit v21 on v20

--- a/solution.py
+++ b/solution.py
@@ -24,11 +24,15 @@
     return (1 - 2 * (number & 1)).astype(jnp.float32)
 
 
-def add_products(x_ref, sign_ref, low, high, out_ref, part, wide):
+def spans_of(width):
+    return [(0, 1024), (1024, 2048)] + [(first, first + 2048) for first in range(2048, width, 2048)]
+
+
+def add_products(x_ref, sign_ref, low, high, out_ref, span):
     rows, kept = out_ref.shape
-    blocks = wide // LOW
+    first, blocks = span[0] // LOW, (span[1] - span[0]) // LOW
     stack = []
-    for block in range(part * blocks, (part + 1) * blocks):
+    for block in range(first, first + blocks):
         cols = slice(block * LOW, (block + 1) * LOW)
         stack.append(x_ref[:, cols] * sign_ref[:, cols].astype(jnp.bfloat16))
     stack = jnp.concatenate(stack, axis=0)
@@ -37,29 +41,29 @@
         products = jnp.dot(stack, low[:, cols], preferred_element_type=jnp.float32)
         total = None
         for at in range(blocks):
-            row = part * blocks + at
+            row = first + at
             term = products[at * rows:(at + 1) * rows] * high[row:row + 1, cols]
             total = term if total is None else total + term
-        if part > 0:
+        if first > 0:
             total = total + out_ref[:, cols]
         out_ref[:, cols] = total
 
 
-def send_kernel(total_bits, parts, x_hbm, s_hbm, col_hbm, send_ref, x_keep, signs, low, high, x_buf, col_buf, sems):
+def send_kernel(total_bits, x_hbm, s_hbm, col_hbm, send_ref, x_keep, signs, low, high, x_buf, col_buf, sems):
     half, kept = send_ref.shape
-    wide = x_hbm.shape[1] // parts
+    spans = spans_of(x_hbm.shape[1])
+    parts = len(spans)
     me = lax.axis_index("feat")
     mine = lax.rem(me, 2)
     col_copy = pltpu.make_async_copy(col_hbm, col_buf, sems.at[parts])
     sign_copy = pltpu.make_async_copy(s_hbm, signs, sems.at[parts + 1])
-    col_copy.start()
-    sign_copy.start()
     copies = []
-    for part in range(parts):
-        cols = pl.ds(part * wide, wide)
+    for part, (first, last) in enumerate(spans):
+        cols = pl.ds(first, last - first)
         rows = pl.ds(pl.multiple_of((1 - mine) * half, half), half)
         copies.append(pltpu.make_async_copy(x_hbm.at[rows, cols], x_buf.at[:, cols], sems.at[part]))
-        copies[-1].start()
+    for copy in (col_copy, copies[0], sign_copy, *copies[1:]):
+        copy.start()
     rows = pl.ds(pl.multiple_of(mine * half, half), half)
     keep_copy = pltpu.make_async_copy(x_hbm.at[rows, :], x_keep, sems.at[parts + 2])
     keep_copy.start()
@@ -73,22 +77,21 @@
     high_index = lax.broadcasted_iota(jnp.int32, high.shape, 0) + me * high.shape[0]
     high[...] = parity_sign(high_index & (col >> 8), total_bits - 8)
     sign_copy.wait()
-    for part in range(parts):
-        copies[part].wait()
-        add_products(x_buf, signs, low, high, send_ref, part, wide)
+    for span, copy in zip(spans, copies):
+        copy.wait()
+        add_products(x_buf, signs, low, high, send_ref, span)
     keep_copy.wait()
 
 
-def keep_kernel(parts, x_keep, signs, low, high, keep_ref):
-    wide = x_keep.shape[1] // parts
-    for part in range(parts):
-        add_products(x_keep, signs, low, high, keep_ref, part, wide)
+def keep_kernel(x_keep, signs, low, high, keep_ref):
+    for first in range(0, x_keep.shape[1], 2048):
+        add_products(x_keep, signs, low, high, keep_ref, (first, first + 2048))
 
 
 def partial_halves(features, signs, columns, feat_count):
     rows, width = features.shape
     kept = columns.shape[0]
-    parts = max(1, width // 2048)
+    parts = len(spans_of(width))
     half = rows // 2
     total_bits = (width * feat_count).bit_length() - 1
     params = pltpu.CompilerParams(vmem_limit_bytes=VMEM_LIMIT)
@@ -97,7 +100,7 @@
     )
     total_type = jax.ShapeDtypeStruct((half, kept), jnp.float32)
     send, *held = pl.pallas_call(
-        functools.partial(send_kernel, total_bits, parts),
+        functools.partial(send_kernel, total_bits),
         in_specs=[pl.BlockSpec(memory_space=pltpu.HBM)] * 3,
         out_specs=[pl.BlockSpec(memory_space=pltpu.VMEM)] * 5,
         out_shape=[
@@ -121,7 +124,7 @@
     ))
     got = swap(send, (0, 1))
     keep = pl.pallas_call(
-        functools.partial(keep_kernel, parts),
+        keep_kernel,
         out_shape=total_type,
         compiler_params=params,
         cost_estimate=cost,
@@ -209,7 +212,7 @@
     return code * scale
 
 
-def first_kernel(stride, keep_ref, got_ref, total_ref, there_ref, here_ref, again_ref):
+def first_kernel(stride, keep_ref, got_ref, total_ref, far_ref, second_ref, third_ref, there_ref, here_ref):
     size = total_ref.shape[0]
     digit = lax.rem(lax.axis_index("feat") // stride, 2)
 
@@ -218,15 +221,18 @@
         return keep_ref[span, :] + got_ref[span, :]
 
     encode(piece(1 - digit), there_ref)
-    again_ref[...] = there_ref[...]
     total = piece(digit)
     total_ref[...] = total
     encode(total, here_ref)
-
-
-def square_kernel(total_ref, both_ref, z_ref, x_ref, sum_ref, out_ref):
+    even = lax.rem(lax.axis_index("feat"), 2) == 0
+    far_ref[...] = there_ref[...]
+    second_ref[...] = jnp.where(even, here_ref[...], there_ref[...])
+    third_ref[...] = jnp.where(even, there_ref[...], here_ref[...])
+
+
+def square_kernel(total_ref, far_ref, second_ref, third_ref, sum_ref, out_ref):
     size = total_ref.shape[0]
-    total = (total_ref[...] + decode(x_ref, size)) + (decode(z_ref, size) + decode(both_ref, size))
+    total = (total_ref[...] + decode(far_ref, size)) + (decode(second_ref, size) + decode(third_ref, size))
     sum_ref[...] = total
     encode(total, out_ref)
 
@@ -250,10 +256,11 @@
         row_ref[:, kept:] = label
 
 
-def local_call(kernel, name, *operands, out_shape):
+def local_call(kernel, name, *operands, out_shape, scratch=()):
     return pl.pallas_call(
         kernel,
         out_shape=out_shape,
+        scratch_shapes=scratch,
         compiler_params=pltpu.CompilerParams(vmem_limit_bytes=VMEM_LIMIT),
         name=name,
     )(*operands)
@@ -282,18 +289,19 @@
     row_type = jax.ShapeDtypeStruct((size, kept + LANES), jnp.bfloat16)
 
     keep, got = partial_halves(features, signs, columns, feat_count)
-    total, there, here, again = local_call(
+    total, far, second, third = local_call(
         functools.partial(first_kernel, 2),
         "first_split",
         keep,
         got,
         out_shape=[total_type, word_type, word_type, word_type],
+        scratch=[pltpu.VMEM(word_type.shape, word_type.dtype)] * 2,
     )
-    both = swap(again, (0, 10), (0, 6))
-    z_word = swap(here, (0, 8), (0, 4))
-    x_word = swap(there, (0, 2))
+    far = swap(far, (0, 10), (0, 6))
+    second = swap(second, (0, 8), (0, 2))
+    third = swap(third, (0, 2), (0, 4))
     total, word = local_call(
-        square_kernel, "add_square", total, both, z_word, x_word, out_shape=[total_type, word_type]
+        square_kernel, "add_square", total, far, second, third, out_shape=[total_type, word_type]
     )
     word = swap(word, (0, 4), (0, 8))
     stride = 16

time: 29.9 us -> 30 us (level)
  no operation moved by 1% of the time
where the time goes in v21:
time: 30 us; the launch traced here: 29.7 us
  starting transfers between devices  11.8 us (39%)
  waiting for transfers between devices  10.5 us (35%)
  Pallas kernels  7.38 us (25%)
    ppermute x12, starting transfers between devices, swap(): return lax.ppermute(array, ('feat', 'tok'), pairs)  11.8 us
    ppermute x12, waiting for transfers between devices, swap(): return lax.ppermute(array, ('feat', 'tok'), pairs)  10.5 us
    pallas_call x1, Pallas kernels, partial_halves(): pl.pallas_call(functools.partial(send_kernel, total_bits), in_specs=[pl.B...  2.96 us
    pallas_call x1, Pallas kernels, gram_blocks(): pl.pallas_call(functools.partial(gram_kernel, shard, group, factor), in_s...  2.49 us
    pallas_call x1, Pallas kernels, partial_halves(): pl.pallas_call(keep_kernel, out_shape=total_type, compiler_params=params,...  1.3 us
    pallas_call x3, Pallas kernels, local_call(): pl.pallas_call(kernel, out_shape=out_shape, scratch_shapes=scratch, compi...  0.63 us
  transfers between devices with their start and end apart: 12, of which 6 were waited for; matrix products, arithmetic and copies ran while one was open for 0% of the time, Pallas kernels for 4%

profile of v21, /device:TPU:0, one launch (start us, length us, event | category | flops | bytes accessed | tf_op | source)
XLA Modules:
  0.0 29.7 jit_solution(443456761815451221)
XLA Ops:
  0.0 3.0 %partial_sent.1 = (f32[64,1024]{1,0:T(8,128)S(1)}, bf16[64,8192]{1,0:T(8,128)(2,1)S(1)}, s32[1,8192]{1,0:T(1,128)S(1)}, bf16[256,1024]{1,0:T(8,128)(2,1)S(1)}, f32[32,1024]{1,0:T(8,128)S(1)}) custom-call(bf16[128,8192]{1,0:T(8,128)(2,1)} %x_hbm.1, s32[1,8192]{1,0:T(1,128)} %bitcast.5, s32[1,1024]{1,0:T(1,128)} %bitcast.6), custom_call_target="tpu_custom_call" | custom-call | flops 1073741824 | bytes 2359296 | tf_op jit(solution)/shard_map/partial_sent/pallas_call | solution.py:102
  3.0 0.5 %collective-permute-start = (f32[64,1024]{1,0:T(8,128)S(1)}, f32[64,1024]{1,0:T(8,128)S(1)}, u32[]{:S(2)}, u32[]{:S(2)}) collective-permute-start(f32[64,1024]{1,0:T(8,128)S(1)} %get-tuple-element.25), channel_id=1, source_target_pairs={{0,2},{1,3},{2,0},{3,1},{4,6},{5,7},{6,4},{7,5},{8,10},{9,11},{10,... | collective-permute-start | bytes 786440 | tf_op jit(solution)/shard_map/ppermute | solution.py:277
  3.5 1.3 %partial_kept.1.keep_ref = f32[64,1024]{1,0:T(8,128)S(1)} custom-call(bf16[64,8192]{1,0:T(8,128)(2,1)S(1)} %get-tuple-element.21.x_keep, s32[1,8192]{1,0:T(1,128)S(1)} %get-tuple-element.22.signs, bf16[256,1024]{1,0:T(8,128)(2,1)S(1)} %get-tuple-element.23.low, f32[32,1024]{1,0:T(8,128)S(1)} %get-tuple-element.24.high), custom_call_target="tpu_custom_call" | custom-call | flops 1073741824 | bytes 2359296 | tf_op jit(solution)/shard_map/partial_kept/pallas_call | solution.py:126
  4.8 0.0 collective-permute-done.got_ref
  4.8 0.2 first_split.1
  5.0 4.8 %collective-permute-start.1 = (s32[136,128]{1,0:T(8,128)S(1)}, s32[136,128]{1,0:T(8,128)S(1)}, u32[]{:S(2)}, u32[]{:S(2)}) collective-permute-start(s32[136,128]{1,0:T(8,128)S(1)} %get-tuple-element.27), channel_id=1, source_target_pairs={{0,20},{1,21},{2,14},{3,15},{4,16},{5,17},{6,10},{7,11},{8,28},{9,... | collective-permute-start | bytes 208904 | tf_op jit(solution)/shard_map/ppermute | solution.py:277
  9.8 0.3 %collective-permute-start.2 = (s32[136,128]{1,0:T(8,128)S(1)}, s32[136,128]{1,0:T(8,128)S(1)}, u32[]{:S(2)}, u32[]{:S(2)}) collective-permute-start(s32[136,128]{1,0:T(8,128)S(1)} %get-tuple-element.28), channel_id=1, source_target_pairs={{0,16},{1,17},{2,6},{3,7},{4,20},{5,21},{6,2},{7,3},{8,24},{9,25},... | collective-permute-start | bytes 208904 | tf_op jit(solution)/shard_map/ppermute | solution.py:277
  10.1 0.3 %collective-permute-start.3 = (s32[136,128]{1,0:T(8,128)S(1)}, s32[136,128]{1,0:T(8,128)S(1)}, u32[]{:S(2)}, u32[]{:S(2)}) collective-permute-start(s32[136,128]{1,0:T(8,128)S(1)} %get-tuple-element.29), channel_id=1, source_target_pairs={{0,4},{1,5},{2,10},{3,11},{4,0},{5,1},{6,14},{7,15},{8,12},{9,13},... | collective-permute-start | bytes 208904 | tf_op jit(solution)/shard_map/ppermute | solution.py:277
  10.4 1.7 %collective-permute-done.1.far_ref = s32[136,128]{1,0:T(8,128)S(1)} collective-permute-done((s32[136,128]{1,0:T(8,128)S(1)}, s32[136,128]{1,0:T(8,128)S(1)}, u32[]{:S(2)}, u32[]{:S(2)}) %collective-permute-start.1) | collective-permute-done | bytes 69664 | tf_op jit(solution)/shard_map/ppermute | solution.py:277
  12.1 2.8 %collective-permute-done.2.second_ref = s32[136,128]{1,0:T(8,128)S(1)} collective-permute-done((s32[136,128]{1,0:T(8,128)S(1)}, s32[136,128]{1,0:T(8,128)S(1)}, u32[]{:S(2)}, u32[]{:S(2)}) %collective-permute-start.2) | collective-permute-done | bytes 69664 | tf_op jit(solution)/shard_map/ppermute | solution.py:277
  15.0 0.3 add_square.1
  15.2 1.6 %collective-permute-start.4 = (s32[136,128]{1,0:T(8,128)S(1)}, s32[136,128]{1,0:T(8,128)S(1)}, u32[]{:S(2)}, u32[]{:S(2)}) collective-permute-start(s32[136,128]{1,0:T(8,128)S(1)} %get-tuple-element.31), channel_id=1, source_target_pairs={{0,8},{1,9},{2,18},{3,19},{4,12},{5,13},{6,22},{7,23},{8,0},{9,1},... | collective-permute-start | bytes 208904 | tf_op jit(solution)/shard_map/ppermute | solution.py:277
  16.9 2.7 %collective-permute-done.4.word_ref = s32[136,128]{1,0:T(8,128)S(1)} collective-permute-done((s32[136,128]{1,0:T(8,128)S(1)}, s32[136,128]{1,0:T(8,128)S(1)}, u32[]{:S(2)}, u32[]{:S(2)}) %collective-permute-start.4) | collective-permute-done | bytes 69664 | tf_op jit(solution)/shard_map/ppermute | solution.py:277
  19.6 0.2 sketch_rows.1
  19.8 1.6 %collective-permute-start.5 = (bf16[32,1152]{1,0:T(8,128)(2,1)S(1)}, bf16[32,1152]{1,0:T(8,128)(2,1)S(1)}, u32[]{:S(2)}, u32[]{:S(2)}) collective-permute-start(bf16[32,1152]{1,0:T(8,128)(2,1)S(1)} %get-tuple-element.33), channel_id=1, source_target_pairs={{0,5},{1,4},{2,7},{3,6},{4,1},{5,0},{6,3},{7,2},{8,13},{9,12},{10,... | collective-permute-start | bytes 221192 | tf_op jit(solution)/shard_map/ppermute | solution.py:277
  21.4 1.5 %collective-permute-start.6 = (bf16[32,1152]{1,0:T(8,128)(2,1)S(1)}, bf16[32,1152]{1,0:T(8,128)(2,1)S(1)}, u32[]{:S(2)}, u32[]{:S(2)}) collective-permute-start(bf16[32,1152]{1,0:T(8,128)(2,1)S(1)} %get-tuple-element.34), channel_id=1, source_target_pairs={{0,4},{1,5},{2,3},{3,2},{4,0},{5,1},{6,7},{7,6},{8,12},{9,13},{10,... | collective-permute-start | bytes 221192 | tf_op jit(solution)/shard_map/ppermute | solution.py:277
  22.9 0.5 %collective-permute-start.7 = (bf16[32,1152]{1,0:T(8,128)(2,1)S(1)}, bf16[32,1152]{1,0:T(8,128)(2,1)S(1)}, u32[]{:S(2)}, u32[]{:S(2)}) collective-permute-start(bf16[32,1152]{1,0:T(8,128)(2,1)S(1)} %get-tuple-element.35), channel_id=1, source_target_pairs={{0,1},{1,0},{2,6},{3,7},{4,5},{5,4},{6,2},{7,3},{8,9},{9,8},{10,14... | collective-permute-start | bytes 221192 | tf_op jit(solution)/shard_map/ppermute | solution.py:277
  23.4 0.7 %collective-permute-start.8 = (bf16[32,1152]{1,0:T(8,128)(2,1)S(1)}, bf16[32,1152]{1,0:T(8,128)(2,1)S(1)}, u32[]{:S(2)}, u32[]{:S(2)}) collective-permute-start(bf16[32,1152]{1,0:T(8,128)(2,1)S(1)} %get-tuple-element.32.refs_0_), channel_id=1, source_target_pairs={{0,2},{1,3},{2,0},{3,1},{4,6},{5,7},{6,4},{7,5},{8,10},{9,11},{10,... | collective-permute-start | bytes 221192 | tf_op jit(solution)/shard_map/ppermute | solution.py:277
  24.0 1.5 %collective-permute-done.5.refs_1_ = bf16[32,1152]{1,0:T(8,128)(2,1)S(1)} collective-permute-done((bf16[32,1152]{1,0:T(8,128)(2,1)S(1)}, bf16[32,1152]{1,0:T(8,128)(2,1)S(1)}, u32[]{:S(2)}, u32[]{:S(2)}) %collective-permute-start.5) | collective-permute-done | bytes 73760 | tf_op jit(solution)/shard_map/ppermute | solution.py:277
  25.5 0.5 %collective-permute-done.6.refs_2_ = bf16[32,1152]{1,0:T(8,128)(2,1)S(1)} collective-permute-done((bf16[32,1152]{1,0:T(8,128)(2,1)S(1)}, bf16[32,1152]{1,0:T(8,128)(2,1)S(1)}, u32[]{:S(2)}, u32[]{:S(2)}) %collective-permute-start.6) | collective-permute-done | bytes 73760 | tf_op jit(solution)/shard_map/ppermute | solution.py:277
  26.0 0.0 collective-permute-start.10
  26.0 1.2 %collective-permute-done.7.refs_3_ = bf16[32,1152]{1,0:T(8,128)(2,1)S(1)} collective-permute-done((bf16[32,1152]{1,0:T(8,128)(2,1)S(1)}, bf16[32,1152]{1,0:T(8,128)(2,1)S(1)}, u32[]{:S(2)}, u32[]{:S(2)}) %collective-permute-start.7) | collective-permute-done | bytes 73760 | tf_op jit(solution)/shard_map/ppermute | solution.py:277
  27.2 0.0 collective-permute-done.10.refs_6_
  27.2 2.5 %gram.1 = f32[1024,1024]{1,0:T(8,128)} custom-call(bf16[32,1152]{1,0:T(8,128)(2,1)S(1)} %get-tuple-element.32.refs_0_, bf16[32,1152]{1,0:T(8,128)(2,1)S(1)} %collective-permute-done.5.refs_1_, bf16[32,1152]{1,0:T(8,128)(2,1)S(1)} %collective-permute-done.6.refs_2_, bf16[32,1152]{1,0:T(8,128)(2,1)S(1)} %collective-permute-done.7.refs_3_, ...), custom_call_target="tpu_custom_call" | custom-call | flops 536870912 | bytes 4194304 | tf_op jit(solution)/shard_map/gram/pallas_call | solution.py:169
  (8 shorter events, 0.0 us)
Async XLA Ops:
  0.0 19.6 %copy-start = (s32[128,1]{0,1:T(1,128)S(1)}, s32[128,1]{0,1:T(1,128)}, u32[]{:S(2)}) copy-start(s32[128,1]{0,1:T(1,128)} %param.7) | copy-start | bytes 1540
  3.0 1.8 %collective-permute-start = (f32[64,1024]{1,0:T(8,128)S(1)}, f32[64,1024]{1,0:T(8,128)S(1)}, u32[]{:S(2)}, u32[]{:S(2)}) collective-permute-start(f32[64,1024]{1,0:T(8,128)S(1)} %get-tuple-element.25), channel_id=1, source_target_pairs={{0,2},{1,3},{2,0},{3,1},{4,6},{5,7},{6,4},{7,5},{8,10},{9,11},{10,... | collective-permute-start | bytes 786440 | tf_op jit(solution)/shard_map/ppermute | solution.py:277
  5.0 7.1 %collective-permute-start.1 = (s32[136,128]{1,0:T(8,128)S(1)}, s32[136,128]{1,0:T(8,128)S(1)}, u32[]{:S(2)}, u32[]{:S(2)}) collective-permute-start(s32[136,128]{1,0:T(8,128)S(1)} %get-tuple-element.27), channel_id=1, source_target_pairs={{0,20},{1,21},{2,14},{3,15},{4,16},{5,17},{6,10},{7,11},{8,28},{9,... | collective-permute-start | bytes 208904 | tf_op jit(solution)/shard_map/ppermute | solution.py:277
  9.8 5.2 %collective-permute-start.2 = (s32[136,128]{1,0:T(8,128)S(1)}, s32[136,128]{1,0:T(8,128)S(1)}, u32[]{:S(2)}, u32[]{:S(2)}) collective-permute-start(s32[136,128]{1,0:T(8,128)S(1)} %get-tuple-element.28), channel_id=1, source_target_pairs={{0,16},{1,17},{2,6},{3,7},{4,20},{5,21},{6,2},{7,3},{8,24},{9,25},... | collective-permute-start | bytes 208904 | tf_op jit(solution)/shard_map/ppermute | solution.py:277
  10.1 4.9 %collective-permute-start.3 = (s32[136,128]{1,0:T(8,128)S(1)}, s32[136,128]{1,0:T(8,128)S(1)}, u32[]{:S(2)}, u32[]{:S(2)}) collective-permute-start(s32[136,128]{1,0:T(8,128)S(1)} %get-tuple-element.29), channel_id=1, source_target_pairs={{0,4},{1,5},{2,10},{3,11},{4,0},{5,1},{6,14},{7,15},{8,12},{9,13},... | collective-permute-start | bytes 208904 | tf_op jit(solution)/shard_map/ppermute | solution.py:277
  15.2 4.4 %collective-permute-start.4 = (s32[136,128]{1,0:T(8,128)S(1)}, s32[136,128]{1,0:T(8,128)S(1)}, u32[]{:S(2)}, u32[]{:S(2)}) collective-permute-start(s32[136,128]{1,0:T(8,128)S(1)} %get-tuple-element.31), channel_id=1, source_target_pairs={{0,8},{1,9},{2,18},{3,19},{4,12},{5,13},{6,22},{7,23},{8,0},{9,1},... | collective-permute-start | bytes 208904 | tf_op jit(solution)/shard_map/ppermute | solution.py:277
  19.8 5.7 %collective-permute-start.5 = (bf16[32,1152]{1,0:T(8,128)(2,1)S(1)}, bf16[32,1152]{1,0:T(8,128)(2,1)S(1)}, u32[]{:S(2)}, u32[]{:S(2)}) collective-permute-start(bf16[32,1152]{1,0:T(8,128)(2,1)S(1)} %get-tuple-element.33), channel_id=1, source_target_pairs={{0,5},{1,4},{2,7},{3,6},{4,1},{5,0},{6,3},{7,2},{8,13},{9,12},{10,... | collective-permute-start | bytes 221192 | tf_op jit(solution)/shard_map/ppermute | solution.py:277
  21.4 4.6 %collective-permute-start.6 = (bf16[32,1152]{1,0:T(8,128)(2,1)S(1)}, bf16[32,1152]{1,0:T(8,128)(2,1)S(1)}, u32[]{:S(2)}, u32[]{:S(2)}) collective-permute-start(bf16[32,1152]{1,0:T(8,128)(2,1)S(1)} %get-tuple-element.34), channel_id=1, source_target_pairs={{0,4},{1,5},{2,3},{3,2},{4,0},{5,1},{6,7},{7,6},{8,12},{9,13},{10,... | collective-permute-start | bytes 221192 | tf_op jit(solution)/shard_map/ppermute | solution.py:277
  22.9 4.4 %collective-permute-start.7 = (bf16[32,1152]{1,0:T(8,128)(2,1)S(1)}, bf16[32,1152]{1,0:T(8,128)(2,1)S(1)}, u32[]{:S(2)}, u32[]{:S(2)}) collective-permute-start(bf16[32,1152]{1,0:T(8,128)(2,1)S(1)} %get-tuple-element.35), channel_id=1, source_target_pairs={{0,1},{1,0},{2,6},{3,7},{4,5},{5,4},{6,2},{7,3},{8,9},{9,8},{10,14... | collective-permute-start | bytes 221192 | tf_op jit(solution)/shard_map/ppermute | solution.py:277
  23.4 3.9 %collective-permute-start.11 = (bf16[32,1152]{1,0:T(8,128)(2,1)S(1)}, bf16[32,1152]{1,0:T(8,128)(2,1)S(1)}, u32[]{:S(2)}, u32[]{:S(2)}) collective-permute-start(bf16[32,1152]{1,0:T(8,128)(2,1)S(1)} %get-tuple-element.36), channel_id=1, source_target_pairs={{0,3},{1,2},{2,4},{3,5},{4,7},{5,6},{6,0},{7,1},{8,11},{9,10},{10,... | collective-permute-start | bytes 221192 | tf_op jit(solution)/shard_map/ppermute | solution.py:277
  23.4 3.9 %collective-permute-start.8 = (bf16[32,1152]{1,0:T(8,128)(2,1)S(1)}, bf16[32,1152]{1,0:T(8,128)(2,1)S(1)}, u32[]{:S(2)}, u32[]{:S(2)}) collective-permute-start(bf16[32,1152]{1,0:T(8,128)(2,1)S(1)} %get-tuple-element.32.refs_0_), channel_id=1, source_target_pairs={{0,2},{1,3},{2,0},{3,1},{4,6},{5,7},{6,4},{7,5},{8,10},{9,11},{10,... | collective-permute-start | bytes 221192 | tf_op jit(solution)/shard_map/ppermute | solution.py:277
  25.5 1.7 %collective-permute-start.9 = (bf16[32,1152]{1,0:T(8,128)(2,1)S(1)}, bf16[32,1152]{1,0:T(8,128)(2,1)S(1)}, u32[]{:S(2)}, u32[]{:S(2)}) collective-permute-start(bf16[32,1152]{1,0:T(8,128)(2,1)S(1)} %collective-permute-done.5.refs_1_), channel_id=1, source_target_pairs={{0,2},{1,3},{2,0},{3,1},{4,6},{5,7},{6,4},{7,5},{8,10},{9,11},{10,... | collective-permute-start | bytes 221192 | tf_op jit(solution)/shard_map/ppermute | solution.py:277
  26.0 1.3 %collective-permute-start.10 = (bf16[32,1152]{1,0:T(8,128)(2,1)S(1)}, bf16[32,1152]{1,0:T(8,128)(2,1)S(1)}, u32[]{:S(2)}, u32[]{:S(2)}) collective-permute-start(bf16[32,1152]{1,0:T(8,128)(2,1)S(1)} %collective-permute-done.6.refs_2_), channel_id=1, source_target_pairs={{0,2},{1,3},{2,0},{3,1},{4,6},{5,7},{6,4},{7,5},{8,10},{9,11},{10,... | collective-permute-start | bytes 221192 | tf_op jit(solution)/shard_map/ppermute | solution.py:277

commit v22 on v20

--- a/solution.py
+++ b/solution.py
@@ -88,7 +88,7 @@
 def partial_halves(features, signs, columns, feat_count):
     rows, width = features.shape
     kept = columns.shape[0]
-    parts = max(1, width // 2048)
+    parts = max(1, width // 4096)
     half = rows // 2
     total_bits = (width * feat_count).bit_length() - 1
     params = pltpu.CompilerParams(vmem_limit_bytes=VMEM_LIMIT)
@@ -316,7 +316,7 @@
         copies = [jnp.concatenate([copies[0], swap(copies[0], (stride, 0))], axis=0)] * 4
         own = copies[0]
         stride *= 2
-    far = swap(copies[0], (1, 2))
+    far = swap(copies[0], (1, 3))
     second = swap(copies[1], (0, 2), (1, 0))
     third = swap(copies[2], (1, 0), (0, 2))
     crossed = swap(copies[3], (1, 1), (0, 3))

time: 29.9 us -> 29.4 us (0.983)
  waiting for transfers between devices: 10.5 us -> 8.95 us
  starting transfers between devices: 11.8 us -> 13.3 us
  Pallas kernels: 7.27 us -> 6.94 us
    ppermute x12, waiting for transfers between devices: 10.5 us -> 8.95 us  [swap(): return lax.ppermute(array, ('feat', 'tok'), pairs)]
    ppermute x12, starting transfers between devices: 11.8 us -> 13.3 us  [swap(): return lax.ppermute(array, ('feat', 'tok'), pairs)]
  transfers between devices with their start and end apart: 12 -> 12, of which waited for: 6 -> 7; matrix products, arithmetic and copies ran while one was open for 0% -> 0% of each run, Pallas kernels for 4% -> 4%
where the time goes in v22:
time: 29.4 us; the launch traced here: 29.3 us
  starting transfers between devices  13.3 us (45%)
  waiting for transfers between devices  8.95 us (30%)
  Pallas kernels  6.94 us (24%)
    ppermute x12, starting transfers between devices, swap(): return lax.ppermute(array, ('feat', 'tok'), pairs)  13.3 us
    ppermute x12, waiting for transfers between devices, swap(): return lax.ppermute(array, ('feat', 'tok'), pairs)  8.95 us
    pallas_call x1, Pallas kernels, partial_halves(): pl.pallas_call(functools.partial(send_kernel, total_bits, parts), in_spec...  2.58 us
    pallas_call x1, Pallas kernels, gram_blocks(): pl.pallas_call(functools.partial(gram_kernel, shard, group, factor), in_s...  2.49 us
    pallas_call x1, Pallas kernels, partial_halves(): pl.pallas_call(functools.partial(keep_kernel, parts), out_shape=total_typ...  1.26 us
    pallas_call x3, Pallas kernels, local_call(): pl.pallas_call(kernel, out_shape=out_shape, compiler_params=pltpu.Compile...  0.62 us
  transfers between devices with their start and end apart: 12, of which 7 were waited for; matrix products, arithmetic and copies ran while one was open for 0% of the time, Pallas kernels for 4%

profile of v22, /device:TPU:0, one launch (start us, length us, event | category | flops | bytes accessed | tf_op | source)
XLA Modules:
  0.0 29.3 jit_solution(2022166757757692288)
XLA Ops:
  0.0 2.6 %partial_sent.1 = (f32[64,1024]{1,0:T(8,128)S(1)}, bf16[64,8192]{1,0:T(8,128)(2,1)S(1)}, s32[1,8192]{1,0:T(1,128)S(1)}, bf16[256,1024]{1,0:T(8,128)(2,1)S(1)}, f32[32,1024]{1,0:T(8,128)S(1)}) custom-call(bf16[128,8192]{1,0:T(8,128)(2,1)} %x_hbm.1, s32[1,8192]{1,0:T(1,128)} %bitcast.5, s32[1,1024]{1,0:T(1,128)} %bitcast.6), custom_call_target="tpu_custom_call" | custom-call | flops 1073741824 | bytes 2359296 | tf_op jit(solution)/shard_map/partial_sent/pallas_call | solution.py:99
  2.6 0.5 %collective-permute-start = (f32[64,1024]{1,0:T(8,128)S(1)}, f32[64,1024]{1,0:T(8,128)S(1)}, u32[]{:S(2)}, u32[]{:S(2)}) collective-permute-start(f32[64,1024]{1,0:T(8,128)S(1)} %get-tuple-element.25), channel_id=1, source_target_pairs={{0,2},{1,3},{2,0},{3,1},{4,6},{5,7},{6,4},{7,5},{8,10},{9,11},{10,... | collective-permute-start | bytes 786440 | tf_op jit(solution)/shard_map/ppermute | solution.py:270
  3.1 1.3 %partial_kept.1.keep_ref = f32[64,1024]{1,0:T(8,128)S(1)} custom-call(bf16[64,8192]{1,0:T(8,128)(2,1)S(1)} %get-tuple-element.21.x_keep, s32[1,8192]{1,0:T(1,128)S(1)} %get-tuple-element.22.signs, bf16[256,1024]{1,0:T(8,128)(2,1)S(1)} %get-tuple-element.23.low, f32[32,1024]{1,0:T(8,128)S(1)} %get-tuple-element.24.high), custom_call_target="tpu_custom_call" | custom-call | flops 1073741824 | bytes 2359296 | tf_op jit(solution)/shard_map/partial_kept/pallas_call | solution.py:123
  4.4 0.0 collective-permute-done.got_ref
  4.4 0.2 first_split.1
  4.5 4.8 %collective-permute-start.1 = (s32[136,128]{1,0:T(8,128)S(1)}, s32[136,128]{1,0:T(8,128)S(1)}, u32[]{:S(2)}, u32[]{:S(2)}) collective-permute-start(s32[136,128]{1,0:T(8,128)S(1)} %get-tuple-element.27), channel_id=1, source_target_pairs={{0,20},{1,21},{2,14},{3,15},{4,16},{5,17},{6,10},{7,11},{8,28},{9,... | collective-permute-start | bytes 208904 | tf_op jit(solution)/shard_map/ppermute | solution.py:270
  9.4 0.3 %collective-permute-start.2 = (s32[136,128]{1,0:T(8,128)S(1)}, s32[136,128]{1,0:T(8,128)S(1)}, u32[]{:S(2)}, u32[]{:S(2)}) collective-permute-start(s32[136,128]{1,0:T(8,128)S(1)} %get-tuple-element.28), channel_id=1, source_target_pairs={{0,16},{1,17},{2,10},{3,11},{4,20},{5,21},{6,14},{7,15},{8,24},{9,... | collective-permute-start | bytes 208904 | tf_op jit(solution)/shard_map/ppermute | solution.py:270
  9.7 0.3 %collective-permute-start.3 = (s32[136,128]{1,0:T(8,128)S(1)}, s32[136,128]{1,0:T(8,128)S(1)}, u32[]{:S(2)}, u32[]{:S(2)}) collective-permute-start(s32[136,128]{1,0:T(8,128)S(1)} %get-tuple-element.29), channel_id=1, source_target_pairs={{0,4},{1,5},{2,6},{3,7},{4,0},{5,1},{6,2},{7,3},{8,12},{9,13},{10,... | collective-permute-start | bytes 208904 | tf_op jit(solution)/shard_map/ppermute | solution.py:270
  10.0 1.7 %collective-permute-done.1.both_ref = s32[136,128]{1,0:T(8,128)S(1)} collective-permute-done((s32[136,128]{1,0:T(8,128)S(1)}, s32[136,128]{1,0:T(8,128)S(1)}, u32[]{:S(2)}, u32[]{:S(2)}) %collective-permute-start.1) | collective-permute-done | bytes 69664 | tf_op jit(solution)/shard_map/ppermute | solution.py:270
  11.7 2.8 %collective-permute-done.2.z_ref = s32[136,128]{1,0:T(8,128)S(1)} collective-permute-done((s32[136,128]{1,0:T(8,128)S(1)}, s32[136,128]{1,0:T(8,128)S(1)}, u32[]{:S(2)}, u32[]{:S(2)}) %collective-permute-start.2) | collective-permute-done | bytes 69664 | tf_op jit(solution)/shard_map/ppermute | solution.py:270
  14.6 0.3 add_square.1
  14.9 1.6 %collective-permute-start.4 = (s32[136,128]{1,0:T(8,128)S(1)}, s32[136,128]{1,0:T(8,128)S(1)}, u32[]{:S(2)}, u32[]{:S(2)}) collective-permute-start(s32[136,128]{1,0:T(8,128)S(1)} %get-tuple-element.31), channel_id=1, source_target_pairs={{0,8},{1,9},{2,18},{3,19},{4,12},{5,13},{6,22},{7,23},{8,0},{9,1},... | collective-permute-start | bytes 208904 | tf_op jit(solution)/shard_map/ppermute | solution.py:270
  16.5 2.7 %collective-permute-done.4.word_ref = s32[136,128]{1,0:T(8,128)S(1)} collective-permute-done((s32[136,128]{1,0:T(8,128)S(1)}, s32[136,128]{1,0:T(8,128)S(1)}, u32[]{:S(2)}, u32[]{:S(2)}) %collective-permute-start.4) | collective-permute-done | bytes 69664 | tf_op jit(solution)/shard_map/ppermute | solution.py:270
  19.2 0.2 sketch_rows.1
  19.4 0.1 collective-permute-start.5
  19.5 0.6 %collective-permute-start.6 = (bf16[32,1152]{1,0:T(8,128)(2,1)S(1)}, bf16[32,1152]{1,0:T(8,128)(2,1)S(1)}, u32[]{:S(2)}, u32[]{:S(2)}) collective-permute-start(bf16[32,1152]{1,0:T(8,128)(2,1)S(1)} %get-tuple-element.34), channel_id=1, source_target_pairs={{0,4},{1,5},{2,3},{3,2},{4,0},{5,1},{6,7},{7,6},{8,12},{9,13},{10,... | collective-permute-start | bytes 221192 | tf_op jit(solution)/shard_map/ppermute | solution.py:270
  20.1 1.5 %collective-permute-start.7 = (bf16[32,1152]{1,0:T(8,128)(2,1)S(1)}, bf16[32,1152]{1,0:T(8,128)(2,1)S(1)}, u32[]{:S(2)}, u32[]{:S(2)}) collective-permute-start(bf16[32,1152]{1,0:T(8,128)(2,1)S(1)} %get-tuple-element.35), channel_id=1, source_target_pairs={{0,1},{1,0},{2,6},{3,7},{4,5},{5,4},{6,2},{7,3},{8,9},{9,8},{10,14... | collective-permute-start | bytes 221192 | tf_op jit(solution)/shard_map/ppermute | solution.py:270
  21.6 2.0 %collective-permute-start.11 = (bf16[32,1152]{1,0:T(8,128)(2,1)S(1)}, bf16[32,1152]{1,0:T(8,128)(2,1)S(1)}, u32[]{:S(2)}, u32[]{:S(2)}) collective-permute-start(bf16[32,1152]{1,0:T(8,128)(2,1)S(1)} %get-tuple-element.36), channel_id=1, source_target_pairs={{0,3},{1,2},{2,4},{3,5},{4,7},{5,6},{6,0},{7,1},{8,11},{9,10},{10,... | collective-permute-start | bytes 221192 | tf_op jit(solution)/shard_map/ppermute | solution.py:270
  23.7 0.6 %collective-permute-done.5.refs_1_ = bf16[32,1152]{1,0:T(8,128)(2,1)S(1)} collective-permute-done((bf16[32,1152]{1,0:T(8,128)(2,1)S(1)}, bf16[32,1152]{1,0:T(8,128)(2,1)S(1)}, u32[]{:S(2)}, u32[]{:S(2)}) %collective-permute-start.5) | collective-permute-done | bytes 73760 | tf_op jit(solution)/shard_map/ppermute | solution.py:270
  24.3 0.1 collective-permute-done.6.refs_2_
  24.4 1.5 %collective-permute-start.10 = (bf16[32,1152]{1,0:T(8,128)(2,1)S(1)}, bf16[32,1152]{1,0:T(8,128)(2,1)S(1)}, u32[]{:S(2)}, u32[]{:S(2)}) collective-permute-start(bf16[32,1152]{1,0:T(8,128)(2,1)S(1)} %collective-permute-done.6.refs_2_), channel_id=1, source_target_pairs={{0,2},{1,3},{2,0},{3,1},{4,6},{5,7},{6,4},{7,5},{8,10},{9,11},{10,... | collective-permute-start | bytes 221192 | tf_op jit(solution)/shard_map/ppermute | solution.py:270
  25.9 0.4 %collective-permute-done.11.refs_7_ = bf16[32,1152]{1,0:T(8,128)(2,1)S(1)} collective-permute-done((bf16[32,1152]{1,0:T(8,128)(2,1)S(1)}, bf16[32,1152]{1,0:T(8,128)(2,1)S(1)}, u32[]{:S(2)}, u32[]{:S(2)}) %collective-permute-start.11) | collective-permute-done | bytes 73760 | tf_op jit(solution)/shard_map/ppermute | solution.py:270
  26.3 0.5 %collective-permute-done.10.refs_6_ = bf16[32,1152]{1,0:T(8,128)(2,1)S(1)} collective-permute-done((bf16[32,1152]{1,0:T(8,128)(2,1)S(1)}, bf16[32,1152]{1,0:T(8,128)(2,1)S(1)}, u32[]{:S(2)}, u32[]{:S(2)}) %collective-permute-start.10) | collective-permute-done | bytes 73760 | tf_op jit(solution)/shard_map/ppermute | solution.py:270
  26.8 2.5 %gram.1 = f32[1024,1024]{1,0:T(8,128)} custom-call(bf16[32,1152]{1,0:T(8,128)(2,1)S(1)} %get-tuple-element.32.refs_0_, bf16[32,1152]{1,0:T(8,128)(2,1)S(1)} %collective-permute-done.5.refs_1_, bf16[32,1152]{1,0:T(8,128)(2,1)S(1)} %collective-permute-done.6.refs_2_, bf16[32,1152]{1,0:T(8,128)(2,1)S(1)} %collective-permute-done.7.refs_3_, ...), custom_call_target="tpu_custom_call" | custom-call | flops 536870912 | bytes 4194304 | tf_op jit(solution)/shard_map/gram/pallas_call | solution.py:166
  (8 shorter events, 0.0 us)
Async XLA Ops:
  0.0 19.2 %copy-start = (s32[128,1]{0,1:T(1,128)S(1)}, s32[128,1]{0,1:T(1,128)}, u32[]{:S(2)}) copy-start(s32[128,1]{0,1:T(1,128)} %param.7) | copy-start | bytes 1540
  2.6 1.8 %collective-permute-start = (f32[64,1024]{1,0:T(8,128)S(1)}, f32[64,1024]{1,0:T(8,128)S(1)}, u32[]{:S(2)}, u32[]{:S(2)}) collective-permute-start(f32[64,1024]{1,0:T(8,128)S(1)} %get-tuple-element.25), channel_id=1, source_target_pairs={{0,2},{1,3},{2,0},{3,1},{4,6},{5,7},{6,4},{7,5},{8,10},{9,11},{10,... | collective-permute-start | bytes 786440 | tf_op jit(solution)/shard_map/ppermute | solution.py:270
  4.5 7.2 %collective-permute-start.1 = (s32[136,128]{1,0:T(8,128)S(1)}, s32[136,128]{1,0:T(8,128)S(1)}, u32[]{:S(2)}, u32[]{:S(2)}) collective-permute-start(s32[136,128]{1,0:T(8,128)S(1)} %get-tuple-element.27), channel_id=1, source_target_pairs={{0,20},{1,21},{2,14},{3,15},{4,16},{5,17},{6,10},{7,11},{8,28},{9,... | collective-permute-start | bytes 208904 | tf_op jit(solution)/shard_map/ppermute | solution.py:270
  9.4 5.2 %collective-permute-start.2 = (s32[136,128]{1,0:T(8,128)S(1)}, s32[136,128]{1,0:T(8,128)S(1)}, u32[]{:S(2)}, u32[]{:S(2)}) collective-permute-start(s32[136,128]{1,0:T(8,128)S(1)} %get-tuple-element.28), channel_id=1, source_target_pairs={{0,16},{1,17},{2,10},{3,11},{4,20},{5,21},{6,14},{7,15},{8,24},{9,... | collective-permute-start | bytes 208904 | tf_op jit(solution)/shard_map/ppermute | solution.py:270
  9.7 4.9 %collective-permute-start.3 = (s32[136,128]{1,0:T(8,128)S(1)}, s32[136,128]{1,0:T(8,128)S(1)}, u32[]{:S(2)}, u32[]{:S(2)}) collective-permute-start(s32[136,128]{1,0:T(8,128)S(1)} %get-tuple-element.29), channel_id=1, source_target_pairs={{0,4},{1,5},{2,6},{3,7},{4,0},{5,1},{6,2},{7,3},{8,12},{9,13},{10,... | collective-permute-start | bytes 208904 | tf_op jit(solution)/shard_map/ppermute | solution.py:270
  14.9 4.4 %collective-permute-start.4 = (s32[136,128]{1,0:T(8,128)S(1)}, s32[136,128]{1,0:T(8,128)S(1)}, u32[]{:S(2)}, u32[]{:S(2)}) collective-permute-start(s32[136,128]{1,0:T(8,128)S(1)} %get-tuple-element.31), channel_id=1, source_target_pairs={{0,8},{1,9},{2,18},{3,19},{4,12},{5,13},{6,22},{7,23},{8,0},{9,1},... | collective-permute-start | bytes 208904 | tf_op jit(solution)/shard_map/ppermute | solution.py:270
  19.4 4.9 %collective-permute-start.5 = (bf16[32,1152]{1,0:T(8,128)(2,1)S(1)}, bf16[32,1152]{1,0:T(8,128)(2,1)S(1)}, u32[]{:S(2)}, u32[]{:S(2)}) collective-permute-start(bf16[32,1152]{1,0:T(8,128)(2,1)S(1)} %get-tuple-element.33), channel_id=1, source_target_pairs={{0,7},{1,6},{2,5},{3,4},{4,3},{5,2},{6,1},{7,0},{8,15},{9,14},{10,... | collective-permute-start | bytes 221192 | tf_op jit(solution)/shard_map/ppermute | solution.py:270
  19.5 4.9 %collective-permute-start.6 = (bf16[32,1152]{1,0:T(8,128)(2,1)S(1)}, bf16[32,1152]{1,0:T(8,128)(2,1)S(1)}, u32[]{:S(2)}, u32[]{:S(2)}) collective-permute-start(bf16[32,1152]{1,0:T(8,128)(2,1)S(1)} %get-tuple-element.34), channel_id=1, source_target_pairs={{0,4},{1,5},{2,3},{3,2},{4,0},{5,1},{6,7},{7,6},{8,12},{9,13},{10,... | collective-permute-start | bytes 221192 | tf_op jit(solution)/shard_map/ppermute | solution.py:270
  20.1 5.8 %collective-permute-start.7 = (bf16[32,1152]{1,0:T(8,128)(2,1)S(1)}, bf16[32,1152]{1,0:T(8,128)(2,1)S(1)}, u32[]{:S(2)}, u32[]{:S(2)}) collective-permute-start(bf16[32,1152]{1,0:T(8,128)(2,1)S(1)} %get-tuple-element.35), channel_id=1, source_target_pairs={{0,1},{1,0},{2,6},{3,7},{4,5},{5,4},{6,2},{7,3},{8,9},{9,8},{10,14... | collective-permute-start | bytes 221192 | tf_op jit(solution)/shard_map/ppermute | solution.py:270
  21.6 4.7 %collective-permute-start.11 = (bf16[32,1152]{1,0:T(8,128)(2,1)S(1)}, bf16[32,1152]{1,0:T(8,128)(2,1)S(1)}, u32[]{:S(2)}, u32[]{:S(2)}) collective-permute-start(bf16[32,1152]{1,0:T(8,128)(2,1)S(1)} %get-tuple-element.36), channel_id=1, source_target_pairs={{0,3},{1,2},{2,4},{3,5},{4,7},{5,6},{6,0},{7,1},{8,11},{9,10},{10,... | collective-permute-start | bytes 221192 | tf_op jit(solution)/shard_map/ppermute | solution.py:270
  23.7 2.6 %collective-permute-start.8 = (bf16[32,1152]{1,0:T(8,128)(2,1)S(1)}, bf16[32,1152]{1,0:T(8,128)(2,1)S(1)}, u32[]{:S(2)}, u32[]{:S(2)}) collective-permute-start(bf16[32,1152]{1,0:T(8,128)(2,1)S(1)} %get-tuple-element.32.refs_0_), channel_id=1, source_target_pairs={{0,2},{1,3},{2,0},{3,1},{4,6},{5,7},{6,4},{7,5},{8,10},{9,11},{10,... | collective-permute-start | bytes 221192 | tf_op jit(solution)/shard_map/ppermute | solution.py:270
  24.3 2.0 %collective-permute-start.9 = (bf16[32,1152]{1,0:T(8,128)(2,1)S(1)}, bf16[32,1152]{1,0:T(8,128)(2,1)S(1)}, u32[]{:S(2)}, u32[]{:S(2)}) collective-permute-start(bf16[32,1152]{1,0:T(8,128)(2,1)S(1)} %collective-permute-done.5.refs_1_), channel_id=1, source_target_pairs={{0,2},{1,3},{2,0},{3,1},{4,6},{5,7},{6,4},{7,5},{8,10},{9,11},{10,... | collective-permute-start | bytes 221192 | tf_op jit(solution)/shard_map/ppermute | solution.py:270
  24.4 2.4 %collective-permute-start.10 = (bf16[32,1152]{1,0:T(8,128)(2,1)S(1)}, bf16[32,1152]{1,0:T(8,128)(2,1)S(1)}, u32[]{:S(2)}, u32[]{:S(2)}) collective-permute-start(bf16[32,1152]{1,0:T(8,128)(2,1)S(1)} %collective-permute-done.6.refs_2_), channel_id=1, source_target_pairs={{0,2},{1,3},{2,0},{3,1},{4,6},{5,7},{6,4},{7,5},{8,10},{9,11},{10,... | collective-permute-start | bytes 221192 | tf_op jit(solution)/shard_map/ppermute | solution.py:270

commit v23 on v22

--- a/solution.py
+++ b/solution.py
@@ -88,7 +88,7 @@
 def partial_halves(features, signs, columns, feat_count):
     rows, width = features.shape
     kept = columns.shape[0]
-    parts = max(1, width // 4096)
+    parts = 1
     half = rows // 2
     total_bits = (width * feat_count).bit_length() - 1
     params = pltpu.CompilerParams(vmem_limit_bytes=VMEM_LIMIT)

time: 29.4 us -> 29.4 us (level)
  no operation moved by 1% of the time
where the time goes in v23:
time: 29.4 us; the launch traced here: 29.2 us
  starting transfers between devices  13.3 us (45%)
  waiting for transfers between devices  8.95 us (30%)
  Pallas kernels  6.93 us (24%)
    ppermute x12, starting transfers between devices, swap(): return lax.ppermute(array, ('feat', 'tok'), pairs)  13.3 us
    ppermute x12, waiting for transfers between devices, swap(): return lax.ppermute(array, ('feat', 'tok'), pairs)  8.95 us
    pallas_call x1, Pallas kernels, partial_halves(): pl.pallas_call(functools.partial(send_kernel, total_bits, parts), in_spec...  2.57 us
    pallas_call x1, Pallas kernels, gram_blocks(): pl.pallas_call(functools.partial(gram_kernel, shard, group, factor), in_s...  2.49 us
    pallas_call x1, Pallas kernels, partial_halves(): pl.pallas_call(functools.partial(keep_kernel, parts), out_shape=total_typ...  1.25 us
    pallas_call x3, Pallas kernels, local_call(): pl.pallas_call(kernel, out_shape=out_shape, compiler_params=pltpu.Compile...  0.62 us
  transfers between devices with their start and end apart: 12, of which 7 were waited for; matrix products, arithmetic and copies ran while one was open for 0% of the time, Pallas kernels for 4%

profile of v23, /device:TPU:0, one launch (start us, length us, event | category | flops | bytes accessed | tf_op | source)
XLA Modules:
  0.0 29.2 jit_solution(1597854731320221162)
XLA Ops:
  0.0 2.6 %partial_sent.1 = (f32[64,1024]{1,0:T(8,128)S(1)}, bf16[64,8192]{1,0:T(8,128)(2,1)S(1)}, s32[1,8192]{1,0:T(1,128)S(1)}, bf16[256,1024]{1,0:T(8,128)(2,1)S(1)}, f32[32,1024]{1,0:T(8,128)S(1)}) custom-call(bf16[128,8192]{1,0:T(8,128)(2,1)} %x_hbm.1, s32[1,8192]{1,0:T(1,128)} %bitcast.5, s32[1,1024]{1,0:T(1,128)} %bitcast.6), custom_call_target="tpu_custom_call" | custom-call | flops 1073741824 | bytes 2359296 | tf_op jit(solution)/shard_map/partial_sent/pallas_call | solution.py:99
  2.6 0.5 %collective-permute-start = (f32[64,1024]{1,0:T(8,128)S(1)}, f32[64,1024]{1,0:T(8,128)S(1)}, u32[]{:S(2)}, u32[]{:S(2)}) collective-permute-start(f32[64,1024]{1,0:T(8,128)S(1)} %get-tuple-element.25), channel_id=1, source_target_pairs={{0,2},{1,3},{2,0},{3,1},{4,6},{5,7},{6,4},{7,5},{8,10},{9,11},{10,... | collective-permute-start | bytes 786440 | tf_op jit(solution)/shard_map/ppermute | solution.py:270
  3.1 1.3 %partial_kept.1.keep_ref = f32[64,1024]{1,0:T(8,128)S(1)} custom-call(bf16[64,8192]{1,0:T(8,128)(2,1)S(1)} %get-tuple-element.21.x_keep, s32[1,8192]{1,0:T(1,128)S(1)} %get-tuple-element.22.signs, bf16[256,1024]{1,0:T(8,128)(2,1)S(1)} %get-tuple-element.23.low, f32[32,1024]{1,0:T(8,128)S(1)} %get-tuple-element.24.high), custom_call_target="tpu_custom_call" | custom-call | flops 1073741824 | bytes 2359296 | tf_op jit(solution)/shard_map/partial_kept/pallas_call | solution.py:123
  4.4 0.0 collective-permute-done.got_ref
  4.4 0.2 first_split.1
  4.5 4.8 %collective-permute-start.1 = (s32[136,128]{1,0:T(8,128)S(1)}, s32[136,128]{1,0:T(8,128)S(1)}, u32[]{:S(2)}, u32[]{:S(2)}) collective-permute-start(s32[136,128]{1,0:T(8,128)S(1)} %get-tuple-element.27), channel_id=1, source_target_pairs={{0,20},{1,21},{2,14},{3,15},{4,16},{5,17},{6,10},{7,11},{8,28},{9,... | collective-permute-start | bytes 208904 | tf_op jit(solution)/shard_map/ppermute | solution.py:270
  9.4 0.3 %collective-permute-start.2 = (s32[136,128]{1,0:T(8,128)S(1)}, s32[136,128]{1,0:T(8,128)S(1)}, u32[]{:S(2)}, u32[]{:S(2)}) collective-permute-start(s32[136,128]{1,0:T(8,128)S(1)} %get-tuple-element.28), channel_id=1, source_target_pairs={{0,16},{1,17},{2,10},{3,11},{4,20},{5,21},{6,14},{7,15},{8,24},{9,... | collective-permute-start | bytes 208904 | tf_op jit(solution)/shard_map/ppermute | solution.py:270
  9.7 0.3 %collective-permute-start.3 = (s32[136,128]{1,0:T(8,128)S(1)}, s32[136,128]{1,0:T(8,128)S(1)}, u32[]{:S(2)}, u32[]{:S(2)}) collective-permute-start(s32[136,128]{1,0:T(8,128)S(1)} %get-tuple-element.29), channel_id=1, source_target_pairs={{0,4},{1,5},{2,6},{3,7},{4,0},{5,1},{6,2},{7,3},{8,12},{9,13},{10,... | collective-permute-start | bytes 208904 | tf_op jit(solution)/shard_map/ppermute | solution.py:270
  10.0 1.8 %collective-permute-done.1.both_ref = s32[136,128]{1,0:T(8,128)S(1)} collective-permute-done((s32[136,128]{1,0:T(8,128)S(1)}, s32[136,128]{1,0:T(8,128)S(1)}, u32[]{:S(2)}, u32[]{:S(2)}) %collective-permute-start.1) | collective-permute-done | bytes 69664 | tf_op jit(solution)/shard_map/ppermute | solution.py:270
  11.8 2.8 %collective-permute-done.2.z_ref = s32[136,128]{1,0:T(8,128)S(1)} collective-permute-done((s32[136,128]{1,0:T(8,128)S(1)}, s32[136,128]{1,0:T(8,128)S(1)}, u32[]{:S(2)}, u32[]{:S(2)}) %collective-permute-start.2) | collective-permute-done | bytes 69664 | tf_op jit(solution)/shard_map/ppermute | solution.py:270
  14.6 0.3 add_square.1
  14.8 1.6 %collective-permute-start.4 = (s32[136,128]{1,0:T(8,128)S(1)}, s32[136,128]{1,0:T(8,128)S(1)}, u32[]{:S(2)}, u32[]{:S(2)}) collective-permute-start(s32[136,128]{1,0:T(8,128)S(1)} %get-tuple-element.31), channel_id=1, source_target_pairs={{0,8},{1,9},{2,18},{3,19},{4,12},{5,13},{6,22},{7,23},{8,0},{9,1},... | collective-permute-start | bytes 208904 | tf_op jit(solution)/shard_map/ppermute | solution.py:270
  16.5 2.7 %collective-permute-done.4.word_ref = s32[136,128]{1,0:T(8,128)S(1)} collective-permute-done((s32[136,128]{1,0:T(8,128)S(1)}, s32[136,128]{1,0:T(8,128)S(1)}, u32[]{:S(2)}, u32[]{:S(2)}) %collective-permute-start.4) | collective-permute-done | bytes 69664 | tf_op jit(solution)/shard_map/ppermute | solution.py:270
  19.2 0.2 sketch_rows.1
  19.4 0.1 collective-permute-start.5
  19.5 0.6 %collective-permute-start.6 = (bf16[32,1152]{1,0:T(8,128)(2,1)S(1)}, bf16[32,1152]{1,0:T(8,128)(2,1)S(1)}, u32[]{:S(2)}, u32[]{:S(2)}) collective-permute-start(bf16[32,1152]{1,0:T(8,128)(2,1)S(1)} %get-tuple-element.34), channel_id=1, source_target_pairs={{0,4},{1,5},{2,3},{3,2},{4,0},{5,1},{6,7},{7,6},{8,12},{9,13},{10,... | collective-permute-start | bytes 221192 | tf_op jit(solution)/shard_map/ppermute | solution.py:270
  20.1 1.5 %collective-permute-start.7 = (bf16[32,1152]{1,0:T(8,128)(2,1)S(1)}, bf16[32,1152]{1,0:T(8,128)(2,1)S(1)}, u32[]{:S(2)}, u32[]{:S(2)}) collective-permute-start(bf16[32,1152]{1,0:T(8,128)(2,1)S(1)} %get-tuple-element.35), channel_id=1, source_target_pairs={{0,1},{1,0},{2,6},{3,7},{4,5},{5,4},{6,2},{7,3},{8,9},{9,8},{10,14... | collective-permute-start | bytes 221192 | tf_op jit(solution)/shard_map/ppermute | solution.py:270
  21.6 2.0 %collective-permute-start.11 = (bf16[32,1152]{1,0:T(8,128)(2,1)S(1)}, bf16[32,1152]{1,0:T(8,128)(2,1)S(1)}, u32[]{:S(2)}, u32[]{:S(2)}) collective-permute-start(bf16[32,1152]{1,0:T(8,128)(2,1)S(1)} %get-tuple-element.36), channel_id=1, source_target_pairs={{0,3},{1,2},{2,4},{3,5},{4,7},{5,6},{6,0},{7,1},{8,11},{9,10},{10,... | collective-permute-start | bytes 221192 | tf_op jit(solution)/shard_map/ppermute | solution.py:270
  23.6 0.6 %collective-permute-done.5.refs_1_ = bf16[32,1152]{1,0:T(8,128)(2,1)S(1)} collective-permute-done((bf16[32,1152]{1,0:T(8,128)(2,1)S(1)}, bf16[32,1152]{1,0:T(8,128)(2,1)S(1)}, u32[]{:S(2)}, u32[]{:S(2)}) %collective-permute-start.5) | collective-permute-done | bytes 73760 | tf_op jit(solution)/shard_map/ppermute | solution.py:270
  24.3 0.1 collective-permute-done.6.refs_2_
  24.4 1.5 %collective-permute-start.10 = (bf16[32,1152]{1,0:T(8,128)(2,1)S(1)}, bf16[32,1152]{1,0:T(8,128)(2,1)S(1)}, u32[]{:S(2)}, u32[]{:S(2)}) collective-permute-start(bf16[32,1152]{1,0:T(8,128)(2,1)S(1)} %collective-permute-done.6.refs_2_), channel_id=1, source_target_pairs={{0,2},{1,3},{2,0},{3,1},{4,6},{5,7},{6,4},{7,5},{8,10},{9,11},{10,... | collective-permute-start | bytes 221192 | tf_op jit(solution)/shard_map/ppermute | solution.py:270
  25.9 0.4 %collective-permute-done.11.refs_7_ = bf16[32,1152]{1,0:T(8,128)(2,1)S(1)} collective-permute-done((bf16[32,1152]{1,0:T(8,128)(2,1)S(1)}, bf16[32,1152]{1,0:T(8,128)(2,1)S(1)}, u32[]{:S(2)}, u32[]{:S(2)}) %collective-permute-start.11) | collective-permute-done | bytes 73760 | tf_op jit(solution)/shard_map/ppermute | solution.py:270
  26.3 0.5 %collective-permute-done.10.refs_6_ = bf16[32,1152]{1,0:T(8,128)(2,1)S(1)} collective-permute-done((bf16[32,1152]{1,0:T(8,128)(2,1)S(1)}, bf16[32,1152]{1,0:T(8,128)(2,1)S(1)}, u32[]{:S(2)}, u32[]{:S(2)}) %collective-permute-start.10) | collective-permute-done | bytes 73760 | tf_op jit(solution)/shard_map/ppermute | solution.py:270
  26.8 2.5 %gram.1 = f32[1024,1024]{1,0:T(8,128)} custom-call(bf16[32,1152]{1,0:T(8,128)(2,1)S(1)} %get-tuple-element.32.refs_0_, bf16[32,1152]{1,0:T(8,128)(2,1)S(1)} %collective-permute-done.5.refs_1_, bf16[32,1152]{1,0:T(8,128)(2,1)S(1)} %collective-permute-done.6.refs_2_, bf16[32,1152]{1,0:T(8,128)(2,1)S(1)} %collective-permute-done.7.refs_3_, ...), custom_call_target="tpu_custom_call" | custom-call | flops 536870912 | bytes 4194304 | tf_op jit(solution)/shard_map/gram/pallas_call | solution.py:166
  (8 shorter events, 0.0 us)
Async XLA Ops:
  0.0 19.2 %copy-start = (s32[128,1]{0,1:T(1,128)S(1)}, s32[128,1]{0,1:T(1,128)}, u32[]{:S(2)}) copy-start(s32[128,1]{0,1:T(1,128)} %param.7) | copy-start | bytes 1540
  2.6 1.8 %collective-permute-start = (f32[64,1024]{1,0:T(8,128)S(1)}, f32[64,1024]{1,0:T(8,128)S(1)}, u32[]{:S(2)}, u32[]{:S(2)}) collective-permute-start(f32[64,1024]{1,0:T(8,128)S(1)} %get-tuple-element.25), channel_id=1, source_target_pairs={{0,2},{1,3},{2,0},{3,1},{4,6},{5,7},{6,4},{7,5},{8,10},{9,11},{10,... | collective-permute-start | bytes 786440 | tf_op jit(solution)/shard_map/ppermute | solution.py:270
  4.5 7.3 %collective-permute-start.1 = (s32[136,128]{1,0:T(8,128)S(1)}, s32[136,128]{1,0:T(8,128)S(1)}, u32[]{:S(2)}, u32[]{:S(2)}) collective-permute-start(s32[136,128]{1,0:T(8,128)S(1)} %get-tuple-element.27), channel_id=1, source_target_pairs={{0,20},{1,21},{2,14},{3,15},{4,16},{5,17},{6,10},{7,11},{8,28},{9,... | collective-permute-start | bytes 208904 | tf_op jit(solution)/shard_map/ppermute | solution.py:270
  9.4 5.2 %collective-permute-start.2 = (s32[136,128]{1,0:T(8,128)S(1)}, s32[136,128]{1,0:T(8,128)S(1)}, u32[]{:S(2)}, u32[]{:S(2)}) collective-permute-start(s32[136,128]{1,0:T(8,128)S(1)} %get-tuple-element.28), channel_id=1, source_target_pairs={{0,16},{1,17},{2,10},{3,11},{4,20},{5,21},{6,14},{7,15},{8,24},{9,... | collective-permute-start | bytes 208904 | tf_op jit(solution)/shard_map/ppermute | solution.py:270
  9.7 4.9 %collective-permute-start.3 = (s32[136,128]{1,0:T(8,128)S(1)}, s32[136,128]{1,0:T(8,128)S(1)}, u32[]{:S(2)}, u32[]{:S(2)}) collective-permute-start(s32[136,128]{1,0:T(8,128)S(1)} %get-tuple-element.29), channel_id=1, source_target_pairs={{0,4},{1,5},{2,6},{3,7},{4,0},{5,1},{6,2},{7,3},{8,12},{9,13},{10,... | collective-permute-start | bytes 208904 | tf_op jit(solution)/shard_map/ppermute | solution.py:270
  14.8 4.4 %collective-permute-start.4 = (s32[136,128]{1,0:T(8,128)S(1)}, s32[136,128]{1,0:T(8,128)S(1)}, u32[]{:S(2)}, u32[]{:S(2)}) collective-permute-start(s32[136,128]{1,0:T(8,128)S(1)} %get-tuple-element.31), channel_id=1, source_target_pairs={{0,8},{1,9},{2,18},{3,19},{4,12},{5,13},{6,22},{7,23},{8,0},{9,1},... | collective-permute-start | bytes 208904 | tf_op jit(solution)/shard_map/ppermute | solution.py:270
  19.4 4.9 %collective-permute-start.5 = (bf16[32,1152]{1,0:T(8,128)(2,1)S(1)}, bf16[32,1152]{1,0:T(8,128)(2,1)S(1)}, u32[]{:S(2)}, u32[]{:S(2)}) collective-permute-start(bf16[32,1152]{1,0:T(8,128)(2,1)S(1)} %get-tuple-element.33), channel_id=1, source_target_pairs={{0,7},{1,6},{2,5},{3,4},{4,3},{5,2},{6,1},{7,0},{8,15},{9,14},{10,... | collective-permute-start | bytes 221192 | tf_op jit(solution)/shard_map/ppermute | solution.py:270
  19.5 4.9 %collective-permute-start.6 = (bf16[32,1152]{1,0:T(8,128)(2,1)S(1)}, bf16[32,1152]{1,0:T(8,128)(2,1)S(1)}, u32[]{:S(2)}, u32[]{:S(2)}) collective-permute-start(bf16[32,1152]{1,0:T(8,128)(2,1)S(1)} %get-tuple-element.34), channel_id=1, source_target_pairs={{0,4},{1,5},{2,3},{3,2},{4,0},{5,1},{6,7},{7,6},{8,12},{9,13},{10,... | collective-permute-start | bytes 221192 | tf_op jit(solution)/shard_map/ppermute | solution.py:270
  20.1 5.8 %collective-permute-start.7 = (bf16[32,1152]{1,0:T(8,128)(2,1)S(1)}, bf16[32,1152]{1,0:T(8,128)(2,1)S(1)}, u32[]{:S(2)}, u32[]{:S(2)}) collective-permute-start(bf16[32,1152]{1,0:T(8,128)(2,1)S(1)} %get-tuple-element.35), channel_id=1, source_target_pairs={{0,1},{1,0},{2,6},{3,7},{4,5},{5,4},{6,2},{7,3},{8,9},{9,8},{10,14... | collective-permute-start | bytes 221192 | tf_op jit(solution)/shard_map/ppermute | solution.py:270
  21.6 4.7 %collective-permute-start.11 = (bf16[32,1152]{1,0:T(8,128)(2,1)S(1)}, bf16[32,1152]{1,0:T(8,128)(2,1)S(1)}, u32[]{:S(2)}, u32[]{:S(2)}) collective-permute-start(bf16[32,1152]{1,0:T(8,128)(2,1)S(1)} %get-tuple-element.36), channel_id=1, source_target_pairs={{0,3},{1,2},{2,4},{3,5},{4,7},{5,6},{6,0},{7,1},{8,11},{9,10},{10,... | collective-permute-start | bytes 221192 | tf_op jit(solution)/shard_map/ppermute | solution.py:270
  23.6 2.6 %collective-permute-start.8 = (bf16[32,1152]{1,0:T(8,128)(2,1)S(1)}, bf16[32,1152]{1,0:T(8,128)(2,1)S(1)}, u32[]{:S(2)}, u32[]{:S(2)}) collective-permute-start(bf16[32,1152]{1,0:T(8,128)(2,1)S(1)} %get-tuple-element.32.refs_0_), channel_id=1, source_target_pairs={{0,2},{1,3},{2,0},{3,1},{4,6},{5,7},{6,4},{7,5},{8,10},{9,11},{10,... | collective-permute-start | bytes 221192 | tf_op jit(solution)/shard_map/ppermute | solution.py:270
  24.3 2.0 %collective-permute-start.9 = (bf16[32,1152]{1,0:T(8,128)(2,1)S(1)}, bf16[32,1152]{1,0:T(8,128)(2,1)S(1)}, u32[]{:S(2)}, u32[]{:S(2)}) collective-permute-start(bf16[32,1152]{1,0:T(8,128)(2,1)S(1)} %collective-permute-done.5.refs_1_), channel_id=1, source_target_pairs={{0,2},{1,3},{2,0},{3,1},{4,6},{5,7},{6,4},{7,5},{8,10},{9,11},{10,... | collective-permute-start | bytes 221192 | tf_op jit(solution)/shard_map/ppermute | solution.py:270
  24.4 2.4 %collective-permute-start.10 = (bf16[32,1152]{1,0:T(8,128)(2,1)S(1)}, bf16[32,1152]{1,0:T(8,128)(2,1)S(1)}, u32[]{:S(2)}, u32[]{:S(2)}) collective-permute-start(bf16[32,1152]{1,0:T(8,128)(2,1)S(1)} %collective-permute-done.6.refs_2_), channel_id=1, source_target_pairs={{0,2},{1,3},{2,0},{3,1},{4,6},{5,7},{6,4},{7,5},{8,10},{9,11},{10,... | collective-permute-start | bytes 221192 | tf_op jit(solution)/shard_map/ppermute | solution.py:270

commit v24 on v22

--- a/solution.py
+++ b/solution.py
@@ -289,13 +289,13 @@
         got,
         out_shape=[total_type, word_type, word_type, word_type],
     )
-    both = swap(again, (0, 10), (0, 6))
-    z_word = swap(here, (0, 8), (0, 4))
+    both = swap(again, (0, 6), (0, 10))
+    z_word = swap(here, (0, 4), (0, 8))
     x_word = swap(there, (0, 2))
     total, word = local_call(
         square_kernel, "add_square", total, both, z_word, x_word, out_shape=[total_type, word_type]
     )
-    word = swap(word, (0, 4), (0, 8))
+    word = swap(word, (0, 8), (0, 4))
     stride = 16
     while stride < feat_count:
         total, word = local_call(middle_kernel, "add_encode", total, word, out_shape=[total_type, word_type])

time: 29.4 us -> 29.9 us (1.017)
  waiting for transfers between devices: 8.95 us -> 9.32 us
    ppermute x12, waiting for transfers between devices: 8.95 us -> 9.32 us  [swap(): return lax.ppermute(array, ('feat', 'tok'), pairs)]
  transfers between devices with their start and end apart: 12 -> 12, of which waited for: 7 -> 6; matrix products, arithmetic and copies ran while one was open for 0% -> 0% of each run, Pallas kernels for 4% -> 4%
where the time goes in v24:
time: 29.9 us; the launch traced here: 29.8 us
  starting transfers between devices  13.4 us (45%)
  waiting for transfers between devices  9.32 us (31%)
  Pallas kernels  6.94 us (23%)
    ppermute x12, starting transfers between devices, swap(): return lax.ppermute(array, ('feat', 'tok'), pairs)  13.4 us
    ppermute x12, waiting for transfers between devices, swap(): return lax.ppermute(array, ('feat', 'tok'), pairs)  9.32 us
    pallas_call x1, Pallas kernels, partial_halves(): pl.pallas_call(functools.partial(send_kernel, total_bits, parts), in_spec...  2.58 us
    pallas_call x1, Pallas kernels, gram_blocks(): pl.pallas_call(functools.partial(gram_kernel, shard, group, factor), in_s...  2.48 us
    pallas_call x1, Pallas kernels, partial_halves(): pl.pallas_call(functools.partial(keep_kernel, parts), out_shape=total_typ...  1.26 us
    pallas_call x3, Pallas kernels, local_call(): pl.pallas_call(kernel, out_shape=out_shape, compiler_params=pltpu.Compile...  0.62 us
  transfers between devices with their start and end apart: 12, of which 6 were waited for; matrix products, arithmetic and copies ran while one was open for 0% of the time, Pallas kernels for 4%

profile of v24, /device:TPU:0, one launch (start us, length us, event | category | flops | bytes accessed | tf_op | source)
XLA Modules:
  0.0 29.8 jit_solution(16131922396332806087)
XLA Ops:
  0.0 2.6 %partial_sent.1 = (f32[64,1024]{1,0:T(8,128)S(1)}, bf16[64,8192]{1,0:T(8,128)(2,1)S(1)}, s32[1,8192]{1,0:T(1,128)S(1)}, bf16[256,1024]{1,0:T(8,128)(2,1)S(1)}, f32[32,1024]{1,0:T(8,128)S(1)}) custom-call(bf16[128,8192]{1,0:T(8,128)(2,1)} %x_hbm.1, s32[1,8192]{1,0:T(1,128)} %bitcast.5, s32[1,1024]{1,0:T(1,128)} %bitcast.6), custom_call_target="tpu_custom_call" | custom-call | flops 1073741824 | bytes 2359296 | tf_op jit(solution)/shard_map/partial_sent/pallas_call | solution.py:99
  2.6 0.5 %collective-permute-start = (f32[64,1024]{1,0:T(8,128)S(1)}, f32[64,1024]{1,0:T(8,128)S(1)}, u32[]{:S(2)}, u32[]{:S(2)}) collective-permute-start(f32[64,1024]{1,0:T(8,128)S(1)} %get-tuple-element.25), channel_id=1, source_target_pairs={{0,2},{1,3},{2,0},{3,1},{4,6},{5,7},{6,4},{7,5},{8,10},{9,11},{10,... | collective-permute-start | bytes 786440 | tf_op jit(solution)/shard_map/ppermute | solution.py:270
  3.1 1.3 %partial_kept.1.keep_ref = f32[64,1024]{1,0:T(8,128)S(1)} custom-call(bf16[64,8192]{1,0:T(8,128)(2,1)S(1)} %get-tuple-element.21.x_keep, s32[1,8192]{1,0:T(1,128)S(1)} %get-tuple-element.22.signs, bf16[256,1024]{1,0:T(8,128)(2,1)S(1)} %get-tuple-element.23.low, f32[32,1024]{1,0:T(8,128)S(1)} %get-tuple-element.24.high), custom_call_target="tpu_custom_call" | custom-call | flops 1073741824 | bytes 2359296 | tf_op jit(solution)/shard_map/partial_kept/pallas_call | solution.py:123
  4.4 0.2 first_split.1
  4.5 3.8 %collective-permute-start.1 = (s32[136,128]{1,0:T(8,128)S(1)}, s32[136,128]{1,0:T(8,128)S(1)}, u32[]{:S(2)}, u32[]{:S(2)}) collective-permute-start(s32[136,128]{1,0:T(8,128)S(1)} %get-tuple-element.27), channel_id=1, source_target_pairs={{0,12},{1,13},{2,22},{3,23},{4,8},{5,9},{6,18},{7,19},{8,4},{9,5},... | collective-permute-start | bytes 208904 | tf_op jit(solution)/shard_map/ppermute | solution.py:270
  8.4 0.4 %collective-permute-start.2 = (s32[136,128]{1,0:T(8,128)S(1)}, s32[136,128]{1,0:T(8,128)S(1)}, u32[]{:S(2)}, u32[]{:S(2)}) collective-permute-start(s32[136,128]{1,0:T(8,128)S(1)} %get-tuple-element.28), channel_id=1, source_target_pairs={{0,8},{1,9},{2,18},{3,19},{4,12},{5,13},{6,22},{7,23},{8,0},{9,1},... | collective-permute-start | bytes 208904 | tf_op jit(solution)/shard_map/ppermute | solution.py:270
  8.8 0.2 collective-permute-start.3
  9.0 2.4 %collective-permute-done.1.both_ref = s32[136,128]{1,0:T(8,128)S(1)} collective-permute-done((s32[136,128]{1,0:T(8,128)S(1)}, s32[136,128]{1,0:T(8,128)S(1)}, u32[]{:S(2)}, u32[]{:S(2)}) %collective-permute-start.1) | collective-permute-done | bytes 69664 | tf_op jit(solution)/shard_map/ppermute | solution.py:270
  11.4 1.3 %collective-permute-done.2.z_ref = s32[136,128]{1,0:T(8,128)S(1)} collective-permute-done((s32[136,128]{1,0:T(8,128)S(1)}, s32[136,128]{1,0:T(8,128)S(1)}, u32[]{:S(2)}, u32[]{:S(2)}) %collective-permute-start.2) | collective-permute-done | bytes 69664 | tf_op jit(solution)/shard_map/ppermute | solution.py:270
  12.7 0.8 %collective-permute-done.3.x_ref = s32[136,128]{1,0:T(8,128)S(1)} collective-permute-done((s32[136,128]{1,0:T(8,128)S(1)}, s32[136,128]{1,0:T(8,128)S(1)}, u32[]{:S(2)}, u32[]{:S(2)}) %collective-permute-start.3) | collective-permute-done | bytes 69664 | tf_op jit(solution)/shard_map/ppermute | solution.py:270
  13.5 0.3 add_square.1
  13.8 2.7 %collective-permute-start.4 = (s32[136,128]{1,0:T(8,128)S(1)}, s32[136,128]{1,0:T(8,128)S(1)}, u32[]{:S(2)}, u32[]{:S(2)}) collective-permute-start(s32[136,128]{1,0:T(8,128)S(1)} %get-tuple-element.31), channel_id=1, source_target_pairs={{0,16},{1,17},{2,10},{3,11},{4,20},{5,21},{6,14},{7,15},{8,24},{9,... | collective-permute-start | bytes 208904 | tf_op jit(solution)/shard_map/ppermute | solution.py:270
  16.4 2.6 %collective-permute-done.4.word_ref = s32[136,128]{1,0:T(8,128)S(1)} collective-permute-done((s32[136,128]{1,0:T(8,128)S(1)}, s32[136,128]{1,0:T(8,128)S(1)}, u32[]{:S(2)}, u32[]{:S(2)}) %collective-permute-start.4) | collective-permute-done | bytes 69664 | tf_op jit(solution)/shard_map/ppermute | solution.py:270
  19.1 0.2 sketch_rows.1
  19.2 0.1 collective-permute-start.5
  19.3 1.3 %collective-permute-start.6 = (bf16[32,1152]{1,0:T(8,128)(2,1)S(1)}, bf16[32,1152]{1,0:T(8,128)(2,1)S(1)}, u32[]{:S(2)}, u32[]{:S(2)}) collective-permute-start(bf16[32,1152]{1,0:T(8,128)(2,1)S(1)} %get-tuple-element.34), channel_id=1, source_target_pairs={{0,4},{1,5},{2,3},{3,2},{4,0},{5,1},{6,7},{7,6},{8,12},{9,13},{10,... | collective-permute-start | bytes 221192 | tf_op jit(solution)/shard_map/ppermute | solution.py:270
  20.7 1.5 %collective-permute-start.7 = (bf16[32,1152]{1,0:T(8,128)(2,1)S(1)}, bf16[32,1152]{1,0:T(8,128)(2,1)S(1)}, u32[]{:S(2)}, u32[]{:S(2)}) collective-permute-start(bf16[32,1152]{1,0:T(8,128)(2,1)S(1)} %get-tuple-element.35), channel_id=1, source_target_pairs={{0,1},{1,0},{2,6},{3,7},{4,5},{5,4},{6,2},{7,3},{8,9},{9,8},{10,14... | collective-permute-start | bytes 221192 | tf_op jit(solution)/shard_map/ppermute | solution.py:270
  22.2 1.3 %collective-permute-start.11 = (bf16[32,1152]{1,0:T(8,128)(2,1)S(1)}, bf16[32,1152]{1,0:T(8,128)(2,1)S(1)}, u32[]{:S(2)}, u32[]{:S(2)}) collective-permute-start(bf16[32,1152]{1,0:T(8,128)(2,1)S(1)} %get-tuple-element.36), channel_id=1, source_target_pairs={{0,3},{1,2},{2,4},{3,5},{4,7},{5,6},{6,0},{7,1},{8,11},{9,10},{10,... | collective-permute-start | bytes 221192 | tf_op jit(solution)/shard_map/ppermute | solution.py:270
  23.5 1.3 %collective-permute-done.5.refs_1_ = bf16[32,1152]{1,0:T(8,128)(2,1)S(1)} collective-permute-done((bf16[32,1152]{1,0:T(8,128)(2,1)S(1)}, bf16[32,1152]{1,0:T(8,128)(2,1)S(1)}, u32[]{:S(2)}, u32[]{:S(2)}) %collective-permute-start.5) | collective-permute-done | bytes 73760 | tf_op jit(solution)/shard_map/ppermute | solution.py:270
  24.8 0.0 collective-permute-start.9
  24.8 0.0 collective-permute-done.6.refs_2_
  24.8 1.6 %collective-permute-start.10 = (bf16[32,1152]{1,0:T(8,128)(2,1)S(1)}, bf16[32,1152]{1,0:T(8,128)(2,1)S(1)}, u32[]{:S(2)}, u32[]{:S(2)}) collective-permute-start(bf16[32,1152]{1,0:T(8,128)(2,1)S(1)} %collective-permute-done.6.refs_2_), channel_id=1, source_target_pairs={{0,2},{1,3},{2,0},{3,1},{4,6},{5,7},{6,4},{7,5},{8,10},{9,11},{10,... | collective-permute-start | bytes 221192 | tf_op jit(solution)/shard_map/ppermute | solution.py:270
  26.4 0.9 %collective-permute-done.10.refs_6_ = bf16[32,1152]{1,0:T(8,128)(2,1)S(1)} collective-permute-done((bf16[32,1152]{1,0:T(8,128)(2,1)S(1)}, bf16[32,1152]{1,0:T(8,128)(2,1)S(1)}, u32[]{:S(2)}, u32[]{:S(2)}) %collective-permute-start.10) | collective-permute-done | bytes 73760 | tf_op jit(solution)/shard_map/ppermute | solution.py:270
  27.3 2.5 %gram.1 = f32[1024,1024]{1,0:T(8,128)} custom-call(bf16[32,1152]{1,0:T(8,128)(2,1)S(1)} %get-tuple-element.32.refs_0_, bf16[32,1152]{1,0:T(8,128)(2,1)S(1)} %collective-permute-done.5.refs_1_, bf16[32,1152]{1,0:T(8,128)(2,1)S(1)} %collective-permute-done.6.refs_2_, bf16[32,1152]{1,0:T(8,128)(2,1)S(1)} %collective-permute-done.7.refs_3_, ...), custom_call_target="tpu_custom_call" | custom-call | flops 536870912 | bytes 4194304 | tf_op jit(solution)/shard_map/gram/pallas_call | solution.py:166
  (8 shorter events, 0.0 us)
Async XLA Ops:
  0.0 19.1 %copy-start = (s32[128,1]{0,1:T(1,128)S(1)}, s32[128,1]{0,1:T(1,128)}, u32[]{:S(2)}) copy-start(s32[128,1]{0,1:T(1,128)} %param.7) | copy-start | bytes 1540
  2.6 1.8 %collective-permute-start = (f32[64,1024]{1,0:T(8,128)S(1)}, f32[64,1024]{1,0:T(8,128)S(1)}, u32[]{:S(2)}, u32[]{:S(2)}) collective-permute-start(f32[64,1024]{1,0:T(8,128)S(1)} %get-tuple-element.25), channel_id=1, source_target_pairs={{0,2},{1,3},{2,0},{3,1},{4,6},{5,7},{6,4},{7,5},{8,10},{9,11},{10,... | collective-permute-start | bytes 786440 | tf_op jit(solution)/shard_map/ppermute | solution.py:270
  4.5 6.8 %collective-permute-start.1 = (s32[136,128]{1,0:T(8,128)S(1)}, s32[136,128]{1,0:T(8,128)S(1)}, u32[]{:S(2)}, u32[]{:S(2)}) collective-permute-start(s32[136,128]{1,0:T(8,128)S(1)} %get-tuple-element.27), channel_id=1, source_target_pairs={{0,12},{1,13},{2,22},{3,23},{4,8},{5,9},{6,18},{7,19},{8,4},{9,5},... | collective-permute-start | bytes 208904 | tf_op jit(solution)/shard_map/ppermute | solution.py:270
  8.4 4.3 %collective-permute-start.2 = (s32[136,128]{1,0:T(8,128)S(1)}, s32[136,128]{1,0:T(8,128)S(1)}, u32[]{:S(2)}, u32[]{:S(2)}) collective-permute-start(s32[136,128]{1,0:T(8,128)S(1)} %get-tuple-element.28), channel_id=1, source_target_pairs={{0,8},{1,9},{2,18},{3,19},{4,12},{5,13},{6,22},{7,23},{8,0},{9,1},... | collective-permute-start | bytes 208904 | tf_op jit(solution)/shard_map/ppermute | solution.py:270
  8.8 4.7 %collective-permute-start.3 = (s32[136,128]{1,0:T(8,128)S(1)}, s32[136,128]{1,0:T(8,128)S(1)}, u32[]{:S(2)}, u32[]{:S(2)}) collective-permute-start(s32[136,128]{1,0:T(8,128)S(1)} %get-tuple-element.29), channel_id=1, source_target_pairs={{0,4},{1,5},{2,6},{3,7},{4,0},{5,1},{6,2},{7,3},{8,12},{9,13},{10,... | collective-permute-start | bytes 208904 | tf_op jit(solution)/shard_map/ppermute | solution.py:270
  13.8 5.3 %collective-permute-start.4 = (s32[136,128]{1,0:T(8,128)S(1)}, s32[136,128]{1,0:T(8,128)S(1)}, u32[]{:S(2)}, u32[]{:S(2)}) collective-permute-start(s32[136,128]{1,0:T(8,128)S(1)} %get-tuple-element.31), channel_id=1, source_target_pairs={{0,16},{1,17},{2,10},{3,11},{4,20},{5,21},{6,14},{7,15},{8,24},{9,... | collective-permute-start | bytes 208904 | tf_op jit(solution)/shard_map/ppermute | solution.py:270
  19.2 5.5 %collective-permute-start.5 = (bf16[32,1152]{1,0:T(8,128)(2,1)S(1)}, bf16[32,1152]{1,0:T(8,128)(2,1)S(1)}, u32[]{:S(2)}, u32[]{:S(2)}) collective-permute-start(bf16[32,1152]{1,0:T(8,128)(2,1)S(1)} %get-tuple-element.33), channel_id=1, source_target_pairs={{0,7},{1,6},{2,5},{3,4},{4,3},{5,2},{6,1},{7,0},{8,15},{9,14},{10,... | collective-permute-start | bytes 221192 | tf_op jit(solution)/shard_map/ppermute | solution.py:270
  19.3 5.5 %collective-permute-start.6 = (bf16[32,1152]{1,0:T(8,128)(2,1)S(1)}, bf16[32,1152]{1,0:T(8,128)(2,1)S(1)}, u32[]{:S(2)}, u32[]{:S(2)}) collective-permute-start(bf16[32,1152]{1,0:T(8,128)(2,1)S(1)} %get-tuple-element.34), channel_id=1, source_target_pairs={{0,4},{1,5},{2,3},{3,2},{4,0},{5,1},{6,7},{7,6},{8,12},{9,13},{10,... | collective-permute-start | bytes 221192 | tf_op jit(solution)/shard_map/ppermute | solution.py:270
  20.7 5.7 %collective-permute-start.7 = (bf16[32,1152]{1,0:T(8,128)(2,1)S(1)}, bf16[32,1152]{1,0:T(8,128)(2,1)S(1)}, u32[]{:S(2)}, u32[]{:S(2)}) collective-permute-start(bf16[32,1152]{1,0:T(8,128)(2,1)S(1)} %get-tuple-element.35), channel_id=1, source_target_pairs={{0,1},{1,0},{2,6},{3,7},{4,5},{5,4},{6,2},{7,3},{8,9},{9,8},{10,14... | collective-permute-start | bytes 221192 | tf_op jit(solution)/shard_map/ppermute | solution.py:270
  22.2 4.2 %collective-permute-start.11 = (bf16[32,1152]{1,0:T(8,128)(2,1)S(1)}, bf16[32,1152]{1,0:T(8,128)(2,1)S(1)}, u32[]{:S(2)}, u32[]{:S(2)}) collective-permute-start(bf16[32,1152]{1,0:T(8,128)(2,1)S(1)} %get-tuple-element.36), channel_id=1, source_target_pairs={{0,3},{1,2},{2,4},{3,5},{4,7},{5,6},{6,0},{7,1},{8,11},{9,10},{10,... | collective-permute-start | bytes 221192 | tf_op jit(solution)/shard_map/ppermute | solution.py:270
  23.5 2.9 %collective-permute-start.8 = (bf16[32,1152]{1,0:T(8,128)(2,1)S(1)}, bf16[32,1152]{1,0:T(8,128)(2,1)S(1)}, u32[]{:S(2)}, u32[]{:S(2)}) collective-permute-start(bf16[32,1152]{1,0:T(8,128)(2,1)S(1)} %get-tuple-element.32.refs_0_), channel_id=1, source_target_pairs={{0,2},{1,3},{2,0},{3,1},{4,6},{5,7},{6,4},{7,5},{8,10},{9,11},{10,... | collective-permute-start | bytes 221192 | tf_op jit(solution)/shard_map/ppermute | solution.py:270
  24.8 1.6 %collective-permute-start.9 = (bf16[32,1152]{1,0:T(8,128)(2,1)S(1)}, bf16[32,1152]{1,0:T(8,128)(2,1)S(1)}, u32[]{:S(2)}, u32[]{:S(2)}) collective-permute-start(bf16[32,1152]{1,0:T(8,128)(2,1)S(1)} %collective-permute-done.5.refs_1_), channel_id=1, source_target_pairs={{0,2},{1,3},{2,0},{3,1},{4,6},{5,7},{6,4},{7,5},{8,10},{9,11},{10,... | collective-permute-start | bytes 221192 | tf_op jit(solution)/shard_map/ppermute | solution.py:270
  24.8 2.5 %collective-permute-start.10 = (bf16[32,1152]{1,0:T(8,128)(2,1)S(1)}, bf16[32,1152]{1,0:T(8,128)(2,1)S(1)}, u32[]{:S(2)}, u32[]{:S(2)}) collective-permute-start(bf16[32,1152]{1,0:T(8,128)(2,1)S(1)} %collective-permute-done.6.refs_2_), channel_id=1, source_target_pairs={{0,2},{1,3},{2,0},{3,1},{4,6},{5,7},{6,4},{7,5},{8,10},{9,11},{10,... | collective-permute-start | bytes 221192 | tf_op jit(solution)/shard_map/ppermute | solution.py:270

commit v25 on v22

--- a/solution.py
+++ b/solution.py
@@ -11,6 +11,7 @@
 C = 32
 LOW = 256
 LANES = 128
+TILE = 16
 VMEM_LIMIT = 48 * 1024 * 1024
 
 
@@ -130,19 +131,31 @@
     return keep, got
 
 
-def gram_kernel(shard, group, factor, *refs):
+def gram_kernel(shard, group, factor, size, *refs):
     pieces, (out_hbm, rows, blocks, sems) = refs[:-4], refs[-4:]
     steps, wide, kept = blocks.shape
+    stride = kept // LANES * size + TILE
+    lane = lax.broadcasted_iota(jnp.int32, (8, LANES), 1)
     place = 0
+    names = []
     for piece in pieces:
-        rows[place:place + piece.shape[0]] = piece[:, :kept]
-        place += piece.shape[0]
+        for start in range(0, piece.shape[0], stride):
+            for column in range(kept // LANES):
+                at = start + column * size
+                rows[place:place + size, column * LANES:(column + 1) * LANES] = piece[at:at + size]
+            named = piece[start + stride - TILE:start + stride].astype(jnp.float32)[:8]
+            shift = place % LANES
+            if shift == 0:
+                names.append(named)
+            else:
+                names[-1] = jnp.where(lane // size == shift // size, pltpu.roll(named, shift, 1), names[-1])
+            place += size
+    named = jnp.concatenate(names, axis=1)[:1, :place]
     first = lax.axis_index("feat") * shard
     start = pl.multiple_of(first // LANES * LANES, LANES)
     window = rows[:, pl.ds(start, LANES)].astype(jnp.float32) * factor
     window = pltpu.roll(window, lax.rem(LANES - (first - start), LANES), 1)
     own = jnp.concatenate([window.T[:shard]] * group, axis=0)
-    named = jnp.concatenate([piece[:, kept:].astype(jnp.float32) for piece in pieces], axis=0).T[:1]
     label = named.astype(jnp.int32) - lax.broadcasted_iota(jnp.int32, own.shape, 0) // shard
     base = lax.axis_index("tok") * steps * group
     copies = []
@@ -157,14 +170,13 @@
         copy.wait()
 
 
-def gram_blocks(pieces, concepts, shard, factor):
-    tokens = sum(piece.shape[0] for piece in pieces)
-    kept = pieces[0].shape[1] - LANES
+def gram_blocks(pieces, size, kept, concepts, shard, factor):
+    tokens = sum(piece.shape[0] for piece in pieces) // (kept // LANES * size + TILE) * size
     group = max(1, min(concepts, LOW // shard))
     wide = group * shard
     steps = concepts // group
     return pl.pallas_call(
-        functools.partial(gram_kernel, shard, group, factor),
+        functools.partial(gram_kernel, shard, group, factor, size),
         in_specs=[pl.BlockSpec(memory_space=pltpu.VMEM)] * len(pieces),
         out_specs=pl.BlockSpec(memory_space=pltpu.HBM),
         out_shape=jax.ShapeDtypeStruct((concepts * shard, kept), jnp.float32),
@@ -244,10 +256,11 @@
     first = lax.rem(me, 2) * 2 * size + lax.rem(me // 2, 2) * size
     label = jnp.broadcast_to(label_ref[...].astype(jnp.float32), (8, LANES))
     label = pltpu.roll(label, lax.rem(LANES - first, LANES), 1)
-    label = jnp.broadcast_to(label[:1], (LANES, LANES)).T[:size].astype(jnp.bfloat16)
+    label = jnp.broadcast_to(label[:1], (TILE, LANES)).astype(jnp.bfloat16)
     for row_ref in row_refs:
-        row_ref[:, :kept] = row
-        row_ref[:, kept:] = label
+        for column in range(kept // LANES):
+            row_ref[column * size:(column + 1) * size] = row[:, column * LANES:(column + 1) * LANES]
+        row_ref[kept // LANES * size:] = label
 
 
 def local_call(kernel, name, *operands, out_shape):
@@ -279,7 +292,7 @@
     size = rows // 4
     total_type = jax.ShapeDtypeStruct((size, kept), jnp.float32)
     word_type = jax.ShapeDtypeStruct((kept // LANES * (size // 2) + 8, LANES), jnp.int32)
-    row_type = jax.ShapeDtypeStruct((size, kept + LANES), jnp.bfloat16)
+    row_type = jax.ShapeDtypeStruct((kept // LANES * size + TILE, LANES), jnp.bfloat16)
 
     keep, got = partial_halves(features, signs, columns, feat_count)
     total, there, here, again = local_call(
@@ -322,7 +335,7 @@
     crossed = swap(copies[3], (1, 1), (0, 3))
     pieces = [own, far, second, third] + [swap(block, (0, 1)) for block in (own, far, second)] + [crossed]
     concepts = C // tok_count
-    gram = gram_blocks(pieces, concepts, shard, C / (rows * tok_count))
+    gram = gram_blocks(pieces, size, kept, concepts, shard, C / (rows * tok_count))
     return gram.reshape(concepts, shard, kept)
 
 

time: 29.4 us -> 29.3 us (level)
  no operation moved by 1% of the time
where the time goes in v25:
time: 29.3 us; the launch traced here: 29.2 us
  starting transfers between devices  13.3 us (45%)
  waiting for transfers between devices  8.86 us (30%)
  Pallas kernels  7 us (24%)
    ppermute x12, starting transfers between devices, swap(): return lax.ppermute(array, ('feat', 'tok'), pairs)  13.3 us
    ppermute x12, waiting for transfers between devices, swap(): return lax.ppermute(array, ('feat', 'tok'), pairs)  8.86 us
    pallas_call x1, Pallas kernels, partial_halves(): pl.pallas_call(functools.partial(send_kernel, total_bits, parts), in_spec...  2.58 us
    pallas_call x1, Pallas kernels, gram_blocks(): pl.pallas_call(functools.partial(gram_kernel, shard, group, factor, size)...  2.55 us
    pallas_call x1, Pallas kernels, partial_halves(): pl.pallas_call(functools.partial(keep_kernel, parts), out_shape=total_typ...  1.26 us
    pallas_call x3, Pallas kernels, local_call(): pl.pallas_call(kernel, out_shape=out_shape, compiler_params=pltpu.Compile...  0.61 us
  transfers between devices with their start and end apart: 12, of which 7 were waited for; matrix products, arithmetic and copies ran while one was open for 0% of the time, Pallas kernels for 4%

profile of v25, /device:TPU:0, one launch (start us, length us, event | category | flops | bytes accessed | tf_op | source)
XLA Modules:
  0.0 29.2 jit_solution(4680332440292988366)
XLA Ops:
  0.0 2.6 %partial_sent.1 = (f32[64,1024]{1,0:T(8,128)S(1)}, bf16[64,8192]{1,0:T(8,128)(2,1)S(1)}, s32[1,8192]{1,0:T(1,128)S(1)}, bf16[256,1024]{1,0:T(8,128)(2,1)S(1)}, f32[32,1024]{1,0:T(8,128)S(1)}) custom-call(bf16[128,8192]{1,0:T(8,128)(2,1)} %x_hbm.1, s32[1,8192]{1,0:T(1,128)} %bitcast.5, s32[1,1024]{1,0:T(1,128)} %bitcast.6), custom_call_target="tpu_custom_call" | custom-call | flops 1073741824 | bytes 2359296 | tf_op jit(solution)/shard_map/partial_sent/pallas_call | solution.py:100
  2.6 0.5 %collective-permute-start = (f32[64,1024]{1,0:T(8,128)S(1)}, f32[64,1024]{1,0:T(8,128)S(1)}, u32[]{:S(2)}, u32[]{:S(2)}) collective-permute-start(f32[64,1024]{1,0:T(8,128)S(1)} %get-tuple-element.25), channel_id=1, source_target_pairs={{0,2},{1,3},{2,0},{3,1},{4,6},{5,7},{6,4},{7,5},{8,10},{9,11},{10,... | collective-permute-start | bytes 786440 | tf_op jit(solution)/shard_map/ppermute | solution.py:283
  3.1 1.3 %partial_kept.1.keep_ref = f32[64,1024]{1,0:T(8,128)S(1)} custom-call(bf16[64,8192]{1,0:T(8,128)(2,1)S(1)} %get-tuple-element.21.x_keep, s32[1,8192]{1,0:T(1,128)S(1)} %get-tuple-element.22.signs, bf16[256,1024]{1,0:T(8,128)(2,1)S(1)} %get-tuple-element.23.low, f32[32,1024]{1,0:T(8,128)S(1)} %get-tuple-element.24.high), custom_call_target="tpu_custom_call" | custom-call | flops 1073741824 | bytes 2359296 | tf_op jit(solution)/shard_map/partial_kept/pallas_call | solution.py:124
  4.4 0.0 collective-permute-done.got_ref
  4.4 0.2 first_split.1
  4.5 4.8 %collective-permute-start.1 = (s32[136,128]{1,0:T(8,128)S(1)}, s32[136,128]{1,0:T(8,128)S(1)}, u32[]{:S(2)}, u32[]{:S(2)}) collective-permute-start(s32[136,128]{1,0:T(8,128)S(1)} %get-tuple-element.27), channel_id=1, source_target_pairs={{0,20},{1,21},{2,14},{3,15},{4,16},{5,17},{6,10},{7,11},{8,28},{9,... | collective-permute-start | bytes 208904 | tf_op jit(solution)/shard_map/ppermute | solution.py:283
  9.4 0.3 %collective-permute-start.2 = (s32[136,128]{1,0:T(8,128)S(1)}, s32[136,128]{1,0:T(8,128)S(1)}, u32[]{:S(2)}, u32[]{:S(2)}) collective-permute-start(s32[136,128]{1,0:T(8,128)S(1)} %get-tuple-element.28), channel_id=1, source_target_pairs={{0,16},{1,17},{2,10},{3,11},{4,20},{5,21},{6,14},{7,15},{8,24},{9,... | collective-permute-start | bytes 208904 | tf_op jit(solution)/shard_map/ppermute | solution.py:283
  9.7 0.3 %collective-permute-start.3 = (s32[136,128]{1,0:T(8,128)S(1)}, s32[136,128]{1,0:T(8,128)S(1)}, u32[]{:S(2)}, u32[]{:S(2)}) collective-permute-start(s32[136,128]{1,0:T(8,128)S(1)} %get-tuple-element.29), channel_id=1, source_target_pairs={{0,4},{1,5},{2,6},{3,7},{4,0},{5,1},{6,2},{7,3},{8,12},{9,13},{10,... | collective-permute-start | bytes 208904 | tf_op jit(solution)/shard_map/ppermute | solution.py:283
  10.0 1.7 %collective-permute-done.1.both_ref = s32[136,128]{1,0:T(8,128)S(1)} collective-permute-done((s32[136,128]{1,0:T(8,128)S(1)}, s32[136,128]{1,0:T(8,128)S(1)}, u32[]{:S(2)}, u32[]{:S(2)}) %collective-permute-start.1) | collective-permute-done | bytes 69664 | tf_op jit(solution)/shard_map/ppermute | solution.py:283
  11.7 2.8 %collective-permute-done.2.z_ref = s32[136,128]{1,0:T(8,128)S(1)} collective-permute-done((s32[136,128]{1,0:T(8,128)S(1)}, s32[136,128]{1,0:T(8,128)S(1)}, u32[]{:S(2)}, u32[]{:S(2)}) %collective-permute-start.2) | collective-permute-done | bytes 69664 | tf_op jit(solution)/shard_map/ppermute | solution.py:283
  14.6 0.3 add_square.1
  14.9 1.6 %collective-permute-start.4 = (s32[136,128]{1,0:T(8,128)S(1)}, s32[136,128]{1,0:T(8,128)S(1)}, u32[]{:S(2)}, u32[]{:S(2)}) collective-permute-start(s32[136,128]{1,0:T(8,128)S(1)} %get-tuple-element.31), channel_id=1, source_target_pairs={{0,8},{1,9},{2,18},{3,19},{4,12},{5,13},{6,22},{7,23},{8,0},{9,1},... | collective-permute-start | bytes 208904 | tf_op jit(solution)/shard_map/ppermute | solution.py:283
  16.5 2.7 %collective-permute-done.4.word_ref = s32[136,128]{1,0:T(8,128)S(1)} collective-permute-done((s32[136,128]{1,0:T(8,128)S(1)}, s32[136,128]{1,0:T(8,128)S(1)}, u32[]{:S(2)}, u32[]{:S(2)}) %collective-permute-start.4) | collective-permute-done | bytes 69664 | tf_op jit(solution)/shard_map/ppermute | solution.py:283
  19.2 0.2 sketch_rows.1
  19.4 0.1 collective-permute-start.5
  19.5 0.6 %collective-permute-start.6 = (bf16[272,128]{1,0:T(8,128)(2,1)S(1)}, bf16[272,128]{1,0:T(8,128)(2,1)S(1)}, u32[]{:S(2)}, u32[]{:S(2)}) collective-permute-start(bf16[272,128]{1,0:T(8,128)(2,1)S(1)} %get-tuple-element.34), channel_id=1, source_target_pairs={{0,4},{1,5},{2,3},{3,2},{4,0},{5,1},{6,7},{7,6},{8,12},{9,13},{10,... | collective-permute-start | bytes 208904 | tf_op jit(solution)/shard_map/ppermute | solution.py:283
  20.1 1.5 %collective-permute-start.7 = (bf16[272,128]{1,0:T(8,128)(2,1)S(1)}, bf16[272,128]{1,0:T(8,128)(2,1)S(1)}, u32[]{:S(2)}, u32[]{:S(2)}) collective-permute-start(bf16[272,128]{1,0:T(8,128)(2,1)S(1)} %get-tuple-element.35), channel_id=1, source_target_pairs={{0,1},{1,0},{2,6},{3,7},{4,5},{5,4},{6,2},{7,3},{8,9},{9,8},{10,14... | collective-permute-start | bytes 208904 | tf_op jit(solution)/shard_map/ppermute | solution.py:283
  21.6 2.0 %collective-permute-start.11 = (bf16[272,128]{1,0:T(8,128)(2,1)S(1)}, bf16[272,128]{1,0:T(8,128)(2,1)S(1)}, u32[]{:S(2)}, u32[]{:S(2)}) collective-permute-start(bf16[272,128]{1,0:T(8,128)(2,1)S(1)} %get-tuple-element.36), channel_id=1, source_target_pairs={{0,3},{1,2},{2,4},{3,5},{4,7},{5,6},{6,0},{7,1},{8,11},{9,10},{10,... | collective-permute-start | bytes 208904 | tf_op jit(solution)/shard_map/ppermute | solution.py:283
  23.6 0.5 %collective-permute-done.5.refs_1_ = bf16[272,128]{1,0:T(8,128)(2,1)S(1)} collective-permute-done((bf16[272,128]{1,0:T(8,128)(2,1)S(1)}, bf16[272,128]{1,0:T(8,128)(2,1)S(1)}, u32[]{:S(2)}, u32[]{:S(2)}) %collective-permute-start.5) | collective-permute-done | bytes 69664 | tf_op jit(solution)/shard_map/ppermute | solution.py:283
  24.2 0.1 collective-permute-done.6.refs_2_
  24.3 1.4 %collective-permute-start.10 = (bf16[272,128]{1,0:T(8,128)(2,1)S(1)}, bf16[272,128]{1,0:T(8,128)(2,1)S(1)}, u32[]{:S(2)}, u32[]{:S(2)}) collective-permute-start(bf16[272,128]{1,0:T(8,128)(2,1)S(1)} %collective-permute-done.6.refs_2_), channel_id=1, source_target_pairs={{0,2},{1,3},{2,0},{3,1},{4,6},{5,7},{6,4},{7,5},{8,10},{9,11},{10,... | collective-permute-start | bytes 208904 | tf_op jit(solution)/shard_map/ppermute | solution.py:283
  25.7 0.4 %collective-permute-done.11.refs_7_ = bf16[272,128]{1,0:T(8,128)(2,1)S(1)} collective-permute-done((bf16[272,128]{1,0:T(8,128)(2,1)S(1)}, bf16[272,128]{1,0:T(8,128)(2,1)S(1)}, u32[]{:S(2)}, u32[]{:S(2)}) %collective-permute-start.11) | collective-permute-done | bytes 69664 | tf_op jit(solution)/shard_map/ppermute | solution.py:283
  26.1 0.5 %collective-permute-done.10.refs_6_ = bf16[272,128]{1,0:T(8,128)(2,1)S(1)} collective-permute-done((bf16[272,128]{1,0:T(8,128)(2,1)S(1)}, bf16[272,128]{1,0:T(8,128)(2,1)S(1)}, u32[]{:S(2)}, u32[]{:S(2)}) %collective-permute-start.10) | collective-permute-done | bytes 69664 | tf_op jit(solution)/shard_map/ppermute | solution.py:283
  26.6 2.6 %gram.1 = f32[1024,1024]{1,0:T(8,128)} custom-call(bf16[272,128]{1,0:T(8,128)(2,1)S(1)} %get-tuple-element.32.refs_0_, bf16[272,128]{1,0:T(8,128)(2,1)S(1)} %collective-permute-done.5.refs_1_, bf16[272,128]{1,0:T(8,128)(2,1)S(1)} %collective-permute-done.6.refs_2_, bf16[272,128]{1,0:T(8,128)(2,1)S(1)} %collective-permute-done.7.refs_3_, ...), custom_call_target="tpu_custom_call" | custom-call | flops 536870912 | bytes 4194304 | tf_op jit(solution)/shard_map/gram/pallas_call | solution.py:178
  (8 shorter events, 0.0 us)
Async XLA Ops:
  0.0 19.2 %copy-start = (s32[128,1]{0,1:T(1,128)S(1)}, s32[128,1]{0,1:T(1,128)}, u32[]{:S(2)}) copy-start(s32[128,1]{0,1:T(1,128)} %param.7) | copy-start | bytes 1540
  2.6 1.8 %collective-permute-start = (f32[64,1024]{1,0:T(8,128)S(1)}, f32[64,1024]{1,0:T(8,128)S(1)}, u32[]{:S(2)}, u32[]{:S(2)}) collective-permute-start(f32[64,1024]{1,0:T(8,128)S(1)} %get-tuple-element.25), channel_id=1, source_target_pairs={{0,2},{1,3},{2,0},{3,1},{4,6},{5,7},{6,4},{7,5},{8,10},{9,11},{10,... | collective-permute-start | bytes 786440 | tf_op jit(solution)/shard_map/ppermute | solution.py:283
  4.5 7.2 %collective-permute-start.1 = (s32[136,128]{1,0:T(8,128)S(1)}, s32[136,128]{1,0:T(8,128)S(1)}, u32[]{:S(2)}, u32[]{:S(2)}) collective-permute-start(s32[136,128]{1,0:T(8,128)S(1)} %get-tuple-element.27), channel_id=1, source_target_pairs={{0,20},{1,21},{2,14},{3,15},{4,16},{5,17},{6,10},{7,11},{8,28},{9,... | collective-permute-start | bytes 208904 | tf_op jit(solution)/shard_map/ppermute | solution.py:283
  9.4 5.2 %collective-permute-start.2 = (s32[136,128]{1,0:T(8,128)S(1)}, s32[136,128]{1,0:T(8,128)S(1)}, u32[]{:S(2)}, u32[]{:S(2)}) collective-permute-start(s32[136,128]{1,0:T(8,128)S(1)} %get-tuple-element.28), channel_id=1, source_target_pairs={{0,16},{1,17},{2,10},{3,11},{4,20},{5,21},{6,14},{7,15},{8,24},{9,... | collective-permute-start | bytes 208904 | tf_op jit(solution)/shard_map/ppermute | solution.py:283
  9.7 4.9 %collective-permute-start.3 = (s32[136,128]{1,0:T(8,128)S(1)}, s32[136,128]{1,0:T(8,128)S(1)}, u32[]{:S(2)}, u32[]{:S(2)}) collective-permute-start(s32[136,128]{1,0:T(8,128)S(1)} %get-tuple-element.29), channel_id=1, source_target_pairs={{0,4},{1,5},{2,6},{3,7},{4,0},{5,1},{6,2},{7,3},{8,12},{9,13},{10,... | collective-permute-start | bytes 208904 | tf_op jit(solution)/shard_map/ppermute | solution.py:283
  14.9 4.4 %collective-permute-start.4 = (s32[136,128]{1,0:T(8,128)S(1)}, s32[136,128]{1,0:T(8,128)S(1)}, u32[]{:S(2)}, u32[]{:S(2)}) collective-permute-start(s32[136,128]{1,0:T(8,128)S(1)} %get-tuple-element.31), channel_id=1, source_target_pairs={{0,8},{1,9},{2,18},{3,19},{4,12},{5,13},{6,22},{7,23},{8,0},{9,1},... | collective-permute-start | bytes 208904 | tf_op jit(solution)/shard_map/ppermute | solution.py:283
  19.4 4.8 %collective-permute-start.5 = (bf16[272,128]{1,0:T(8,128)(2,1)S(1)}, bf16[272,128]{1,0:T(8,128)(2,1)S(1)}, u32[]{:S(2)}, u32[]{:S(2)}) collective-permute-start(bf16[272,128]{1,0:T(8,128)(2,1)S(1)} %get-tuple-element.33), channel_id=1, source_target_pairs={{0,7},{1,6},{2,5},{3,4},{4,3},{5,2},{6,1},{7,0},{8,15},{9,14},{10,... | collective-permute-start | bytes 208904 | tf_op jit(solution)/shard_map/ppermute | solution.py:283
  19.5 4.8 %collective-permute-start.6 = (bf16[272,128]{1,0:T(8,128)(2,1)S(1)}, bf16[272,128]{1,0:T(8,128)(2,1)S(1)}, u32[]{:S(2)}, u32[]{:S(2)}) collective-permute-start(bf16[272,128]{1,0:T(8,128)(2,1)S(1)} %get-tuple-element.34), channel_id=1, source_target_pairs={{0,4},{1,5},{2,3},{3,2},{4,0},{5,1},{6,7},{7,6},{8,12},{9,13},{10,... | collective-permute-start | bytes 208904 | tf_op jit(solution)/shard_map/ppermute | solution.py:283
  20.1 5.6 %collective-permute-start.7 = (bf16[272,128]{1,0:T(8,128)(2,1)S(1)}, bf16[272,128]{1,0:T(8,128)(2,1)S(1)}, u32[]{:S(2)}, u32[]{:S(2)}) collective-permute-start(bf16[272,128]{1,0:T(8,128)(2,1)S(1)} %get-tuple-element.35), channel_id=1, source_target_pairs={{0,1},{1,0},{2,6},{3,7},{4,5},{5,4},{6,2},{7,3},{8,9},{9,8},{10,14... | collective-permute-start | bytes 208904 | tf_op jit(solution)/shard_map/ppermute | solution.py:283
  21.6 4.5 %collective-permute-start.11 = (bf16[272,128]{1,0:T(8,128)(2,1)S(1)}, bf16[272,128]{1,0:T(8,128)(2,1)S(1)}, u32[]{:S(2)}, u32[]{:S(2)}) collective-permute-start(bf16[272,128]{1,0:T(8,128)(2,1)S(1)} %get-tuple-element.36), channel_id=1, source_target_pairs={{0,3},{1,2},{2,4},{3,5},{4,7},{5,6},{6,0},{7,1},{8,11},{9,10},{10,... | collective-permute-start | bytes 208904 | tf_op jit(solution)/shard_map/ppermute | solution.py:283
  23.6 2.5 %collective-permute-start.8 = (bf16[272,128]{1,0:T(8,128)(2,1)S(1)}, bf16[272,128]{1,0:T(8,128)(2,1)S(1)}, u32[]{:S(2)}, u32[]{:S(2)}) collective-permute-start(bf16[272,128]{1,0:T(8,128)(2,1)S(1)} %get-tuple-element.32.refs_0_), channel_id=1, source_target_pairs={{0,2},{1,3},{2,0},{3,1},{4,6},{5,7},{6,4},{7,5},{8,10},{9,11},{10,... | collective-permute-start | bytes 208904 | tf_op jit(solution)/shard_map/ppermute | solution.py:283
  24.2 1.9 %collective-permute-start.9 = (bf16[272,128]{1,0:T(8,128)(2,1)S(1)}, bf16[272,128]{1,0:T(8,128)(2,1)S(1)}, u32[]{:S(2)}, u32[]{:S(2)}) collective-permute-start(bf16[272,128]{1,0:T(8,128)(2,1)S(1)} %collective-permute-done.5.refs_1_), channel_id=1, source_target_pairs={{0,2},{1,3},{2,0},{3,1},{4,6},{5,7},{6,4},{7,5},{8,10},{9,11},{10,... | collective-permute-start | bytes 208904 | tf_op jit(solution)/shard_map/ppermute | solution.py:283
  24.3 2.3 %collective-permute-start.10 = (bf16[272,128]{1,0:T(8,128)(2,1)S(1)}, bf16[272,128]{1,0:T(8,128)(2,1)S(1)}, u32[]{:S(2)}, u32[]{:S(2)}) collective-permute-start(bf16[272,128]{1,0:T(8,128)(2,1)S(1)} %collective-permute-done.6.refs_2_), channel_id=1, source_target_pairs={{0,2},{1,3},{2,0},{3,1},{4,6},{5,7},{6,4},{7,5},{8,10},{9,11},{10,... | collective-permute-start | bytes 208904 | tf_op jit(solution)/shard_map/ppermute | solution.py:283

commit v26 on v25

--- a/solution.py
+++ b/solution.py
@@ -53,14 +53,13 @@
     mine = lax.rem(me, 2)
     col_copy = pltpu.make_async_copy(col_hbm, col_buf, sems.at[parts])
     sign_copy = pltpu.make_async_copy(s_hbm, signs, sems.at[parts + 1])
-    col_copy.start()
-    sign_copy.start()
     copies = []
     for part in range(parts):
         cols = pl.ds(part * wide, wide)
         rows = pl.ds(pl.multiple_of((1 - mine) * half, half), half)
         copies.append(pltpu.make_async_copy(x_hbm.at[rows, cols], x_buf.at[:, cols], sems.at[part]))
-        copies[-1].start()
+    for copy in (copies[0], col_copy, sign_copy, *copies[1:]):
+        copy.start()
     rows = pl.ds(pl.multiple_of(mine * half, half), half)
     keep_copy = pltpu.make_async_copy(x_hbm.at[rows, :], x_keep, sems.at[parts + 2])
     keep_copy.start()
@@ -236,9 +235,13 @@
     encode(total, here_ref)
 
 
-def square_kernel(total_ref, both_ref, z_ref, x_ref, sum_ref, out_ref):
+def far_kernel(total_ref, far_ref, sum_ref):
+    sum_ref[...] = total_ref[...] + decode(far_ref, total_ref.shape[0])
+
+
+def square_kernel(total_ref, z_ref, x_ref, sum_ref, out_ref):
     size = total_ref.shape[0]
-    total = (total_ref[...] + decode(x_ref, size)) + (decode(z_ref, size) + decode(both_ref, size))
+    total = total_ref[...] + (decode(z_ref, size) + decode(x_ref, size))
     sum_ref[...] = total
     encode(total, out_ref)
 
@@ -305,8 +308,9 @@
     both = swap(again, (0, 10), (0, 6))
     z_word = swap(here, (0, 8), (0, 4))
     x_word = swap(there, (0, 2))
+    total = local_call(far_kernel, "add_far", total, both, out_shape=total_type)
     total, word = local_call(
-        square_kernel, "add_square", total, both, z_word, x_word, out_shape=[total_type, word_type]
+        square_kernel, "add_square", total, z_word, x_word, out_shape=[total_type, word_type]
     )
     word = swap(word, (0, 4), (0, 8))
     stride = 16

time: 29.3 us -> 29.3 us (level)
    pallas_call x3 -> x4, Pallas kernels: 0.61 us -> 0.77 us  [local_call(): pl.pallas_call(kernel, out_shape=out_shape, compiler_params=pltpu.Compile...]
  transfers between devices with their start and end apart: 12 -> 12, of which waited for: 7 -> 7; matrix products, arithmetic and copies ran while one was open for 0% -> 0% of each run, Pallas kernels for 4% -> 5%
where the time goes in v26:
time: 29.3 us; the launch traced here: 29.2 us
  starting transfers between devices  13.3 us (45%)
  waiting for transfers between devices  8.7 us (30%)
  Pallas kernels  7.12 us (24%)
    ppermute x12, starting transfers between devices, swap(): return lax.ppermute(array, ('feat', 'tok'), pairs)  13.3 us
    ppermute x12, waiting for transfers between devices, swap(): return lax.ppermute(array, ('feat', 'tok'), pairs)  8.7 us
    pallas_call x1, Pallas kernels, gram_blocks(): pl.pallas_call(functools.partial(gram_kernel, shard, group, factor, size)...  2.55 us
    pallas_call x1, Pallas kernels, partial_halves(): pl.pallas_call(functools.partial(send_kernel, total_bits, parts), in_spec...  2.54 us
    pallas_call x1, Pallas kernels, partial_halves(): pl.pallas_call(functools.partial(keep_kernel, parts), out_shape=total_typ...  1.26 us
    pallas_call x4, Pallas kernels, local_call(): pl.pallas_call(kernel, out_shape=out_shape, compiler_params=pltpu.Compile...  0.77 us
  transfers between devices with their start and end apart: 12, of which 7 were waited for; matrix products, arithmetic and copies ran while one was open for 0% of the time, Pallas kernels for 5%

profile of v26, /device:TPU:0, one launch (start us, length us, event | category | flops | bytes accessed | tf_op | source)
XLA Modules:
  0.0 29.2 jit_solution(16468204880402502267)
XLA Ops:
  0.0 2.5 %partial_sent.1 = (f32[64,1024]{1,0:T(8,128)S(1)}, bf16[64,8192]{1,0:T(8,128)(2,1)S(1)}, s32[1,8192]{1,0:T(1,128)S(1)}, bf16[256,1024]{1,0:T(8,128)(2,1)S(1)}, f32[32,1024]{1,0:T(8,128)S(1)}) custom-call(bf16[128,8192]{1,0:T(8,128)(2,1)} %x_hbm.1, s32[1,8192]{1,0:T(1,128)} %bitcast.5, s32[1,1024]{1,0:T(1,128)} %bitcast.6), custom_call_target="tpu_custom_call" | custom-call | flops 1073741824 | bytes 2359296 | tf_op jit(solution)/shard_map/partial_sent/pallas_call | solution.py:99
  2.5 0.5 %collective-permute-start = (f32[64,1024]{1,0:T(8,128)S(1)}, f32[64,1024]{1,0:T(8,128)S(1)}, u32[]{:S(2)}, u32[]{:S(2)}) collective-permute-start(f32[64,1024]{1,0:T(8,128)S(1)} %get-tuple-element.25), channel_id=1, source_target_pairs={{0,2},{1,3},{2,0},{3,1},{4,6},{5,7},{6,4},{7,5},{8,10},{9,11},{10,... | collective-permute-start | bytes 786440 | tf_op jit(solution)/shard_map/ppermute | solution.py:286
  3.1 1.3 %partial_kept.1.keep_ref = f32[64,1024]{1,0:T(8,128)S(1)} custom-call(bf16[64,8192]{1,0:T(8,128)(2,1)S(1)} %get-tuple-element.21.x_keep, s32[1,8192]{1,0:T(1,128)S(1)} %get-tuple-element.22.signs, bf16[256,1024]{1,0:T(8,128)(2,1)S(1)} %get-tuple-element.23.low, f32[32,1024]{1,0:T(8,128)S(1)} %get-tuple-element.24.high), custom_call_target="tpu_custom_call" | custom-call | flops 1073741824 | bytes 2359296 | tf_op jit(solution)/shard_map/partial_kept/pallas_call | solution.py:123
  4.3 0.2 first_split.1
  4.5 4.8 %collective-permute-start.1 = (s32[136,128]{1,0:T(8,128)S(1)}, s32[136,128]{1,0:T(8,128)S(1)}, u32[]{:S(2)}, u32[]{:S(2)}) collective-permute-start(s32[136,128]{1,0:T(8,128)S(1)} %get-tuple-element.27), channel_id=1, source_target_pairs={{0,20},{1,21},{2,14},{3,15},{4,16},{5,17},{6,10},{7,11},{8,28},{9,... | collective-permute-start | bytes 208904 | tf_op jit(solution)/shard_map/ppermute | solution.py:286
  9.3 0.3 %collective-permute-start.2 = (s32[136,128]{1,0:T(8,128)S(1)}, s32[136,128]{1,0:T(8,128)S(1)}, u32[]{:S(2)}, u32[]{:S(2)}) collective-permute-start(s32[136,128]{1,0:T(8,128)S(1)} %get-tuple-element.28), channel_id=1, source_target_pairs={{0,16},{1,17},{2,10},{3,11},{4,20},{5,21},{6,14},{7,15},{8,24},{9,... | collective-permute-start | bytes 208904 | tf_op jit(solution)/shard_map/ppermute | solution.py:286
  9.7 0.3 %collective-permute-start.3 = (s32[136,128]{1,0:T(8,128)S(1)}, s32[136,128]{1,0:T(8,128)S(1)}, u32[]{:S(2)}, u32[]{:S(2)}) collective-permute-start(s32[136,128]{1,0:T(8,128)S(1)} %get-tuple-element.29), channel_id=1, source_target_pairs={{0,4},{1,5},{2,6},{3,7},{4,0},{5,1},{6,2},{7,3},{8,12},{9,13},{10,... | collective-permute-start | bytes 208904 | tf_op jit(solution)/shard_map/ppermute | solution.py:286
  10.0 1.8 %collective-permute-done.1.far_ref = s32[136,128]{1,0:T(8,128)S(1)} collective-permute-done((s32[136,128]{1,0:T(8,128)S(1)}, s32[136,128]{1,0:T(8,128)S(1)}, u32[]{:S(2)}, u32[]{:S(2)}) %collective-permute-start.1) | collective-permute-done | bytes 69664 | tf_op jit(solution)/shard_map/ppermute | solution.py:286
  11.8 0.2 add_far.1.total_ref
  11.9 2.6 %collective-permute-done.2.z_ref = s32[136,128]{1,0:T(8,128)S(1)} collective-permute-done((s32[136,128]{1,0:T(8,128)S(1)}, s32[136,128]{1,0:T(8,128)S(1)}, u32[]{:S(2)}, u32[]{:S(2)}) %collective-permute-start.2) | collective-permute-done | bytes 69664 | tf_op jit(solution)/shard_map/ppermute | solution.py:286
  14.5 0.3 add_square.1
  14.8 1.6 %collective-permute-start.4 = (s32[136,128]{1,0:T(8,128)S(1)}, s32[136,128]{1,0:T(8,128)S(1)}, u32[]{:S(2)}, u32[]{:S(2)}) collective-permute-start(s32[136,128]{1,0:T(8,128)S(1)} %get-tuple-element.31), channel_id=1, source_target_pairs={{0,8},{1,9},{2,18},{3,19},{4,12},{5,13},{6,22},{7,23},{8,0},{9,1},... | collective-permute-start | bytes 208904 | tf_op jit(solution)/shard_map/ppermute | solution.py:286
  16.5 2.7 %collective-permute-done.4.word_ref = s32[136,128]{1,0:T(8,128)S(1)} collective-permute-done((s32[136,128]{1,0:T(8,128)S(1)}, s32[136,128]{1,0:T(8,128)S(1)}, u32[]{:S(2)}, u32[]{:S(2)}) %collective-permute-start.4) | collective-permute-done | bytes 69664 | tf_op jit(solution)/shard_map/ppermute | solution.py:286
  19.2 0.2 sketch_rows.1
  19.4 0.1 collective-permute-start.5
  19.5 0.6 %collective-permute-start.6 = (bf16[272,128]{1,0:T(8,128)(2,1)S(1)}, bf16[272,128]{1,0:T(8,128)(2,1)S(1)}, u32[]{:S(2)}, u32[]{:S(2)}) collective-permute-start(bf16[272,128]{1,0:T(8,128)(2,1)S(1)} %get-tuple-element.34), channel_id=1, source_target_pairs={{0,4},{1,5},{2,3},{3,2},{4,0},{5,1},{6,7},{7,6},{8,12},{9,13},{10,... | collective-permute-start | bytes 208904 | tf_op jit(solution)/shard_map/ppermute | solution.py:286
  20.1 1.5 %collective-permute-start.7 = (bf16[272,128]{1,0:T(8,128)(2,1)S(1)}, bf16[272,128]{1,0:T(8,128)(2,1)S(1)}, u32[]{:S(2)}, u32[]{:S(2)}) collective-permute-start(bf16[272,128]{1,0:T(8,128)(2,1)S(1)} %get-tuple-element.35), channel_id=1, source_target_pairs={{0,1},{1,0},{2,6},{3,7},{4,5},{5,4},{6,2},{7,3},{8,9},{9,8},{10,14... | collective-permute-start | bytes 208904 | tf_op jit(solution)/shard_map/ppermute | solution.py:286
  21.6 2.0 %collective-permute-start.11 = (bf16[272,128]{1,0:T(8,128)(2,1)S(1)}, bf16[272,128]{1,0:T(8,128)(2,1)S(1)}, u32[]{:S(2)}, u32[]{:S(2)}) collective-permute-start(bf16[272,128]{1,0:T(8,128)(2,1)S(1)} %get-tuple-element.36), channel_id=1, source_target_pairs={{0,3},{1,2},{2,4},{3,5},{4,7},{5,6},{6,0},{7,1},{8,11},{9,10},{10,... | collective-permute-start | bytes 208904 | tf_op jit(solution)/shard_map/ppermute | solution.py:286
  23.6 0.5 %collective-permute-done.5.refs_1_ = bf16[272,128]{1,0:T(8,128)(2,1)S(1)} collective-permute-done((bf16[272,128]{1,0:T(8,128)(2,1)S(1)}, bf16[272,128]{1,0:T(8,128)(2,1)S(1)}, u32[]{:S(2)}, u32[]{:S(2)}) %collective-permute-start.5) | collective-permute-done | bytes 69664 | tf_op jit(solution)/shard_map/ppermute | solution.py:286
  24.2 0.1 collective-permute-done.6.refs_2_
  24.3 1.4 %collective-permute-start.10 = (bf16[272,128]{1,0:T(8,128)(2,1)S(1)}, bf16[272,128]{1,0:T(8,128)(2,1)S(1)}, u32[]{:S(2)}, u32[]{:S(2)}) collective-permute-start(bf16[272,128]{1,0:T(8,128)(2,1)S(1)} %collective-permute-done.6.refs_2_), channel_id=1, source_target_pairs={{0,2},{1,3},{2,0},{3,1},{4,6},{5,7},{6,4},{7,5},{8,10},{9,11},{10,... | collective-permute-start | bytes 208904 | tf_op jit(solution)/shard_map/ppermute | solution.py:286
  25.7 0.4 %collective-permute-done.11.refs_7_ = bf16[272,128]{1,0:T(8,128)(2,1)S(1)} collective-permute-done((bf16[272,128]{1,0:T(8,128)(2,1)S(1)}, bf16[272,128]{1,0:T(8,128)(2,1)S(1)}, u32[]{:S(2)}, u32[]{:S(2)}) %collective-permute-start.11) | collective-permute-done | bytes 69664 | tf_op jit(solution)/shard_map/ppermute | solution.py:286
  26.1 0.5 %collective-permute-done.10.refs_6_ = bf16[272,128]{1,0:T(8,128)(2,1)S(1)} collective-permute-done((bf16[272,128]{1,0:T(8,128)(2,1)S(1)}, bf16[272,128]{1,0:T(8,128)(2,1)S(1)}, u32[]{:S(2)}, u32[]{:S(2)}) %collective-permute-start.10) | collective-permute-done | bytes 69664 | tf_op jit(solution)/shard_map/ppermute | solution.py:286
  26.6 2.6 %gram.1 = f32[1024,1024]{1,0:T(8,128)} custom-call(bf16[272,128]{1,0:T(8,128)(2,1)S(1)} %get-tuple-element.32.refs_0_, bf16[272,128]{1,0:T(8,128)(2,1)S(1)} %collective-permute-done.5.refs_1_, bf16[272,128]{1,0:T(8,128)(2,1)S(1)} %collective-permute-done.6.refs_2_, bf16[272,128]{1,0:T(8,128)(2,1)S(1)} %collective-permute-done.7.refs_3_, ...), custom_call_target="tpu_custom_call" | custom-call | flops 536870912 | bytes 4194304 | tf_op jit(solution)/shard_map/gram/pallas_call | solution.py:177
  (9 shorter events, 0.0 us)
Async XLA Ops:
  0.0 19.2 %copy-start = (s32[128,1]{0,1:T(1,128)S(1)}, s32[128,1]{0,1:T(1,128)}, u32[]{:S(2)}) copy-start(s32[128,1]{0,1:T(1,128)} %param.7) | copy-start | bytes 1540
  2.5 1.8 %collective-permute-start = (f32[64,1024]{1,0:T(8,128)S(1)}, f32[64,1024]{1,0:T(8,128)S(1)}, u32[]{:S(2)}, u32[]{:S(2)}) collective-permute-start(f32[64,1024]{1,0:T(8,128)S(1)} %get-tuple-element.25), channel_id=1, source_target_pairs={{0,2},{1,3},{2,0},{3,1},{4,6},{5,7},{6,4},{7,5},{8,10},{9,11},{10,... | collective-permute-start | bytes 786440 | tf_op jit(solution)/shard_map/ppermute | solution.py:286
  4.5 7.3 %collective-permute-start.1 = (s32[136,128]{1,0:T(8,128)S(1)}, s32[136,128]{1,0:T(8,128)S(1)}, u32[]{:S(2)}, u32[]{:S(2)}) collective-permute-start(s32[136,128]{1,0:T(8,128)S(1)} %get-tuple-element.27), channel_id=1, source_target_pairs={{0,20},{1,21},{2,14},{3,15},{4,16},{5,17},{6,10},{7,11},{8,28},{9,... | collective-permute-start | bytes 208904 | tf_op jit(solution)/shard_map/ppermute | solution.py:286
  9.3 5.2 %collective-permute-start.2 = (s32[136,128]{1,0:T(8,128)S(1)}, s32[136,128]{1,0:T(8,128)S(1)}, u32[]{:S(2)}, u32[]{:S(2)}) collective-permute-start(s32[136,128]{1,0:T(8,128)S(1)} %get-tuple-element.28), channel_id=1, source_target_pairs={{0,16},{1,17},{2,10},{3,11},{4,20},{5,21},{6,14},{7,15},{8,24},{9,... | collective-permute-start | bytes 208904 | tf_op jit(solution)/shard_map/ppermute | solution.py:286
  9.7 4.9 %collective-permute-start.3 = (s32[136,128]{1,0:T(8,128)S(1)}, s32[136,128]{1,0:T(8,128)S(1)}, u32[]{:S(2)}, u32[]{:S(2)}) collective-permute-start(s32[136,128]{1,0:T(8,128)S(1)} %get-tuple-element.29), channel_id=1, source_target_pairs={{0,4},{1,5},{2,6},{3,7},{4,0},{5,1},{6,2},{7,3},{8,12},{9,13},{10,... | collective-permute-start | bytes 208904 | tf_op jit(solution)/shard_map/ppermute | solution.py:286
  14.8 4.4 %collective-permute-start.4 = (s32[136,128]{1,0:T(8,128)S(1)}, s32[136,128]{1,0:T(8,128)S(1)}, u32[]{:S(2)}, u32[]{:S(2)}) collective-permute-start(s32[136,128]{1,0:T(8,128)S(1)} %get-tuple-element.31), channel_id=1, source_target_pairs={{0,8},{1,9},{2,18},{3,19},{4,12},{5,13},{6,22},{7,23},{8,0},{9,1},... | collective-permute-start | bytes 208904 | tf_op jit(solution)/shard_map/ppermute | solution.py:286
  19.4 4.8 %collective-permute-start.5 = (bf16[272,128]{1,0:T(8,128)(2,1)S(1)}, bf16[272,128]{1,0:T(8,128)(2,1)S(1)}, u32[]{:S(2)}, u32[]{:S(2)}) collective-permute-start(bf16[272,128]{1,0:T(8,128)(2,1)S(1)} %get-tuple-element.33), channel_id=1, source_target_pairs={{0,7},{1,6},{2,5},{3,4},{4,3},{5,2},{6,1},{7,0},{8,15},{9,14},{10,... | collective-permute-start | bytes 208904 | tf_op jit(solution)/shard_map/ppermute | solution.py:286
  19.5 4.8 %collective-permute-start.6 = (bf16[272,128]{1,0:T(8,128)(2,1)S(1)}, bf16[272,128]{1,0:T(8,128)(2,1)S(1)}, u32[]{:S(2)}, u32[]{:S(2)}) collective-permute-start(bf16[272,128]{1,0:T(8,128)(2,1)S(1)} %get-tuple-element.34), channel_id=1, source_target_pairs={{0,4},{1,5},{2,3},{3,2},{4,0},{5,1},{6,7},{7,6},{8,12},{9,13},{10,... | collective-permute-start | bytes 208904 | tf_op jit(solution)/shard_map/ppermute | solution.py:286
  20.1 5.6 %collective-permute-start.7 = (bf16[272,128]{1,0:T(8,128)(2,1)S(1)}, bf16[272,128]{1,0:T(8,128)(2,1)S(1)}, u32[]{:S(2)}, u32[]{:S(2)}) collective-permute-start(bf16[272,128]{1,0:T(8,128)(2,1)S(1)} %get-tuple-element.35), channel_id=1, source_target_pairs={{0,1},{1,0},{2,6},{3,7},{4,5},{5,4},{6,2},{7,3},{8,9},{9,8},{10,14... | collective-permute-start | bytes 208904 | tf_op jit(solution)/shard_map/ppermute | solution.py:286
  21.6 4.5 %collective-permute-start.11 = (bf16[272,128]{1,0:T(8,128)(2,1)S(1)}, bf16[272,128]{1,0:T(8,128)(2,1)S(1)}, u32[]{:S(2)}, u32[]{:S(2)}) collective-permute-start(bf16[272,128]{1,0:T(8,128)(2,1)S(1)} %get-tuple-element.36), channel_id=1, source_target_pairs={{0,3},{1,2},{2,4},{3,5},{4,7},{5,6},{6,0},{7,1},{8,11},{9,10},{10,... | collective-permute-start | bytes 208904 | tf_op jit(solution)/shard_map/ppermute | solution.py:286
  23.6 2.5 %collective-permute-start.8 = (bf16[272,128]{1,0:T(8,128)(2,1)S(1)}, bf16[272,128]{1,0:T(8,128)(2,1)S(1)}, u32[]{:S(2)}, u32[]{:S(2)}) collective-permute-start(bf16[272,128]{1,0:T(8,128)(2,1)S(1)} %get-tuple-element.32.refs_0_), channel_id=1, source_target_pairs={{0,2},{1,3},{2,0},{3,1},{4,6},{5,7},{6,4},{7,5},{8,10},{9,11},{10,... | collective-permute-start | bytes 208904 | tf_op jit(solution)/shard_map/ppermute | solution.py:286
  24.2 1.9 %collective-permute-start.9 = (bf16[272,128]{1,0:T(8,128)(2,1)S(1)}, bf16[272,128]{1,0:T(8,128)(2,1)S(1)}, u32[]{:S(2)}, u32[]{:S(2)}) collective-permute-start(bf16[272,128]{1,0:T(8,128)(2,1)S(1)} %collective-permute-done.5.refs_1_), channel_id=1, source_target_pairs={{0,2},{1,3},{2,0},{3,1},{4,6},{5,7},{6,4},{7,5},{8,10},{9,11},{10,... | collective-permute-start | bytes 208904 | tf_op jit(solution)/shard_map/ppermute | solution.py:286
  24.3 2.3 %collective-permute-start.10 = (bf16[272,128]{1,0:T(8,128)(2,1)S(1)}, bf16[272,128]{1,0:T(8,128)(2,1)S(1)}, u32[]{:S(2)}, u32[]{:S(2)}) collective-permute-start(bf16[272,128]{1,0:T(8,128)(2,1)S(1)} %collective-permute-done.6.refs_2_), channel_id=1, source_target_pairs={{0,2},{1,3},{2,0},{3,1},{4,6},{5,7},{6,4},{7,5},{8,10},{9,11},{10,... | collective-permute-start | bytes 208904 | tf_op jit(solution)/shard_map/ppermute | solution.py:286

commit v27 on v26

--- a/solution.py
+++ b/solution.py
@@ -326,18 +326,18 @@
         total,
         word,
         labels.reshape(1, rows),
-        out_shape=[row_type] * 5,
+        out_shape=[row_type] * 4,
     )
     stride = 2
     while stride < tok_count:
-        copies = [jnp.concatenate([copies[0], swap(copies[0], (stride, 0))], axis=0)] * 4
+        copies = [jnp.concatenate([copies[0], swap(copies[0], (stride, 0))], axis=0)] * 3
         own = copies[0]
         stride *= 2
-    far = swap(copies[0], (1, 3))
-    second = swap(copies[1], (0, 2), (1, 0))
-    third = swap(copies[2], (1, 0), (0, 2))
-    crossed = swap(copies[3], (1, 1), (0, 3))
-    pieces = [own, far, second, third] + [swap(block, (0, 1)) for block in (own, far, second)] + [crossed]
+    crossed = swap(copies[0], (1, 1), (0, 3))
+    far = swap(copies[1], (1, 2))
+    second = swap(copies[2], (0, 2), (1, 0))
+    pieces = [own, crossed, far, second]
+    pieces += [swap(block, (0, 1)) for block in pieces]
     concepts = C // tok_count
     gram = gram_blocks(pieces, size, kept, concepts, shard, C / (rows * tok_count))
     return gram.reshape(concepts, shard, kept)

time: 29.3 us -> 29.8 us (1.017)
  waiting for transfers between devices: 8.7 us -> 11.2 us
  starting transfers between devices: 13.3 us -> 11.3 us
    ppermute x12, waiting for transfers between devices: 8.7 us -> 11.2 us  [swap(): return lax.ppermute(array, ('feat', 'tok'), pairs)]
    ppermute x12, starting transfers between devices: 13.3 us -> 11.3 us  [swap(): return lax.ppermute(array, ('feat', 'tok'), pairs)]
  transfers between devices with their start and end apart: 12 -> 12, of which waited for: 7 -> 8; matrix products, arithmetic and copies ran while one was open for 0% -> 0% of each run, Pallas kernels for 5% -> 5%
where the time goes in v27:
time: 29.8 us; the launch traced here: 29.7 us
  starting transfers between devices  11.3 us (38%)
  waiting for transfers between devices  11.2 us (38%)
  Pallas kernels  7.11 us (24%)
    ppermute x12, starting transfers between devices, swap(): return lax.ppermute(array, ('feat', 'tok'), pairs)  11.3 us
    ppermute x12, waiting for transfers between devices, swap(): return lax.ppermute(array, ('feat', 'tok'), pairs)  11.2 us
    pallas_call x1, Pallas kernels, gram_blocks(): pl.pallas_call(functools.partial(gram_kernel, shard, group, factor, size)...  2.55 us
    pallas_call x1, Pallas kernels, partial_halves(): pl.pallas_call(functools.partial(send_kernel, total_bits, parts), in_spec...  2.54 us
    pallas_call x1, Pallas kernels, partial_halves(): pl.pallas_call(functools.partial(keep_kernel, parts), out_shape=total_typ...  1.26 us
    pallas_call x4, Pallas kernels, local_call(): pl.pallas_call(kernel, out_shape=out_shape, compiler_params=pltpu.Compile...  0.76 us
  transfers between devices with their start and end apart: 12, of which 8 were waited for; matrix products, arithmetic and copies ran while one was open for 0% of the time, Pallas kernels for 5%

profile of v27, /device:TPU:0, one launch (start us, length us, event | category | flops | bytes accessed | tf_op | source)
XLA Modules:
  0.0 29.7 jit_solution(274332415265467959)
XLA Ops:
  0.0 2.5 %partial_sent.1 = (f32[64,1024]{1,0:T(8,128)S(1)}, bf16[64,8192]{1,0:T(8,128)(2,1)S(1)}, s32[1,8192]{1,0:T(1,128)S(1)}, bf16[256,1024]{1,0:T(8,128)(2,1)S(1)}, f32[32,1024]{1,0:T(8,128)S(1)}) custom-call(bf16[128,8192]{1,0:T(8,128)(2,1)} %x_hbm.1, s32[1,8192]{1,0:T(1,128)} %bitcast.5, s32[1,1024]{1,0:T(1,128)} %bitcast.6), custom_call_target="tpu_custom_call" | custom-call | flops 1073741824 | bytes 2359296 | tf_op jit(solution)/shard_map/partial_sent/pallas_call | solution.py:99
  2.5 0.5 %collective-permute-start = (f32[64,1024]{1,0:T(8,128)S(1)}, f32[64,1024]{1,0:T(8,128)S(1)}, u32[]{:S(2)}, u32[]{:S(2)}) collective-permute-start(f32[64,1024]{1,0:T(8,128)S(1)} %get-tuple-element.24), channel_id=1, source_target_pairs={{0,2},{1,3},{2,0},{3,1},{4,6},{5,7},{6,4},{7,5},{8,10},{9,11},{10,... | collective-permute-start | bytes 786440 | tf_op jit(solution)/shard_map/ppermute | solution.py:286
  3.1 1.3 %partial_kept.1.keep_ref = f32[64,1024]{1,0:T(8,128)S(1)} custom-call(bf16[64,8192]{1,0:T(8,128)(2,1)S(1)} %get-tuple-element.20.x_keep, s32[1,8192]{1,0:T(1,128)S(1)} %get-tuple-element.21.signs, bf16[256,1024]{1,0:T(8,128)(2,1)S(1)} %get-tuple-element.22.low, f32[32,1024]{1,0:T(8,128)S(1)} %get-tuple-element.23.high), custom_call_target="tpu_custom_call" | custom-call | flops 1073741824 | bytes 2359296 | tf_op jit(solution)/shard_map/partial_kept/pallas_call | solution.py:123
  4.3 0.2 first_split.1
  4.5 4.8 %collective-permute-start.1 = (s32[136,128]{1,0:T(8,128)S(1)}, s32[136,128]{1,0:T(8,128)S(1)}, u32[]{:S(2)}, u32[]{:S(2)}) collective-permute-start(s32[136,128]{1,0:T(8,128)S(1)} %get-tuple-element.26), channel_id=1, source_target_pairs={{0,20},{1,21},{2,14},{3,15},{4,16},{5,17},{6,10},{7,11},{8,28},{9,... | collective-permute-start | bytes 208904 | tf_op jit(solution)/shard_map/ppermute | solution.py:286
  9.3 0.3 %collective-permute-start.2 = (s32[136,128]{1,0:T(8,128)S(1)}, s32[136,128]{1,0:T(8,128)S(1)}, u32[]{:S(2)}, u32[]{:S(2)}) collective-permute-start(s32[136,128]{1,0:T(8,128)S(1)} %get-tuple-element.27), channel_id=1, source_target_pairs={{0,16},{1,17},{2,10},{3,11},{4,20},{5,21},{6,14},{7,15},{8,24},{9,... | collective-permute-start | bytes 208904 | tf_op jit(solution)/shard_map/ppermute | solution.py:286
  9.7 0.3 %collective-permute-start.3 = (s32[136,128]{1,0:T(8,128)S(1)}, s32[136,128]{1,0:T(8,128)S(1)}, u32[]{:S(2)}, u32[]{:S(2)}) collective-permute-start(s32[136,128]{1,0:T(8,128)S(1)} %get-tuple-element.28), channel_id=1, source_target_pairs={{0,4},{1,5},{2,6},{3,7},{4,0},{5,1},{6,2},{7,3},{8,12},{9,13},{10,... | collective-permute-start | bytes 208904 | tf_op jit(solution)/shard_map/ppermute | solution.py:286
  10.0 1.8 %collective-permute-done.1.far_ref = s32[136,128]{1,0:T(8,128)S(1)} collective-permute-done((s32[136,128]{1,0:T(8,128)S(1)}, s32[136,128]{1,0:T(8,128)S(1)}, u32[]{:S(2)}, u32[]{:S(2)}) %collective-permute-start.1) | collective-permute-done | bytes 69664 | tf_op jit(solution)/shard_map/ppermute | solution.py:286
  11.8 0.2 add_far.1.total_ref
  11.9 2.6 %collective-permute-done.2.z_ref = s32[136,128]{1,0:T(8,128)S(1)} collective-permute-done((s32[136,128]{1,0:T(8,128)S(1)}, s32[136,128]{1,0:T(8,128)S(1)}, u32[]{:S(2)}, u32[]{:S(2)}) %collective-permute-start.2) | collective-permute-done | bytes 69664 | tf_op jit(solution)/shard_map/ppermute | solution.py:286
  14.5 0.3 add_square.1
  14.8 1.6 %collective-permute-start.4 = (s32[136,128]{1,0:T(8,128)S(1)}, s32[136,128]{1,0:T(8,128)S(1)}, u32[]{:S(2)}, u32[]{:S(2)}) collective-permute-start(s32[136,128]{1,0:T(8,128)S(1)} %get-tuple-element.30), channel_id=1, source_target_pairs={{0,8},{1,9},{2,18},{3,19},{4,12},{5,13},{6,22},{7,23},{8,0},{9,1},... | collective-permute-start | bytes 208904 | tf_op jit(solution)/shard_map/ppermute | solution.py:286
  16.5 2.7 %collective-permute-done.4.word_ref = s32[136,128]{1,0:T(8,128)S(1)} collective-permute-done((s32[136,128]{1,0:T(8,128)S(1)}, s32[136,128]{1,0:T(8,128)S(1)}, u32[]{:S(2)}, u32[]{:S(2)}) %collective-permute-start.4) | collective-permute-done | bytes 69664 | tf_op jit(solution)/shard_map/ppermute | solution.py:286
  19.2 0.2 sketch_rows.1
  19.4 1.6 %collective-permute-start.6 = (bf16[272,128]{1,0:T(8,128)(2,1)S(1)}, bf16[272,128]{1,0:T(8,128)(2,1)S(1)}, u32[]{:S(2)}, u32[]{:S(2)}) collective-permute-start(bf16[272,128]{1,0:T(8,128)(2,1)S(1)} %get-tuple-element.33), channel_id=1, source_target_pairs={{0,5},{1,4},{2,7},{3,6},{4,1},{5,0},{6,3},{7,2},{8,13},{9,12},{10,... | collective-permute-start | bytes 208904 | tf_op jit(solution)/shard_map/ppermute | solution.py:286
  21.0 1.5 %collective-permute-start.7 = (bf16[272,128]{1,0:T(8,128)(2,1)S(1)}, bf16[272,128]{1,0:T(8,128)(2,1)S(1)}, u32[]{:S(2)}, u32[]{:S(2)}) collective-permute-start(bf16[272,128]{1,0:T(8,128)(2,1)S(1)} %get-tuple-element.34), channel_id=1, source_target_pairs={{0,4},{1,5},{2,3},{3,2},{4,0},{5,1},{6,7},{7,6},{8,12},{9,13},{10,... | collective-permute-start | bytes 208904 | tf_op jit(solution)/shard_map/ppermute | solution.py:286
  22.5 0.7 %collective-permute-done.5.refs_1_ = bf16[272,128]{1,0:T(8,128)(2,1)S(1)} collective-permute-done((bf16[272,128]{1,0:T(8,128)(2,1)S(1)}, bf16[272,128]{1,0:T(8,128)(2,1)S(1)}, u32[]{:S(2)}, u32[]{:S(2)}) %collective-permute-start.5) | collective-permute-done | bytes 69664 | tf_op jit(solution)/shard_map/ppermute | solution.py:286
  23.3 2.2 %collective-permute-done.6.refs_2_ = bf16[272,128]{1,0:T(8,128)(2,1)S(1)} collective-permute-done((bf16[272,128]{1,0:T(8,128)(2,1)S(1)}, bf16[272,128]{1,0:T(8,128)(2,1)S(1)}, u32[]{:S(2)}, u32[]{:S(2)}) %collective-permute-start.6) | collective-permute-done | bytes 69664 | tf_op jit(solution)/shard_map/ppermute | solution.py:286
  25.5 0.2 collective-permute-start.10
  25.6 0.2 collective-permute-done.7.refs_3_
  25.9 0.3 %collective-permute-start.11 = (bf16[272,128]{1,0:T(8,128)(2,1)S(1)}, bf16[272,128]{1,0:T(8,128)(2,1)S(1)}, u32[]{:S(2)}, u32[]{:S(2)}) collective-permute-start(bf16[272,128]{1,0:T(8,128)(2,1)S(1)} %collective-permute-done.7.refs_3_), channel_id=1, source_target_pairs={{0,2},{1,3},{2,0},{3,1},{4,6},{5,7},{6,4},{7,5},{8,10},{9,11},{10,... | collective-permute-start | bytes 208904 | tf_op jit(solution)/shard_map/ppermute | solution.py:286
  26.2 0.5 %collective-permute-done.10.refs_6_ = bf16[272,128]{1,0:T(8,128)(2,1)S(1)} collective-permute-done((bf16[272,128]{1,0:T(8,128)(2,1)S(1)}, bf16[272,128]{1,0:T(8,128)(2,1)S(1)}, u32[]{:S(2)}, u32[]{:S(2)}) %collective-permute-start.10) | collective-permute-done | bytes 69664 | tf_op jit(solution)/shard_map/ppermute | solution.py:286
  26.7 0.4 %collective-permute-done.11.refs_7_ = bf16[272,128]{1,0:T(8,128)(2,1)S(1)} collective-permute-done((bf16[272,128]{1,0:T(8,128)(2,1)S(1)}, bf16[272,128]{1,0:T(8,128)(2,1)S(1)}, u32[]{:S(2)}, u32[]{:S(2)}) %collective-permute-start.11) | collective-permute-done | bytes 69664 | tf_op jit(solution)/shard_map/ppermute | solution.py:286
  27.1 2.6 %gram.1 = f32[1024,1024]{1,0:T(8,128)} custom-call(bf16[272,128]{1,0:T(8,128)(2,1)S(1)} %get-tuple-element.31.refs_0_, bf16[272,128]{1,0:T(8,128)(2,1)S(1)} %collective-permute-done.5.refs_1_, bf16[272,128]{1,0:T(8,128)(2,1)S(1)} %collective-permute-done.6.refs_2_, bf16[272,128]{1,0:T(8,128)(2,1)S(1)} %collective-permute-done.7.refs_3_, ...), custom_call_target="tpu_custom_call" | custom-call | flops 536870912 | bytes 4194304 | tf_op jit(solution)/shard_map/gram/pallas_call | solution.py:177
  (9 shorter events, 0.2 us)
Async XLA Ops:
  0.0 19.2 %copy-start = (s32[128,1]{0,1:T(1,128)S(1)}, s32[128,1]{0,1:T(1,128)}, u32[]{:S(2)}) copy-start(s32[128,1]{0,1:T(1,128)} %param.7) | copy-start | bytes 1540
  2.5 1.8 %collective-permute-start = (f32[64,1024]{1,0:T(8,128)S(1)}, f32[64,1024]{1,0:T(8,128)S(1)}, u32[]{:S(2)}, u32[]{:S(2)}) collective-permute-start(f32[64,1024]{1,0:T(8,128)S(1)} %get-tuple-element.24), channel_id=1, source_target_pairs={{0,2},{1,3},{2,0},{3,1},{4,6},{5,7},{6,4},{7,5},{8,10},{9,11},{10,... | collective-permute-start | bytes 786440 | tf_op jit(solution)/shard_map/ppermute | solution.py:286
  4.5 7.3 %collective-permute-start.1 = (s32[136,128]{1,0:T(8,128)S(1)}, s32[136,128]{1,0:T(8,128)S(1)}, u32[]{:S(2)}, u32[]{:S(2)}) collective-permute-start(s32[136,128]{1,0:T(8,128)S(1)} %get-tuple-element.26), channel_id=1, source_target_pairs={{0,20},{1,21},{2,14},{3,15},{4,16},{5,17},{6,10},{7,11},{8,28},{9,... | collective-permute-start | bytes 208904 | tf_op jit(solution)/shard_map/ppermute | solution.py:286
  9.3 5.2 %collective-permute-start.2 = (s32[136,128]{1,0:T(8,128)S(1)}, s32[136,128]{1,0:T(8,128)S(1)}, u32[]{:S(2)}, u32[]{:S(2)}) collective-permute-start(s32[136,128]{1,0:T(8,128)S(1)} %get-tuple-element.27), channel_id=1, source_target_pairs={{0,16},{1,17},{2,10},{3,11},{4,20},{5,21},{6,14},{7,15},{8,24},{9,... | collective-permute-start | bytes 208904 | tf_op jit(solution)/shard_map/ppermute | solution.py:286
  9.7 4.9 %collective-permute-start.3 = (s32[136,128]{1,0:T(8,128)S(1)}, s32[136,128]{1,0:T(8,128)S(1)}, u32[]{:S(2)}, u32[]{:S(2)}) collective-permute-start(s32[136,128]{1,0:T(8,128)S(1)} %get-tuple-element.28), channel_id=1, source_target_pairs={{0,4},{1,5},{2,6},{3,7},{4,0},{5,1},{6,2},{7,3},{8,12},{9,13},{10,... | collective-permute-start | bytes 208904 | tf_op jit(solution)/shard_map/ppermute | solution.py:286
  14.8 4.4 %collective-permute-start.4 = (s32[136,128]{1,0:T(8,128)S(1)}, s32[136,128]{1,0:T(8,128)S(1)}, u32[]{:S(2)}, u32[]{:S(2)}) collective-permute-start(s32[136,128]{1,0:T(8,128)S(1)} %get-tuple-element.30), channel_id=1, source_target_pairs={{0,8},{1,9},{2,18},{3,19},{4,12},{5,13},{6,22},{7,23},{8,0},{9,1},... | collective-permute-start | bytes 208904 | tf_op jit(solution)/shard_map/ppermute | solution.py:286
  19.4 3.8 %collective-permute-start.5 = (bf16[272,128]{1,0:T(8,128)(2,1)S(1)}, bf16[272,128]{1,0:T(8,128)(2,1)S(1)}, u32[]{:S(2)}, u32[]{:S(2)}) collective-permute-start(bf16[272,128]{1,0:T(8,128)(2,1)S(1)} %get-tuple-element.32), channel_id=1, source_target_pairs={{0,3},{1,2},{2,4},{3,5},{4,7},{5,6},{6,0},{7,1},{8,11},{9,10},{10,... | collective-permute-start | bytes 208904 | tf_op jit(solution)/shard_map/ppermute | solution.py:286
  19.4 6.0 %collective-permute-start.6 = (bf16[272,128]{1,0:T(8,128)(2,1)S(1)}, bf16[272,128]{1,0:T(8,128)(2,1)S(1)}, u32[]{:S(2)}, u32[]{:S(2)}) collective-permute-start(bf16[272,128]{1,0:T(8,128)(2,1)S(1)} %get-tuple-element.33), channel_id=1, source_target_pairs={{0,5},{1,4},{2,7},{3,6},{4,1},{5,0},{6,3},{7,2},{8,13},{9,12},{10,... | collective-permute-start | bytes 208904 | tf_op jit(solution)/shard_map/ppermute | solution.py:286
  21.0 4.9 %collective-permute-start.7 = (bf16[272,128]{1,0:T(8,128)(2,1)S(1)}, bf16[272,128]{1,0:T(8,128)(2,1)S(1)}, u32[]{:S(2)}, u32[]{:S(2)}) collective-permute-start(bf16[272,128]{1,0:T(8,128)(2,1)S(1)} %get-tuple-element.34), channel_id=1, source_target_pairs={{0,4},{1,5},{2,3},{3,2},{4,0},{5,1},{6,7},{7,6},{8,12},{9,13},{10,... | collective-permute-start | bytes 208904 | tf_op jit(solution)/shard_map/ppermute | solution.py:286
  22.5 3.7 %collective-permute-start.8 = (bf16[272,128]{1,0:T(8,128)(2,1)S(1)}, bf16[272,128]{1,0:T(8,128)(2,1)S(1)}, u32[]{:S(2)}, u32[]{:S(2)}) collective-permute-start(bf16[272,128]{1,0:T(8,128)(2,1)S(1)} %get-tuple-element.31.refs_0_), channel_id=1, source_target_pairs={{0,2},{1,3},{2,0},{3,1},{4,6},{5,7},{6,4},{7,5},{8,10},{9,11},{10,... | collective-permute-start | bytes 208904 | tf_op jit(solution)/shard_map/ppermute | solution.py:286
  23.2 3.0 %collective-permute-start.9 = (bf16[272,128]{1,0:T(8,128)(2,1)S(1)}, bf16[272,128]{1,0:T(8,128)(2,1)S(1)}, u32[]{:S(2)}, u32[]{:S(2)}) collective-permute-start(bf16[272,128]{1,0:T(8,128)(2,1)S(1)} %collective-permute-done.5.refs_1_), channel_id=1, source_target_pairs={{0,2},{1,3},{2,0},{3,1},{4,6},{5,7},{6,4},{7,5},{8,10},{9,11},{10,... | collective-permute-start | bytes 208904 | tf_op jit(solution)/shard_map/ppermute | solution.py:286
  25.5 1.3 %collective-permute-start.10 = (bf16[272,128]{1,0:T(8,128)(2,1)S(1)}, bf16[272,128]{1,0:T(8,128)(2,1)S(1)}, u32[]{:S(2)}, u32[]{:S(2)}) collective-permute-start(bf16[272,128]{1,0:T(8,128)(2,1)S(1)} %collective-permute-done.6.refs_2_), channel_id=1, source_target_pairs={{0,2},{1,3},{2,0},{3,1},{4,6},{5,7},{6,4},{7,5},{8,10},{9,11},{10,... | collective-permute-start | bytes 208904 | tf_op jit(solution)/shard_map/ppermute | solution.py:286
  25.9 1.3 %collective-permute-start.11 = (bf16[272,128]{1,0:T(8,128)(2,1)S(1)}, bf16[272,128]{1,0:T(8,128)(2,1)S(1)}, u32[]{:S(2)}, u32[]{:S(2)}) collective-permute-start(bf16[272,128]{1,0:T(8,128)(2,1)S(1)} %collective-permute-done.7.refs_3_), channel_id=1, source_target_pairs={{0,2},{1,3},{2,0},{3,1},{4,6},{5,7},{6,4},{7,5},{8,10},{9,11},{10,... | collective-permute-start | bytes 208904 | tf_op jit(solution)/shard_map/ppermute | solution.py:286

commit v28 on v25

--- a/solution.py
+++ b/solution.py
@@ -330,9 +330,9 @@
         own = copies[0]
         stride *= 2
     far = swap(copies[0], (1, 3))
-    second = swap(copies[1], (0, 2), (1, 0))
-    third = swap(copies[2], (1, 0), (0, 2))
-    crossed = swap(copies[3], (1, 1), (0, 3))
+    second = swap(copies[1], (1, 0), (0, 2))
+    third = swap(copies[2], (0, 2), (1, 0))
+    crossed = swap(copies[3], (0, 3), (1, 1))
     pieces = [own, far, second, third] + [swap(block, (0, 1)) for block in (own, far, second)] + [crossed]
     concepts = C // tok_count
     gram = gram_blocks(pieces, size, kept, concepts, shard, C / (rows * tok_count))

time: 29.3 us -> 29.1 us (level)
  starting transfers between devices: 13.3 us -> 11.4 us
  waiting for transfers between devices: 8.86 us -> 10.5 us
    ppermute x12, starting transfers between devices: 13.3 us -> 11.4 us  [swap(): return lax.ppermute(array, ('feat', 'tok'), pairs)]
    ppermute x12, waiting for transfers between devices: 8.86 us -> 10.5 us  [swap(): return lax.ppermute(array, ('feat', 'tok'), pairs)]
where the time goes in v28:
time: 29.1 us; the launch traced here: 29 us
  starting transfers between devices  11.4 us (39%)
  waiting for transfers between devices  10.5 us (36%)
  Pallas kernels  7 us (24%)
    ppermute x12, starting transfers between devices, swap(): return lax.ppermute(array, ('feat', 'tok'), pairs)  11.4 us
    ppermute x12, waiting for transfers between devices, swap(): return lax.ppermute(array, ('feat', 'tok'), pairs)  10.5 us
    pallas_call x1, Pallas kernels, partial_halves(): pl.pallas_call(functools.partial(send_kernel, total_bits, parts), in_spec...  2.58 us
    pallas_call x1, Pallas kernels, gram_blocks(): pl.pallas_call(functools.partial(gram_kernel, shard, group, factor, size)...  2.56 us
    pallas_call x1, Pallas kernels, partial_halves(): pl.pallas_call(functools.partial(keep_kernel, parts), out_shape=total_typ...  1.26 us
    pallas_call x3, Pallas kernels, local_call(): pl.pallas_call(kernel, out_shape=out_shape, compiler_params=pltpu.Compile...  0.61 us
  transfers between devices with their start and end apart: 12, of which 7 were waited for; matrix products, arithmetic and copies ran while one was open for 0% of the time, Pallas kernels for 4%

profile of v28, /device:TPU:0, one launch (start us, length us, event | category | flops | bytes accessed | tf_op | source)
XLA Modules:
  0.0 29.0 jit_solution(18220702627134494351)
XLA Ops:
  0.0 2.6 %partial_sent.1 = (f32[64,1024]{1,0:T(8,128)S(1)}, bf16[64,8192]{1,0:T(8,128)(2,1)S(1)}, s32[1,8192]{1,0:T(1,128)S(1)}, bf16[256,1024]{1,0:T(8,128)(2,1)S(1)}, f32[32,1024]{1,0:T(8,128)S(1)}) custom-call(bf16[128,8192]{1,0:T(8,128)(2,1)} %x_hbm.1, s32[1,8192]{1,0:T(1,128)} %bitcast.5, s32[1,1024]{1,0:T(1,128)} %bitcast.6), custom_call_target="tpu_custom_call" | custom-call | flops 1073741824 | bytes 2359296 | tf_op jit(solution)/shard_map/partial_sent/pallas_call | solution.py:100
  2.6 0.5 %collective-permute-start = (f32[64,1024]{1,0:T(8,128)S(1)}, f32[64,1024]{1,0:T(8,128)S(1)}, u32[]{:S(2)}, u32[]{:S(2)}) collective-permute-start(f32[64,1024]{1,0:T(8,128)S(1)} %get-tuple-element.25), channel_id=1, source_target_pairs={{0,2},{1,3},{2,0},{3,1},{4,6},{5,7},{6,4},{7,5},{8,10},{9,11},{10,... | collective-permute-start | bytes 786440 | tf_op jit(solution)/shard_map/ppermute | solution.py:283
  3.1 1.3 %partial_kept.1.keep_ref = f32[64,1024]{1,0:T(8,128)S(1)} custom-call(bf16[64,8192]{1,0:T(8,128)(2,1)S(1)} %get-tuple-element.21.x_keep, s32[1,8192]{1,0:T(1,128)S(1)} %get-tuple-element.22.signs, bf16[256,1024]{1,0:T(8,128)(2,1)S(1)} %get-tuple-element.23.low, f32[32,1024]{1,0:T(8,128)S(1)} %get-tuple-element.24.high), custom_call_target="tpu_custom_call" | custom-call | flops 1073741824 | bytes 2359296 | tf_op jit(solution)/shard_map/partial_kept/pallas_call | solution.py:124
  4.4 0.2 first_split.1
  4.5 4.8 %collective-permute-start.1 = (s32[136,128]{1,0:T(8,128)S(1)}, s32[136,128]{1,0:T(8,128)S(1)}, u32[]{:S(2)}, u32[]{:S(2)}) collective-permute-start(s32[136,128]{1,0:T(8,128)S(1)} %get-tuple-element.27), channel_id=1, source_target_pairs={{0,20},{1,21},{2,14},{3,15},{4,16},{5,17},{6,10},{7,11},{8,28},{9,... | collective-permute-start | bytes 208904 | tf_op jit(solution)/shard_map/ppermute | solution.py:283
  9.4 0.3 %collective-permute-start.2 = (s32[136,128]{1,0:T(8,128)S(1)}, s32[136,128]{1,0:T(8,128)S(1)}, u32[]{:S(2)}, u32[]{:S(2)}) collective-permute-start(s32[136,128]{1,0:T(8,128)S(1)} %get-tuple-element.28), channel_id=1, source_target_pairs={{0,16},{1,17},{2,10},{3,11},{4,20},{5,21},{6,14},{7,15},{8,24},{9,... | collective-permute-start | bytes 208904 | tf_op jit(solution)/shard_map/ppermute | solution.py:283
  9.7 0.3 %collective-permute-start.3 = (s32[136,128]{1,0:T(8,128)S(1)}, s32[136,128]{1,0:T(8,128)S(1)}, u32[]{:S(2)}, u32[]{:S(2)}) collective-permute-start(s32[136,128]{1,0:T(8,128)S(1)} %get-tuple-element.29), channel_id=1, source_target_pairs={{0,4},{1,5},{2,6},{3,7},{4,0},{5,1},{6,2},{7,3},{8,12},{9,13},{10,... | collective-permute-start | bytes 208904 | tf_op jit(solution)/shard_map/ppermute | solution.py:283
  10.0 1.7 %collective-permute-done.1.both_ref = s32[136,128]{1,0:T(8,128)S(1)} collective-permute-done((s32[136,128]{1,0:T(8,128)S(1)}, s32[136,128]{1,0:T(8,128)S(1)}, u32[]{:S(2)}, u32[]{:S(2)}) %collective-permute-start.1) | collective-permute-done | bytes 69664 | tf_op jit(solution)/shard_map/ppermute | solution.py:283
  11.7 2.8 %collective-permute-done.2.z_ref = s32[136,128]{1,0:T(8,128)S(1)} collective-permute-done((s32[136,128]{1,0:T(8,128)S(1)}, s32[136,128]{1,0:T(8,128)S(1)}, u32[]{:S(2)}, u32[]{:S(2)}) %collective-permute-start.2) | collective-permute-done | bytes 69664 | tf_op jit(solution)/shard_map/ppermute | solution.py:283
  14.6 0.0 collective-permute-done.3.x_ref
  14.6 0.3 add_square.1
  14.9 1.6 %collective-permute-start.4 = (s32[136,128]{1,0:T(8,128)S(1)}, s32[136,128]{1,0:T(8,128)S(1)}, u32[]{:S(2)}, u32[]{:S(2)}) collective-permute-start(s32[136,128]{1,0:T(8,128)S(1)} %get-tuple-element.31), channel_id=1, source_target_pairs={{0,8},{1,9},{2,18},{3,19},{4,12},{5,13},{6,22},{7,23},{8,0},{9,1},... | collective-permute-start | bytes 208904 | tf_op jit(solution)/shard_map/ppermute | solution.py:283
  16.5 2.7 %collective-permute-done.4.word_ref = s32[136,128]{1,0:T(8,128)S(1)} collective-permute-done((s32[136,128]{1,0:T(8,128)S(1)}, s32[136,128]{1,0:T(8,128)S(1)}, u32[]{:S(2)}, u32[]{:S(2)}) %collective-permute-start.4) | collective-permute-done | bytes 69664 | tf_op jit(solution)/shard_map/ppermute | solution.py:283
  19.2 0.2 sketch_rows.1
  19.4 0.1 collective-permute-start.5
  19.5 1.6 %collective-permute-start.6 = (bf16[272,128]{1,0:T(8,128)(2,1)S(1)}, bf16[272,128]{1,0:T(8,128)(2,1)S(1)}, u32[]{:S(2)}, u32[]{:S(2)}) collective-permute-start(bf16[272,128]{1,0:T(8,128)(2,1)S(1)} %get-tuple-element.34), channel_id=1, source_target_pairs={{0,1},{1,0},{2,6},{3,7},{4,5},{5,4},{6,2},{7,3},{8,9},{9,8},{10,14... | collective-permute-start | bytes 208904 | tf_op jit(solution)/shard_map/ppermute | solution.py:283
  21.1 0.5 %collective-permute-start.7 = (bf16[272,128]{1,0:T(8,128)(2,1)S(1)}, bf16[272,128]{1,0:T(8,128)(2,1)S(1)}, u32[]{:S(2)}, u32[]{:S(2)}) collective-permute-start(bf16[272,128]{1,0:T(8,128)(2,1)S(1)} %get-tuple-element.35), channel_id=1, source_target_pairs={{0,4},{1,5},{2,3},{3,2},{4,0},{5,1},{6,7},{7,6},{8,12},{9,13},{10,... | collective-permute-start | bytes 208904 | tf_op jit(solution)/shard_map/ppermute | solution.py:283
  21.6 1.0 %collective-permute-start.11 = (bf16[272,128]{1,0:T(8,128)(2,1)S(1)}, bf16[272,128]{1,0:T(8,128)(2,1)S(1)}, u32[]{:S(2)}, u32[]{:S(2)}) collective-permute-start(bf16[272,128]{1,0:T(8,128)(2,1)S(1)} %get-tuple-element.36), channel_id=1, source_target_pairs={{0,6},{1,7},{2,1},{3,0},{4,2},{5,3},{6,5},{7,4},{8,14},{9,15},{10,... | collective-permute-start | bytes 208904 | tf_op jit(solution)/shard_map/ppermute | solution.py:283
  22.7 1.5 %collective-permute-done.5.refs_1_ = bf16[272,128]{1,0:T(8,128)(2,1)S(1)} collective-permute-done((bf16[272,128]{1,0:T(8,128)(2,1)S(1)}, bf16[272,128]{1,0:T(8,128)(2,1)S(1)}, u32[]{:S(2)}, u32[]{:S(2)}) %collective-permute-start.5) | collective-permute-done | bytes 69664 | tf_op jit(solution)/shard_map/ppermute | solution.py:283
  24.2 0.6 %collective-permute-done.6.refs_2_ = bf16[272,128]{1,0:T(8,128)(2,1)S(1)} collective-permute-done((bf16[272,128]{1,0:T(8,128)(2,1)S(1)}, bf16[272,128]{1,0:T(8,128)(2,1)S(1)}, u32[]{:S(2)}, u32[]{:S(2)}) %collective-permute-start.6) | collective-permute-done | bytes 69664 | tf_op jit(solution)/shard_map/ppermute | solution.py:283
  24.7 0.5 %collective-permute-start.10 = (bf16[272,128]{1,0:T(8,128)(2,1)S(1)}, bf16[272,128]{1,0:T(8,128)(2,1)S(1)}, u32[]{:S(2)}, u32[]{:S(2)}) collective-permute-start(bf16[272,128]{1,0:T(8,128)(2,1)S(1)} %collective-permute-done.6.refs_2_), channel_id=1, source_target_pairs={{0,2},{1,3},{2,0},{3,1},{4,6},{5,7},{6,4},{7,5},{8,10},{9,11},{10,... | collective-permute-start | bytes 208904 | tf_op jit(solution)/shard_map/ppermute | solution.py:283
  25.3 0.4 %collective-permute-done.7.refs_3_ = bf16[272,128]{1,0:T(8,128)(2,1)S(1)} collective-permute-done((bf16[272,128]{1,0:T(8,128)(2,1)S(1)}, bf16[272,128]{1,0:T(8,128)(2,1)S(1)}, u32[]{:S(2)}, u32[]{:S(2)}) %collective-permute-start.7) | collective-permute-done | bytes 69664 | tf_op jit(solution)/shard_map/ppermute | solution.py:283
  25.7 0.7 %collective-permute-done.11.refs_7_ = bf16[272,128]{1,0:T(8,128)(2,1)S(1)} collective-permute-done((bf16[272,128]{1,0:T(8,128)(2,1)S(1)}, bf16[272,128]{1,0:T(8,128)(2,1)S(1)}, u32[]{:S(2)}, u32[]{:S(2)}) %collective-permute-start.11) | collective-permute-done | bytes 69664 | tf_op jit(solution)/shard_map/ppermute | solution.py:283
  26.4 2.6 %gram.1 = f32[1024,1024]{1,0:T(8,128)} custom-call(bf16[272,128]{1,0:T(8,128)(2,1)S(1)} %get-tuple-element.32.refs_0_, bf16[272,128]{1,0:T(8,128)(2,1)S(1)} %collective-permute-done.5.refs_1_, bf16[272,128]{1,0:T(8,128)(2,1)S(1)} %collective-permute-done.6.refs_2_, bf16[272,128]{1,0:T(8,128)(2,1)S(1)} %collective-permute-done.7.refs_3_, ...), custom_call_target="tpu_custom_call" | custom-call | flops 536870912 | bytes 4194304 | tf_op jit(solution)/shard_map/gram/pallas_call | solution.py:178
  (8 shorter events, 0.0 us)
Async XLA Ops:
  0.0 19.2 %copy-start = (s32[128,1]{0,1:T(1,128)S(1)}, s32[128,1]{0,1:T(1,128)}, u32[]{:S(2)}) copy-start(s32[128,1]{0,1:T(1,128)} %param.7) | copy-start | bytes 1540
  2.6 1.8 %collective-permute-start = (f32[64,1024]{1,0:T(8,128)S(1)}, f32[64,1024]{1,0:T(8,128)S(1)}, u32[]{:S(2)}, u32[]{:S(2)}) collective-permute-start(f32[64,1024]{1,0:T(8,128)S(1)} %get-tuple-element.25), channel_id=1, source_target_pairs={{0,2},{1,3},{2,0},{3,1},{4,6},{5,7},{6,4},{7,5},{8,10},{9,11},{10,... | collective-permute-start | bytes 786440 | tf_op jit(solution)/shard_map/ppermute | solution.py:283
  4.5 7.2 %collective-permute-start.1 = (s32[136,128]{1,0:T(8,128)S(1)}, s32[136,128]{1,0:T(8,128)S(1)}, u32[]{:S(2)}, u32[]{:S(2)}) collective-permute-start(s32[136,128]{1,0:T(8,128)S(1)} %get-tuple-element.27), channel_id=1, source_target_pairs={{0,20},{1,21},{2,14},{3,15},{4,16},{5,17},{6,10},{7,11},{8,28},{9,... | collective-permute-start | bytes 208904 | tf_op jit(solution)/shard_map/ppermute | solution.py:283
  9.4 5.2 %collective-permute-start.2 = (s32[136,128]{1,0:T(8,128)S(1)}, s32[136,128]{1,0:T(8,128)S(1)}, u32[]{:S(2)}, u32[]{:S(2)}) collective-permute-start(s32[136,128]{1,0:T(8,128)S(1)} %get-tuple-element.28), channel_id=1, source_target_pairs={{0,16},{1,17},{2,10},{3,11},{4,20},{5,21},{6,14},{7,15},{8,24},{9,... | collective-permute-start | bytes 208904 | tf_op jit(solution)/shard_map/ppermute | solution.py:283
  9.7 4.9 %collective-permute-start.3 = (s32[136,128]{1,0:T(8,128)S(1)}, s32[136,128]{1,0:T(8,128)S(1)}, u32[]{:S(2)}, u32[]{:S(2)}) collective-permute-start(s32[136,128]{1,0:T(8,128)S(1)} %get-tuple-element.29), channel_id=1, source_target_pairs={{0,4},{1,5},{2,6},{3,7},{4,0},{5,1},{6,2},{7,3},{8,12},{9,13},{10,... | collective-permute-start | bytes 208904 | tf_op jit(solution)/shard_map/ppermute | solution.py:283
  14.9 4.4 %collective-permute-start.4 = (s32[136,128]{1,0:T(8,128)S(1)}, s32[136,128]{1,0:T(8,128)S(1)}, u32[]{:S(2)}, u32[]{:S(2)}) collective-permute-start(s32[136,128]{1,0:T(8,128)S(1)} %get-tuple-element.31), channel_id=1, source_target_pairs={{0,8},{1,9},{2,18},{3,19},{4,12},{5,13},{6,22},{7,23},{8,0},{9,1},... | collective-permute-start | bytes 208904 | tf_op jit(solution)/shard_map/ppermute | solution.py:283
  19.4 4.8 %collective-permute-start.5 = (bf16[272,128]{1,0:T(8,128)(2,1)S(1)}, bf16[272,128]{1,0:T(8,128)(2,1)S(1)}, u32[]{:S(2)}, u32[]{:S(2)}) collective-permute-start(bf16[272,128]{1,0:T(8,128)(2,1)S(1)} %get-tuple-element.33), channel_id=1, source_target_pairs={{0,7},{1,6},{2,5},{3,4},{4,3},{5,2},{6,1},{7,0},{8,15},{9,14},{10,... | collective-permute-start | bytes 208904 | tf_op jit(solution)/shard_map/ppermute | solution.py:283
  19.5 5.3 %collective-permute-start.6 = (bf16[272,128]{1,0:T(8,128)(2,1)S(1)}, bf16[272,128]{1,0:T(8,128)(2,1)S(1)}, u32[]{:S(2)}, u32[]{:S(2)}) collective-permute-start(bf16[272,128]{1,0:T(8,128)(2,1)S(1)} %get-tuple-element.34), channel_id=1, source_target_pairs={{0,1},{1,0},{2,6},{3,7},{4,5},{5,4},{6,2},{7,3},{8,9},{9,8},{10,14... | collective-permute-start | bytes 208904 | tf_op jit(solution)/shard_map/ppermute | solution.py:283
  21.1 4.6 %collective-permute-start.7 = (bf16[272,128]{1,0:T(8,128)(2,1)S(1)}, bf16[272,128]{1,0:T(8,128)(2,1)S(1)}, u32[]{:S(2)}, u32[]{:S(2)}) collective-permute-start(bf16[272,128]{1,0:T(8,128)(2,1)S(1)} %get-tuple-element.35), channel_id=1, source_target_pairs={{0,4},{1,5},{2,3},{3,2},{4,0},{5,1},{6,7},{7,6},{8,12},{9,13},{10,... | collective-permute-start | bytes 208904 | tf_op jit(solution)/shard_map/ppermute | solution.py:283
  21.6 4.8 %collective-permute-start.11 = (bf16[272,128]{1,0:T(8,128)(2,1)S(1)}, bf16[272,128]{1,0:T(8,128)(2,1)S(1)}, u32[]{:S(2)}, u32[]{:S(2)}) collective-permute-start(bf16[272,128]{1,0:T(8,128)(2,1)S(1)} %get-tuple-element.36), channel_id=1, source_target_pairs={{0,6},{1,7},{2,1},{3,0},{4,2},{5,3},{6,5},{7,4},{8,14},{9,15},{10,... | collective-permute-start | bytes 208904 | tf_op jit(solution)/shard_map/ppermute | solution.py:283
  22.7 3.7 %collective-permute-start.8 = (bf16[272,128]{1,0:T(8,128)(2,1)S(1)}, bf16[272,128]{1,0:T(8,128)(2,1)S(1)}, u32[]{:S(2)}, u32[]{:S(2)}) collective-permute-start(bf16[272,128]{1,0:T(8,128)(2,1)S(1)} %get-tuple-element.32.refs_0_), channel_id=1, source_target_pairs={{0,2},{1,3},{2,0},{3,1},{4,6},{5,7},{6,4},{7,5},{8,10},{9,11},{10,... | collective-permute-start | bytes 208904 | tf_op jit(solution)/shard_map/ppermute | solution.py:283
  24.2 2.2 %collective-permute-start.9 = (bf16[272,128]{1,0:T(8,128)(2,1)S(1)}, bf16[272,128]{1,0:T(8,128)(2,1)S(1)}, u32[]{:S(2)}, u32[]{:S(2)}) collective-permute-start(bf16[272,128]{1,0:T(8,128)(2,1)S(1)} %collective-permute-done.5.refs_1_), channel_id=1, source_target_pairs={{0,2},{1,3},{2,0},{3,1},{4,6},{5,7},{6,4},{7,5},{8,10},{9,11},{10,... | collective-permute-start | bytes 208904 | tf_op jit(solution)/shard_map/ppermute | solution.py:283
  24.7 1.6 %collective-permute-start.10 = (bf16[272,128]{1,0:T(8,128)(2,1)S(1)}, bf16[272,128]{1,0:T(8,128)(2,1)S(1)}, u32[]{:S(2)}, u32[]{:S(2)}) collective-permute-start(bf16[272,128]{1,0:T(8,128)(2,1)S(1)} %collective-permute-done.6.refs_2_), channel_id=1, source_target_pairs={{0,2},{1,3},{2,0},{3,1},{4,6},{5,7},{6,4},{7,5},{8,10},{9,11},{10,... | collective-permute-start | bytes 208904 | tf_op jit(solution)/shard_map/ppermute | solution.py:283
